TPU v7x, 32 devices: a whole 2x2x4 slice. The times are simulated.
32 devices in a mesh: groups: 2 (over y), seg: 4 (over z), sta: 2 (over x), pol: 2 (over core).
Axes of the slice: x: 2, y: 2, z: 4, core: 2. Of those that a mesh axis runs over, the one named last changes fastest.
Arguments:
- raw_spectra: bfloat16 [8, 16, 2, 2048], P(('groups', 'seg'), 'sta', None, 'pol'), parts along dimension 0
- owner_plan: int32 [6], P('groups'), parts along dimension 0, may hold values from 0 to 1
- pair_valid: int32 [8, 16, 16], P(('groups', 'seg'), None, 'sta'), parts along dimension 0, may hold values 0 or 1
- quality: int32 [8, 16], P(('groups', 'seg')), parts along dimension 0, may hold values 0 or 1
Outputs:
- pair_functions: float32 [6, 8, 16, 4096], P('groups', None, 'sta', ('seg', 'pol')), parts along dimension 0
There are 2 independent parts, one for each index of `groups`. A program takes and returns all parts, laid end to end along the dimension named above; each array names one. Nothing has to cross between parts.
All inputs are finite; a program needn't handle non-finite values. No bound on the sum of `pair_valid` or of `quality` on one device may be relied on, other than what follows from the above.
Results may differ from a plain program's by a relative error of at most 0.0041.
Values may be sent and summed in bfloat16 or wider, within the bound.
No kernel may reach another device: no remote copies, remote signals or barrier semaphores. Data moves between devices by JAX's collectives and lax.ppermute only.
A program may use at most 64 MiB of HBM per device.

v0:
```python
import math

import jax
import jax.numpy as jnp
from jax import lax
from jax.sharding import PartitionSpec as P

STEPS = 3
BAND = 128


def broadcast(block, axis, source):
    block = jnp.where(lax.axis_index(axis) == source, block, jnp.zeros_like(block))
    return lax.psum(block, axis)


def whiten(raw_values, band_len):
    values = raw_values.astype(jnp.float32)
    dims_all = values.shape
    blocks = values.reshape(dims_all[0], dims_all[1], 2, dims_all[3] // band_len, band_len)
    power = jnp.mean(blocks * blocks, axis=(2, 4), keepdims=True)
    return (blocks / jnp.sqrt(power + 1e-06)).reshape(dims_all).astype(jnp.bfloat16)


def cross_stack(source, locals_white, weight):
    high = lax.Precision.HIGHEST
    real_src = source[:, :, 0].astype(jnp.float32)
    imag_src = source[:, :, 1].astype(jnp.float32)
    real_loc = locals_white[:, :, 0].astype(jnp.float32)
    imag_loc = locals_white[:, :, 1].astype(jnp.float32)
    real_part = jnp.einsum(
        "gij,gif,gjf->ijf", weight, real_src, real_loc, precision=high
    ) + jnp.einsum("gij,gif,gjf->ijf", weight, imag_src, imag_loc, precision=high)
    imag_part = jnp.einsum(
        "gij,gif,gjf->ijf", weight, imag_src, real_loc, precision=high
    ) - jnp.einsum("gij,gif,gjf->ijf", weight, real_src, imag_loc, precision=high)
    return jnp.stack([real_part, imag_part], axis=2)


def lag_table(first_lag, count, bin_first, bin_count, total_lags):
    lag_index = first_lag + jnp.arange(count, dtype=jnp.int32)
    bin_index = bin_first + jnp.arange(bin_count, dtype=jnp.int32)
    phase = lag_index[:, None] * bin_index[None, :] % total_lags
    angle = phase.astype(jnp.float32) * jnp.float32(2.0 * math.pi / total_lags)
    factor = jnp.where(bin_index == 0, 1.0, 2.0).astype(jnp.float32)[None, :]
    return jnp.concatenate([jnp.cos(angle) * factor, -jnp.sin(angle) * factor], axis=1)


def transform(flat, first_lag, count, bin_first, bin_count, total_lags):
    block_len = 128
    blocks_count = count // block_len

    def one_block(block_id):
        table = lag_table(
            first_lag + block_id * block_len, block_len, bin_first, bin_count, total_lags
        )
        return lax.dot_general(
            table,
            flat,
            (((1,), (1,)), ((), ())),
            precision=lax.Precision.HIGHEST,
            preferred_element_type=jnp.float32,
        )

    result = lax.map(one_block, jnp.arange(blocks_count, dtype=jnp.int32))
    return result.reshape(count, flat.shape[0])


def shards(raw_spectra, owner_plan, pair_valid, quality):
    seg_count, station_count, _, bin_count = raw_spectra.shape
    total_lags = 2 * bin_count * lax.axis_size("pol")
    segment_total = seg_count * lax.axis_size("seg")
    scale = 1.0 / math.sqrt(bin_count * lax.axis_size("pol") * segment_total)
    bin_first = lax.axis_index("pol") * bin_count
    owned_white = whiten(raw_spectra, BAND)
    flags = quality.astype(jnp.float32)
    local_flags = lax.dynamic_slice_in_dim(
        flags, lax.axis_index("sta") * station_count, station_count, 1
    )
    stacks = []
    for step in range(STEPS):
        first = owner_plan[step] * station_count
        source = whiten(broadcast(raw_spectra, "sta", owner_plan[step]), BAND)
        valid = lax.dynamic_slice_in_dim(pair_valid, first, station_count, 1).astype(jnp.float32)
        source_flags = lax.dynamic_slice_in_dim(flags, first, station_count, 1)
        weight = valid * source_flags[:, :, None] * local_flags[:, None, :]
        stacks.append(cross_stack(source, owned_white, weight))
    pair_count = STEPS * station_count * station_count
    flat = (jnp.stack(stacks) * scale).reshape(pair_count, 2 * bin_count)
    lag_rows = total_lags // (lax.axis_size("seg") * lax.axis_size("pol"))
    shares = lax.psum_scatter(flat, "seg", scatter_dimension=0, tiled=True)
    partial_lags = transform(shares, 0, total_lags, bin_first, bin_count, total_lags)
    moved = lax.all_to_all(partial_lags, "seg", split_axis=0, concat_axis=1, tiled=True)
    summed = lax.psum_scatter(moved, "pol", scatter_dimension=0, tiled=True)
    return jnp.transpose(summed).reshape(STEPS, station_count, station_count, lag_rows)


def solution(mesh):
    placed = (
        P(("groups", "seg"), "sta", None, "pol"),
        P("groups"),
        P(("groups", "seg"), None, "sta"),
        P(("groups", "seg"), None),
    )
    return jax.shard_map(
        shards,
        mesh=mesh,
        in_specs=placed,
        out_specs=P("groups", None, "sta", ("seg", "pol")),
        check_vma=False,
    )
```

profile of v0, /device:TPU:0, one launch (start us, length us, event | category | flops | bytes accessed | tf_op | source)
XLA Modules:
  0.0 303.8 jit_solution(14506578424154899249)
XLA Ops:
  16.8 18.6 %all-reduce.3.cloned.1.call-done = (bf16[1,8,2,1024]{3,1,2,0:T(8,128)(2,1)}, bf16[1,8,2,1024]{3,1,2,0:T(8,128)(2,1)}, bf16[1,8,2,1024]{3,1,2,0:T(8,128)(2,1)}) async-done(((bf16[1,8,2,1024]{3,1,2,0:T(8,128)(2,1)}, bf16[1,8,2,1024]{3,1,2,0:T(8,128)(2,1)}, bf16[1,8,2,1024]{3,1,2,0:T(8,128)(2,1)}), (bf16[1,8,2,1024]{3,1,2,0:T(8,128)(2,1)}, bf16[1,8,2,1024]{3,1,2,0:T(8,128)(2,1)}, ...) | async-done | bytes 98320 | tf_op jit(solution)/shard_map/psum | solution.py:14
  41.7 35.4 %reduce-scatter.3.cloned.1.call-done = f32[48,2048]{1,0:T(8,128)} async-done(((f32[192,2048]{1,0:T(8,128)}), f32[48,2048]{1,0:T(8,128)}) %reduce-scatter.3.cloned.1.call-update) | async-done | bytes 393232 | tf_op jit(solution)/shard_map/reduce_scatter | solution.py:91
  77.1 188.6 %while.12 = (s32[]{:T(128)}, f32[32,128,48]{1,0,2:T(8,128)S(1)}, s32[32]{0:T(128)S(1)}, s32[]{:T(128)}, f32[48,2048]{1,0:T(8,128)}, /*index=5*/s32[]{:T(128)}, s32[1]{0:T(128)}, s32[]{:T(128)}) while((s32[]{:T(128)}, f32[32,128,48]{1,0,2:T(8,128)S(1)}, s32[32]{0:T(128)S(1)}, s32[]{:T(128)}, f32[48,2048]{1,0:T(8,128)}, ...), condition=%wide.region_13.14_spmd, body=%wide.region_12.13_spmd.sunk | while | flops 153489536 | bytes 2581629 | solution.py:65
  86.6 2.2 fusion.49
  92.5 2.2 fusion.49
  98.4 2.2 fusion.49
  104.3 2.2 fusion.49
  121.9 2.2 fusion.49
  127.8 2.2 fusion.49
  133.7 2.2 fusion.49
  139.6 2.2 fusion.49
  157.3 2.2 fusion.49
  163.2 2.2 fusion.49
  169.1 2.2 fusion.49
  175.0 2.2 fusion.49
  192.7 2.2 fusion.49
  198.6 2.2 fusion.49
  204.4 2.2 fusion.49
  210.3 2.2 fusion.49
  228.0 2.2 fusion.49
  233.9 2.2 fusion.49
  239.8 2.2 fusion.49
  266.5 23.3 %all_to_all.19 = f32[4,1024,48]{1,2,0:T(8,128)} all-to-all(f32[4,1024,48]{1,2,0:T(8,128)S(1)} %copy.57), channel_id=1, replica_groups=mesh['groups'=2,'seg'=4,'sta'=2,'pol'=2] {'seg'}, dimensions={0} | all-to-all | bytes 1572864 | tf_op jit(solution)/shard_map/all_to_all | solution.py:93
  289.8 7.4 %reduce-scatter.5.cloned.1.call-done = f32[512,192]{0,1:T(8,128)} async-done(((f32[1024,192]{0,1:T(8,128)}), f32[512,192]{0,1:T(8,128)}) %reduce-scatter.5.cloned.1.call-update) | async-done | bytes 393232 | tf_op jit(solution)/shard_map/reduce_scatter | solution.py:94
  (251 shorter events, 136.6 us)
Async XLA Ops:
  6.5 28.9 %all-reduce.3.cloned.1.call-start = ((), (), s32[]{:S(2)}) async-start(), calls=%async_computation.5 | async-start | bytes 196608 | tf_op jit(solution)/shard_map/psum | solution.py:14
  11.3 65.9 %reduce-scatter.3.cloned.1.call-start = ((), (), s32[]{:S(2)}) async-start(), calls=%async_computation.3 | async-start | bytes 1966080 | tf_op jit(solution)/shard_map/reduce_scatter | solution.py:91
  41.7 255.6 %reduce-scatter.5.cloned.1.call-start = ((), (), s32[]{:S(2)}) async-start(), calls=%async_computation.4 | async-start | bytes 1179648 | tf_op jit(solution)/shard_map/reduce_scatter | solution.py:94
Sparse Core Ops, SparseCore 0:
  11.4 24.0 all-reduce.2
  41.8 35.3 reduce-scatter.2
  289.9 7.2 reduce-scatter.4
where the time goes:
time: 306 us; the launch traced here: 304 us
  other arithmetic  79.2 us (26%)
  matrix products  69.6 us (23%)
  waiting for transfers between devices  61.5 us (20%)
  local copies, waits for them, and re-layouts  29 us (9%)
  loops' own time  24.1 us (8%)
  blocking collectives  23.3 us (8%)
  between operations  17 us (6%)
    dot_general x32, matrix products, one_block(): lax.dot_general(table, flat, (((1,), (1,)), ((), ())), precision=lax.Prec...  69.6 us
    mul x32, other arithmetic, lag_table(): jnp.cos(angle) * factor  69.1 us
    reduce_scatter x1, waiting for transfers between devices, shards(): shares = lax.psum_scatter(flat, 'seg', scatter_dimension=0, tiled=True)  35.4 us
    another operation x1, loops' own time, transform(): result = lax.map(one_block, jnp.arange(blocks_count, dtype=jnp.int32))  24.1 us
    all_to_all x1, blocking collectives, shards(): lax.all_to_all(partial_lags, 'seg', split_axis=0, concat_axis=1, tiled=True)  23.3 us
    dynamic_slice x32, local copies, waits for them, and re-layouts, transform(): result = lax.map(one_block, jnp.arange(blocks_count, dtype=jnp.int32))  21.3 us
    psum x1, waiting for transfers between devices, broadcast(): return lax.psum(block, axis)  18.6 us
    reduce_scatter x1, waiting for transfers between devices, shards(): summed = lax.psum_scatter(moved, 'pol', scatter_dimension=0, tiled=True)  7.44 us
  transfers between devices with their start and end apart: 3, of which 3 were waited for; matrix products, arithmetic and copies ran while one was open for 1% of the time, Pallas kernels for 0%

commit v1 on v0

v1 whole, which is shorter than its diff:
```python
import functools
import math

import jax
import jax.numpy as jnp
import numpy as np
from jax import lax
from jax.experimental import pallas as pl
from jax.experimental.pallas import tpu as pltpu
from jax.sharding import PartitionSpec as P

STEPS = 3
BAND = 128
LANES = 128


def lag_table(lags, bins, scale):
    bin_index = np.arange(bins, dtype=np.int64)
    phase = (bin_index[:, None] * np.arange(lags, dtype=np.int64)[None, :]) % (2 * bins)
    angle = phase * (2.0 * math.pi / (2 * bins))
    factor = np.where(bin_index == 0, 1.0, 2.0)[:, None] * scale
    parts = np.stack([np.cos(angle) * factor, -np.sin(angle) * factor])
    parts = parts.reshape(2, bins // LANES, LANES, lags).transpose(1, 0, 2, 3)
    return parts.reshape(2 * bins, lags).astype(jnp.bfloat16)


def phase_table(blocks):
    phase = (np.arange(blocks)[:, None] * np.arange(LANES)[None, :]) % blocks
    angle = phase * (2.0 * math.pi / blocks)
    parts = np.stack([np.cos(angle), np.sin(angle)], axis=1).astype(np.float32)
    return np.repeat(parts[:, :, None, :], 8, axis=2)


def prepare_kernel(sizes, plan_ref, raw_ref, valid_ref, quality_ref, out_ref, wide):
    stations, bands, sta, blocks, weight_rows = sizes
    total = stations * sta
    me = lax.axis_index("sta")
    wide[...] = raw_ref[...].astype(jnp.float32)
    count = stations * bands
    real = wide[pl.ds(0, count, stride=2), :]
    imag = wide[pl.ds(1, count, stride=2), :]
    power = jnp.sum(real * real + imag * imag, axis=1, keepdims=True) * (1.0 / (2 * BAND))
    inverse = 1.0 / jnp.sqrt(power + 1e-06)
    real = (real * inverse).reshape(stations, bands, LANES)
    imag = (imag * inverse).reshape(stations, bands, LANES)
    white = jnp.concatenate([real, imag], axis=1).reshape(2 * count, LANES)
    out_ref[pl.ds(0, 2 * count), :] = white.astype(jnp.bfloat16)

    valid = valid_ref[...].astype(jnp.float32).astype(jnp.bfloat16)
    quality = jnp.broadcast_to(quality_ref[...].astype(jnp.float32), (8, total)).astype(jnp.bfloat16)
    rows = []
    for row in range(weight_rows):
        pair = row * LANES + lax.broadcasted_iota(jnp.int32, (total, LANES), 1)
        station = lax.broadcasted_iota(jnp.int32, (total, LANES), 0)
        block = pair // (stations * stations)
        first = jnp.zeros_like(pair)
        for k in range(blocks):
            owner = k if sta == blocks else plan_ref[k]
            first = jnp.where(block == k, owner * stations, first)
        source = first + pair // stations % stations
        local = me * stations + pair % stations
        pick_source = (station == source).astype(jnp.float32).astype(jnp.bfloat16)
        pick_local = (station == local).astype(jnp.float32).astype(jnp.bfloat16)
        dot = functools.partial(jnp.dot, preferred_element_type=jnp.float32)
        valid_pairs = dot(valid, pick_source)
        mine = lax.broadcasted_iota(jnp.int32, (stations, LANES), 0) == (
            lax.broadcasted_iota(jnp.int32, (stations, LANES), 1) % stations
        )
        valid_row = jnp.sum(jnp.where(mine, valid_pairs, 0.0), axis=0, keepdims=True)
        flags = dot(quality, pick_source) * dot(quality, pick_local)
        rows.append(valid_row * flags[:1])
    rows.append(jnp.zeros((16 - weight_rows, LANES), jnp.float32))
    out_ref[pl.ds(2 * count, 16), :] = jnp.concatenate(rows, axis=0).astype(jnp.bfloat16)


def stack_kernel(
    sizes, plan_ref, spectra_ref, table_ref, phase_ref, out_ref, wide_weight, local, real_x, imag_x, packed, lags_x
):
    stations, bands, seg, sta, pol, blocks, weight_rows = sizes
    pairs = blocks * stations * stations
    me = lax.axis_index("sta")
    lag_block = lax.axis_index("seg") * pol + lax.axis_index("pol")

    diagonal = lax.broadcasted_iota(jnp.int32, (LANES, LANES), 0) == lax.broadcasted_iota(
        jnp.int32, (LANES, LANES), 1
    )
    ones = jnp.ones((LANES, LANES), jnp.bfloat16)
    for g in range(seg):
        rows = spectra_ref[(g * sta + me) * pol, pl.ds(2 * stations * bands, 16), :].astype(jnp.float32)
        for row in range(weight_rows):
            spread = jnp.where(diagonal, rows[row : row + 1], 0.0).astype(jnp.bfloat16)
            wide_weight[g, pl.ds(row * LANES, LANES), :] = jnp.dot(
                spread, ones, preferred_element_type=jnp.float32
            )

    cosine = phase_ref[lag_block, 0]
    sine = phase_ref[lag_block, 1]
    for p in range(pol):
        for g in range(seg):
            for j in range(stations):
                tile = spectra_ref[(g * sta + me) * pol + p, pl.ds(j * 16, 16), :].astype(jnp.float32)
                local[g, j, 0] = tile[:8] * cosine + tile[8:] * sine
                local[g, j, 1] = tile[8:] * cosine - tile[:8] * sine
        for k in range(blocks):
            owner = k if sta == blocks else plan_ref[k]

            def one_source(a, carry):
                start = pl.multiple_of(a * 16, 16)
                tiles = [
                    spectra_ref[(g * sta + owner) * pol + p, pl.ds(start, 16), :].astype(jnp.float32)
                    for g in range(seg)
                ]
                for j in range(stations):
                    pair = (k * stations + a) * stations + j
                    real_sum = imag_sum = None
                    for g in range(seg):
                        weight = jnp.broadcast_to(wide_weight[g, pl.ds(pair, 1), :], (8, LANES))
                        real_src = tiles[g][:8] * weight
                        imag_src = tiles[g][8:] * weight
                        real_loc = local[g, j, 0]
                        imag_loc = local[g, j, 1]
                        real_term = real_src * real_loc + imag_src * imag_loc
                        imag_term = imag_src * real_loc - real_src * imag_loc
                        real_sum = real_term if g == 0 else real_sum + real_term
                        imag_sum = imag_term if g == 0 else imag_sum + imag_term
                    at = pl.ds(pl.multiple_of(pair * 8, 8), 8)
                    real_x[at, :] = real_sum
                    imag_x[at, :] = imag_sum
                return carry

            lax.fori_loop(0, stations, one_source, 0)
        for band in range(bands):
            column = (p * bands + band) * 2 * LANES
            packed[:, pl.ds(column, LANES)] = real_x[pl.ds(band, pairs, stride=8), :].astype(jnp.bfloat16)
            packed[:, pl.ds(column + LANES, LANES)] = imag_x[pl.ds(band, pairs, stride=8), :].astype(jnp.bfloat16)
    lags_x[...] = jnp.dot(packed[...], table_ref[...], preferred_element_type=jnp.float32)
    block_pairs = stations * stations
    for step in range(STEPS):
        first = (plan_ref[step] if sta == blocks else step) * block_pairs
        out_ref[step] = lags_x[pl.ds(pl.multiple_of(first, block_pairs), block_pairs), :]


def shards(table, phases, raw_spectra, owner_plan, pair_valid, quality):
    seg, sta, pol = (lax.axis_size(name) for name in ("seg", "sta", "pol"))
    _, stations, _, bins = raw_spectra.shape
    bands = bins // BAND
    blocks = min(sta, STEPS)
    pairs = blocks * stations * stations
    weight_rows = -(-pairs // LANES)
    lags = table.shape[1]
    rows = 2 * stations * bands + 16

    raw = raw_spectra.reshape(stations, 2, bands, BAND).transpose(0, 2, 1, 3).reshape(-1, BAND)
    vmem = pl.BlockSpec(memory_space=pltpu.VMEM)
    smem = pl.BlockSpec(memory_space=pltpu.SMEM)
    payload = pl.pallas_call(
        functools.partial(prepare_kernel, (stations, bands, sta, blocks, weight_rows)),
        out_shape=jax.ShapeDtypeStruct((rows, LANES), jnp.bfloat16),
        in_specs=[smem, vmem, vmem, vmem],
        out_specs=vmem,
        scratch_shapes=[pltpu.VMEM((2 * stations * bands, LANES), jnp.float32)],
        name="prepare",
    )(owner_plan, raw, jnp.transpose(pair_valid[0]), quality)

    spectra = lax.all_gather(payload, ("seg", "sta", "pol"))

    out = pl.pallas_call(
        functools.partial(stack_kernel, (stations, bands, seg, sta, pol, blocks, weight_rows)),
        out_shape=jax.ShapeDtypeStruct((STEPS, stations * stations, lags), jnp.float32),
        in_specs=[smem, vmem, vmem, vmem],
        out_specs=vmem,
        scratch_shapes=[
            pltpu.VMEM((seg, weight_rows * LANES, LANES), jnp.float32),
            pltpu.VMEM((seg, stations, 2, 8, LANES), jnp.float32),
            pltpu.VMEM((pairs * 8, LANES), jnp.float32),
            pltpu.VMEM((pairs * 8, LANES), jnp.float32),
            pltpu.VMEM((pairs, table.shape[0]), jnp.bfloat16),
            pltpu.VMEM((pairs, lags), jnp.float32),
        ],
        compiler_params=pltpu.CompilerParams(vmem_limit_bytes=48 * 1024 * 1024),
        name="stack",
    )(owner_plan, spectra, table, phases)
    return out.reshape(STEPS, stations, stations, lags)


def solution(mesh):
    placed = (
        P(("groups", "seg"), "sta", None, "pol"),
        P("groups"),
        P(("groups", "seg"), None, "sta"),
        P(("groups", "seg"), None),
    )

    def whole(raw_spectra, owner_plan, pair_valid, quality):
        seg, pol = mesh.shape["seg"], mesh.shape["pol"]
        bins = raw_spectra.shape[3]
        segments = raw_spectra.shape[0] // mesh.shape["groups"]
        lag_blocks = seg * pol
        table = lag_table(2 * bins // lag_blocks, bins, 1.0 / math.sqrt(bins * segments))
        phases = phase_table(lag_blocks)
        return jax.shard_map(
            shards,
            mesh=mesh,
            in_specs=(P(), P()) + placed,
            out_specs=P("groups", None, "sta", ("seg", "pol")),
            check_vma=False,
        )(jnp.asarray(table), jnp.asarray(phases), raw_spectra, owner_plan, pair_valid, quality)

    return whole
```

time: 306 us -> 34.7 us (0.11)
  other arithmetic: 79.2 us -> 0 us
  matrix products: 69.6 us -> 0 us
  waiting for transfers between devices: 61.5 us -> 0 us
  local copies, waits for them, and re-layouts: 29 us -> 3.68 us
  loops' own time: 24.1 us -> 0 us
  between operations: 17 us -> 0.01 us
  Pallas kernels: 0 us -> 5.68 us
    mul x33 -> x0, other arithmetic: 70.4 us -> none  [the longest x32 69.1 us: lag_table(): jnp.cos(angle) * factor]
    dot_general x32 -> x0, matrix products: 69.6 us -> none  [one_block(): lax.dot_general(table, flat, (((1,), (1,)), ((), ())), precision=lax.Prec...]
    reduce_scatter x2 -> x0, waiting for transfers between devices: 42.8 us -> none  [the longest x1 35.4 us: shards(): shares = lax.psum_scatter(flat, 'seg', scatter_dimension=0, tiled=True)]
    all_gather x0 -> x1, blocking collectives: none -> 25 us  [shards(): spectra = lax.all_gather(payload, ('seg', 'sta', 'pol'))]
    another operation x1 -> x0, loops' own time: 24.1 us -> none  [transform(): result = lax.map(one_block, jnp.arange(blocks_count, dtype=jnp.int32))]
    all_to_all x1 -> x0, blocking collectives: 23.3 us -> none  [shards(): lax.all_to_all(partial_lags, 'seg', split_axis=0, concat_axis=1, tiled=True)]
    dynamic_slice x33 -> x0, local copies, waits for them, and re-layouts: 22.2 us -> none  [the longest x32 21.3 us: transform(): result = lax.map(one_block, jnp.arange(blocks_count, dtype=jnp.int32))]
    psum x1 -> x0, waiting for transfers between devices: 18.6 us -> none  [broadcast(): return lax.psum(block, axis)]
  transfers between devices with their start and end apart: 3 -> 0, of which waited for: 3 -> 0; matrix products, arithmetic and copies ran while one was open for 1% -> 0% of each run, Pallas kernels for 0% -> 0%
where the time goes in v1:
time: 34.7 us; the launch traced here: 34.4 us
  blocking collectives  25 us (72%)
  Pallas kernels  5.68 us (16%)
  local copies, waits for them, and re-layouts  3.68 us (11%)
    all_gather x1, blocking collectives, shards(): spectra = lax.all_gather(payload, ('seg', 'sta', 'pol'))  25 us
    pallas_call x1, Pallas kernels, shards(): pl.pallas_call(functools.partial(stack_kernel, (stations, bands, seg, sta...  4.12 us
    unnamed x6, local copies, waits for them, and re-layouts  3.68 us
    pallas_call x1, Pallas kernels, shards(): pl.pallas_call(functools.partial(prepare_kernel, (stations, bands, sta, b...  1.56 us

profile of v1, /device:TPU:0, one launch (start us, length us, event | category | flops | bytes accessed | tf_op | source)
XLA Modules:
  0.0 34.4 jit_solution(15407203817796344889)
XLA Ops:
  0.0 1.6 %prepare.1 = bf16[144,128]{1,0:T(8,128)(2,1)} custom-call(s32[3]{0:T(128)} %plan_ref.3, bf16[128,128]{1,0:T(8,128)(2,1)} %bitcast.11, s32[8,16]{1,0:T(8,128)} %bitcast.12, s32[1,16]{1,0:T(1,128)} %quality_ref.1), custom_call_target="tpu_custom_call" | custom-call | tf_op jit(solution)/shard_map/prepare/pallas_call | solution.py:156
  1.6 25.0 %all-gather = bf16[2304,128]{1,0:T(8,128)(2,1)S(1)} all-gather(bf16[144,128]{1,0:T(8,128)(2,1)} %prepare.1), channel_id=2, replica_groups=mesh['groups'=2,'seg'=4,'sta'=2,'pol'=2] {'seg','sta','pol'}, dimensions={0}, use_global_device_ids=true | all-gather | bytes 626688 | tf_op jit(solution)/shard_map/all_gather | solution.py:165
  26.6 0.0 copy-start
  26.6 2.2 %copy-done = bf16[4096,512]{1,0:T(8,128)(2,1)S(1)} copy-done((bf16[4096,512]{1,0:T(8,128)(2,1)S(1)}, bf16[4096,512]{1,0:T(8,128)(2,1)}, u32[]{:S(2)}) %copy-start) | copy-done | bytes 4194328
  28.8 0.0 copy-start.1
  28.8 0.8 %copy-done.1 = f32[8,2,8,128]{3,2,1,0:T(8,128)S(1)} copy-done((f32[8,2,8,128]{3,2,1,0:T(8,128)S(1)}, f32[8,2,8,128]{3,2,1,0:T(8,128)}, u32[]{:S(2)}) %copy-start.1) | copy-done | bytes 65560
  29.6 0.0 copy-start.2
  29.6 0.7 %copy-done.2 = s32[3]{0:T(128)S(1)} copy-done((s32[3]{0:T(128)S(1)}, s32[3]{0:T(128)}, u32[]{:S(2)}) %copy-start.2) | copy-done | bytes 36
  30.3 4.1 %stack.1 = f32[3,64,512]{2,1,0:T(8,128)} custom-call(s32[3]{0:T(128)S(1)} %copy-done.2, bf16[16,144,128]{2,1,0:T(8,128)(2,1)S(1)} %bitcast.10, bf16[4096,512]{1,0:T(8,128)(2,1)S(1)} %copy-done, f32[8,2,8,128]{3,2,1,0:T(8,128)S(1)} %copy-done.1), custom_call_target="tpu_custom_call" | custom-call | tf_op jit(solution)/shard_map/stack/pallas_call | solution.py:167
Async XLA Ops:
  26.6 2.2 %copy-start = (bf16[4096,512]{1,0:T(8,128)(2,1)S(1)}, bf16[4096,512]{1,0:T(8,128)(2,1)}, u32[]{:S(2)}) copy-start(bf16[4096,512]{1,0:T(8,128)(2,1)} %constant.4.clone.table_ref) | copy-start | bytes 12582916
  28.8 0.8 %copy-start.1 = (f32[8,2,8,128]{3,2,1,0:T(8,128)S(1)}, f32[8,2,8,128]{3,2,1,0:T(8,128)}, u32[]{:S(2)}) copy-start(f32[8,2,8,128]{3,2,1,0:T(8,128)} %constant.5.clone.phase_ref) | copy-start | bytes 196612
  29.6 0.7 %copy-start.2 = (s32[3]{0:T(128)S(1)}, s32[3]{0:T(128)}, u32[]{:S(2)}) copy-start(s32[3]{0:T(128)} %plan_ref.3) | copy-start | bytes 40

commit v2 on v1

--- a/solution.py
+++ b/solution.py
@@ -73,71 +73,111 @@
     out_ref[pl.ds(2 * count, 16), :] = jnp.concatenate(rows, axis=0).astype(jnp.bfloat16)
 
 
-def stack_kernel(
-    sizes, plan_ref, spectra_ref, table_ref, phase_ref, out_ref, wide_weight, local, real_x, imag_x, packed, lags_x
-):
+def partner(index, step, size):
+    return index ^ step if size & (size - 1) == 0 else (index + step) % size
+
+
+def half_kernel(sizes, distance, *refs):
     stations, bands, seg, sta, pol, blocks, weight_rows = sizes
+    held = seg * sta
+    plan_ref, table_hbm, phase_hbm = refs[:3]
+    spectra_hbm = refs[3 : 3 + held]
+    rest = refs[3 + held :]
+    if distance:
+        before_hbm, rest = rest[0], rest[1:]
+    out_ref, table, phase, spectra, before, wide_weight, local, real_x, imag_x, packed, sems = rest
+    last = distance == pol - 1
     pairs = blocks * stations * stations
     me = lax.axis_index("sta")
     lag_block = lax.axis_index("seg") * pol + lax.axis_index("pol")
+    half = partner(lax.axis_index("pol"), distance, pol)
+    rows = 2 * bands * LANES
+
+    copies = [pltpu.make_async_copy(spectra_hbm[n], spectra.at[n], sems.at[n]) for n in range(held)]
+    copies.append(pltpu.make_async_copy(phase_hbm.at[lag_block], phase, sems.at[held]))
+    late = [
+        pltpu.make_async_copy(
+            table_hbm.at[pl.ds(pl.multiple_of(half * rows, rows), rows)], table, sems.at[held + 1]
+        )
+    ]
+    if distance:
+        late.append(pltpu.make_async_copy(before_hbm, before, sems.at[held + 2]))
+    for copy in copies + late:
+        copy.start()
+    for copy in copies:
+        copy.wait()
 
     diagonal = lax.broadcasted_iota(jnp.int32, (LANES, LANES), 0) == lax.broadcasted_iota(
         jnp.int32, (LANES, LANES), 1
     )
     ones = jnp.ones((LANES, LANES), jnp.bfloat16)
     for g in range(seg):
-        rows = spectra_ref[(g * sta + me) * pol, pl.ds(2 * stations * bands, 16), :].astype(jnp.float32)
+        flags = spectra[g * sta, pl.ds(2 * stations * bands, 16), :].astype(jnp.float32)
         for row in range(weight_rows):
-            spread = jnp.where(diagonal, rows[row : row + 1], 0.0).astype(jnp.bfloat16)
+            spread = jnp.where(diagonal, flags[row : row + 1], 0.0).astype(jnp.bfloat16)
             wide_weight[g, pl.ds(row * LANES, LANES), :] = jnp.dot(
                 spread, ones, preferred_element_type=jnp.float32
             )
 
-    cosine = phase_ref[lag_block, 0]
-    sine = phase_ref[lag_block, 1]
-    for p in range(pol):
-        for g in range(seg):
+    cosine = phase[0]
+    sine = phase[1]
+    for g in range(seg):
+        for j in range(stations):
+            tile = spectra[g * sta, pl.ds(j * 16, 16), :].astype(jnp.float32)
+            local[g, j, 0] = tile[:8] * cosine + tile[8:] * sine
+            local[g, j, 1] = tile[8:] * cosine - tile[:8] * sine
+    for k in range(blocks):
+        owner = partner(k if sta == blocks else plan_ref[k], me, sta)
+
+        def one_source(a, carry):
+            start = pl.multiple_of(a * 16, 16)
+            tiles = [
+                spectra[g * sta + owner, pl.ds(start, 16), :].astype(jnp.float32) for g in range(seg)
+            ]
             for j in range(stations):
-                tile = spectra_ref[(g * sta + me) * pol + p, pl.ds(j * 16, 16), :].astype(jnp.float32)
-                local[g, j, 0] = tile[:8] * cosine + tile[8:] * sine
-                local[g, j, 1] = tile[8:] * cosine - tile[:8] * sine
-        for k in range(blocks):
-            owner = k if sta == blocks else plan_ref[k]
-
-            def one_source(a, carry):
-                start = pl.multiple_of(a * 16, 16)
-                tiles = [
-                    spectra_ref[(g * sta + owner) * pol + p, pl.ds(start, 16), :].astype(jnp.float32)
-                    for g in range(seg)
-                ]
-                for j in range(stations):
-                    pair = (k * stations + a) * stations + j
-                    real_sum = imag_sum = None
-                    for g in range(seg):
-                        weight = jnp.broadcast_to(wide_weight[g, pl.ds(pair, 1), :], (8, LANES))
-                        real_src = tiles[g][:8] * weight
-                        imag_src = tiles[g][8:] * weight
-                        real_loc = local[g, j, 0]
-                        imag_loc = local[g, j, 1]
-                        real_term = real_src * real_loc + imag_src * imag_loc
-                        imag_term = imag_src * real_loc - real_src * imag_loc
-                        real_sum = real_term if g == 0 else real_sum + real_term
-                        imag_sum = imag_term if g == 0 else imag_sum + imag_term
-                    at = pl.ds(pl.multiple_of(pair * 8, 8), 8)
-                    real_x[at, :] = real_sum
-                    imag_x[at, :] = imag_sum
-                return carry
-
-            lax.fori_loop(0, stations, one_source, 0)
-        for band in range(bands):
-            column = (p * bands + band) * 2 * LANES
-            packed[:, pl.ds(column, LANES)] = real_x[pl.ds(band, pairs, stride=8), :].astype(jnp.bfloat16)
-            packed[:, pl.ds(column + LANES, LANES)] = imag_x[pl.ds(band, pairs, stride=8), :].astype(jnp.bfloat16)
-    lags_x[...] = jnp.dot(packed[...], table_ref[...], preferred_element_type=jnp.float32)
+                pair = (k * stations + a) * stations + j
+                real_sum = imag_sum = None
+                for g in range(seg):
+                    weight = jnp.broadcast_to(wide_weight[g, pl.ds(pair, 1), :], (8, LANES))
+                    real_src = tiles[g][:8] * weight
+                    imag_src = tiles[g][8:] * weight
+                    real_loc = local[g, j, 0]
+                    imag_loc = local[g, j, 1]
+                    real_term = real_src * real_loc + imag_src * imag_loc
+                    imag_term = imag_src * real_loc - real_src * imag_loc
+                    real_sum = real_term if g == 0 else real_sum + real_term
+                    imag_sum = imag_term if g == 0 else imag_sum + imag_term
+                at = pl.ds(pl.multiple_of(pair * 8, 8), 8)
+                real_x[at, :] = real_sum
+                imag_x[at, :] = imag_sum
+            return carry
+
+        lax.fori_loop(0, stations, one_source, 0)
+    for band in range(bands):
+        column = band * 2 * LANES
+        packed[:, pl.ds(column, LANES)] = real_x[pl.ds(band, pairs, stride=8), :].astype(jnp.bfloat16)
+        packed[:, pl.ds(column + LANES, LANES)] = imag_x[pl.ds(band, pairs, stride=8), :].astype(jnp.bfloat16)
+    for copy in late:
+        copy.wait()
+    part = jnp.dot(packed[...], table[...], preferred_element_type=jnp.float32)
+    if distance:
+        part = before[...] + part
+    if not last:
+        out_ref[...] = part
+        return
+    before[...] = part
     block_pairs = stations * stations
     for step in range(STEPS):
         first = (plan_ref[step] if sta == blocks else step) * block_pairs
-        out_ref[step] = lags_x[pl.ds(pl.multiple_of(first, block_pairs), block_pairs), :]
+        out_ref[step] = before[pl.ds(pl.multiple_of(first, block_pairs), block_pairs), :]
+
+
+def swap(value, axes, sizes, steps):
+    pairs = []
+    for index in np.ndindex(*sizes):
+        source = tuple(partner(i, d, n) for i, d, n in zip(index, steps, sizes))
+        pairs.append((int(np.ravel_multi_index(source, sizes)), int(np.ravel_multi_index(index, sizes))))
+    return lax.ppermute(value, axes, pairs)
 
 
 def shards(table, phases, raw_spectra, owner_plan, pair_valid, quality):
@@ -153,6 +193,7 @@
     raw = raw_spectra.reshape(stations, 2, bands, BAND).transpose(0, 2, 1, 3).reshape(-1, BAND)
     vmem = pl.BlockSpec(memory_space=pltpu.VMEM)
     smem = pl.BlockSpec(memory_space=pltpu.SMEM)
+    anywhere = pl.BlockSpec(memory_space=pl.ANY)
     payload = pl.pallas_call(
         functools.partial(prepare_kernel, (stations, bands, sta, blocks, weight_rows)),
         out_shape=jax.ShapeDtypeStruct((rows, LANES), jnp.bfloat16),
@@ -162,24 +203,40 @@
         name="prepare",
     )(owner_plan, raw, jnp.transpose(pair_valid[0]), quality)
 
-    spectra = lax.all_gather(payload, ("seg", "sta", "pol"))
-
-    out = pl.pallas_call(
-        functools.partial(stack_kernel, (stations, bands, seg, sta, pol, blocks, weight_rows)),
-        out_shape=jax.ShapeDtypeStruct((STEPS, stations * stations, lags), jnp.float32),
-        in_specs=[smem, vmem, vmem, vmem],
-        out_specs=vmem,
-        scratch_shapes=[
-            pltpu.VMEM((seg, weight_rows * LANES, LANES), jnp.float32),
-            pltpu.VMEM((seg, stations, 2, 8, LANES), jnp.float32),
-            pltpu.VMEM((pairs * 8, LANES), jnp.float32),
-            pltpu.VMEM((pairs * 8, LANES), jnp.float32),
-            pltpu.VMEM((pairs, table.shape[0]), jnp.bfloat16),
-            pltpu.VMEM((pairs, lags), jnp.float32),
-        ],
-        compiler_params=pltpu.CompilerParams(vmem_limit_bytes=48 * 1024 * 1024),
-        name="stack",
-    )(owner_plan, spectra, table, phases)
+    spectra = [
+        swap(payload, ("seg", "sta"), (seg, sta), (g, q)) if g or q else payload
+        for g in range(seg)
+        for q in range(sta)
+    ]
+    held = len(spectra)
+    sizes = (stations, bands, seg, sta, pol, blocks, weight_rows)
+    out = None
+    for distance in range(pol):
+        last = distance == pol - 1
+        theirs = [swap(x, ("pol",), (pol,), (distance,)) for x in spectra] if distance else spectra
+        out_shape = (STEPS, stations * stations, lags) if last else (pairs, lags)
+        flops = 2 * pairs * 2 * bins * lags
+        out = pl.pallas_call(
+            functools.partial(half_kernel, sizes, distance),
+            out_shape=jax.ShapeDtypeStruct(out_shape, jnp.float32),
+            in_specs=[smem] + [anywhere] * (2 + held + (1 if distance else 0)),
+            out_specs=vmem,
+            scratch_shapes=[
+                pltpu.VMEM((2 * bins, lags), jnp.bfloat16),
+                pltpu.VMEM((2, 8, LANES), jnp.float32),
+                pltpu.VMEM((held, rows, LANES), jnp.bfloat16),
+                pltpu.VMEM((pairs, lags), jnp.float32),
+                pltpu.VMEM((seg, weight_rows * LANES, LANES), jnp.float32),
+                pltpu.VMEM((seg, stations, 2, 8, LANES), jnp.float32),
+                pltpu.VMEM((pairs * 8, LANES), jnp.float32),
+                pltpu.VMEM((pairs * 8, LANES), jnp.float32),
+                pltpu.VMEM((pairs, 2 * bins), jnp.bfloat16),
+                pltpu.SemaphoreType.DMA((held + 3,)),
+            ],
+            compiler_params=pltpu.CompilerParams(vmem_limit_bytes=48 * 1024 * 1024),
+            cost_estimate=pl.CostEstimate(flops=8 * flops, bytes_accessed=4 * 1024 * 1024, transcendentals=0),
+            name="stack_first" if distance == 0 else "stack_rest",
+        )(owner_plan, table, phases, *theirs, *([out] if distance else []))
     return out.reshape(STEPS, stations, stations, lags)
 
 

time: 34.7 us -> 30.2 us (0.87)
  blocking collectives: 25 us -> 0 us
  starting transfers between devices: 0 us -> 13.9 us
  waiting for transfers between devices: 0 us -> 3.39 us
  Pallas kernels: 5.68 us -> 8.08 us
  local copies, waits for them, and re-layouts: 3.68 us -> 4.45 us
    all_gather x1 -> x0, blocking collectives: 25 us -> none  [shards(): spectra = lax.all_gather(payload, ('seg', 'sta', 'pol'))]
    ppermute x0 -> x15, starting transfers between devices: none -> 13.9 us  [swap(): return lax.ppermute(value, axes, pairs)]
    ppermute x0 -> x15, waiting for transfers between devices: none -> 3.39 us  [swap(): return lax.ppermute(value, axes, pairs)]
    pallas_call x1 -> x2, Pallas kernels: 4.12 us -> 6.52 us  [shards(): pl.pallas_call(functools.partial(half_kernel, sizes, distance), out_shape...]
    unnamed x6 -> x8, local copies, waits for them, and re-layouts: 3.68 us -> 4.45 us
  transfers between devices with their start and end apart: 0 -> 15, of which waited for: 0 -> 5; matrix products, arithmetic and copies ran while one was open for 0% -> 0% of each run, Pallas kernels for 0% -> 10%
where the time goes in v2:
time: 30.2 us; the launch traced here: 29.9 us
  starting transfers between devices  13.9 us (46%)
  Pallas kernels  8.08 us (27%)
  local copies, waits for them, and re-layouts  4.45 us (15%)
  waiting for transfers between devices  3.39 us (11%)
    ppermute x15, starting transfers between devices, swap(): return lax.ppermute(value, axes, pairs)  13.9 us
    pallas_call x2, Pallas kernels, shards(): pl.pallas_call(functools.partial(half_kernel, sizes, distance), out_shape...  6.52 us
    unnamed x8, local copies, waits for them, and re-layouts  4.45 us
    ppermute x15, waiting for transfers between devices, swap(): return lax.ppermute(value, axes, pairs)  3.39 us
    pallas_call x1, Pallas kernels, shards(): pl.pallas_call(functools.partial(prepare_kernel, (stations, bands, sta, b...  1.56 us
  transfers between devices with their start and end apart: 15, of which 5 were waited for; matrix products, arithmetic and copies ran while one was open for 0% of the time, Pallas kernels for 10%

profile of v2, /device:TPU:0, one launch (start us, length us, event | category | flops | bytes accessed | tf_op | source)
XLA Modules:
  0.0 29.9 jit_solution(3293949737884584290)
XLA Ops:
  0.0 1.6 %prepare.1.refs_3_ = bf16[144,128]{1,0:T(8,128)(2,1)} custom-call(s32[3]{0:T(128)} %refs_0_.3, bf16[128,128]{1,0:T(8,128)(2,1)} %bitcast.9, s32[8,16]{1,0:T(8,128)} %bitcast.10, s32[1,16]{1,0:T(1,128)} %quality_ref.1), custom_call_target="tpu_custom_call" | custom-call | tf_op jit(solution)/shard_map/prepare/pallas_call | solution.py:197
  1.6 6.0 %collective-permute-start.13 = (bf16[144,128]{1,0:T(8,128)(2,1)}, bf16[144,128]{1,0:T(8,128)(2,1)S(1)}, u32[]{:S(2)}, u32[]{:S(2)}) collective-permute-start(bf16[144,128]{1,0:T(8,128)(2,1)} %prepare.1.refs_3_), channel_id=1, source_target_pairs={{14,0},{12,2},{10,4},{8,6},{6,8},{4,10},{2,12},{0,14},{15,1},{13,3... | collective-permute-start | bytes 110600 | tf_op jit(solution)/shard_map/ppermute | solution.py:180
  7.5 0.2 collective-permute-start.11
  7.8 0.8 %collective-permute-start.9 = (bf16[144,128]{1,0:T(8,128)(2,1)}, bf16[144,128]{1,0:T(8,128)(2,1)S(1)}, u32[]{:S(2)}, u32[]{:S(2)}) collective-permute-start(bf16[144,128]{1,0:T(8,128)(2,1)} %prepare.1.refs_3_), channel_id=1, source_target_pairs={{10,0},{8,2},{14,4},{12,6},{2,8},{0,10},{6,12},{4,14},{11,1},{9,3}... | collective-permute-start | bytes 110600 | tf_op jit(solution)/shard_map/ppermute | solution.py:180
  8.5 1.9 %collective-permute-start.7 = (bf16[144,128]{1,0:T(8,128)(2,1)}, bf16[144,128]{1,0:T(8,128)(2,1)S(1)}, u32[]{:S(2)}, u32[]{:S(2)}) collective-permute-start(bf16[144,128]{1,0:T(8,128)(2,1)} %prepare.1.refs_3_), channel_id=1, source_target_pairs={{8,0},{10,2},{12,4},{14,6},{0,8},{2,10},{4,12},{6,14},{9,1},{11,3}... | collective-permute-start | bytes 110600 | tf_op jit(solution)/shard_map/ppermute | solution.py:180
  10.5 2.4 %collective-permute-start.5 = (bf16[144,128]{1,0:T(8,128)(2,1)}, bf16[144,128]{1,0:T(8,128)(2,1)S(1)}, u32[]{:S(2)}, u32[]{:S(2)}) collective-permute-start(bf16[144,128]{1,0:T(8,128)(2,1)} %prepare.1.refs_3_), channel_id=1, source_target_pairs={{6,0},{4,2},{2,4},{0,6},{14,8},{12,10},{10,12},{8,14},{7,1},{5,3},... | collective-permute-start | bytes 110600 | tf_op jit(solution)/shard_map/ppermute | solution.py:180
  12.8 0.8 %collective-permute-start.3 = (bf16[144,128]{1,0:T(8,128)(2,1)}, bf16[144,128]{1,0:T(8,128)(2,1)S(1)}, u32[]{:S(2)}, u32[]{:S(2)}) collective-permute-start(bf16[144,128]{1,0:T(8,128)(2,1)} %prepare.1.refs_3_), channel_id=1, source_target_pairs={{4,0},{6,2},{0,4},{2,6},{12,8},{14,10},{8,12},{10,14},{5,1},{7,3},... | collective-permute-start | bytes 110600 | tf_op jit(solution)/shard_map/ppermute | solution.py:180
  13.6 0.6 %collective-permute-start.1 = (bf16[144,128]{1,0:T(8,128)(2,1)}, bf16[144,128]{1,0:T(8,128)(2,1)S(1)}, u32[]{:S(2)}, u32[]{:S(2)}) collective-permute-start(bf16[144,128]{1,0:T(8,128)(2,1)} %prepare.1.refs_3_), channel_id=1, source_target_pairs={{2,0},{0,2},{6,4},{4,6},{10,8},{8,10},{14,12},{12,14},{3,1},{1,3},... | collective-permute-start | bytes 110600 | tf_op jit(solution)/shard_map/ppermute | solution.py:180
  14.2 0.3 collective-permute-done.9.refs_8_
  14.4 0.0 collective-permute-start
  14.4 0.3 collective-permute-done.7.refs_7_
  14.7 0.2 collective-permute-start.14
  14.9 0.7 %collective-permute-done.5.refs_6_ = bf16[144,128]{1,0:T(8,128)(2,1)S(1)} collective-permute-done((bf16[144,128]{1,0:T(8,128)(2,1)}, bf16[144,128]{1,0:T(8,128)(2,1)S(1)}, u32[]{:S(2)}, u32[]{:S(2)}) %collective-permute-start.5) | collective-permute-done | bytes 36896 | tf_op jit(solution)/shard_map/ppermute | solution.py:180
  15.6 1.4 %collective-permute-done.3.refs_5_ = bf16[144,128]{1,0:T(8,128)(2,1)S(1)} collective-permute-done((bf16[144,128]{1,0:T(8,128)(2,1)}, bf16[144,128]{1,0:T(8,128)(2,1)S(1)}, u32[]{:S(2)}, u32[]{:S(2)}) %collective-permute-start.3) | collective-permute-done | bytes 36896 | tf_op jit(solution)/shard_map/ppermute | solution.py:180
  17.0 0.8 %collective-permute-done.1.refs_4_ = bf16[144,128]{1,0:T(8,128)(2,1)S(1)} collective-permute-done((bf16[144,128]{1,0:T(8,128)(2,1)}, bf16[144,128]{1,0:T(8,128)(2,1)S(1)}, u32[]{:S(2)}, u32[]{:S(2)}) %collective-permute-start.1) | collective-permute-done | bytes 36896 | tf_op jit(solution)/shard_map/ppermute | solution.py:180
  17.8 0.5 %collective-permute-start.6 = (bf16[144,128]{1,0:T(8,128)(2,1)S(1)}, bf16[144,128]{1,0:T(8,128)(2,1)S(1)}, u32[]{:S(2)}, u32[]{:S(2)}) collective-permute-start(bf16[144,128]{1,0:T(8,128)(2,1)S(1)} %collective-permute-done.5.refs_6_), channel_id=1, source_target_pairs={{1,0},{0,1},{3,2},{2,3},{5,4},{4,5},{7,6},{6,7},{9,8},{8,9},{11,10... | collective-permute-start | bytes 110600 | tf_op jit(solution)/shard_map/ppermute | solution.py:180
  18.3 0.1 collective-permute-start.4
  18.4 0.4 %collective-permute-start.2 = (bf16[144,128]{1,0:T(8,128)(2,1)S(1)}, bf16[144,128]{1,0:T(8,128)(2,1)S(1)}, u32[]{:S(2)}, u32[]{:S(2)}) collective-permute-start(bf16[144,128]{1,0:T(8,128)(2,1)S(1)} %collective-permute-done.1.refs_4_), channel_id=1, source_target_pairs={{1,0},{0,1},{3,2},{2,3},{5,4},{4,5},{7,6},{6,7},{9,8},{8,9},{11,10... | collective-permute-start | bytes 110600 | tf_op jit(solution)/shard_map/ppermute | solution.py:180
  18.8 0.8 %copy-done = bf16[144,128]{1,0:T(8,128)(2,1)S(1)} copy-done((bf16[144,128]{1,0:T(8,128)(2,1)S(1)}, bf16[144,128]{1,0:T(8,128)(2,1)}, u32[]{:S(2)}) %copy-start) | copy-done | bytes 36888
  19.6 0.7 %copy-done.1 = s32[3]{0:T(128)S(1)} copy-done((s32[3]{0:T(128)S(1)}, s32[3]{0:T(128)}, u32[]{:S(2)}) %copy-start.1) | copy-done | bytes 36
  20.2 2.2 %copy-done.2 = bf16[4096,512]{1,0:T(8,128)(2,1)S(1)} copy-done((bf16[4096,512]{1,0:T(8,128)(2,1)S(1)}, bf16[4096,512]{1,0:T(8,128)(2,1)}, u32[]{:S(2)}) %copy-start.2) | copy-done | bytes 4194328
  22.4 0.8 %copy-done.3 = f32[8,2,8,128]{3,2,1,0:T(8,128)S(1)} copy-done((f32[8,2,8,128]{3,2,1,0:T(8,128)S(1)}, f32[8,2,8,128]{3,2,1,0:T(8,128)}, u32[]{:S(2)}) %copy-start.3) | copy-done | bytes 65560
  23.3 2.9 %stack_first.1.refs_11_ = f32[128,512]{1,0:T(8,128)S(1)} custom-call(s32[3]{0:T(128)S(1)} %copy-done.1, bf16[4096,512]{1,0:T(8,128)(2,1)S(1)} %copy-done.2, f32[8,2,8,128]{3,2,1,0:T(8,128)S(1)} %copy-done.3, bf16[144,128]{1,0:T(8,128)(2,1)S(1)} %copy-done, bf16[144,128]{1,0:T(8,128)(2,1)S(1)} %collective-permute-done.1.refs_4_, ...), custom_call_target="tpu_custom_call" | custom-call | flops 2147483648 | bytes 4194304 | tf_op jit(solution)/shard_map/stack_first/pallas_call | solution.py:219
  26.2 3.7 %stack_rest.1 = f32[3,64,512]{2,1,0:T(8,128)} custom-call(s32[3]{0:T(128)S(1)} %copy-done.1, bf16[4096,512]{1,0:T(8,128)(2,1)S(1)} %copy-done.2, f32[8,2,8,128]{3,2,1,0:T(8,128)S(1)} %copy-done.3, bf16[144,128]{1,0:T(8,128)(2,1)S(1)} %collective-permute-done.refs_3_, bf16[144,128]{1,0:T(8,128)(2,1)S(1)} %collective-permute-done.2.refs_4_, ...), custom_call_target="tpu_custom_call" | custom-call | flops 2147483648 | bytes 4194304 | tf_op jit(solution)/shard_map/stack_rest/pallas_call | solution.py:219
  (17 shorter events, 0.0 us)
Async XLA Ops:
  1.6 11.3 %collective-permute-start.13 = (bf16[144,128]{1,0:T(8,128)(2,1)}, bf16[144,128]{1,0:T(8,128)(2,1)S(1)}, u32[]{:S(2)}, u32[]{:S(2)}) collective-permute-start(bf16[144,128]{1,0:T(8,128)(2,1)} %prepare.1.refs_3_), channel_id=1, source_target_pairs={{14,0},{12,2},{10,4},{8,6},{6,8},{4,10},{2,12},{0,14},{15,1},{13,3... | collective-permute-start | bytes 110600 | tf_op jit(solution)/shard_map/ppermute | solution.py:180
  7.5 6.1 %collective-permute-start.11 = (bf16[144,128]{1,0:T(8,128)(2,1)}, bf16[144,128]{1,0:T(8,128)(2,1)S(1)}, u32[]{:S(2)}, u32[]{:S(2)}) collective-permute-start(bf16[144,128]{1,0:T(8,128)(2,1)} %prepare.1.refs_3_), channel_id=1, source_target_pairs={{12,0},{14,2},{8,4},{10,6},{4,8},{6,10},{0,12},{2,14},{13,1},{15,3... | collective-permute-start | bytes 110600 | tf_op jit(solution)/shard_map/ppermute | solution.py:180
  7.8 6.7 %collective-permute-start.9 = (bf16[144,128]{1,0:T(8,128)(2,1)}, bf16[144,128]{1,0:T(8,128)(2,1)S(1)}, u32[]{:S(2)}, u32[]{:S(2)}) collective-permute-start(bf16[144,128]{1,0:T(8,128)(2,1)} %prepare.1.refs_3_), channel_id=1, source_target_pairs={{10,0},{8,2},{14,4},{12,6},{2,8},{0,10},{6,12},{4,14},{11,1},{9,3}... | collective-permute-start | bytes 110600 | tf_op jit(solution)/shard_map/ppermute | solution.py:180
  8.5 6.2 %collective-permute-start.7 = (bf16[144,128]{1,0:T(8,128)(2,1)}, bf16[144,128]{1,0:T(8,128)(2,1)S(1)}, u32[]{:S(2)}, u32[]{:S(2)}) collective-permute-start(bf16[144,128]{1,0:T(8,128)(2,1)} %prepare.1.refs_3_), channel_id=1, source_target_pairs={{8,0},{10,2},{12,4},{14,6},{0,8},{2,10},{4,12},{6,14},{9,1},{11,3}... | collective-permute-start | bytes 110600 | tf_op jit(solution)/shard_map/ppermute | solution.py:180
  10.5 5.1 %collective-permute-start.5 = (bf16[144,128]{1,0:T(8,128)(2,1)}, bf16[144,128]{1,0:T(8,128)(2,1)S(1)}, u32[]{:S(2)}, u32[]{:S(2)}) collective-permute-start(bf16[144,128]{1,0:T(8,128)(2,1)} %prepare.1.refs_3_), channel_id=1, source_target_pairs={{6,0},{4,2},{2,4},{0,6},{14,8},{12,10},{10,12},{8,14},{7,1},{5,3},... | collective-permute-start | bytes 110600 | tf_op jit(solution)/shard_map/ppermute | solution.py:180
  12.8 4.2 %collective-permute-start.3 = (bf16[144,128]{1,0:T(8,128)(2,1)}, bf16[144,128]{1,0:T(8,128)(2,1)S(1)}, u32[]{:S(2)}, u32[]{:S(2)}) collective-permute-start(bf16[144,128]{1,0:T(8,128)(2,1)} %prepare.1.refs_3_), channel_id=1, source_target_pairs={{4,0},{6,2},{0,4},{2,6},{12,8},{14,10},{8,12},{10,14},{5,1},{7,3},... | collective-permute-start | bytes 110600 | tf_op jit(solution)/shard_map/ppermute | solution.py:180
  13.6 4.2 %collective-permute-start.1 = (bf16[144,128]{1,0:T(8,128)(2,1)}, bf16[144,128]{1,0:T(8,128)(2,1)S(1)}, u32[]{:S(2)}, u32[]{:S(2)}) collective-permute-start(bf16[144,128]{1,0:T(8,128)(2,1)} %prepare.1.refs_3_), channel_id=1, source_target_pairs={{2,0},{0,2},{6,4},{4,6},{10,8},{8,10},{14,12},{12,14},{3,1},{1,3},... | collective-permute-start | bytes 110600 | tf_op jit(solution)/shard_map/ppermute | solution.py:180
  14.4 3.4 %collective-permute-start = (bf16[144,128]{1,0:T(8,128)(2,1)}, bf16[144,128]{1,0:T(8,128)(2,1)S(1)}, u32[]{:S(2)}, u32[]{:S(2)}) collective-permute-start(bf16[144,128]{1,0:T(8,128)(2,1)} %prepare.1.refs_3_), channel_id=1, source_target_pairs={{1,0},{0,1},{3,2},{2,3},{5,4},{4,5},{7,6},{6,7},{9,8},{8,9},{11,10... | collective-permute-start | bytes 110600 | tf_op jit(solution)/shard_map/ppermute | solution.py:180
  14.7 3.6 %collective-permute-start.14 = (bf16[144,128]{1,0:T(8,128)(2,1)S(1)}, bf16[144,128]{1,0:T(8,128)(2,1)S(1)}, u32[]{:S(2)}, u32[]{:S(2)}) collective-permute-start(bf16[144,128]{1,0:T(8,128)(2,1)S(1)} %collective-permute-done.13.refs_10_), channel_id=1, source_target_pairs={{1,0},{0,1},{3,2},{2,3},{5,4},{4,5},{7,6},{6,7},{9,8},{8,9},{11,10... | collective-permute-start | bytes 110600 | tf_op jit(solution)/shard_map/ppermute | solution.py:180
  15.6 2.8 %collective-permute-start.12 = (bf16[144,128]{1,0:T(8,128)(2,1)S(1)}, bf16[144,128]{1,0:T(8,128)(2,1)S(1)}, u32[]{:S(2)}, u32[]{:S(2)}) collective-permute-start(bf16[144,128]{1,0:T(8,128)(2,1)S(1)} %collective-permute-done.11.refs_9_), channel_id=1, source_target_pairs={{1,0},{0,1},{3,2},{2,3},{5,4},{4,5},{7,6},{6,7},{9,8},{8,9},{11,10... | collective-permute-start | bytes 110600 | tf_op jit(solution)/shard_map/ppermute | solution.py:180
  17.0 9.1 %collective-permute-start.10 = (bf16[144,128]{1,0:T(8,128)(2,1)S(1)}, bf16[144,128]{1,0:T(8,128)(2,1)S(1)}, u32[]{:S(2)}, u32[]{:S(2)}) collective-permute-start(bf16[144,128]{1,0:T(8,128)(2,1)S(1)} %collective-permute-done.9.refs_8_), channel_id=1, source_target_pairs={{1,0},{0,1},{3,2},{2,3},{5,4},{4,5},{7,6},{6,7},{9,8},{8,9},{11,10... | collective-permute-start | bytes 110600 | tf_op jit(solution)/shard_map/ppermute | solution.py:180
  17.8 8.4 %collective-permute-start.8 = (bf16[144,128]{1,0:T(8,128)(2,1)S(1)}, bf16[144,128]{1,0:T(8,128)(2,1)S(1)}, u32[]{:S(2)}, u32[]{:S(2)}) collective-permute-start(bf16[144,128]{1,0:T(8,128)(2,1)S(1)} %collective-permute-done.7.refs_7_), channel_id=1, source_target_pairs={{1,0},{0,1},{3,2},{2,3},{5,4},{4,5},{7,6},{6,7},{9,8},{8,9},{11,10... | collective-permute-start | bytes 110600 | tf_op jit(solution)/shard_map/ppermute | solution.py:180
  17.8 8.4 %collective-permute-start.6 = (bf16[144,128]{1,0:T(8,128)(2,1)S(1)}, bf16[144,128]{1,0:T(8,128)(2,1)S(1)}, u32[]{:S(2)}, u32[]{:S(2)}) collective-permute-start(bf16[144,128]{1,0:T(8,128)(2,1)S(1)} %collective-permute-done.5.refs_6_), channel_id=1, source_target_pairs={{1,0},{0,1},{3,2},{2,3},{5,4},{4,5},{7,6},{6,7},{9,8},{8,9},{11,10... | collective-permute-start | bytes 110600 | tf_op jit(solution)/shard_map/ppermute | solution.py:180
  18.3 7.9 %collective-permute-start.4 = (bf16[144,128]{1,0:T(8,128)(2,1)S(1)}, bf16[144,128]{1,0:T(8,128)(2,1)S(1)}, u32[]{:S(2)}, u32[]{:S(2)}) collective-permute-start(bf16[144,128]{1,0:T(8,128)(2,1)S(1)} %collective-permute-done.3.refs_5_), channel_id=1, source_target_pairs={{1,0},{0,1},{3,2},{2,3},{5,4},{4,5},{7,6},{6,7},{9,8},{8,9},{11,10... | collective-permute-start | bytes 110600 | tf_op jit(solution)/shard_map/ppermute | solution.py:180
  18.4 7.8 %collective-permute-start.2 = (bf16[144,128]{1,0:T(8,128)(2,1)S(1)}, bf16[144,128]{1,0:T(8,128)(2,1)S(1)}, u32[]{:S(2)}, u32[]{:S(2)}) collective-permute-start(bf16[144,128]{1,0:T(8,128)(2,1)S(1)} %collective-permute-done.1.refs_4_), channel_id=1, source_target_pairs={{1,0},{0,1},{3,2},{2,3},{5,4},{4,5},{7,6},{6,7},{9,8},{8,9},{11,10... | collective-permute-start | bytes 110600 | tf_op jit(solution)/shard_map/ppermute | solution.py:180
  18.8 0.8 %copy-start = (bf16[144,128]{1,0:T(8,128)(2,1)S(1)}, bf16[144,128]{1,0:T(8,128)(2,1)}, u32[]{:S(2)}) copy-start(bf16[144,128]{1,0:T(8,128)(2,1)} %prepare.1.refs_3_) | copy-start | bytes 110596
  19.6 0.7 %copy-start.1 = (s32[3]{0:T(128)S(1)}, s32[3]{0:T(128)}, u32[]{:S(2)}) copy-start(s32[3]{0:T(128)} %refs_0_.3) | copy-start | bytes 40
  20.2 2.2 %copy-start.2 = (bf16[4096,512]{1,0:T(8,128)(2,1)S(1)}, bf16[4096,512]{1,0:T(8,128)(2,1)}, u32[]{:S(2)}) copy-start(bf16[4096,512]{1,0:T(8,128)(2,1)} %constant.4.clone.refs_1_) | copy-start | bytes 12582916
  22.4 0.8 %copy-start.3 = (f32[8,2,8,128]{3,2,1,0:T(8,128)S(1)}, f32[8,2,8,128]{3,2,1,0:T(8,128)}, u32[]{:S(2)}) copy-start(f32[8,2,8,128]{3,2,1,0:T(8,128)} %constant.5.clone.refs_2_) | copy-start | bytes 196612

commit v3 on v2

--- a/solution.py
+++ b/solution.py
@@ -24,15 +24,19 @@
     return parts.reshape(2 * bins, lags).astype(jnp.bfloat16)
 
 
-def phase_table(blocks):
-    phase = (np.arange(blocks)[:, None] * np.arange(LANES)[None, :]) % blocks
-    angle = phase * (2.0 * math.pi / blocks)
-    parts = np.stack([np.cos(angle), np.sin(angle)], axis=1).astype(np.float32)
-    return np.repeat(parts[:, :, None, :], 8, axis=2)
-
-
-def prepare_kernel(sizes, plan_ref, raw_ref, valid_ref, quality_ref, out_ref, wide):
+def phases_of(block, blocks):
+    turn = lax.broadcasted_iota(jnp.int32, (8, LANES), 1) * block % blocks
+    cosine = sine = jnp.zeros((8, LANES), jnp.float32)
+    for part in range(blocks):
+        angle = 2.0 * math.pi * part / blocks
+        cosine = jnp.where(turn == part, math.cos(angle), cosine)
+        sine = jnp.where(turn == part, math.sin(angle), sine)
+    return cosine, sine
+
+
+def prepare_kernel(sizes, *refs):
     stations, bands, sta, blocks, weight_rows = sizes
+    *plan, raw_ref, valid_ref, quality_ref, out_ref, wide = refs
     total = stations * sta
     me = lax.axis_index("sta")
     wide[...] = raw_ref[...].astype(jnp.float32)
@@ -44,7 +48,7 @@
     real = (real * inverse).reshape(stations, bands, LANES)
     imag = (imag * inverse).reshape(stations, bands, LANES)
     white = jnp.concatenate([real, imag], axis=1).reshape(2 * count, LANES)
-    out_ref[pl.ds(0, 2 * count), :] = white.astype(jnp.bfloat16)
+    white = white.astype(jnp.bfloat16)
 
     valid = valid_ref[...].astype(jnp.float32).astype(jnp.bfloat16)
     quality = jnp.broadcast_to(quality_ref[...].astype(jnp.float32), (8, total)).astype(jnp.bfloat16)
@@ -55,7 +59,7 @@
         block = pair // (stations * stations)
         first = jnp.zeros_like(pair)
         for k in range(blocks):
-            owner = k if sta == blocks else plan_ref[k]
+            owner = plan[0][k] if plan else k
             first = jnp.where(block == k, owner * stations, first)
         source = first + pair // stations % stations
         local = me * stations + pair % stations
@@ -70,7 +74,10 @@
         flags = dot(quality, pick_source) * dot(quality, pick_local)
         rows.append(valid_row * flags[:1])
     rows.append(jnp.zeros((16 - weight_rows, LANES), jnp.float32))
-    out_ref[pl.ds(2 * count, 16), :] = jnp.concatenate(rows, axis=0).astype(jnp.bfloat16)
+    weights = jnp.concatenate(rows, axis=0).astype(jnp.bfloat16)
+    for target in range(out_ref.shape[0]):
+        out_ref[target, pl.ds(0, 2 * count), :] = white
+        out_ref[target, pl.ds(2 * count, 16), :] = weights
 
 
 def partner(index, step, size):
@@ -79,55 +86,50 @@
 
 def half_kernel(sizes, distance, *refs):
     stations, bands, seg, sta, pol, blocks, weight_rows = sizes
-    held = seg * sta
-    plan_ref, table_hbm, phase_hbm = refs[:3]
-    spectra_hbm = refs[3 : 3 + held]
-    rest = refs[3 + held :]
+    all_blocks = sta == blocks
+    last = distance == pol - 1
+    if last or not all_blocks:
+        plan_ref, refs = refs[0], refs[1:]
+    table_hbm, spectra, *rest = refs
     if distance:
         before_hbm, rest = rest[0], rest[1:]
-    out_ref, table, phase, spectra, before, wide_weight, local, real_x, imag_x, packed, sems = rest
-    last = distance == pol - 1
+    out_ref, table, before, wide_weight, local, real_x, imag_x, packed, sems = rest
     pairs = blocks * stations * stations
     me = lax.axis_index("sta")
     lag_block = lax.axis_index("seg") * pol + lax.axis_index("pol")
     half = partner(lax.axis_index("pol"), distance, pol)
     rows = 2 * bands * LANES
 
-    copies = [pltpu.make_async_copy(spectra_hbm[n], spectra.at[n], sems.at[n]) for n in range(held)]
-    copies.append(pltpu.make_async_copy(phase_hbm.at[lag_block], phase, sems.at[held]))
     late = [
         pltpu.make_async_copy(
-            table_hbm.at[pl.ds(pl.multiple_of(half * rows, rows), rows)], table, sems.at[held + 1]
+            table_hbm.at[pl.ds(pl.multiple_of(half * rows, rows), rows)], table, sems.at[0]
         )
     ]
     if distance:
-        late.append(pltpu.make_async_copy(before_hbm, before, sems.at[held + 2]))
-    for copy in copies + late:
+        late.append(pltpu.make_async_copy(before_hbm, before, sems.at[1]))
+    for copy in late:
         copy.start()
-    for copy in copies:
-        copy.wait()
 
     diagonal = lax.broadcasted_iota(jnp.int32, (LANES, LANES), 0) == lax.broadcasted_iota(
         jnp.int32, (LANES, LANES), 1
     )
     ones = jnp.ones((LANES, LANES), jnp.bfloat16)
     for g in range(seg):
-        flags = spectra[g * sta, pl.ds(2 * stations * bands, 16), :].astype(jnp.float32)
+        flags = spectra[g * sta + me, pl.ds(2 * stations * bands, 16), :].astype(jnp.float32)
         for row in range(weight_rows):
             spread = jnp.where(diagonal, flags[row : row + 1], 0.0).astype(jnp.bfloat16)
             wide_weight[g, pl.ds(row * LANES, LANES), :] = jnp.dot(
                 spread, ones, preferred_element_type=jnp.float32
             )
 
-    cosine = phase[0]
-    sine = phase[1]
+    cosine, sine = phases_of(lag_block, seg * pol)
     for g in range(seg):
         for j in range(stations):
-            tile = spectra[g * sta, pl.ds(j * 16, 16), :].astype(jnp.float32)
+            tile = spectra[g * sta + me, pl.ds(j * 16, 16), :].astype(jnp.float32)
             local[g, j, 0] = tile[:8] * cosine + tile[8:] * sine
             local[g, j, 1] = tile[8:] * cosine - tile[:8] * sine
     for k in range(blocks):
-        owner = partner(k if sta == blocks else plan_ref[k], me, sta)
+        owner = k if all_blocks else plan_ref[k]
 
         def one_source(a, carry):
             start = pl.multiple_of(a * 16, 16)
@@ -168,19 +170,11 @@
     before[...] = part
     block_pairs = stations * stations
     for step in range(STEPS):
-        first = (plan_ref[step] if sta == blocks else step) * block_pairs
+        first = (plan_ref[step] if all_blocks else step) * block_pairs
         out_ref[step] = before[pl.ds(pl.multiple_of(first, block_pairs), block_pairs), :]
 
 
-def swap(value, axes, sizes, steps):
-    pairs = []
-    for index in np.ndindex(*sizes):
-        source = tuple(partner(i, d, n) for i, d, n in zip(index, steps, sizes))
-        pairs.append((int(np.ravel_multi_index(source, sizes)), int(np.ravel_multi_index(index, sizes))))
-    return lax.ppermute(value, axes, pairs)
-
-
-def shards(table, phases, raw_spectra, owner_plan, pair_valid, quality):
+def shards(table, raw_spectra, owner_plan, pair_valid, quality):
     seg, sta, pol = (lax.axis_size(name) for name in ("seg", "sta", "pol"))
     _, stations, _, bins = raw_spectra.shape
     bands = bins // BAND
@@ -193,50 +187,47 @@
     raw = raw_spectra.reshape(stations, 2, bands, BAND).transpose(0, 2, 1, 3).reshape(-1, BAND)
     vmem = pl.BlockSpec(memory_space=pltpu.VMEM)
     smem = pl.BlockSpec(memory_space=pltpu.SMEM)
-    anywhere = pl.BlockSpec(memory_space=pl.ANY)
+    hbm = pl.BlockSpec(memory_space=pltpu.HBM)
+    plan, plan_specs = ([], []) if sta == blocks else ([owner_plan], [smem])
     payload = pl.pallas_call(
         functools.partial(prepare_kernel, (stations, bands, sta, blocks, weight_rows)),
-        out_shape=jax.ShapeDtypeStruct((rows, LANES), jnp.bfloat16),
-        in_specs=[smem, vmem, vmem, vmem],
+        out_shape=jax.ShapeDtypeStruct((seg * sta, rows, LANES), jnp.bfloat16),
+        in_specs=plan_specs + [vmem, vmem, vmem],
         out_specs=vmem,
         scratch_shapes=[pltpu.VMEM((2 * stations * bands, LANES), jnp.float32)],
         name="prepare",
-    )(owner_plan, raw, jnp.transpose(pair_valid[0]), quality)
-
-    spectra = [
-        swap(payload, ("seg", "sta"), (seg, sta), (g, q)) if g or q else payload
-        for g in range(seg)
-        for q in range(sta)
-    ]
-    held = len(spectra)
+    )(*plan, raw, jnp.transpose(pair_valid[0]), quality)
+
+    spectra = lax.all_to_all(payload, ("seg", "sta"), split_axis=0, concat_axis=0)
     sizes = (stations, bands, seg, sta, pol, blocks, weight_rows)
     out = None
     for distance in range(pol):
         last = distance == pol - 1
-        theirs = [swap(x, ("pol",), (pol,), (distance,)) for x in spectra] if distance else spectra
+        pairs_of = [(partner(i, distance, pol), i) for i in range(pol)]
+        if last:
+            plan, plan_specs = [owner_plan], [smem]
+        theirs = lax.ppermute(spectra, "pol", pairs_of) if distance else spectra
         out_shape = (STEPS, stations * stations, lags) if last else (pairs, lags)
         flops = 2 * pairs * 2 * bins * lags
         out = pl.pallas_call(
             functools.partial(half_kernel, sizes, distance),
             out_shape=jax.ShapeDtypeStruct(out_shape, jnp.float32),
-            in_specs=[smem] + [anywhere] * (2 + held + (1 if distance else 0)),
+            in_specs=plan_specs + [hbm, vmem] + [hbm] * (1 if distance else 0),
             out_specs=vmem,
             scratch_shapes=[
                 pltpu.VMEM((2 * bins, lags), jnp.bfloat16),
-                pltpu.VMEM((2, 8, LANES), jnp.float32),
-                pltpu.VMEM((held, rows, LANES), jnp.bfloat16),
                 pltpu.VMEM((pairs, lags), jnp.float32),
                 pltpu.VMEM((seg, weight_rows * LANES, LANES), jnp.float32),
                 pltpu.VMEM((seg, stations, 2, 8, LANES), jnp.float32),
                 pltpu.VMEM((pairs * 8, LANES), jnp.float32),
                 pltpu.VMEM((pairs * 8, LANES), jnp.float32),
                 pltpu.VMEM((pairs, 2 * bins), jnp.bfloat16),
-                pltpu.SemaphoreType.DMA((held + 3,)),
+                pltpu.SemaphoreType.DMA((2,)),
             ],
-            compiler_params=pltpu.CompilerParams(vmem_limit_bytes=48 * 1024 * 1024),
+            compiler_params=pltpu.CompilerParams(vmem_limit_bytes=52 * 1024 * 1024),
             cost_estimate=pl.CostEstimate(flops=8 * flops, bytes_accessed=4 * 1024 * 1024, transcendentals=0),
             name="stack_first" if distance == 0 else "stack_rest",
-        )(owner_plan, table, phases, *theirs, *([out] if distance else []))
+        )(*plan, table, theirs, *([out] if distance else []))
     return out.reshape(STEPS, stations, stations, lags)
 
 
@@ -254,13 +245,12 @@
         segments = raw_spectra.shape[0] // mesh.shape["groups"]
         lag_blocks = seg * pol
         table = lag_table(2 * bins // lag_blocks, bins, 1.0 / math.sqrt(bins * segments))
-        phases = phase_table(lag_blocks)
         return jax.shard_map(
             shards,
             mesh=mesh,
-            in_specs=(P(), P()) + placed,
+            in_specs=(P(),) + placed,
             out_specs=P("groups", None, "sta", ("seg", "pol")),
             check_vma=False,
-        )(jnp.asarray(table), jnp.asarray(phases), raw_spectra, owner_plan, pair_valid, quality)
+        )(jnp.asarray(table), raw_spectra, owner_plan, pair_valid, quality)
 
     return whole

time: 30.2 us -> 25.2 us (0.83)
  blocking collectives: 0 us -> 17.7 us
  starting transfers between devices: 13.9 us -> 0.01 us
  local copies, waits for them, and re-layouts: 4.45 us -> 0.01 us
  waiting for transfers between devices: 3.39 us -> 0.01 us
  Pallas kernels: 8.08 us -> 7.09 us
    all_to_all x0 -> x1, blocking collectives: none -> 17.7 us  [shards(): lax.all_to_all(payload, ('seg', 'sta'), split_axis=0, concat_axis=0)]
    ppermute x15 -> x1, starting transfers between devices: 13.9 us -> 0.01 us  [shards(): theirs = lax.ppermute(spectra, 'pol', pairs_of) if distance else spectra]
    unnamed x8 -> x2, local copies, waits for them, and re-layouts: 4.45 us -> 0.01 us
    ppermute x15 -> x1, waiting for transfers between devices: 3.39 us -> 0.01 us  [shards(): theirs = lax.ppermute(spectra, 'pol', pairs_of) if distance else spectra]
    pallas_call x2, Pallas kernels: 6.52 us -> 5.46 us  [shards(): pl.pallas_call(functools.partial(half_kernel, sizes, distance), out_shape...]
  transfers between devices with their start and end apart: 15 -> 1, of which waited for: 5 -> 0; matrix products, arithmetic and copies ran while one was open for 0% -> 0% of each run, Pallas kernels for 10% -> 8%
where the time goes in v3:
time: 25.2 us; the launch traced here: 24.8 us
  blocking collectives  17.7 us (70%)
  Pallas kernels  7.09 us (28%)
    all_to_all x1, blocking collectives, shards(): lax.all_to_all(payload, ('seg', 'sta'), split_axis=0, concat_axis=0)  17.7 us
    pallas_call x2, Pallas kernels, shards(): pl.pallas_call(functools.partial(half_kernel, sizes, distance), out_shape...  5.46 us
    pallas_call x1, Pallas kernels, shards(): pl.pallas_call(functools.partial(prepare_kernel, (stations, bands, sta, b...  1.63 us
  transfers between devices with their start and end apart: 1, of which 0 were waited for; matrix products, arithmetic and copies ran while one was open for 0% of the time, Pallas kernels for 8%

profile of v3, /device:TPU:0, one launch (start us, length us, event | category | flops | bytes accessed | tf_op | source)
XLA Modules:
  0.0 24.8 jit_solution(17483137208156687821)
XLA Ops:
  0.0 1.6 %prepare.1 = bf16[8,144,128]{2,1,0:T(8,128)(2,1)} custom-call(bf16[128,128]{1,0:T(8,128)(2,1)} %bitcast.9, s32[8,16]{1,0:T(8,128)} %bitcast.10, s32[1,16]{1,0:T(1,128)} %refs_2_.1), custom_call_target="tpu_custom_call" | custom-call | tf_op jit(solution)/shard_map/prepare/pallas_call | solution.py:192
  1.6 0.0 copy-start
  1.6 17.7 %all_to_all.5.refs_1_ = bf16[8,144,128]{2,1,0:T(8,128)(2,1)S(1)} all-to-all(bf16[8,144,128]{2,1,0:T(8,128)(2,1)} %prepare.1), channel_id=1, replica_groups=mesh['groups'=2,'seg'=4,'sta'=2,'pol'=2] {'seg','sta'}, dimensions={0} | all-to-all | bytes 589824 | tf_op jit(solution)/shard_map/all_to_all | solution.py:201
  19.4 0.0 collective-permute-start
  19.4 2.1 %stack_first.1.refs_3_ = f32[128,512]{1,0:T(8,128)S(1)} custom-call(bf16[4096,512]{1,0:T(8,128)(2,1)} %constant.2.clone.refs_0_.refs_1_, bf16[8,144,128]{2,1,0:T(8,128)(2,1)S(1)} %all_to_all.5.refs_1_), custom_call_target="tpu_custom_call" | custom-call | flops 2147483648 | bytes 4194304 | tf_op jit(solution)/shard_map/stack_first/pallas_call | solution.py:212
  21.4 0.0 collective-permute-done.refs_2_
  21.4 0.0 copy-done
  21.5 3.4 %stack_rest.1 = f32[3,64,512]{2,1,0:T(8,128)} custom-call(s32[3]{0:T(128)S(1)} %copy-done, bf16[4096,512]{1,0:T(8,128)(2,1)} %constant.2.clone.refs_0_.refs_1_, bf16[8,144,128]{2,1,0:T(8,128)(2,1)S(1)} %collective-permute-done.refs_2_, f32[128,512]{1,0:T(8,128)S(1)} %stack_first.1.refs_3_), custom_call_target="tpu_custom_call" | custom-call | flops 2147483648 | bytes 4194304 | tf_op jit(solution)/shard_map/stack_rest/pallas_call | solution.py:212
Async XLA Ops:
  1.6 19.8 %copy-start = (s32[3]{0:T(128)S(1)}, s32[3]{0:T(128)}, u32[]{:S(2)}) copy-start(s32[3]{0:T(128)} %refs_0_.2) | copy-start | bytes 40
  19.4 2.1 %collective-permute-start = (bf16[8,144,128]{2,1,0:T(8,128)(2,1)S(1)}, bf16[8,144,128]{2,1,0:T(8,128)(2,1)S(1)}, u32[]{:S(2)}, u32[]{:S(2)}) collective-permute-start(bf16[8,144,128]{2,1,0:T(8,128)(2,1)S(1)} %all_to_all.5.refs_1_), channel_id=1, source_target_pairs={{1,0},{0,1},{3,2},{2,3},{5,4},{4,5},{7,6},{6,7},{9,8},{8,9},{11,10... | collective-permute-start | bytes 884744 | tf_op jit(solution)/shard_map/ppermute | solution.py:209

commit v4 on v3

v4 whole, which is shorter than its diff:
```python
import functools
import math

import jax
import jax.numpy as jnp
import numpy as np
from jax import lax
from jax.experimental import pallas as pl
from jax.experimental.pallas import tpu as pltpu
from jax.sharding import PartitionSpec as P

STEPS = 3
BAND = 128
LANES = 128


def lag_table(lags, bins, scale):
    bin_index = np.arange(bins, dtype=np.int64)
    phase = (bin_index[:, None] * np.arange(lags, dtype=np.int64)[None, :]) % (2 * bins)
    angle = phase * (2.0 * math.pi / (2 * bins))
    factor = np.where(bin_index == 0, 1.0, 2.0)[:, None] * scale
    parts = np.stack([np.cos(angle) * factor, -np.sin(angle) * factor])
    parts = parts.reshape(2, bins // LANES, LANES, lags).transpose(1, 0, 2, 3)
    return parts.reshape(2 * bins, lags).astype(jnp.bfloat16)


def phases_of(block, blocks):
    turn = lax.broadcasted_iota(jnp.int32, (8, LANES), 1) * block % blocks
    cosine = sine = jnp.zeros((8, LANES), jnp.float32)
    for part in range(blocks):
        angle = 2.0 * math.pi * part / blocks
        cosine = jnp.where(turn == part, math.cos(angle), cosine)
        sine = jnp.where(turn == part, math.sin(angle), sine)
    return cosine, sine


def prepare_kernel(sizes, *refs):
    stations, bands, sta, blocks = sizes
    *plan, raw_ref, valid_ref, quality_ref, out_ref, wide = refs
    total = stations * sta
    me = lax.axis_index("sta")
    wide[...] = raw_ref[...].astype(jnp.float32)
    count = stations * bands
    real = wide[pl.ds(0, count, stride=2), :]
    imag = wide[pl.ds(1, count, stride=2), :]
    power = jnp.sum(real * real + imag * imag, axis=1, keepdims=True) * (1.0 / (2 * BAND))
    inverse = 1.0 / jnp.sqrt(power + 1e-06)
    real = (real * inverse).reshape(stations, bands, LANES)
    imag = (imag * inverse).reshape(stations, bands, LANES)
    white = jnp.concatenate([real, imag], axis=1).reshape(2 * count, LANES).astype(jnp.bfloat16)

    valid = valid_ref[...].astype(jnp.float32).astype(jnp.bfloat16)
    quality = jnp.broadcast_to(quality_ref[...].astype(jnp.float32), (8, total)).astype(jnp.bfloat16)
    pair = lax.broadcasted_iota(jnp.int32, (total, LANES), 1)
    station = lax.broadcasted_iota(jnp.int32, (total, LANES), 0)
    mine = lax.broadcasted_iota(jnp.int32, (stations, LANES), 0) == (
        lax.broadcasted_iota(jnp.int32, (stations, LANES), 1) % stations
    )
    dot = functools.partial(jnp.dot, preferred_element_type=jnp.float32)
    pick_local = (station == me * stations + pair % stations).astype(jnp.float32).astype(jnp.bfloat16)
    local_flags = dot(quality, pick_local)
    rows = []
    for k in range(blocks):
        source = (plan[0][k] if plan else k) * stations + pair // stations
        pick_source = (station == source).astype(jnp.float32).astype(jnp.bfloat16)
        valid_row = jnp.sum(jnp.where(mine, dot(valid, pick_source), 0.0), axis=0, keepdims=True)
        rows.append(valid_row * (dot(quality, pick_source) * local_flags)[:1])
    rows.append(jnp.zeros((16 - blocks, LANES), jnp.float32))
    weights = jnp.concatenate(rows, axis=0).astype(jnp.bfloat16)
    for target in range(out_ref.shape[0]):
        out_ref[target, pl.ds(0, 2 * count), :] = white
        out_ref[target, pl.ds(2 * count, 16), :] = weights


def stack(sizes, block, locals_ref, source_ref, wide_weight, local, real_x, imag_x, packed):
    stations, bands, seg, lag_blocks = sizes
    pairs = stations * stations
    row_index = lax.broadcasted_iota(jnp.int32, (16, LANES), 0)
    diagonal = lax.broadcasted_iota(jnp.int32, (pairs, LANES), 0) == lax.broadcasted_iota(
        jnp.int32, (pairs, LANES), 1
    )
    ones = jnp.ones((LANES, LANES), jnp.bfloat16)
    for g in range(seg):
        flags = locals_ref[g, pl.ds(2 * stations * bands, 16), :].astype(jnp.float32)
        flags = jnp.sum(jnp.where(row_index == block, flags, 0.0), axis=0, keepdims=True)
        spread = jnp.where(diagonal, flags, 0.0).astype(jnp.bfloat16)
        wide_weight[g] = jnp.dot(spread, ones, preferred_element_type=jnp.float32)

    lag_block = lax.axis_index("seg") * lax.axis_size("pol") + lax.axis_index("pol")
    cosine, sine = phases_of(lag_block, lag_blocks)
    for g in range(seg):
        for j in range(stations):
            tile = locals_ref[g, pl.ds(j * 16, 16), :].astype(jnp.float32)
            local[g, j, 0] = tile[:8] * cosine + tile[8:] * sine
            local[g, j, 1] = tile[8:] * cosine - tile[:8] * sine

    def one_source(a, carry):
        start = pl.multiple_of(a * 16, 16)
        tiles = [source_ref[g, pl.ds(start, 16), :].astype(jnp.float32) for g in range(seg)]
        for j in range(stations):
            pair = a * stations + j
            real_sum = imag_sum = None
            for g in range(seg):
                weight = jnp.broadcast_to(wide_weight[g, pl.ds(pair, 1), :], (8, LANES))
                real_src = tiles[g][:8] * weight
                imag_src = tiles[g][8:] * weight
                real_loc = local[g, j, 0]
                imag_loc = local[g, j, 1]
                real_term = real_src * real_loc + imag_src * imag_loc
                imag_term = imag_src * real_loc - real_src * imag_loc
                real_sum = real_term if g == 0 else real_sum + real_term
                imag_sum = imag_term if g == 0 else imag_sum + imag_term
            at = pl.ds(pl.multiple_of(pair * 8, 8), 8)
            real_x[at, :] = real_sum
            imag_x[at, :] = imag_sum
        return carry

    lax.fori_loop(0, stations, one_source, 0)
    for band in range(bands):
        column = band * 2 * LANES
        packed[:, pl.ds(column, LANES)] = real_x[pl.ds(band, pairs, stride=8), :].astype(jnp.bfloat16)
        packed[:, pl.ds(column + LANES, LANES)] = imag_x[pl.ds(band, pairs, stride=8), :].astype(jnp.bfloat16)


def stack_kernel(sizes, piece, halves, pieces, *refs):
    stations, bands, seg, sta, pol, blocks = sizes
    own_first = sta == blocks
    final = piece == pieces - 1 and halves[-1] == pol - 1
    refs = list(refs)
    plan_ref = refs.pop(0) if final else None
    table_hbm = refs.pop(0)
    spectra = [(refs.pop(0), refs.pop(0)) for _ in halves]
    others = [refs.pop(0) for _ in range(piece if final else 0)]
    before = refs.pop(0) if halves[0] else None
    out_ref = refs.pop(0)
    tables, total, wide_weight, local, real_x, imag_x, packed, sems = refs
    me = lax.axis_index("sta")
    block = me ^ piece if own_first else piece
    rows = 2 * bands * LANES

    copies = []
    for n, half in enumerate(halves):
        start = pl.multiple_of((lax.axis_index("pol") ^ half) * rows, rows)
        copies.append(pltpu.make_async_copy(table_hbm.at[pl.ds(start, rows)], tables.at[n], sems.at[n]))
    for n, other in enumerate(others):
        copies.append(pltpu.make_async_copy(other, total.at[n], sems.at[len(halves) + n]))
    for copy in copies:
        copy.start()

    part = None
    for n, (locals_ref, source_ref) in enumerate(spectra):
        stack(
            (stations, bands, seg, seg * pol), block, locals_ref, source_ref,
            wide_weight, local, real_x, imag_x, packed,
        )
        copies[n].wait()
        term = jnp.dot(packed[...], tables[n], preferred_element_type=jnp.float32)
        part = term if part is None else part + term
    if before is not None:
        part = part + before[...]
    if not final:
        out_ref[...] = part
        return
    total[piece] = part
    for copy in copies[len(halves) :]:
        copy.wait()
    for step in range(STEPS):
        out_ref[step] = total[plan_ref[step] ^ me] if own_first else total[step]


def exchange(value, axis, distance):
    size = lax.axis_size(axis)
    return lax.ppermute(value, axis, [(i ^ distance, i) for i in range(size)]) if distance else value


def shards(table, raw_spectra, owner_plan, pair_valid, quality):
    seg, sta, pol = (lax.axis_size(name) for name in ("seg", "sta", "pol"))
    _, stations, _, bins = raw_spectra.shape
    bands = bins // BAND
    blocks = min(sta, STEPS)
    pairs = stations * stations
    lags = table.shape[1]
    rows = 2 * stations * bands + 16
    sizes = (stations, bands, seg, sta, pol, blocks)

    raw = raw_spectra.reshape(stations, 2, bands, BAND).transpose(0, 2, 1, 3).reshape(-1, BAND)
    vmem = pl.BlockSpec(memory_space=pltpu.VMEM)
    smem = pl.BlockSpec(memory_space=pltpu.SMEM)
    hbm = pl.BlockSpec(memory_space=pltpu.HBM)
    plan = [] if sta == blocks else [owner_plan]
    payload = pl.pallas_call(
        functools.partial(prepare_kernel, (stations, bands, sta, blocks)),
        out_shape=jax.ShapeDtypeStruct((seg, rows, LANES), jnp.bfloat16),
        in_specs=[smem] * len(plan) + [vmem, vmem, vmem],
        out_specs=vmem,
        scratch_shapes=[pltpu.VMEM((2 * stations * bands, LANES), jnp.float32)],
        name="prepare",
    )(*plan, raw, jnp.transpose(pair_valid[0]), quality)

    mine = lax.all_to_all(payload, "seg", split_axis=0, concat_axis=0)
    if sta == blocks:
        sources = [exchange(mine, "sta", distance) for distance in range(sta)]
    else:
        gathered = lax.all_gather(mine, "sta")
        sources = [gathered[owner_plan[k]] for k in range(blocks)]

    done = []
    for piece in range(blocks):
        last = piece == blocks - 1
        before = []
        for halves in [(h,) for h in range(pol)] if last else [tuple(range(pol))]:
            final = last and halves[-1] == pol - 1
            spectra = [x for h in halves for x in (exchange(mine, "pol", h), exchange(sources[piece], "pol", h))]
            others = done if final else []
            flops = 2 * pairs * 2 * bins * lags * len(halves)
            result = pl.pallas_call(
                functools.partial(stack_kernel, sizes, piece, halves, blocks),
                out_shape=jax.ShapeDtypeStruct((STEPS, pairs, lags) if final else (pairs, lags), jnp.float32),
                in_specs=[smem] * final + [hbm] + [vmem] * len(spectra) + [hbm] * len(others) + [vmem] * len(before),
                out_specs=vmem,
                scratch_shapes=[
                    pltpu.VMEM((len(halves), 2 * bins, lags), jnp.bfloat16),
                    pltpu.VMEM((blocks, pairs, lags), jnp.float32),
                    pltpu.VMEM((seg, pairs, LANES), jnp.float32),
                    pltpu.VMEM((seg, stations, 2, 8, LANES), jnp.float32),
                    pltpu.VMEM((pairs * 8, LANES), jnp.float32),
                    pltpu.VMEM((pairs * 8, LANES), jnp.float32),
                    pltpu.VMEM((pairs, 2 * bins), jnp.bfloat16),
                    pltpu.SemaphoreType.DMA((len(halves) + blocks,)),
                ],
                compiler_params=pltpu.CompilerParams(vmem_limit_bytes=52 * 1024 * 1024),
                cost_estimate=pl.CostEstimate(
                    flops=16 * flops, bytes_accessed=2 * 1024 * 1024 * len(halves), transcendentals=0
                ),
                name="stack",
            )(*([owner_plan] if final else []), table, *spectra, *others, *before)
            before = [result]
        done.append(result)
        if not last:
            sources[piece + 1], done[-1] = lax.optimization_barrier((sources[piece + 1], result))
    return result.reshape(STEPS, stations, stations, lags)


def solution(mesh):
    placed = (
        P(("groups", "seg"), "sta", None, "pol"),
        P("groups"),
        P(("groups", "seg"), None, "sta"),
        P(("groups", "seg"), None),
    )

    def whole(raw_spectra, owner_plan, pair_valid, quality):
        seg, pol = mesh.shape["seg"], mesh.shape["pol"]
        bins = raw_spectra.shape[3]
        segments = raw_spectra.shape[0] // mesh.shape["groups"]
        lag_blocks = seg * pol
        table = lag_table(2 * bins // lag_blocks, bins, 1.0 / math.sqrt(bins * segments))
        return jax.shard_map(
            shards,
            mesh=mesh,
            in_specs=(P(),) + placed,
            out_specs=P("groups", None, "sta", ("seg", "pol")),
            check_vma=False,
        )(jnp.asarray(table), raw_spectra, owner_plan, pair_valid, quality)

    return whole
```

time: 25.2 us -> 26.8 us (1.063)
  blocking collectives: 17.7 us -> 13 us
  Pallas kernels: 7.09 us -> 10.5 us
  starting transfers between devices: 0.01 us -> 1.5 us
  waiting for transfers between devices: 0.01 us -> 1.38 us
    all_to_all x1, blocking collectives: 17.7 us -> 13 us  [shards(): mine = lax.all_to_all(payload, 'seg', split_axis=0, concat_axis=0)]
    pallas_call x2 -> x3, Pallas kernels: 5.46 us -> 8.94 us  [shards(): pl.pallas_call(functools.partial(stack_kernel, sizes, piece, halves, bloc...]
    ppermute x1 -> x3, starting transfers between devices: 0.01 us -> 1.5 us  [exchange(): lax.ppermute(value, axis, [(i ^ distance, i) for i in range(size)])]
    ppermute x1 -> x3, waiting for transfers between devices: 0.01 us -> 1.38 us  [exchange(): lax.ppermute(value, axis, [(i ^ distance, i) for i in range(size)])]
  transfers between devices with their start and end apart: 1 -> 3, of which waited for: 0 -> 1; matrix products, arithmetic and copies ran while one was open for 0% -> 0% of each run, Pallas kernels for 8% -> 21%
where the time goes in v4:
time: 26.8 us; the launch traced here: 26.4 us
  blocking collectives  13 us (49%)
  Pallas kernels  10.5 us (39%)
  starting transfers between devices  1.5 us (6%)
  waiting for transfers between devices  1.38 us (5%)
    all_to_all x1, blocking collectives, shards(): mine = lax.all_to_all(payload, 'seg', split_axis=0, concat_axis=0)  13 us
    pallas_call x3, Pallas kernels, shards(): pl.pallas_call(functools.partial(stack_kernel, sizes, piece, halves, bloc...  8.94 us
    pallas_call x1, Pallas kernels, shards(): pl.pallas_call(functools.partial(prepare_kernel, (stations, bands, sta, b...  1.58 us
    ppermute x3, starting transfers between devices, exchange(): lax.ppermute(value, axis, [(i ^ distance, i) for i in range(size)])  1.5 us
    ppermute x3, waiting for transfers between devices, exchange(): lax.ppermute(value, axis, [(i ^ distance, i) for i in range(size)])  1.38 us
  transfers between devices with their start and end apart: 3, of which 1 were waited for; matrix products, arithmetic and copies ran while one was open for 0% of the time, Pallas kernels for 21%

profile of v4, /device:TPU:0, one launch (start us, length us, event | category | flops | bytes accessed | tf_op | source)
XLA Modules:
  0.0 26.4 jit_solution(14551942118778347321)
XLA Ops:
  0.0 1.6 %prepare.1 = bf16[4,144,128]{2,1,0:T(8,128)(2,1)} custom-call(bf16[128,128]{1,0:T(8,128)(2,1)} %bitcast.9, s32[8,16]{1,0:T(8,128)} %bitcast.10, s32[1,16]{1,0:T(1,128)} %refs_2_.1), custom_call_target="tpu_custom_call" | custom-call | tf_op jit(solution)/shard_map/prepare/pallas_call | solution.py:191
  1.6 13.0 %all_to_all.5.refs_1_.refs_2_ = bf16[4,144,128]{2,1,0:T(8,128)(2,1)S(1)} all-to-all(bf16[4,144,128]{2,1,0:T(8,128)(2,1)} %prepare.1), channel_id=1, replica_groups=mesh['groups'=2,'seg'=4,'sta'=2,'pol'=2] {'seg'}, dimensions={0} | all-to-all | bytes 294912 | tf_op jit(solution)/shard_map/all_to_all | solution.py:200
  14.6 0.0 collective-permute-start
  14.6 1.5 %collective-permute-start.1 = (bf16[4,144,128]{2,1,0:T(8,128)(2,1)S(1)}, bf16[4,144,128]{2,1,0:T(8,128)(2,1)S(1)}, u32[]{:S(2)}, u32[]{:S(2)}) collective-permute-start(bf16[4,144,128]{2,1,0:T(8,128)(2,1)S(1)} %all_to_all.5.refs_1_.refs_2_), channel_id=1, source_target_pairs={{2,0},{0,2},{3,1},{1,3},{6,4},{4,6},{7,5},{5,7},{10,8},{8,10},{11,... | collective-permute-start | bytes 442376 | tf_op jit(solution)/shard_map/ppermute | solution.py:173
  16.1 0.0 collective-permute-done.refs_3_.refs_4_.refs_2_
  16.1 3.4 %stack.3.refs_4_ = f32[64,512]{1,0:T(8,128)S(1)} custom-call(bf16[4096,512]{1,0:T(8,128)(2,1)} %constant.2.clone.refs_0_.refs_1_, bf16[4,144,128]{2,1,0:T(8,128)(2,1)S(1)} %all_to_all.5.refs_1_.refs_2_, bf16[4,144,128]{2,1,0:T(8,128)(2,1)S(1)} %all_to_all.5.refs_1_.refs_2_, bf16[4,144,128]{2,1,0:T(8,128)(2,1)S(1)} %collective-permute-done.refs_3_.refs_4_.refs_2_, ...), custom_call_target="tpu_custom_call" | custom-call | flops 4294967296 | bytes 4194304 | tf_op jit(solution)/shard_map/stack/pallas_call | solution.py:216
  19.4 0.0 copy-start
  19.5 1.4 %collective-permute-done.1.refs_2_ = bf16[4,144,128]{2,1,0:T(8,128)(2,1)S(1)} collective-permute-done((bf16[4,144,128]{2,1,0:T(8,128)(2,1)S(1)}, bf16[4,144,128]{2,1,0:T(8,128)(2,1)S(1)}, u32[]{:S(2)}, u32[]{:S(2)}) %collective-permute-start.1) | collective-permute-done | bytes 147488 | tf_op jit(solution)/shard_map/ppermute | solution.py:173
  20.8 0.0 collective-permute-start.2
  20.8 2.1 %stack.4.refs_5_ = f32[64,512]{1,0:T(8,128)S(1)} custom-call(bf16[4096,512]{1,0:T(8,128)(2,1)} %constant.2.clone.refs_0_.refs_1_, bf16[4,144,128]{2,1,0:T(8,128)(2,1)S(1)} %all_to_all.5.refs_1_.refs_2_, bf16[4,144,128]{2,1,0:T(8,128)(2,1)S(1)} %collective-permute-done.1.refs_2_), custom_call_target="tpu_custom_call" | custom-call | flops 2147483648 | bytes 2097152 | tf_op jit(solution)/shard_map/stack/pallas_call | solution.py:216
  23.0 0.0 collective-permute-done.2.refs_3_
  23.0 0.0 copy-done
  23.0 3.4 %stack.5 = f32[3,64,512]{2,1,0:T(8,128)} custom-call(s32[3]{0:T(128)S(1)} %copy-done, bf16[4096,512]{1,0:T(8,128)(2,1)} %constant.2.clone.refs_0_.refs_1_, bf16[4,144,128]{2,1,0:T(8,128)(2,1)S(1)} %collective-permute-done.refs_3_.refs_4_.refs_2_, bf16[4,144,128]{2,1,0:T(8,128)(2,1)S(1)} %collective-permute-done.2.refs_3_, f32[64,512]{1,0:T(8,128)S(1)} %stack.3.refs_4_, ...), custom_call_target="tpu_custom_call" | custom-call | flops 2147483648 | bytes 2097152 | tf_op jit(solution)/shard_map/stack/pallas_call | solution.py:216
Async XLA Ops:
  14.6 1.5 %collective-permute-start = (bf16[4,144,128]{2,1,0:T(8,128)(2,1)S(1)}, bf16[4,144,128]{2,1,0:T(8,128)(2,1)S(1)}, u32[]{:S(2)}, u32[]{:S(2)}) collective-permute-start(bf16[4,144,128]{2,1,0:T(8,128)(2,1)S(1)} %all_to_all.5.refs_1_.refs_2_), channel_id=1, source_target_pairs={{1,0},{0,1},{3,2},{2,3},{5,4},{4,5},{7,6},{6,7},{9,8},{8,9},{11,10... | collective-permute-start | bytes 442376 | tf_op jit(solution)/shard_map/ppermute | solution.py:173
  14.6 6.3 %collective-permute-start.1 = (bf16[4,144,128]{2,1,0:T(8,128)(2,1)S(1)}, bf16[4,144,128]{2,1,0:T(8,128)(2,1)S(1)}, u32[]{:S(2)}, u32[]{:S(2)}) collective-permute-start(bf16[4,144,128]{2,1,0:T(8,128)(2,1)S(1)} %all_to_all.5.refs_1_.refs_2_), channel_id=1, source_target_pairs={{2,0},{0,2},{3,1},{1,3},{6,4},{4,6},{7,5},{5,7},{10,8},{8,10},{11,... | collective-permute-start | bytes 442376 | tf_op jit(solution)/shard_map/ppermute | solution.py:173
  19.4 3.6 %copy-start = (s32[3]{0:T(128)S(1)}, s32[3]{0:T(128)}, u32[]{:S(2)}) copy-start(s32[3]{0:T(128)} %refs_0_.3) | copy-start | bytes 40
  20.8 2.2 %collective-permute-start.2 = (bf16[4,144,128]{2,1,0:T(8,128)(2,1)S(1)}, bf16[4,144,128]{2,1,0:T(8,128)(2,1)S(1)}, u32[]{:S(2)}, u32[]{:S(2)}) collective-permute-start(bf16[4,144,128]{2,1,0:T(8,128)(2,1)S(1)} %collective-permute-done.1.refs_2_), channel_id=1, source_target_pairs={{1,0},{0,1},{3,2},{2,3},{5,4},{4,5},{7,6},{6,7},{9,8},{8,9},{11,10... | collective-permute-start | bytes 442376 | tf_op jit(solution)/shard_map/ppermute | solution.py:173

commit v5 on v4

v5 whole, which is shorter than its diff:
```python
import functools
import math

import jax
import jax.numpy as jnp
import numpy as np
from jax import lax
from jax.experimental import pallas as pl
from jax.experimental.pallas import tpu as pltpu
from jax.sharding import PartitionSpec as P

STEPS = 3
BAND = 128
LANES = 128


def lag_table(lags, bins, halves, scale):
    bin_index = np.arange(bins, dtype=np.int64)
    lag = 2 * np.arange(lags // 2, dtype=np.int64) + 1
    phase = (bin_index[:, None] * lag[None, :]) % (4 * bins)
    angle = phase * (2.0 * math.pi / (4 * bins))
    factor = np.where(bin_index == 0, 1.0, 2.0)[:, None] * scale
    parts = np.stack([np.cos(angle) * factor, np.sin(angle) * factor])
    parts = parts.reshape(2, halves, bins // halves, lags // 2).transpose(1, 0, 2, 3)
    return parts.astype(jnp.bfloat16)


def turn(count, period):
    count = count % period
    quarter = (count + period // 8) // (period // 4)
    x = (count - quarter * (period // 4)).astype(jnp.float32) * (2.0 * math.pi / period)
    y = x * x
    sine = x * (1.0 + y * (-1 / 6 + y * (1 / 120 + y * (-1 / 5040 + y * (1 / 362880)))))
    cosine = 1.0 + y * (-1 / 2 + y * (1 / 24 + y * (-1 / 720 + y * (1 / 40320))))
    quarter = quarter % 4
    odd = quarter % 2 == 1
    real = jnp.where(odd, sine, cosine)
    imag = jnp.where(odd, cosine, sine)
    real = jnp.where((quarter == 1) | (quarter == 2), -real, real)
    imag = jnp.where(quarter >= 2, -imag, imag)
    return real, imag


def prepare_kernel(sizes, *refs):
    stations, bands, sta, blocks = sizes
    *plan, raw_ref, valid_ref, quality_ref, out_ref, wide = refs
    total = stations * sta
    me = lax.axis_index("sta")
    wide[...] = raw_ref[...].astype(jnp.float32)
    count = stations * bands
    real = wide[pl.ds(0, count, stride=2), :]
    imag = wide[pl.ds(1, count, stride=2), :]
    power = jnp.sum(real * real + imag * imag, axis=1, keepdims=True) * (1.0 / (2 * BAND))
    inverse = 1.0 / jnp.sqrt(power + 1e-06)
    real = (real * inverse).reshape(stations, bands, LANES)
    imag = (imag * inverse).reshape(stations, bands, LANES)
    white = jnp.concatenate([real, imag], axis=1).reshape(2 * count, LANES).astype(jnp.bfloat16)

    valid = valid_ref[...].astype(jnp.float32).astype(jnp.bfloat16)
    quality = jnp.broadcast_to(quality_ref[...].astype(jnp.float32), (8, total)).astype(jnp.bfloat16)
    pair = lax.broadcasted_iota(jnp.int32, (total, LANES), 1)
    station = lax.broadcasted_iota(jnp.int32, (total, LANES), 0)
    mine = lax.broadcasted_iota(jnp.int32, (stations, LANES), 0) == (
        lax.broadcasted_iota(jnp.int32, (stations, LANES), 1) % stations
    )
    dot = functools.partial(jnp.dot, preferred_element_type=jnp.float32)
    pick_local = (station == me * stations + pair % stations).astype(jnp.float32).astype(jnp.bfloat16)
    local_flags = dot(quality, pick_local)
    rows = []
    for k in range(blocks):
        source = (plan[0][k] if plan else k) * stations + pair // stations
        pick_source = (station == source).astype(jnp.float32).astype(jnp.bfloat16)
        valid_row = jnp.sum(jnp.where(mine, dot(valid, pick_source), 0.0), axis=0, keepdims=True)
        rows.append(valid_row * (dot(quality, pick_source) * local_flags)[:1])
    rows.append(jnp.zeros((16 - blocks, LANES), jnp.float32))
    weights = jnp.concatenate(rows, axis=0).astype(jnp.bfloat16)
    out_ref[pl.ds(0, 2 * count), :] = white
    out_ref[pl.ds(2 * count, 16), :] = weights


def stack(sizes, block, half, locals_refs, source_refs, wide_weight, local, real_x, imag_x, packed):
    stations, bands, seg, pol, lags = sizes
    pairs = stations * stations
    row_index = lax.broadcasted_iota(jnp.int32, (16, LANES), 0)
    diagonal = lax.broadcasted_iota(jnp.int32, (pairs, LANES), 0) == lax.broadcasted_iota(
        jnp.int32, (pairs, LANES), 1
    )
    ones = jnp.ones((LANES, LANES), jnp.bfloat16)
    for g in range(seg):
        flags = locals_refs[g][pl.ds(2 * stations * bands, 16), :].astype(jnp.float32)
        flags = jnp.sum(jnp.where(row_index == block, flags, 0.0), axis=0, keepdims=True)
        spread = jnp.where(diagonal, flags, 0.0).astype(jnp.bfloat16)
        wide_weight[g] = jnp.dot(spread, ones, preferred_element_type=jnp.float32)

    lag_block = lax.axis_index("seg") * pol + lax.axis_index("pol")
    row = half * bands + lax.broadcasted_iota(jnp.int32, (bands, LANES), 0)
    bin_index = row * LANES + lax.broadcasted_iota(jnp.int32, (bands, LANES), 1)
    cosine, sine = turn(bin_index * (2 * lags * lag_block + lags - 1), 2 * lags * seg * pol)
    for g in range(seg):
        for j in range(stations):
            tile = locals_refs[g][pl.ds(j * 16, 16), :].astype(jnp.float32)
            local[g, j, 0] = tile[:8] * cosine + tile[8:] * sine
            local[g, j, 1] = tile[8:] * cosine - tile[:8] * sine

    def one_source(a, carry):
        start = pl.multiple_of(a * 16, 16)
        tiles = [source_refs[g][pl.ds(start, 16), :].astype(jnp.float32) for g in range(seg)]
        for j in range(stations):
            pair = a * stations + j
            real_sum = imag_sum = None
            for g in range(seg):
                weight = jnp.broadcast_to(wide_weight[g, pl.ds(pair, 1), :], (8, LANES))
                real_src = tiles[g][:8] * weight
                imag_src = tiles[g][8:] * weight
                real_loc = local[g, j, 0]
                imag_loc = local[g, j, 1]
                real_term = real_src * real_loc + imag_src * imag_loc
                imag_term = imag_src * real_loc - real_src * imag_loc
                real_sum = real_term if g == 0 else real_sum + real_term
                imag_sum = imag_term if g == 0 else imag_sum + imag_term
            at = pl.ds(pl.multiple_of(pair * 8, 8), 8)
            real_x[at, :] = real_sum
            imag_x[at, :] = imag_sum
        return carry

    lax.fori_loop(0, stations, one_source, 0)
    for band in range(bands):
        at = pl.ds(band * LANES, LANES)
        packed[0, :, at] = real_x[pl.ds(band, pairs, stride=8), :].astype(jnp.bfloat16)
        packed[1, :, at] = imag_x[pl.ds(band, pairs, stride=8), :].astype(jnp.bfloat16)


def unfold(even, odd):
    half = even.shape[1]
    after = even - odd
    before = even + odd
    if half % LANES:
        flip = lax.broadcasted_iota(jnp.int32, (half, half), 0) + lax.broadcasted_iota(
            jnp.int32, (half, half), 1
        )
        flip = (flip == half - 1).astype(jnp.float32)
        before = jnp.dot(before, flip, precision=lax.Precision.HIGHEST, preferred_element_type=jnp.float32)
        return jnp.concatenate([before, after], axis=1)
    index = LANES - 1 - lax.broadcasted_iota(jnp.int32, (even.shape[0], LANES), 1)
    runs = [before[:, n * LANES : (n + 1) * LANES] for n in reversed(range(half // LANES))]
    runs = [jnp.take_along_axis(run, index, axis=1, mode="promise_in_bounds") for run in runs]
    return jnp.concatenate(runs + [after], axis=1)


def stack_kernel(sizes, piece, halves, pieces, *refs):
    stations, bands, seg, sta, pol, blocks, lags = sizes
    own_first = sta == blocks
    complete = halves[-1] == pol - 1
    final = complete and piece == pieces - 1
    refs = list(refs)
    plan_ref = refs.pop(0) if final else None
    table_hbm = refs.pop(0)
    spectra = [([refs.pop(0) for _ in range(seg)], [refs.pop(0) for _ in range(seg)]) for _ in halves]
    others = [refs.pop(0) for _ in range(piece if final else 0)]
    sums = refs.pop(0) if halves[0] else None
    out_ref = refs.pop(0)
    tables, result, wide_weight, local, real_x, imag_x, packed, sems, out_sems = refs
    me = lax.axis_index("sta")
    block = me ^ piece if own_first else piece

    copies = []
    for n, distance in enumerate(halves):
        half = lax.axis_index("pol") ^ distance
        copies.append(pltpu.make_async_copy(table_hbm.at[half], tables.at[n], sems.at[n]))
        copies[-1].start()
    if final:
        chosen = [plan_ref[step] ^ me if own_first else step for step in range(STEPS)]
        for step in range(STEPS):
            for n, other in enumerate(others):

                @pl.when(chosen[step] == n)
                def _():
                    pltpu.make_async_copy(other, out_ref.at[step], out_sems.at[step]).start()

    even = odd = None
    for n, (locals_refs, source_refs) in enumerate(spectra):
        half = lax.axis_index("pol") ^ halves[n]
        stack(
            (stations, bands, seg, pol, lags), block, half, locals_refs, source_refs,
            wide_weight, local, real_x, imag_x, packed,
        )
        copies[n].wait()
        even_term = jnp.dot(packed[0], tables[n, 0], preferred_element_type=jnp.float32)
        odd_term = jnp.dot(packed[1], tables[n, 1], preferred_element_type=jnp.float32)
        even = even_term if even is None else even + even_term
        odd = odd_term if odd is None else odd + odd_term
    if sums is not None:
        even = even + sums[0]
        odd = odd + sums[1]
    if not complete:
        out_ref[0] = even
        out_ref[1] = odd
    elif not final:
        out_ref[...] = unfold(even, odd)
    else:
        result[...] = unfold(even, odd)
        for step in range(STEPS):

            @pl.when(chosen[step] == piece)
            def _():
                pltpu.make_async_copy(result, out_ref.at[step], out_sems.at[step]).start()

        for step in range(STEPS):
            pltpu.make_async_copy(result, out_ref.at[step], out_sems.at[step]).wait()


def exchange(value, axis, distance):
    size = lax.axis_size(axis)
    return lax.ppermute(value, axis, [(i ^ distance, i) for i in range(size)]) if distance else value


def shards(table, raw_spectra, owner_plan, pair_valid, quality):
    seg, sta, pol = (lax.axis_size(name) for name in ("seg", "sta", "pol"))
    _, stations, _, bins = raw_spectra.shape
    bands = bins // BAND
    blocks = min(sta, STEPS)
    pairs = stations * stations
    half_lags = table.shape[3]
    lags = 2 * half_lags
    rows = 2 * stations * bands + 16
    sizes = (stations, bands, seg, sta, pol, blocks, lags)

    raw = raw_spectra.reshape(stations, 2, bands, BAND).transpose(0, 2, 1, 3).reshape(-1, BAND)
    vmem = pl.BlockSpec(memory_space=pltpu.VMEM)
    smem = pl.BlockSpec(memory_space=pltpu.SMEM)
    hbm = pl.BlockSpec(memory_space=pltpu.HBM)
    plan = [] if sta == blocks else [owner_plan]
    payload = pl.pallas_call(
        functools.partial(prepare_kernel, (stations, bands, sta, blocks)),
        out_shape=jax.ShapeDtypeStruct((rows, LANES), jnp.bfloat16),
        in_specs=[smem] * len(plan) + [vmem, vmem, vmem],
        out_specs=vmem,
        scratch_shapes=[pltpu.VMEM((2 * stations * bands, LANES), jnp.float32)],
        name="prepare",
    )(*plan, raw, jnp.transpose(pair_valid[0]), quality)

    mine = [exchange(payload, "seg", g) for g in range(seg)]
    if sta == blocks:
        sources = [[exchange(x, "sta", distance) for x in mine] for distance in range(sta)]
    else:
        gathered = lax.all_gather(jnp.stack(mine), "sta")
        chosen = [gathered[owner_plan[k]] for k in range(blocks)]
        sources = [[x[g] for g in range(seg)] for x in chosen]

    done = []
    for piece in range(blocks):
        last = piece == blocks - 1
        sums = []
        for halves in [(h,) for h in range(pol)] if last else [tuple(range(pol))]:
            complete = halves[-1] == pol - 1
            final = last and complete
            spectra = []
            for h in halves:
                spectra += [exchange(x, "pol", h) for x in mine]
                spectra += [exchange(x, "pol", h) for x in sources[piece]]
            others = done if final else []
            if final:
                out_shape = (STEPS, pairs, lags)
            else:
                out_shape = (pairs, lags) if complete else (2, pairs, half_lags)
            flops = 2 * pairs * 2 * bins * lags * len(halves)
            result = pl.pallas_call(
                functools.partial(stack_kernel, sizes, piece, halves, blocks),
                out_shape=jax.ShapeDtypeStruct(out_shape, jnp.float32),
                in_specs=[smem] * final + [hbm] + [vmem] * len(spectra) + [hbm] * len(others) + [vmem] * len(sums),
                out_specs=hbm if final else vmem,
                scratch_shapes=[
                    pltpu.VMEM((len(halves), 2, bins, half_lags), jnp.bfloat16),
                    pltpu.VMEM((pairs, lags), jnp.float32),
                    pltpu.VMEM((seg, pairs, LANES), jnp.float32),
                    pltpu.VMEM((seg, stations, 2, 8, LANES), jnp.float32),
                    pltpu.VMEM((pairs * 8, LANES), jnp.float32),
                    pltpu.VMEM((pairs * 8, LANES), jnp.float32),
                    pltpu.VMEM((2, pairs, bins), jnp.bfloat16),
                    pltpu.SemaphoreType.DMA((len(halves),)),
                    pltpu.SemaphoreType.DMA((STEPS,)),
                ],
                compiler_params=pltpu.CompilerParams(vmem_limit_bytes=52 * 1024 * 1024),
                cost_estimate=pl.CostEstimate(
                    flops=16 * flops, bytes_accessed=1024 * 1024 * len(halves), transcendentals=0
                ),
                name="stack",
            )(*([owner_plan] if final else []), table, *spectra, *others, *sums)
            sums = [result]
        done.append(result)
        if not last:
            sources[piece + 1], done[-1] = lax.optimization_barrier((sources[piece + 1], result))
    return result.reshape(STEPS, stations, stations, lags)


def solution(mesh):
    placed = (
        P(("groups", "seg"), "sta", None, "pol"),
        P("groups"),
        P(("groups", "seg"), None, "sta"),
        P(("groups", "seg"), None),
    )

    def whole(raw_spectra, owner_plan, pair_valid, quality):
        seg, pol = mesh.shape["seg"], mesh.shape["pol"]
        bins = raw_spectra.shape[3]
        segments = raw_spectra.shape[0] // mesh.shape["groups"]
        lag_blocks = seg * pol
        table = lag_table(2 * bins // lag_blocks, bins, pol, 1.0 / math.sqrt(bins * segments))
        return jax.shard_map(
            shards,
            mesh=mesh,
            in_specs=(P(),) + placed,
            out_specs=P("groups", None, "sta", ("seg", "pol")),
            check_vma=False,
        )(jnp.asarray(table), raw_spectra, owner_plan, pair_valid, quality)

    return whole
```

time: 26.8 us -> 25.8 us (0.963)
  blocking collectives: 13 us -> 0 us
  starting transfers between devices: 1.5 us -> 11.3 us
  waiting for transfers between devices: 1.38 us -> 4.53 us
  Pallas kernels: 10.5 us -> 8.77 us
  local copies, waits for them, and re-layouts: 0.01 us -> 0.77 us
    all_to_all x1 -> x0, blocking collectives: 13 us -> none  [shards(): mine = lax.all_to_all(payload, 'seg', split_axis=0, concat_axis=0)]
    ppermute x3 -> x15, starting transfers between devices: 1.5 us -> 11.3 us  [exchange(): lax.ppermute(value, axis, [(i ^ distance, i) for i in range(size)])]
    ppermute x3 -> x15, waiting for transfers between devices: 1.38 us -> 4.53 us  [exchange(): lax.ppermute(value, axis, [(i ^ distance, i) for i in range(size)])]
    pallas_call x3, Pallas kernels: 8.94 us -> 7.24 us  [shards(): pl.pallas_call(functools.partial(stack_kernel, sizes, piece, halves, bloc...]
    unnamed x2 -> x4, local copies, waits for them, and re-layouts: 0.01 us -> 0.77 us
  transfers between devices with their start and end apart: 3 -> 15, of which waited for: 1 -> 2; matrix products, arithmetic and copies ran while one was open for 0% -> 0% of each run, Pallas kernels for 21% -> 17%
where the time goes in v5:
time: 25.8 us; the launch traced here: 25.5 us
  starting transfers between devices  11.3 us (44%)
  Pallas kernels  8.77 us (34%)
  waiting for transfers between devices  4.53 us (18%)
  local copies, waits for them, and re-layouts  0.77 us (3%)
    ppermute x15, starting transfers between devices, exchange(): lax.ppermute(value, axis, [(i ^ distance, i) for i in range(size)])  11.3 us
    pallas_call x3, Pallas kernels, shards(): pl.pallas_call(functools.partial(stack_kernel, sizes, piece, halves, bloc...  7.24 us
    ppermute x15, waiting for transfers between devices, exchange(): lax.ppermute(value, axis, [(i ^ distance, i) for i in range(size)])  4.53 us
    pallas_call x1, Pallas kernels, shards(): pl.pallas_call(functools.partial(prepare_kernel, (stations, bands, sta, b...  1.54 us
    unnamed x4, local copies, waits for them, and re-layouts  0.77 us
  transfers between devices with their start and end apart: 15, of which 2 were waited for; matrix products, arithmetic and copies ran while one was open for 0% of the time, Pallas kernels for 17%

profile of v5, /device:TPU:0, one launch (start us, length us, event | category | flops | bytes accessed | tf_op | source)
XLA Modules:
  0.0 25.5 jit_solution(2664752883748885743)
XLA Ops:
  0.0 1.5 %prepare.1.refs_1_.refs_5_ = bf16[144,128]{1,0:T(8,128)(2,1)} custom-call(bf16[128,128]{1,0:T(8,128)(2,1)} %bitcast.9, s32[8,16]{1,0:T(8,128)} %bitcast.10, s32[1,16]{1,0:T(1,128)} %refs_2_.1), custom_call_target="tpu_custom_call" | custom-call | tf_op jit(solution)/shard_map/prepare/pallas_call | solution.py:233
  1.5 5.0 %collective-permute-start.5 = (bf16[144,128]{1,0:T(8,128)(2,1)}, bf16[144,128]{1,0:T(8,128)(2,1)S(1)}, u32[]{:S(2)}, u32[]{:S(2)}) collective-permute-start(bf16[144,128]{1,0:T(8,128)(2,1)} %prepare.1.refs_1_.refs_5_), channel_id=1, source_target_pairs={{12,0},{8,4},{4,8},{0,12},{13,1},{9,5},{5,9},{1,13},{14,2},{10,6},... | collective-permute-start | bytes 110600 | tf_op jit(solution)/shard_map/ppermute | solution.py:214
  6.6 0.6 %collective-permute-start.1 = (bf16[144,128]{1,0:T(8,128)(2,1)}, bf16[144,128]{1,0:T(8,128)(2,1)S(1)}, u32[]{:S(2)}, u32[]{:S(2)}) collective-permute-start(bf16[144,128]{1,0:T(8,128)(2,1)} %prepare.1.refs_1_.refs_5_), channel_id=1, source_target_pairs={{4,0},{0,4},{12,8},{8,12},{5,1},{1,5},{13,9},{9,13},{6,2},{2,6},{1... | collective-permute-start | bytes 110600 | tf_op jit(solution)/shard_map/ppermute | solution.py:214
  7.2 0.0 collective-permute-start
  7.2 1.6 %collective-permute-done.5.refs_4_.refs_8_ = bf16[144,128]{1,0:T(8,128)(2,1)S(1)} collective-permute-done((bf16[144,128]{1,0:T(8,128)(2,1)}, bf16[144,128]{1,0:T(8,128)(2,1)S(1)}, u32[]{:S(2)}, u32[]{:S(2)}) %collective-permute-start.5) | collective-permute-done | bytes 36896 | tf_op jit(solution)/shard_map/ppermute | solution.py:214
  8.7 0.0 collective-permute-start.6
  8.7 2.9 %collective-permute-done.3.refs_3_.refs_7_ = bf16[144,128]{1,0:T(8,128)(2,1)S(1)} collective-permute-done((bf16[144,128]{1,0:T(8,128)(2,1)}, bf16[144,128]{1,0:T(8,128)(2,1)S(1)}, u32[]{:S(2)}, u32[]{:S(2)}) %collective-permute-start.3) | collective-permute-done | bytes 36896 | tf_op jit(solution)/shard_map/ppermute | solution.py:214
  11.7 0.5 %collective-permute-start.2 = (bf16[144,128]{1,0:T(8,128)(2,1)S(1)}, bf16[144,128]{1,0:T(8,128)(2,1)S(1)}, u32[]{:S(2)}, u32[]{:S(2)}) collective-permute-start(bf16[144,128]{1,0:T(8,128)(2,1)S(1)} %collective-permute-done.1.refs_2_.refs_6_), channel_id=1, source_target_pairs={{1,0},{0,1},{3,2},{2,3},{5,4},{4,5},{7,6},{6,7},{9,8},{8,9},{11,10... | collective-permute-start | bytes 110600 | tf_op jit(solution)/shard_map/ppermute | solution.py:214
  12.2 1.5 %collective-permute-start.7 = (bf16[144,128]{1,0:T(8,128)(2,1)}, bf16[144,128]{1,0:T(8,128)(2,1)S(1)}, u32[]{:S(2)}, u32[]{:S(2)}) collective-permute-start(bf16[144,128]{1,0:T(8,128)(2,1)} %prepare.1.refs_1_.refs_5_), channel_id=1, source_target_pairs={{2,0},{0,2},{3,1},{1,3},{6,4},{4,6},{7,5},{5,7},{10,8},{8,10},{11,... | collective-permute-start | bytes 110600 | tf_op jit(solution)/shard_map/ppermute | solution.py:214
  13.7 0.5 %collective-permute-start.10 = (bf16[144,128]{1,0:T(8,128)(2,1)S(1)}, bf16[144,128]{1,0:T(8,128)(2,1)S(1)}, u32[]{:S(2)}, u32[]{:S(2)}) collective-permute-start(bf16[144,128]{1,0:T(8,128)(2,1)S(1)} %collective-permute-done.5.refs_4_.refs_8_), channel_id=1, source_target_pairs={{2,0},{0,2},{3,1},{1,3},{6,4},{4,6},{7,5},{5,7},{10,8},{8,10},{11,... | collective-permute-start | bytes 110600 | tf_op jit(solution)/shard_map/ppermute | solution.py:214
  14.2 0.0 collective-permute-done.6.refs_12_.refs_16_.refs_5_
  14.2 1.5 %collective-permute-start.9 = (bf16[144,128]{1,0:T(8,128)(2,1)S(1)}, bf16[144,128]{1,0:T(8,128)(2,1)S(1)}, u32[]{:S(2)}, u32[]{:S(2)}) collective-permute-start(bf16[144,128]{1,0:T(8,128)(2,1)S(1)} %collective-permute-done.3.refs_3_.refs_7_), channel_id=1, source_target_pairs={{2,0},{0,2},{3,1},{1,3},{6,4},{4,6},{7,5},{5,7},{10,8},{8,10},{11,... | collective-permute-start | bytes 110600 | tf_op jit(solution)/shard_map/ppermute | solution.py:214
  15.7 0.0 collective-permute-done.4.refs_11_.refs_15_.refs_4_
  15.7 0.5 %collective-permute-start.8 = (bf16[144,128]{1,0:T(8,128)(2,1)S(1)}, bf16[144,128]{1,0:T(8,128)(2,1)S(1)}, u32[]{:S(2)}, u32[]{:S(2)}) collective-permute-start(bf16[144,128]{1,0:T(8,128)(2,1)S(1)} %collective-permute-done.1.refs_2_.refs_6_), channel_id=1, source_target_pairs={{2,0},{0,2},{3,1},{1,3},{6,4},{4,6},{7,5},{5,7},{10,8},{8,10},{11,... | collective-permute-start | bytes 110600 | tf_op jit(solution)/shard_map/ppermute | solution.py:214
  16.2 0.8 %copy-done = bf16[144,128]{1,0:T(8,128)(2,1)S(1)} copy-done((bf16[144,128]{1,0:T(8,128)(2,1)S(1)}, bf16[144,128]{1,0:T(8,128)(2,1)}, u32[]{:S(2)}) %copy-start) | copy-done | bytes 36888
  17.0 2.7 %stack.3.refs_10_ = f32[64,512]{1,0:T(8,128)S(1)} custom-call(bf16[2,2,1024,256]{3,2,1,0:T(8,128)(2,1)} %constant.2.clone.refs_0_.refs_1_, bf16[144,128]{1,0:T(8,128)(2,1)S(1)} %copy-done, bf16[144,128]{1,0:T(8,128)(2,1)S(1)} %collective-permute-done.1.refs_2_.refs_6_, bf16[144,128]{1,0:T(8,128)(2,1)S(1)} %collective-permute-done.3.refs_3_.refs_7_, ...), custom_call_target="tpu_custom_call" | custom-call | flops 4294967296 | bytes 2097152 | tf_op jit(solution)/shard_map/stack/pallas_call | solution.py:267
  19.7 0.0 copy-start.1
  19.7 0.0 collective-permute-done.7.refs_5_
  19.7 0.1 collective-permute-start.11
  19.8 0.5 %collective-permute-start.12 = (bf16[144,128]{1,0:T(8,128)(2,1)S(1)}, bf16[144,128]{1,0:T(8,128)(2,1)S(1)}, u32[]{:S(2)}, u32[]{:S(2)}) collective-permute-start(bf16[144,128]{1,0:T(8,128)(2,1)S(1)} %collective-permute-done.8.refs_6_), channel_id=1, source_target_pairs={{1,0},{0,1},{3,2},{2,3},{5,4},{4,5},{7,6},{6,7},{9,8},{8,9},{11,10... | collective-permute-start | bytes 110600 | tf_op jit(solution)/shard_map/ppermute | solution.py:214
  20.3 0.1 collective-permute-start.13
  20.4 0.4 %collective-permute-start.14 = (bf16[144,128]{1,0:T(8,128)(2,1)S(1)}, bf16[144,128]{1,0:T(8,128)(2,1)S(1)}, u32[]{:S(2)}, u32[]{:S(2)}) collective-permute-start(bf16[144,128]{1,0:T(8,128)(2,1)S(1)} %collective-permute-done.10.refs_8_), channel_id=1, source_target_pairs={{1,0},{0,1},{3,2},{2,3},{5,4},{4,5},{7,6},{6,7},{9,8},{8,9},{11,10... | collective-permute-start | bytes 110600 | tf_op jit(solution)/shard_map/ppermute | solution.py:214
  20.8 1.6 %stack.4.refs_11_ = f32[2,64,256]{2,1,0:T(8,128)S(1)} custom-call(bf16[2,2,1024,256]{3,2,1,0:T(8,128)(2,1)} %constant.2.clone.refs_0_.refs_1_, bf16[144,128]{1,0:T(8,128)(2,1)S(1)} %copy-done, bf16[144,128]{1,0:T(8,128)(2,1)S(1)} %collective-permute-done.1.refs_2_.refs_6_, bf16[144,128]{1,0:T(8,128)(2,1)S(1)} %collective-permute-done.3.refs_3_.refs_7_, ...), custom_call_target="tpu_custom_call" | custom-call | flops 2147483648 | bytes 1048576 | tf_op jit(solution)/shard_map/stack/pallas_call | solution.py:267
  22.5 2.9 %stack.5 = f32[3,64,512]{2,1,0:T(8,128)} custom-call(s32[3]{0:T(128)S(1)} %copy-done.1, bf16[2,2,1024,256]{3,2,1,0:T(8,128)(2,1)} %constant.2.clone.refs_0_.refs_1_, bf16[144,128]{1,0:T(8,128)(2,1)S(1)} %collective-permute-done.refs_9_.refs_13_.refs_2_, bf16[144,128]{1,0:T(8,128)(2,1)S(1)} %collective-permute-done.2.refs_10_.refs_14_.refs_3_, ...), custom_call_target="tpu_custom_call" | custom-call | flops 2147483648 | bytes 1048576 | tf_op jit(solution)/shard_map/stack/pallas_call | solution.py:267
  (14 shorter events, 0.0 us)
Async XLA Ops:
  1.5 7.2 %collective-permute-start.5 = (bf16[144,128]{1,0:T(8,128)(2,1)}, bf16[144,128]{1,0:T(8,128)(2,1)S(1)}, u32[]{:S(2)}, u32[]{:S(2)}) collective-permute-start(bf16[144,128]{1,0:T(8,128)(2,1)} %prepare.1.refs_1_.refs_5_), channel_id=1, source_target_pairs={{12,0},{8,4},{4,8},{0,12},{13,1},{9,5},{5,9},{1,13},{14,2},{10,6},... | collective-permute-start | bytes 110600 | tf_op jit(solution)/shard_map/ppermute | solution.py:214
  6.6 5.1 %collective-permute-start.3 = (bf16[144,128]{1,0:T(8,128)(2,1)}, bf16[144,128]{1,0:T(8,128)(2,1)S(1)}, u32[]{:S(2)}, u32[]{:S(2)}) collective-permute-start(bf16[144,128]{1,0:T(8,128)(2,1)} %prepare.1.refs_1_.refs_5_), channel_id=1, source_target_pairs={{8,0},{12,4},{0,8},{4,12},{9,1},{13,5},{1,9},{5,13},{10,2},{14,6},... | collective-permute-start | bytes 110600 | tf_op jit(solution)/shard_map/ppermute | solution.py:214
  6.6 5.1 %collective-permute-start.1 = (bf16[144,128]{1,0:T(8,128)(2,1)}, bf16[144,128]{1,0:T(8,128)(2,1)S(1)}, u32[]{:S(2)}, u32[]{:S(2)}) collective-permute-start(bf16[144,128]{1,0:T(8,128)(2,1)} %prepare.1.refs_1_.refs_5_), channel_id=1, source_target_pairs={{4,0},{0,4},{12,8},{8,12},{5,1},{1,5},{13,9},{9,13},{6,2},{2,6},{1... | collective-permute-start | bytes 110600 | tf_op jit(solution)/shard_map/ppermute | solution.py:214
  7.2 6.5 %collective-permute-start = (bf16[144,128]{1,0:T(8,128)(2,1)}, bf16[144,128]{1,0:T(8,128)(2,1)S(1)}, u32[]{:S(2)}, u32[]{:S(2)}) collective-permute-start(bf16[144,128]{1,0:T(8,128)(2,1)} %prepare.1.refs_1_.refs_5_), channel_id=1, source_target_pairs={{1,0},{0,1},{3,2},{2,3},{5,4},{4,5},{7,6},{6,7},{9,8},{8,9},{11,10... | collective-permute-start | bytes 110600 | tf_op jit(solution)/shard_map/ppermute | solution.py:214
  8.7 5.5 %collective-permute-start.6 = (bf16[144,128]{1,0:T(8,128)(2,1)S(1)}, bf16[144,128]{1,0:T(8,128)(2,1)S(1)}, u32[]{:S(2)}, u32[]{:S(2)}) collective-permute-start(bf16[144,128]{1,0:T(8,128)(2,1)S(1)} %collective-permute-done.5.refs_4_.refs_8_), channel_id=1, source_target_pairs={{1,0},{0,1},{3,2},{2,3},{5,4},{4,5},{7,6},{6,7},{9,8},{8,9},{11,10... | collective-permute-start | bytes 110600 | tf_op jit(solution)/shard_map/ppermute | solution.py:214
  11.7 4.0 %collective-permute-start.4 = (bf16[144,128]{1,0:T(8,128)(2,1)S(1)}, bf16[144,128]{1,0:T(8,128)(2,1)S(1)}, u32[]{:S(2)}, u32[]{:S(2)}) collective-permute-start(bf16[144,128]{1,0:T(8,128)(2,1)S(1)} %collective-permute-done.3.refs_3_.refs_7_), channel_id=1, source_target_pairs={{1,0},{0,1},{3,2},{2,3},{5,4},{4,5},{7,6},{6,7},{9,8},{8,9},{11,10... | collective-permute-start | bytes 110600 | tf_op jit(solution)/shard_map/ppermute | solution.py:214
  11.7 4.6 %collective-permute-start.2 = (bf16[144,128]{1,0:T(8,128)(2,1)S(1)}, bf16[144,128]{1,0:T(8,128)(2,1)S(1)}, u32[]{:S(2)}, u32[]{:S(2)}) collective-permute-start(bf16[144,128]{1,0:T(8,128)(2,1)S(1)} %collective-permute-done.1.refs_2_.refs_6_), channel_id=1, source_target_pairs={{1,0},{0,1},{3,2},{2,3},{5,4},{4,5},{7,6},{6,7},{9,8},{8,9},{11,10... | collective-permute-start | bytes 110600 | tf_op jit(solution)/shard_map/ppermute | solution.py:214
  12.2 7.5 %collective-permute-start.7 = (bf16[144,128]{1,0:T(8,128)(2,1)}, bf16[144,128]{1,0:T(8,128)(2,1)S(1)}, u32[]{:S(2)}, u32[]{:S(2)}) collective-permute-start(bf16[144,128]{1,0:T(8,128)(2,1)} %prepare.1.refs_1_.refs_5_), channel_id=1, source_target_pairs={{2,0},{0,2},{3,1},{1,3},{6,4},{4,6},{7,5},{5,7},{10,8},{8,10},{11,... | collective-permute-start | bytes 110600 | tf_op jit(solution)/shard_map/ppermute | solution.py:214
  13.7 6.0 %collective-permute-start.10 = (bf16[144,128]{1,0:T(8,128)(2,1)S(1)}, bf16[144,128]{1,0:T(8,128)(2,1)S(1)}, u32[]{:S(2)}, u32[]{:S(2)}) collective-permute-start(bf16[144,128]{1,0:T(8,128)(2,1)S(1)} %collective-permute-done.5.refs_4_.refs_8_), channel_id=1, source_target_pairs={{2,0},{0,2},{3,1},{1,3},{6,4},{4,6},{7,5},{5,7},{10,8},{8,10},{11,... | collective-permute-start | bytes 110600 | tf_op jit(solution)/shard_map/ppermute | solution.py:214
  14.2 5.5 %collective-permute-start.9 = (bf16[144,128]{1,0:T(8,128)(2,1)S(1)}, bf16[144,128]{1,0:T(8,128)(2,1)S(1)}, u32[]{:S(2)}, u32[]{:S(2)}) collective-permute-start(bf16[144,128]{1,0:T(8,128)(2,1)S(1)} %collective-permute-done.3.refs_3_.refs_7_), channel_id=1, source_target_pairs={{2,0},{0,2},{3,1},{1,3},{6,4},{4,6},{7,5},{5,7},{10,8},{8,10},{11,... | collective-permute-start | bytes 110600 | tf_op jit(solution)/shard_map/ppermute | solution.py:214
  15.7 4.0 %collective-permute-start.8 = (bf16[144,128]{1,0:T(8,128)(2,1)S(1)}, bf16[144,128]{1,0:T(8,128)(2,1)S(1)}, u32[]{:S(2)}, u32[]{:S(2)}) collective-permute-start(bf16[144,128]{1,0:T(8,128)(2,1)S(1)} %collective-permute-done.1.refs_2_.refs_6_), channel_id=1, source_target_pairs={{2,0},{0,2},{3,1},{1,3},{6,4},{4,6},{7,5},{5,7},{10,8},{8,10},{11,... | collective-permute-start | bytes 110600 | tf_op jit(solution)/shard_map/ppermute | solution.py:214
  16.2 0.8 %copy-start = (bf16[144,128]{1,0:T(8,128)(2,1)S(1)}, bf16[144,128]{1,0:T(8,128)(2,1)}, u32[]{:S(2)}) copy-start(bf16[144,128]{1,0:T(8,128)(2,1)} %prepare.1.refs_1_.refs_5_) | copy-start | bytes 110596
  19.7 2.8 %copy-start.1 = (s32[3]{0:T(128)S(1)}, s32[3]{0:T(128)}, u32[]{:S(2)}) copy-start(s32[3]{0:T(128)} %refs_0_.3) | copy-start | bytes 40
  19.7 2.7 %collective-permute-start.11 = (bf16[144,128]{1,0:T(8,128)(2,1)S(1)}, bf16[144,128]{1,0:T(8,128)(2,1)S(1)}, u32[]{:S(2)}, u32[]{:S(2)}) collective-permute-start(bf16[144,128]{1,0:T(8,128)(2,1)S(1)} %collective-permute-done.7.refs_5_), channel_id=1, source_target_pairs={{1,0},{0,1},{3,2},{2,3},{5,4},{4,5},{7,6},{6,7},{9,8},{8,9},{11,10... | collective-permute-start | bytes 110600 | tf_op jit(solution)/shard_map/ppermute | solution.py:214
  19.8 2.7 %collective-permute-start.12 = (bf16[144,128]{1,0:T(8,128)(2,1)S(1)}, bf16[144,128]{1,0:T(8,128)(2,1)S(1)}, u32[]{:S(2)}, u32[]{:S(2)}) collective-permute-start(bf16[144,128]{1,0:T(8,128)(2,1)S(1)} %collective-permute-done.8.refs_6_), channel_id=1, source_target_pairs={{1,0},{0,1},{3,2},{2,3},{5,4},{4,5},{7,6},{6,7},{9,8},{8,9},{11,10... | collective-permute-start | bytes 110600 | tf_op jit(solution)/shard_map/ppermute | solution.py:214
  20.3 2.2 %collective-permute-start.13 = (bf16[144,128]{1,0:T(8,128)(2,1)S(1)}, bf16[144,128]{1,0:T(8,128)(2,1)S(1)}, u32[]{:S(2)}, u32[]{:S(2)}) collective-permute-start(bf16[144,128]{1,0:T(8,128)(2,1)S(1)} %collective-permute-done.9.refs_7_), channel_id=1, source_target_pairs={{1,0},{0,1},{3,2},{2,3},{5,4},{4,5},{7,6},{6,7},{9,8},{8,9},{11,10... | collective-permute-start | bytes 110600 | tf_op jit(solution)/shard_map/ppermute | solution.py:214
  20.4 2.1 %collective-permute-start.14 = (bf16[144,128]{1,0:T(8,128)(2,1)S(1)}, bf16[144,128]{1,0:T(8,128)(2,1)S(1)}, u32[]{:S(2)}, u32[]{:S(2)}) collective-permute-start(bf16[144,128]{1,0:T(8,128)(2,1)S(1)} %collective-permute-done.10.refs_8_), channel_id=1, source_target_pairs={{1,0},{0,1},{3,2},{2,3},{5,4},{4,5},{7,6},{6,7},{9,8},{8,9},{11,10... | collective-permute-start | bytes 110600 | tf_op jit(solution)/shard_map/ppermute | solution.py:214

commit v6 on v5

--- a/solution.py
+++ b/solution.py
@@ -12,6 +12,7 @@
 STEPS = 3
 BAND = 128
 LANES = 128
+VMEM_BYTES = 32 * 1024 * 1024
 
 
 def lag_table(lags, bins, halves, scale):
@@ -78,7 +79,7 @@
     out_ref[pl.ds(2 * count, 16), :] = weights
 
 
-def stack(sizes, block, half, locals_refs, source_refs, wide_weight, local, real_x, imag_x, packed):
+def stack(sizes, block, half, locals_ref, source_ref, wide_weight, local, real_x, imag_x, packed):
     stations, bands, seg, pol, lags = sizes
     pairs = stations * stations
     row_index = lax.broadcasted_iota(jnp.int32, (16, LANES), 0)
@@ -87,7 +88,7 @@
     )
     ones = jnp.ones((LANES, LANES), jnp.bfloat16)
     for g in range(seg):
-        flags = locals_refs[g][pl.ds(2 * stations * bands, 16), :].astype(jnp.float32)
+        flags = locals_ref[g, pl.ds(2 * stations * bands, 16), :].astype(jnp.float32)
         flags = jnp.sum(jnp.where(row_index == block, flags, 0.0), axis=0, keepdims=True)
         spread = jnp.where(diagonal, flags, 0.0).astype(jnp.bfloat16)
         wide_weight[g] = jnp.dot(spread, ones, preferred_element_type=jnp.float32)
@@ -98,13 +99,13 @@
     cosine, sine = turn(bin_index * (2 * lags * lag_block + lags - 1), 2 * lags * seg * pol)
     for g in range(seg):
         for j in range(stations):
-            tile = locals_refs[g][pl.ds(j * 16, 16), :].astype(jnp.float32)
+            tile = locals_ref[g, pl.ds(j * 16, 16), :].astype(jnp.float32)
             local[g, j, 0] = tile[:8] * cosine + tile[8:] * sine
             local[g, j, 1] = tile[8:] * cosine - tile[:8] * sine
 
     def one_source(a, carry):
         start = pl.multiple_of(a * 16, 16)
-        tiles = [source_refs[g][pl.ds(start, 16), :].astype(jnp.float32) for g in range(seg)]
+        tiles = [source_ref[g, pl.ds(start, 16), :].astype(jnp.float32) for g in range(seg)]
         for j in range(stations):
             pair = a * stations + j
             real_sum = imag_sum = None
@@ -154,20 +155,15 @@
     final = complete and piece == pieces - 1
     refs = list(refs)
     plan_ref = refs.pop(0) if final else None
-    table_hbm = refs.pop(0)
-    spectra = [([refs.pop(0) for _ in range(seg)], [refs.pop(0) for _ in range(seg)]) for _ in halves]
+    table = refs.pop(0)
+    spectra = [(refs.pop(0), refs.pop(0)) for _ in halves]
     others = [refs.pop(0) for _ in range(piece if final else 0)]
     sums = refs.pop(0) if halves[0] else None
     out_ref = refs.pop(0)
-    tables, result, wide_weight, local, real_x, imag_x, packed, sems, out_sems = refs
+    result, wide_weight, local, real_x, imag_x, packed, out_sems = refs
     me = lax.axis_index("sta")
     block = me ^ piece if own_first else piece
 
-    copies = []
-    for n, distance in enumerate(halves):
-        half = lax.axis_index("pol") ^ distance
-        copies.append(pltpu.make_async_copy(table_hbm.at[half], tables.at[n], sems.at[n]))
-        copies[-1].start()
     if final:
         chosen = [plan_ref[step] ^ me if own_first else step for step in range(STEPS)]
         for step in range(STEPS):
@@ -178,15 +174,14 @@
                     pltpu.make_async_copy(other, out_ref.at[step], out_sems.at[step]).start()
 
     even = odd = None
-    for n, (locals_refs, source_refs) in enumerate(spectra):
+    for n, (locals_ref, source_ref) in enumerate(spectra):
         half = lax.axis_index("pol") ^ halves[n]
         stack(
-            (stations, bands, seg, pol, lags), block, half, locals_refs, source_refs,
+            (stations, bands, seg, pol, lags), block, half, locals_ref, source_ref,
             wide_weight, local, real_x, imag_x, packed,
         )
-        copies[n].wait()
-        even_term = jnp.dot(packed[0], tables[n, 0], preferred_element_type=jnp.float32)
-        odd_term = jnp.dot(packed[1], tables[n, 1], preferred_element_type=jnp.float32)
+        even_term = jnp.dot(packed[0], table[half, 0], preferred_element_type=jnp.float32)
+        odd_term = jnp.dot(packed[1], table[half, 1], preferred_element_type=jnp.float32)
         even = even_term if even is None else even + even_term
         odd = odd_term if odd is None else odd + odd_term
     if sums is not None:
@@ -209,6 +204,23 @@
             pltpu.make_async_copy(result, out_ref.at[step], out_sems.at[step]).wait()
 
 
+def fetch_kernel(table_hbm, payload_hbm, table_ref, payload_ref, sems):
+    copies = [
+        pltpu.make_async_copy(table_hbm, table_ref, sems.at[0]),
+        pltpu.make_async_copy(payload_hbm, payload_ref, sems.at[1]),
+    ]
+    for copy in copies:
+        copy.start()
+    for copy in copies:
+        copy.wait()
+
+
+def join_kernel(*refs):
+    *pieces, out_ref = refs
+    for n, piece in enumerate(pieces):
+        out_ref[n] = piece[...]
+
+
 def exchange(value, axis, distance):
     size = lax.axis_size(axis)
     return lax.ppermute(value, axis, [(i ^ distance, i) for i in range(size)]) if distance else value
@@ -239,13 +251,35 @@
         name="prepare",
     )(*plan, raw, jnp.transpose(pair_valid[0]), quality)
 
-    mine = [exchange(payload, "seg", g) for g in range(seg)]
+    table, near = pl.pallas_call(
+        fetch_kernel,
+        out_shape=[jax.ShapeDtypeStruct(x.shape, x.dtype) for x in (table, payload)],
+        in_specs=[hbm, hbm],
+        out_specs=[vmem, vmem],
+        scratch_shapes=[pltpu.SemaphoreType.DMA((2,))],
+        compiler_params=pltpu.CompilerParams(vmem_limit_bytes=VMEM_BYTES),
+        cost_estimate=pl.CostEstimate(flops=0, bytes_accessed=2 * table.size * 2, transcendentals=0),
+        name="fetch",
+    )(table, payload)
+
+    held = {0: payload}
+    distance = seg // 2
+    while distance:
+        held.update({g ^ distance: exchange(x, "seg", distance) for g, x in held.items()})
+        distance //= 2
+    mine = pl.pallas_call(
+        join_kernel,
+        out_shape=jax.ShapeDtypeStruct((seg, rows, LANES), jnp.bfloat16),
+        in_specs=[vmem] * seg,
+        out_specs=vmem,
+        compiler_params=pltpu.CompilerParams(vmem_limit_bytes=VMEM_BYTES),
+        name="join",
+    )(near, *(held[g] for g in range(1, seg)))
     if sta == blocks:
-        sources = [[exchange(x, "sta", distance) for x in mine] for distance in range(sta)]
+        sources = [exchange(mine, "sta", distance) for distance in range(sta)]
     else:
-        gathered = lax.all_gather(jnp.stack(mine), "sta")
-        chosen = [gathered[owner_plan[k]] for k in range(blocks)]
-        sources = [[x[g] for g in range(seg)] for x in chosen]
+        gathered = lax.all_gather(mine, "sta")
+        sources = [gathered[owner_plan[k]] for k in range(blocks)]
 
     done = []
     for piece in range(blocks):
@@ -256,8 +290,7 @@
             final = last and complete
             spectra = []
             for h in halves:
-                spectra += [exchange(x, "pol", h) for x in mine]
-                spectra += [exchange(x, "pol", h) for x in sources[piece]]
+                spectra += [exchange(mine, "pol", h), exchange(sources[piece], "pol", h)]
             others = done if final else []
             if final:
                 out_shape = (STEPS, pairs, lags)
@@ -267,20 +300,18 @@
             result = pl.pallas_call(
                 functools.partial(stack_kernel, sizes, piece, halves, blocks),
                 out_shape=jax.ShapeDtypeStruct(out_shape, jnp.float32),
-                in_specs=[smem] * final + [hbm] + [vmem] * len(spectra) + [hbm] * len(others) + [vmem] * len(sums),
+                in_specs=[smem] * final + [vmem] * (1 + len(spectra)) + [hbm] * len(others) + [vmem] * len(sums),
                 out_specs=hbm if final else vmem,
                 scratch_shapes=[
-                    pltpu.VMEM((len(halves), 2, bins, half_lags), jnp.bfloat16),
                     pltpu.VMEM((pairs, lags), jnp.float32),
                     pltpu.VMEM((seg, pairs, LANES), jnp.float32),
                     pltpu.VMEM((seg, stations, 2, 8, LANES), jnp.float32),
                     pltpu.VMEM((pairs * 8, LANES), jnp.float32),
                     pltpu.VMEM((pairs * 8, LANES), jnp.float32),
                     pltpu.VMEM((2, pairs, bins), jnp.bfloat16),
-                    pltpu.SemaphoreType.DMA((len(halves),)),
                     pltpu.SemaphoreType.DMA((STEPS,)),
                 ],
-                compiler_params=pltpu.CompilerParams(vmem_limit_bytes=52 * 1024 * 1024),
+                compiler_params=pltpu.CompilerParams(vmem_limit_bytes=VMEM_BYTES),
                 cost_estimate=pl.CostEstimate(
                     flops=16 * flops, bytes_accessed=1024 * 1024 * len(halves), transcendentals=0
                 ),

time: 25.8 us -> 22.4 us (0.87)
  starting transfers between devices: 11.3 us -> 8.81 us
  Pallas kernels: 8.77 us -> 6.73 us
  local copies, waits for them, and re-layouts: 0.77 us -> 2.36 us
  waiting for transfers between devices: 4.53 us -> 4.16 us
    ppermute x15 -> x6, starting transfers between devices: 11.3 us -> 8.81 us  [exchange(): lax.ppermute(value, axis, [(i ^ distance, i) for i in range(size)])]
    pallas_call x3, Pallas kernels: 7.24 us -> 4.98 us  [shards(): pl.pallas_call(functools.partial(stack_kernel, sizes, piece, halves, bloc...]
    unnamed x4 -> x6, local copies, waits for them, and re-layouts: 0.77 us -> 2.36 us
    ppermute x15 -> x6, waiting for transfers between devices: 4.53 us -> 4.16 us  [exchange(): lax.ppermute(value, axis, [(i ^ distance, i) for i in range(size)])]
  transfers between devices with their start and end apart: 15 -> 6, of which waited for: 2 -> 3; matrix products, arithmetic and copies ran while one was open for 0% -> 0% of each run, Pallas kernels for 17% -> 14%
where the time goes in v6:
time: 22.4 us; the launch traced here: 22.1 us
  starting transfers between devices  8.81 us (39%)
  Pallas kernels  6.73 us (30%)
  waiting for transfers between devices  4.16 us (19%)
  local copies, waits for them, and re-layouts  2.36 us (11%)
    ppermute x6, starting transfers between devices, exchange(): lax.ppermute(value, axis, [(i ^ distance, i) for i in range(size)])  8.81 us
    pallas_call x3, Pallas kernels, shards(): pl.pallas_call(functools.partial(stack_kernel, sizes, piece, halves, bloc...  4.98 us
    ppermute x6, waiting for transfers between devices, exchange(): lax.ppermute(value, axis, [(i ^ distance, i) for i in range(size)])  4.16 us
    unnamed x6, local copies, waits for them, and re-layouts  2.36 us
    pallas_call x1, Pallas kernels, shards(): pl.pallas_call(functools.partial(prepare_kernel, (stations, bands, sta, b...  1.54 us
  transfers between devices with their start and end apart: 6, of which 3 were waited for; matrix products, arithmetic and copies ran while one was open for 0% of the time, Pallas kernels for 14%

profile of v6, /device:TPU:0, one launch (start us, length us, event | category | flops | bytes accessed | tf_op | source)
XLA Modules:
  0.0 22.1 jit_solution(17384846063055045567)
XLA Ops:
  0.0 1.5 %prepare.1.payload_hbm = bf16[144,128]{1,0:T(8,128)(2,1)} custom-call(bf16[128,128]{1,0:T(8,128)(2,1)} %bitcast.9, s32[8,16]{1,0:T(8,128)} %bitcast.10, s32[1,16]{1,0:T(1,128)} %refs_2_.1), custom_call_target="tpu_custom_call" | custom-call | tf_op jit(solution)/shard_map/prepare/pallas_call | solution.py:245
  1.5 4.0 %collective-permute-start.1 = (bf16[144,128]{1,0:T(8,128)(2,1)}, bf16[144,128]{1,0:T(8,128)(2,1)S(1)}, u32[]{:S(2)}, u32[]{:S(2)}) collective-permute-start(bf16[144,128]{1,0:T(8,128)(2,1)} %prepare.1.payload_hbm), channel_id=1, source_target_pairs={{8,0},{12,4},{0,8},{4,12},{9,1},{13,5},{1,9},{5,13},{10,2},{14,6},... | collective-permute-start | bytes 110600 | tf_op jit(solution)/shard_map/ppermute | solution.py:226
  5.6 1.6 %collective-permute-start = (bf16[144,128]{1,0:T(8,128)(2,1)}, bf16[144,128]{1,0:T(8,128)(2,1)S(1)}, u32[]{:S(2)}, u32[]{:S(2)}) collective-permute-start(bf16[144,128]{1,0:T(8,128)(2,1)} %prepare.1.payload_hbm), channel_id=1, source_target_pairs={{4,0},{0,4},{12,8},{8,12},{5,1},{1,5},{13,9},{9,13},{6,2},{2,6},{1... | collective-permute-start | bytes 110600 | tf_op jit(solution)/shard_map/ppermute | solution.py:226
  7.2 1.1 %collective-permute-done.1.refs_2_ = bf16[144,128]{1,0:T(8,128)(2,1)S(1)} collective-permute-done((bf16[144,128]{1,0:T(8,128)(2,1)}, bf16[144,128]{1,0:T(8,128)(2,1)S(1)}, u32[]{:S(2)}, u32[]{:S(2)}) %collective-permute-start.1) | collective-permute-done | bytes 36896 | tf_op jit(solution)/shard_map/ppermute | solution.py:226
  8.2 1.4 %collective-permute-start.2 = (bf16[144,128]{1,0:T(8,128)(2,1)S(1)}, bf16[144,128]{1,0:T(8,128)(2,1)S(1)}, u32[]{:S(2)}, u32[]{:S(2)}) collective-permute-start(bf16[144,128]{1,0:T(8,128)(2,1)S(1)} %collective-permute-done.1.refs_2_), channel_id=1, source_target_pairs={{4,0},{0,4},{12,8},{8,12},{5,1},{1,5},{13,9},{9,13},{6,2},{2,6},{1... | collective-permute-start | bytes 110600 | tf_op jit(solution)/shard_map/ppermute | solution.py:226
  9.6 0.0 copy-start
  9.6 1.6 %copy-done = bf16[2,2,1024,256]{3,2,1,0:T(8,128)(2,1)S(1)} copy-done((bf16[2,2,1024,256]{3,2,1,0:T(8,128)(2,1)S(1)}, bf16[2,2,1024,256]{3,2,1,0:T(8,128)(2,1)}, u32[]{:S(2)}) %copy-start) | copy-done | bytes 2097176
  11.2 0.0 copy-start.1
  11.2 0.8 %copy-done.1 = bf16[144,128]{1,0:T(8,128)(2,1)S(1)} copy-done((bf16[144,128]{1,0:T(8,128)(2,1)S(1)}, bf16[144,128]{1,0:T(8,128)(2,1)}, u32[]{:S(2)}) %copy-start.1) | copy-done | bytes 36888
  12.0 0.2 fetch.1
  12.2 0.0 collective-permute-done.refs_1_
  12.2 0.0 collective-permute-done.2.refs_3_
  12.2 0.1 collective-permute-start.3
  12.3 1.7 %collective-permute-start.4 = (bf16[4,144,128]{2,1,0:T(8,128)(2,1)S(1)}, bf16[4,144,128]{2,1,0:T(8,128)(2,1)S(1)}, u32[]{:S(2)}, u32[]{:S(2)}) collective-permute-start(bf16[4,144,128]{2,1,0:T(8,128)(2,1)S(1)} %join.1.refs_1_.refs_2_), channel_id=1, source_target_pairs={{2,0},{0,2},{3,1},{1,3},{6,4},{4,6},{7,5},{5,7},{10,8},{8,10},{11,... | collective-permute-start | bytes 442376 | tf_op jit(solution)/shard_map/ppermute | solution.py:226
  14.0 0.0 collective-permute-done.3.refs_3_.refs_4_.refs_2_
  14.0 1.9 %stack.3.refs_4_ = f32[64,512]{1,0:T(8,128)S(1)} custom-call(bf16[2,2,1024,256]{3,2,1,0:T(8,128)(2,1)S(1)} %get-tuple-element.9.refs_0_.refs_1_, bf16[4,144,128]{2,1,0:T(8,128)(2,1)S(1)} %join.1.refs_1_.refs_2_, bf16[4,144,128]{2,1,0:T(8,128)(2,1)S(1)} %join.1.refs_1_.refs_2_, bf16[4,144,128]{2,1,0:T(8,128)(2,1)S(1)} %collective-permute-done.3.refs_3_.refs_4_.refs_2_, ...), custom_call_target="tpu_custom_call" | custom-call | flops 4294967296 | bytes 2097152 | tf_op jit(solution)/shard_map/stack/pallas_call | solution.py:300
  15.9 0.0 copy-start.2
  16.0 2.6 %collective-permute-done.4.refs_2_ = bf16[4,144,128]{2,1,0:T(8,128)(2,1)S(1)} collective-permute-done((bf16[4,144,128]{2,1,0:T(8,128)(2,1)S(1)}, bf16[4,144,128]{2,1,0:T(8,128)(2,1)S(1)}, u32[]{:S(2)}, u32[]{:S(2)}) %collective-permute-start.4) | collective-permute-done | bytes 147488 | tf_op jit(solution)/shard_map/ppermute | solution.py:226
  18.6 0.0 collective-permute-start.5
  18.6 0.9 %stack.4.refs_5_ = f32[2,64,256]{2,1,0:T(8,128)S(1)} custom-call(bf16[2,2,1024,256]{3,2,1,0:T(8,128)(2,1)S(1)} %get-tuple-element.9.refs_0_.refs_1_, bf16[4,144,128]{2,1,0:T(8,128)(2,1)S(1)} %join.1.refs_1_.refs_2_, bf16[4,144,128]{2,1,0:T(8,128)(2,1)S(1)} %collective-permute-done.4.refs_2_), custom_call_target="tpu_custom_call" | custom-call | flops 2147483648 | bytes 1048576 | tf_op jit(solution)/shard_map/stack/pallas_call | solution.py:300
  19.5 0.5 %collective-permute-done.5.refs_3_ = bf16[4,144,128]{2,1,0:T(8,128)(2,1)S(1)} collective-permute-done((bf16[4,144,128]{2,1,0:T(8,128)(2,1)S(1)}, bf16[4,144,128]{2,1,0:T(8,128)(2,1)S(1)}, u32[]{:S(2)}, u32[]{:S(2)}) %collective-permute-start.5) | collective-permute-done | bytes 147488 | tf_op jit(solution)/shard_map/ppermute | solution.py:226
  20.0 0.0 copy-done.2
  20.0 2.2 %stack.5 = f32[3,64,512]{2,1,0:T(8,128)} custom-call(s32[3]{0:T(128)S(1)} %copy-done.2, bf16[2,2,1024,256]{3,2,1,0:T(8,128)(2,1)S(1)} %get-tuple-element.9.refs_0_.refs_1_, bf16[4,144,128]{2,1,0:T(8,128)(2,1)S(1)} %collective-permute-done.3.refs_3_.refs_4_.refs_2_, bf16[4,144,128]{2,1,0:T(8,128)(2,1)S(1)} %collective-permute-done.5.refs_3_, ...), custom_call_target="tpu_custom_call" | custom-call | flops 2147483648 | bytes 1048576 | tf_op jit(solution)/shard_map/stack/pallas_call | solution.py:300
  (1 shorter events, 0.0 us)
Async XLA Ops:
  1.5 6.7 %collective-permute-start.1 = (bf16[144,128]{1,0:T(8,128)(2,1)}, bf16[144,128]{1,0:T(8,128)(2,1)S(1)}, u32[]{:S(2)}, u32[]{:S(2)}) collective-permute-start(bf16[144,128]{1,0:T(8,128)(2,1)} %prepare.1.payload_hbm), channel_id=1, source_target_pairs={{8,0},{12,4},{0,8},{4,12},{9,1},{13,5},{1,9},{5,13},{10,2},{14,6},... | collective-permute-start | bytes 110600 | tf_op jit(solution)/shard_map/ppermute | solution.py:226
  5.6 6.6 %collective-permute-start = (bf16[144,128]{1,0:T(8,128)(2,1)}, bf16[144,128]{1,0:T(8,128)(2,1)S(1)}, u32[]{:S(2)}, u32[]{:S(2)}) collective-permute-start(bf16[144,128]{1,0:T(8,128)(2,1)} %prepare.1.payload_hbm), channel_id=1, source_target_pairs={{4,0},{0,4},{12,8},{8,12},{5,1},{1,5},{13,9},{9,13},{6,2},{2,6},{1... | collective-permute-start | bytes 110600 | tf_op jit(solution)/shard_map/ppermute | solution.py:226
  8.2 4.0 %collective-permute-start.2 = (bf16[144,128]{1,0:T(8,128)(2,1)S(1)}, bf16[144,128]{1,0:T(8,128)(2,1)S(1)}, u32[]{:S(2)}, u32[]{:S(2)}) collective-permute-start(bf16[144,128]{1,0:T(8,128)(2,1)S(1)} %collective-permute-done.1.refs_2_), channel_id=1, source_target_pairs={{4,0},{0,4},{12,8},{8,12},{5,1},{1,5},{13,9},{9,13},{6,2},{2,6},{1... | collective-permute-start | bytes 110600 | tf_op jit(solution)/shard_map/ppermute | solution.py:226
  9.6 1.6 %copy-start = (bf16[2,2,1024,256]{3,2,1,0:T(8,128)(2,1)S(1)}, bf16[2,2,1024,256]{3,2,1,0:T(8,128)(2,1)}, u32[]{:S(2)}) copy-start(bf16[2,2,1024,256]{3,2,1,0:T(8,128)(2,1)} %constant.2.clone.table_hbm) | copy-start | bytes 6291460
  11.2 0.8 %copy-start.1 = (bf16[144,128]{1,0:T(8,128)(2,1)S(1)}, bf16[144,128]{1,0:T(8,128)(2,1)}, u32[]{:S(2)}) copy-start(bf16[144,128]{1,0:T(8,128)(2,1)} %prepare.1.payload_hbm) | copy-start | bytes 110596
  12.2 1.8 %collective-permute-start.3 = (bf16[4,144,128]{2,1,0:T(8,128)(2,1)S(1)}, bf16[4,144,128]{2,1,0:T(8,128)(2,1)S(1)}, u32[]{:S(2)}, u32[]{:S(2)}) collective-permute-start(bf16[4,144,128]{2,1,0:T(8,128)(2,1)S(1)} %join.1.refs_1_.refs_2_), channel_id=1, source_target_pairs={{1,0},{0,1},{3,2},{2,3},{5,4},{4,5},{7,6},{6,7},{9,8},{8,9},{11,10... | collective-permute-start | bytes 442376 | tf_op jit(solution)/shard_map/ppermute | solution.py:226
  12.3 6.3 %collective-permute-start.4 = (bf16[4,144,128]{2,1,0:T(8,128)(2,1)S(1)}, bf16[4,144,128]{2,1,0:T(8,128)(2,1)S(1)}, u32[]{:S(2)}, u32[]{:S(2)}) collective-permute-start(bf16[4,144,128]{2,1,0:T(8,128)(2,1)S(1)} %join.1.refs_1_.refs_2_), channel_id=1, source_target_pairs={{2,0},{0,2},{3,1},{1,3},{6,4},{4,6},{7,5},{5,7},{10,8},{8,10},{11,... | collective-permute-start | bytes 442376 | tf_op jit(solution)/shard_map/ppermute | solution.py:226
  15.9 4.0 %copy-start.2 = (s32[3]{0:T(128)S(1)}, s32[3]{0:T(128)}, u32[]{:S(2)}) copy-start(s32[3]{0:T(128)} %refs_0_.1) | copy-start | bytes 40
  18.6 1.4 %collective-permute-start.5 = (bf16[4,144,128]{2,1,0:T(8,128)(2,1)S(1)}, bf16[4,144,128]{2,1,0:T(8,128)(2,1)S(1)}, u32[]{:S(2)}, u32[]{:S(2)}) collective-permute-start(bf16[4,144,128]{2,1,0:T(8,128)(2,1)S(1)} %collective-permute-done.4.refs_2_), channel_id=1, source_target_pairs={{1,0},{0,1},{3,2},{2,3},{5,4},{4,5},{7,6},{6,7},{9,8},{8,9},{11,10... | collective-permute-start | bytes 442376 | tf_op jit(solution)/shard_map/ppermute | solution.py:226

commit v7 on v6

--- a/solution.py
+++ b/solution.py
@@ -79,18 +79,24 @@
     out_ref[pl.ds(2 * count, 16), :] = weights
 
 
-def stack(sizes, block, half, locals_ref, source_ref, wide_weight, local, real_x, imag_x, packed):
-    stations, bands, seg, pol, lags = sizes
+def stack(sizes, half, spectra, wide_weight, local, real_x, imag_x, packed):
+    stations, bands, seg, sta, pol, blocks, lags = sizes
+    own_first = sta == blocks
     pairs = stations * stations
+    me = lax.axis_index("sta")
     row_index = lax.broadcasted_iota(jnp.int32, (16, LANES), 0)
     diagonal = lax.broadcasted_iota(jnp.int32, (pairs, LANES), 0) == lax.broadcasted_iota(
         jnp.int32, (pairs, LANES), 1
     )
     ones = jnp.ones((LANES, LANES), jnp.bfloat16)
     for g in range(seg):
-        flags = locals_ref[g, pl.ds(2 * stations * bands, 16), :].astype(jnp.float32)
-        flags = jnp.sum(jnp.where(row_index == block, flags, 0.0), axis=0, keepdims=True)
-        spread = jnp.where(diagonal, flags, 0.0).astype(jnp.bfloat16)
+        flags = spectra[g, pl.ds(2 * stations * bands, 16), :].astype(jnp.float32)
+        spread = []
+        for n in range(blocks):
+            block = me ^ n if own_first else n
+            row = jnp.sum(jnp.where(row_index == block, flags, 0.0), axis=0, keepdims=True)
+            spread.append(jnp.where(diagonal, row, 0.0))
+        spread = jnp.concatenate(spread, axis=0).astype(jnp.bfloat16)
         wide_weight[g] = jnp.dot(spread, ones, preferred_element_type=jnp.float32)
 
     lag_block = lax.axis_index("seg") * pol + lax.axis_index("pol")
@@ -99,13 +105,14 @@
     cosine, sine = turn(bin_index * (2 * lags * lag_block + lags - 1), 2 * lags * seg * pol)
     for g in range(seg):
         for j in range(stations):
-            tile = locals_ref[g, pl.ds(j * 16, 16), :].astype(jnp.float32)
+            tile = spectra[g, pl.ds(j * 16, 16), :].astype(jnp.float32)
             local[g, j, 0] = tile[:8] * cosine + tile[8:] * sine
             local[g, j, 1] = tile[8:] * cosine - tile[:8] * sine
 
     def one_source(a, carry):
-        start = pl.multiple_of(a * 16, 16)
-        tiles = [source_ref[g, pl.ds(start, 16), :].astype(jnp.float32) for g in range(seg)]
+        start = pl.multiple_of(a % stations * 16, 16)
+        held = (a // stations + (0 if own_first else 1)) * seg
+        tiles = [spectra[held + g, pl.ds(start, 16), :].astype(jnp.float32) for g in range(seg)]
         for j in range(stations):
             pair = a * stations + j
             real_sum = imag_sum = None
@@ -124,11 +131,12 @@
             imag_x[at, :] = imag_sum
         return carry
 
-    lax.fori_loop(0, stations, one_source, 0)
+    lax.fori_loop(0, blocks * stations, one_source, 0)
     for band in range(bands):
         at = pl.ds(band * LANES, LANES)
-        packed[0, :, at] = real_x[pl.ds(band, pairs, stride=8), :].astype(jnp.bfloat16)
-        packed[1, :, at] = imag_x[pl.ds(band, pairs, stride=8), :].astype(jnp.bfloat16)
+        rows = pl.ds(band, blocks * pairs, stride=8)
+        packed[0, :, at] = real_x[rows, :].astype(jnp.bfloat16)
+        packed[1, :, at] = imag_x[rows, :].astype(jnp.bfloat16)
 
 
 def unfold(even, odd):
@@ -148,60 +156,34 @@
     return jnp.concatenate(runs + [after], axis=1)
 
 
-def stack_kernel(sizes, piece, halves, pieces, *refs):
+def stack_kernel(sizes, distance, *refs):
     stations, bands, seg, sta, pol, blocks, lags = sizes
-    own_first = sta == blocks
-    complete = halves[-1] == pol - 1
-    final = complete and piece == pieces - 1
+    first, last = distance == 0, distance == pol - 1
     refs = list(refs)
-    plan_ref = refs.pop(0) if final else None
-    table = refs.pop(0)
-    spectra = [(refs.pop(0), refs.pop(0)) for _ in halves]
-    others = [refs.pop(0) for _ in range(piece if final else 0)]
-    sums = refs.pop(0) if halves[0] else None
-    out_ref = refs.pop(0)
-    result, wide_weight, local, real_x, imag_x, packed, out_sems = refs
-    me = lax.axis_index("sta")
-    block = me ^ piece if own_first else piece
-
-    if final:
-        chosen = [plan_ref[step] ^ me if own_first else step for step in range(STEPS)]
-        for step in range(STEPS):
-            for n, other in enumerate(others):
-
-                @pl.when(chosen[step] == n)
-                def _():
-                    pltpu.make_async_copy(other, out_ref.at[step], out_sems.at[step]).start()
-
-    even = odd = None
-    for n, (locals_ref, source_ref) in enumerate(spectra):
-        half = lax.axis_index("pol") ^ halves[n]
-        stack(
-            (stations, bands, seg, pol, lags), block, half, locals_ref, source_ref,
-            wide_weight, local, real_x, imag_x, packed,
-        )
-        even_term = jnp.dot(packed[0], table[half, 0], preferred_element_type=jnp.float32)
-        odd_term = jnp.dot(packed[1], table[half, 1], preferred_element_type=jnp.float32)
-        even = even_term if even is None else even + even_term
-        odd = odd_term if odd is None else odd + odd_term
-    if sums is not None:
+    plan_ref = refs.pop(0) if last else None
+    table, spectra = refs.pop(0), refs.pop(0)
+    sums = None if first else refs.pop(0)
+    out_ref, result, wide_weight, local, real_x, imag_x, packed, sems = refs
+    half = lax.axis_index("pol") ^ distance
+    stack(sizes, half, spectra, wide_weight, local, real_x, imag_x, packed)
+    even = jnp.dot(packed[0], table[half, 0], preferred_element_type=jnp.float32)
+    odd = jnp.dot(packed[1], table[half, 1], preferred_element_type=jnp.float32)
+    if not first:
         even = even + sums[0]
         odd = odd + sums[1]
-    if not complete:
+    if not last:
         out_ref[0] = even
         out_ref[1] = odd
-    elif not final:
-        out_ref[...] = unfold(even, odd)
-    else:
-        result[...] = unfold(even, odd)
-        for step in range(STEPS):
-
-            @pl.when(chosen[step] == piece)
-            def _():
-                pltpu.make_async_copy(result, out_ref.at[step], out_sems.at[step]).start()
-
-        for step in range(STEPS):
-            pltpu.make_async_copy(result, out_ref.at[step], out_sems.at[step]).wait()
+        return
+    pairs = stations * stations
+    result[...] = unfold(even, odd).reshape(blocks, pairs, lags)
+    copies = []
+    for step in range(STEPS):
+        block = plan_ref[step] ^ lax.axis_index("sta") if sta == blocks else step
+        copies.append(pltpu.make_async_copy(result.at[block], out_ref.at[step], sems.at[step]))
+        copies[-1].start()
+    for copy in copies:
+        copy.wait()
 
 
 def fetch_kernel(table_hbm, payload_hbm, table_ref, payload_ref, sems):
@@ -217,13 +199,36 @@
 
 def join_kernel(*refs):
     *pieces, out_ref = refs
-    for n, piece in enumerate(pieces):
-        out_ref[n] = piece[...]
-
-
-def exchange(value, axis, distance):
-    size = lax.axis_size(axis)
-    return lax.ppermute(value, axis, [(i ^ distance, i) for i in range(size)]) if distance else value
+    first = 0
+    for piece in pieces:
+        out_ref[pl.ds(first, piece.shape[0])] = piece[...]
+        first += piece.shape[0]
+
+
+def join(*pieces):
+    vmem = pl.BlockSpec(memory_space=pltpu.VMEM)
+    shape = (sum(piece.shape[0] for piece in pieces),) + pieces[0].shape[1:]
+    return pl.pallas_call(
+        join_kernel,
+        out_shape=jax.ShapeDtypeStruct(shape, pieces[0].dtype),
+        in_specs=[vmem] * len(pieces),
+        out_specs=vmem,
+        compiler_params=pltpu.CompilerParams(vmem_limit_bytes=VMEM_BYTES),
+        name="join",
+    )(*pieces)
+
+
+def exchange(value, axes, steps):
+    if isinstance(axes, str):
+        axes, steps = (axes,), (steps,)
+    if not any(steps):
+        return value
+    sizes = tuple(lax.axis_size(axis) for axis in axes)
+    pairs = []
+    for index in np.ndindex(*sizes):
+        source = tuple(i ^ step for i, step in zip(index, steps))
+        pairs.append((int(np.ravel_multi_index(source, sizes)), int(np.ravel_multi_index(index, sizes))))
+    return lax.ppermute(value, axes, pairs)
 
 
 def shards(table, raw_spectra, owner_plan, pair_valid, quality):
@@ -262,65 +267,47 @@
         name="fetch",
     )(table, payload)
 
-    held = {0: payload}
+    held = near[None]
     distance = seg // 2
-    while distance:
-        held.update({g ^ distance: exchange(x, "seg", distance) for g, x in held.items()})
+    while distance > 1:
+        arrived = exchange(payload[None] if held.shape[0] == 1 else held, "seg", distance)
+        held = join(held, arrived)
         distance //= 2
-    mine = pl.pallas_call(
-        join_kernel,
-        out_shape=jax.ShapeDtypeStruct((seg, rows, LANES), jnp.bfloat16),
-        in_specs=[vmem] * seg,
-        out_specs=vmem,
-        compiler_params=pltpu.CompilerParams(vmem_limit_bytes=VMEM_BYTES),
-        name="join",
-    )(near, *(held[g] for g in range(1, seg)))
-    if sta == blocks:
-        sources = [exchange(mine, "sta", distance) for distance in range(sta)]
+    if sta == 2 and seg > 1:
+        steps = [(1, 0), (0, 1), (1, 1)]
+        spectra = join(held, *(exchange(held, ("seg", "sta"), step) for step in steps))
     else:
+        mine = join(held, exchange(held, "seg", 1)) if seg > 1 else held
         gathered = lax.all_gather(mine, "sta")
-        sources = [gathered[owner_plan[k]] for k in range(blocks)]
-
-    done = []
-    for piece in range(blocks):
-        last = piece == blocks - 1
-        sums = []
-        for halves in [(h,) for h in range(pol)] if last else [tuple(range(pol))]:
-            complete = halves[-1] == pol - 1
-            final = last and complete
-            spectra = []
-            for h in halves:
-                spectra += [exchange(mine, "pol", h), exchange(sources[piece], "pol", h)]
-            others = done if final else []
-            if final:
-                out_shape = (STEPS, pairs, lags)
-            else:
-                out_shape = (pairs, lags) if complete else (2, pairs, half_lags)
-            flops = 2 * pairs * 2 * bins * lags * len(halves)
-            result = pl.pallas_call(
-                functools.partial(stack_kernel, sizes, piece, halves, blocks),
-                out_shape=jax.ShapeDtypeStruct(out_shape, jnp.float32),
-                in_specs=[smem] * final + [vmem] * (1 + len(spectra)) + [hbm] * len(others) + [vmem] * len(sums),
-                out_specs=hbm if final else vmem,
-                scratch_shapes=[
-                    pltpu.VMEM((pairs, lags), jnp.float32),
-                    pltpu.VMEM((seg, pairs, LANES), jnp.float32),
-                    pltpu.VMEM((seg, stations, 2, 8, LANES), jnp.float32),
-                    pltpu.VMEM((pairs * 8, LANES), jnp.float32),
-                    pltpu.VMEM((pairs * 8, LANES), jnp.float32),
-                    pltpu.VMEM((2, pairs, bins), jnp.bfloat16),
-                    pltpu.SemaphoreType.DMA((STEPS,)),
-                ],
-                compiler_params=pltpu.CompilerParams(vmem_limit_bytes=VMEM_BYTES),
-                cost_estimate=pl.CostEstimate(
-                    flops=16 * flops, bytes_accessed=1024 * 1024 * len(halves), transcendentals=0
-                ),
-                name="stack",
-            )(*([owner_plan] if final else []), table, *spectra, *others, *sums)
-            sums = [result]
-        done.append(result)
-        if not last:
-            sources[piece + 1], done[-1] = lax.optimization_barrier((sources[piece + 1], result))
+        if sta == blocks:
+            spectra = join(*(gathered[lax.axis_index("sta") ^ k] for k in range(blocks)))
+        else:
+            spectra = join(mine, *(gathered[owner_plan[k]] for k in range(blocks)))
+
+    result = None
+    for distance in range(pol):
+        last = distance == pol - 1
+        out_shape = (STEPS, pairs, lags) if last else (2, blocks * pairs, half_lags)
+        flops = 2 * blocks * pairs * 2 * bins * lags
+        sums = [] if result is None else [result]
+        result = pl.pallas_call(
+            functools.partial(stack_kernel, sizes, distance),
+            out_shape=jax.ShapeDtypeStruct(out_shape, jnp.float32),
+            in_specs=[smem] * last + [vmem] * (2 + len(sums)),
+            out_specs=hbm if last else vmem,
+            scratch_shapes=[
+                pltpu.VMEM((blocks, pairs, lags), jnp.float32),
+                pltpu.VMEM((seg, blocks * pairs, LANES), jnp.float32),
+                pltpu.VMEM((seg, stations, 2, 8, LANES), jnp.float32),
+                pltpu.VMEM((blocks * pairs * 8, LANES), jnp.float32),
+                pltpu.VMEM((blocks * pairs * 8, LANES), jnp.float32),
+                pltpu.VMEM((2, blocks * pairs, bins), jnp.bfloat16),
+                pltpu.SemaphoreType.DMA((STEPS,)),
+            ],
+            compiler_params=pltpu.CompilerParams(vmem_limit_bytes=VMEM_BYTES),
+            cost_estimate=pl.CostEstimate(flops=16 * flops, bytes_accessed=1024 * 1024, transcendentals=0),
+            name="stack",
+        )(*([owner_plan] if last else []), table, exchange(spectra, "pol", distance), *sums)
     return result.reshape(STEPS, stations, stations, lags)
 
 

time: 22.4 us -> 20.5 us (0.915)
  starting transfers between devices: 8.81 us -> 7.66 us
  Pallas kernels: 6.73 us -> 6.18 us
  waiting for transfers between devices: 4.16 us -> 3.92 us
    ppermute x6 -> x5, starting transfers between devices: 8.81 us -> 7.66 us  [exchange(): return lax.ppermute(value, axes, pairs)]
    pallas_call x4, Pallas kernels: 4.99 us -> 4.44 us  [the longest x2 4.42 us: shards(): pl.pallas_call(functools.partial(stack_kernel, sizes, distance), out_shap...]
    ppermute x6 -> x5, waiting for transfers between devices: 4.16 us -> 3.92 us  [exchange(): return lax.ppermute(value, axes, pairs)]
  transfers between devices with their start and end apart: 6 -> 5, of which waited for: 3 -> 3; matrix products, arithmetic and copies ran while one was open for 0% -> 0% of each run, Pallas kernels for 14% -> 9%
where the time goes in v7:
time: 20.5 us; the launch traced here: 20.2 us
  starting transfers between devices  7.66 us (37%)
  Pallas kernels  6.18 us (30%)
  waiting for transfers between devices  3.92 us (19%)
  local copies, waits for them, and re-layouts  2.36 us (12%)
    ppermute x5, starting transfers between devices, exchange(): return lax.ppermute(value, axes, pairs)  7.66 us
    pallas_call x2, Pallas kernels, shards(): pl.pallas_call(functools.partial(stack_kernel, sizes, distance), out_shap...  4.42 us
    ppermute x5, waiting for transfers between devices, exchange(): return lax.ppermute(value, axes, pairs)  3.92 us
    unnamed x6, local copies, waits for them, and re-layouts  2.36 us
    pallas_call x1, Pallas kernels, shards(): pl.pallas_call(functools.partial(prepare_kernel, (stations, bands, sta, b...  1.54 us
  transfers between devices with their start and end apart: 5, of which 3 were waited for; matrix products, arithmetic and copies ran while one was open for 0% of the time, Pallas kernels for 9%

profile of v7, /device:TPU:0, one launch (start us, length us, event | category | flops | bytes accessed | tf_op | source)
XLA Modules:
  0.0 20.2 jit_solution(9503908441571290548)
XLA Ops:
  0.0 1.5 %prepare.1.payload_hbm = bf16[144,128]{1,0:T(8,128)(2,1)} custom-call(bf16[128,128]{1,0:T(8,128)(2,1)} %bitcast.13, s32[8,16]{1,0:T(8,128)} %bitcast.14, s32[1,16]{1,0:T(1,128)} %refs_2_.1), custom_call_target="tpu_custom_call" | custom-call | tf_op jit(solution)/shard_map/prepare/pallas_call | solution.py:250
  1.5 4.0 %collective-permute-start = (bf16[1,144,128]{2,1,0:T(8,128)(2,1)}, bf16[1,144,128]{2,1,0:T(8,128)(2,1)S(1)}, u32[]{:S(2)}, u32[]{:S(2)}) collective-permute-start(bf16[1,144,128]{2,1,0:T(8,128)(2,1)} %bitcast.11), channel_id=1, source_target_pairs={{8,0},{12,4},{0,8},{4,12},{9,1},{13,5},{1,9},{5,13},{10,2},{14,6},... | collective-permute-start | bytes 110600 | tf_op jit(solution)/shard_map/ppermute | solution.py:231
  5.6 0.0 copy-start
  5.6 1.6 %copy-done = bf16[2,2,1024,256]{3,2,1,0:T(8,128)(2,1)S(1)} copy-done((bf16[2,2,1024,256]{3,2,1,0:T(8,128)(2,1)S(1)}, bf16[2,2,1024,256]{3,2,1,0:T(8,128)(2,1)}, u32[]{:S(2)}) %copy-start) | copy-done | bytes 2097176
  7.2 0.0 copy-start.1
  7.2 0.8 %copy-done.1 = bf16[144,128]{1,0:T(8,128)(2,1)S(1)} copy-done((bf16[144,128]{1,0:T(8,128)(2,1)S(1)}, bf16[144,128]{1,0:T(8,128)(2,1)}, u32[]{:S(2)}) %copy-start.1) | copy-done | bytes 36888
  7.9 0.2 %fetch.1 = (bf16[2,2,1024,256]{3,2,1,0:T(8,128)(2,1)S(1)}, bf16[144,128]{1,0:T(8,128)(2,1)S(1)}) custom-call(bf16[2,2,1024,256]{3,2,1,0:T(8,128)(2,1)S(1)} %copy-done, bf16[144,128]{1,0:T(8,128)(2,1)S(1)} %copy-done.1), custom_call_target="tpu_custom_call" | custom-call | bytes 4194304 | tf_op jit(solution)/shard_map/fetch/pallas_call | solution.py:259
  8.1 0.0 collective-permute-done.refs_1_
  8.2 2.6 %collective-permute-start.3 = (bf16[2,144,128]{2,1,0:T(8,128)(2,1)S(1)}, bf16[2,144,128]{2,1,0:T(8,128)(2,1)S(1)}, u32[]{:S(2)}, u32[]{:S(2)}) collective-permute-start(bf16[2,144,128]{2,1,0:T(8,128)(2,1)S(1)} %join.2.refs_0_), channel_id=1, source_target_pairs={{6,0},{4,2},{2,4},{0,6},{14,8},{12,10},{10,12},{8,14},{7,1},{5,3},... | collective-permute-start | bytes 221192 | tf_op jit(solution)/shard_map/ppermute | solution.py:231
  10.7 0.5 %collective-permute-start.2 = (bf16[2,144,128]{2,1,0:T(8,128)(2,1)S(1)}, bf16[2,144,128]{2,1,0:T(8,128)(2,1)S(1)}, u32[]{:S(2)}, u32[]{:S(2)}) collective-permute-start(bf16[2,144,128]{2,1,0:T(8,128)(2,1)S(1)} %join.2.refs_0_), channel_id=1, source_target_pairs={{2,0},{0,2},{6,4},{4,6},{10,8},{8,10},{14,12},{12,14},{3,1},{1,3},... | collective-permute-start | bytes 221192 | tf_op jit(solution)/shard_map/ppermute | solution.py:231
  11.3 0.4 %collective-permute-start.1 = (bf16[2,144,128]{2,1,0:T(8,128)(2,1)S(1)}, bf16[2,144,128]{2,1,0:T(8,128)(2,1)S(1)}, u32[]{:S(2)}, u32[]{:S(2)}) collective-permute-start(bf16[2,144,128]{2,1,0:T(8,128)(2,1)S(1)} %join.2.refs_0_), channel_id=1, source_target_pairs={{4,0},{6,2},{0,4},{2,6},{12,8},{14,10},{8,12},{10,14},{5,1},{7,3},... | collective-permute-start | bytes 221192 | tf_op jit(solution)/shard_map/ppermute | solution.py:231
  11.7 1.9 %collective-permute-done.3.refs_3_ = bf16[2,144,128]{2,1,0:T(8,128)(2,1)S(1)} collective-permute-done((bf16[2,144,128]{2,1,0:T(8,128)(2,1)S(1)}, bf16[2,144,128]{2,1,0:T(8,128)(2,1)S(1)}, u32[]{:S(2)}, u32[]{:S(2)}) %collective-permute-start.3) | collective-permute-done | bytes 73760 | tf_op jit(solution)/shard_map/ppermute | solution.py:231
  13.6 1.5 %collective-permute-done.2.refs_2_ = bf16[2,144,128]{2,1,0:T(8,128)(2,1)S(1)} collective-permute-done((bf16[2,144,128]{2,1,0:T(8,128)(2,1)S(1)}, bf16[2,144,128]{2,1,0:T(8,128)(2,1)S(1)}, u32[]{:S(2)}, u32[]{:S(2)}) %collective-permute-start.2) | collective-permute-done | bytes 73760 | tf_op jit(solution)/shard_map/ppermute | solution.py:231
  15.1 0.5 %collective-permute-done.1.refs_1_ = bf16[2,144,128]{2,1,0:T(8,128)(2,1)S(1)} collective-permute-done((bf16[2,144,128]{2,1,0:T(8,128)(2,1)S(1)}, bf16[2,144,128]{2,1,0:T(8,128)(2,1)S(1)}, u32[]{:S(2)}, u32[]{:S(2)}) %collective-permute-start.1) | collective-permute-done | bytes 73760 | tf_op jit(solution)/shard_map/ppermute | solution.py:231
  15.7 0.1 collective-permute-start.4
  15.7 0.0 copy-start.2
  15.7 1.5 %stack.2.refs_3_ = f32[2,128,256]{2,1,0:T(8,128)S(1)} custom-call(bf16[2,2,1024,256]{3,2,1,0:T(8,128)(2,1)S(1)} %get-tuple-element.7.refs_0_.refs_1_, bf16[8,144,128]{2,1,0:T(8,128)(2,1)S(1)} %join.3.refs_1_), custom_call_target="tpu_custom_call" | custom-call | flops 4294967296 | bytes 1048576 | tf_op jit(solution)/shard_map/stack/pallas_call | solution.py:293
  17.3 0.0 collective-permute-done.4.refs_2_
  17.3 0.0 copy-done.2
  17.3 2.9 %stack.3 = f32[3,64,512]{2,1,0:T(8,128)} custom-call(s32[3]{0:T(128)S(1)} %copy-done.2, bf16[2,2,1024,256]{3,2,1,0:T(8,128)(2,1)S(1)} %get-tuple-element.7.refs_0_.refs_1_, bf16[8,144,128]{2,1,0:T(8,128)(2,1)S(1)} %collective-permute-done.4.refs_2_, f32[2,128,256]{2,1,0:T(8,128)S(1)} %stack.2.refs_3_), custom_call_target="tpu_custom_call" | custom-call | flops 4294967296 | bytes 1048576 | tf_op jit(solution)/shard_map/stack/pallas_call | solution.py:293
  (2 shorter events, 0.0 us)
Async XLA Ops:
  1.5 6.6 %collective-permute-start = (bf16[1,144,128]{2,1,0:T(8,128)(2,1)}, bf16[1,144,128]{2,1,0:T(8,128)(2,1)S(1)}, u32[]{:S(2)}, u32[]{:S(2)}) collective-permute-start(bf16[1,144,128]{2,1,0:T(8,128)(2,1)} %bitcast.11), channel_id=1, source_target_pairs={{8,0},{12,4},{0,8},{4,12},{9,1},{13,5},{1,9},{5,13},{10,2},{14,6},... | collective-permute-start | bytes 110600 | tf_op jit(solution)/shard_map/ppermute | solution.py:231
  5.6 1.6 %copy-start = (bf16[2,2,1024,256]{3,2,1,0:T(8,128)(2,1)S(1)}, bf16[2,2,1024,256]{3,2,1,0:T(8,128)(2,1)}, u32[]{:S(2)}) copy-start(bf16[2,2,1024,256]{3,2,1,0:T(8,128)(2,1)} %constant.2.clone.table_hbm) | copy-start | bytes 6291460
  7.2 0.8 %copy-start.1 = (bf16[144,128]{1,0:T(8,128)(2,1)S(1)}, bf16[144,128]{1,0:T(8,128)(2,1)}, u32[]{:S(2)}) copy-start(bf16[144,128]{1,0:T(8,128)(2,1)} %prepare.1.payload_hbm) | copy-start | bytes 110596
  8.2 5.4 %collective-permute-start.3 = (bf16[2,144,128]{2,1,0:T(8,128)(2,1)S(1)}, bf16[2,144,128]{2,1,0:T(8,128)(2,1)S(1)}, u32[]{:S(2)}, u32[]{:S(2)}) collective-permute-start(bf16[2,144,128]{2,1,0:T(8,128)(2,1)S(1)} %join.2.refs_0_), channel_id=1, source_target_pairs={{6,0},{4,2},{2,4},{0,6},{14,8},{12,10},{10,12},{8,14},{7,1},{5,3},... | collective-permute-start | bytes 221192 | tf_op jit(solution)/shard_map/ppermute | solution.py:231
  10.7 4.4 %collective-permute-start.2 = (bf16[2,144,128]{2,1,0:T(8,128)(2,1)S(1)}, bf16[2,144,128]{2,1,0:T(8,128)(2,1)S(1)}, u32[]{:S(2)}, u32[]{:S(2)}) collective-permute-start(bf16[2,144,128]{2,1,0:T(8,128)(2,1)S(1)} %join.2.refs_0_), channel_id=1, source_target_pairs={{2,0},{0,2},{6,4},{4,6},{10,8},{8,10},{14,12},{12,14},{3,1},{1,3},... | collective-permute-start | bytes 221192 | tf_op jit(solution)/shard_map/ppermute | solution.py:231
  11.3 4.4 %collective-permute-start.1 = (bf16[2,144,128]{2,1,0:T(8,128)(2,1)S(1)}, bf16[2,144,128]{2,1,0:T(8,128)(2,1)S(1)}, u32[]{:S(2)}, u32[]{:S(2)}) collective-permute-start(bf16[2,144,128]{2,1,0:T(8,128)(2,1)S(1)} %join.2.refs_0_), channel_id=1, source_target_pairs={{4,0},{6,2},{0,4},{2,6},{12,8},{14,10},{8,12},{10,14},{5,1},{7,3},... | collective-permute-start | bytes 221192 | tf_op jit(solution)/shard_map/ppermute | solution.py:231
  15.7 1.6 %collective-permute-start.4 = (bf16[8,144,128]{2,1,0:T(8,128)(2,1)S(1)}, bf16[8,144,128]{2,1,0:T(8,128)(2,1)S(1)}, u32[]{:S(2)}, u32[]{:S(2)}) collective-permute-start(bf16[8,144,128]{2,1,0:T(8,128)(2,1)S(1)} %join.3.refs_1_), channel_id=1, source_target_pairs={{1,0},{0,1},{3,2},{2,3},{5,4},{4,5},{7,6},{6,7},{9,8},{8,9},{11,10... | collective-permute-start | bytes 884744 | tf_op jit(solution)/shard_map/ppermute | solution.py:231
  15.7 1.6 %copy-start.2 = (s32[3]{0:T(128)S(1)}, s32[3]{0:T(128)}, u32[]{:S(2)}) copy-start(s32[3]{0:T(128)} %refs_0_.1) | copy-start | bytes 40

commit v8 on v7

--- a/solution.py
+++ b/solution.py
@@ -79,7 +79,8 @@
     out_ref[pl.ds(2 * count, 16), :] = weights
 
 
-def stack(sizes, half, spectra, wide_weight, local, real_x, imag_x, packed):
+def stack(sizes, half, held, locals_ref, sources_ref, wide_weight, local, real_x, imag_x, packed):
+    first_block, count, base = held
     stations, bands, seg, sta, pol, blocks, lags = sizes
     own_first = sta == blocks
     pairs = stations * stations
@@ -90,9 +91,9 @@
     )
     ones = jnp.ones((LANES, LANES), jnp.bfloat16)
     for g in range(seg):
-        flags = spectra[g, pl.ds(2 * stations * bands, 16), :].astype(jnp.float32)
+        flags = locals_ref[g, pl.ds(2 * stations * bands, 16), :].astype(jnp.float32)
         spread = []
-        for n in range(blocks):
+        for n in range(first_block, first_block + count):
             block = me ^ n if own_first else n
             row = jnp.sum(jnp.where(row_index == block, flags, 0.0), axis=0, keepdims=True)
             spread.append(jnp.where(diagonal, row, 0.0))
@@ -105,14 +106,14 @@
     cosine, sine = turn(bin_index * (2 * lags * lag_block + lags - 1), 2 * lags * seg * pol)
     for g in range(seg):
         for j in range(stations):
-            tile = spectra[g, pl.ds(j * 16, 16), :].astype(jnp.float32)
+            tile = locals_ref[g, pl.ds(j * 16, 16), :].astype(jnp.float32)
             local[g, j, 0] = tile[:8] * cosine + tile[8:] * sine
             local[g, j, 1] = tile[8:] * cosine - tile[:8] * sine
 
     def one_source(a, carry):
         start = pl.multiple_of(a % stations * 16, 16)
-        held = (a // stations + (0 if own_first else 1)) * seg
-        tiles = [spectra[held + g, pl.ds(start, 16), :].astype(jnp.float32) for g in range(seg)]
+        begin = base + a // stations * seg
+        tiles = [sources_ref[begin + g, pl.ds(start, 16), :].astype(jnp.float32) for g in range(seg)]
         for j in range(stations):
             pair = a * stations + j
             real_sum = imag_sum = None
@@ -131,10 +132,10 @@
             imag_x[at, :] = imag_sum
         return carry
 
-    lax.fori_loop(0, blocks * stations, one_source, 0)
+    lax.fori_loop(0, count * stations, one_source, 0, unroll=2)
     for band in range(bands):
         at = pl.ds(band * LANES, LANES)
-        rows = pl.ds(band, blocks * pairs, stride=8)
+        rows = pl.ds(band, count * pairs, stride=8)
         packed[0, :, at] = real_x[rows, :].astype(jnp.bfloat16)
         packed[1, :, at] = imag_x[rows, :].astype(jnp.bfloat16)
 
@@ -156,27 +157,28 @@
     return jnp.concatenate(runs + [after], axis=1)
 
 
-def stack_kernel(sizes, distance, *refs):
+def stack_kernel(sizes, distance, held, before, *refs):
     stations, bands, seg, sta, pol, blocks, lags = sizes
-    first, last = distance == 0, distance == pol - 1
     refs = list(refs)
-    plan_ref = refs.pop(0) if last else None
-    table, spectra = refs.pop(0), refs.pop(0)
-    sums = None if first else refs.pop(0)
-    out_ref, result, wide_weight, local, real_x, imag_x, packed, sems = refs
+    plan_any = refs.pop(0) if before else None
+    table, locals_ref, sources_ref = refs.pop(0), refs.pop(0), refs.pop(0)
+    sums = [refs.pop(0) for _ in range(before)]
+    out_ref, result, wide_weight, local, real_x, imag_x, packed, plan_ref, sems = refs
+    if before:
+        plan_copy = pltpu.make_async_copy(plan_any, plan_ref, sems.at[STEPS])
+        plan_copy.start()
     half = lax.axis_index("pol") ^ distance
-    stack(sizes, half, spectra, wide_weight, local, real_x, imag_x, packed)
+    stack(sizes, half, held, locals_ref, sources_ref, wide_weight, local, real_x, imag_x, packed)
     even = jnp.dot(packed[0], table[half, 0], preferred_element_type=jnp.float32)
     odd = jnp.dot(packed[1], table[half, 1], preferred_element_type=jnp.float32)
-    if not first:
-        even = even + sums[0]
-        odd = odd + sums[1]
-    if not last:
+    if not before:
         out_ref[0] = even
         out_ref[1] = odd
         return
-    pairs = stations * stations
-    result[...] = unfold(even, odd).reshape(blocks, pairs, lags)
+    even = even + jnp.concatenate([part[0] for part in sums], axis=0)
+    odd = odd + jnp.concatenate([part[1] for part in sums], axis=0)
+    result[...] = unfold(even, odd).reshape(blocks, stations * stations, lags)
+    plan_copy.wait()
     copies = []
     for step in range(STEPS):
         block = plan_ref[step] ^ lax.axis_index("sta") if sta == blocks else step
@@ -273,41 +275,49 @@
         arrived = exchange(payload[None] if held.shape[0] == 1 else held, "seg", distance)
         held = join(held, arrived)
         distance //= 2
+    def run(distance, held, locals_, sources, sums):
+        count = held[1]
+        out_shape = (STEPS, pairs, lags) if sums else (2, count * pairs, half_lags)
+        return pl.pallas_call(
+            functools.partial(stack_kernel, sizes, distance, held, len(sums)),
+            out_shape=jax.ShapeDtypeStruct(out_shape, jnp.float32),
+            in_specs=([hbm] if sums else []) + [vmem] * (3 + len(sums)),
+            out_specs=hbm if sums else vmem,
+            scratch_shapes=[
+                pltpu.VMEM((count, pairs, lags), jnp.float32),
+                pltpu.VMEM((seg, count * pairs, LANES), jnp.float32),
+                pltpu.VMEM((seg, stations, 2, 8, LANES), jnp.float32),
+                pltpu.VMEM((count * pairs * 8, LANES), jnp.float32),
+                pltpu.VMEM((count * pairs * 8, LANES), jnp.float32),
+                pltpu.VMEM((2, count * pairs, bins), jnp.bfloat16),
+                pltpu.SMEM((STEPS,), jnp.int32),
+                pltpu.SemaphoreType.DMA((STEPS + 1,)),
+            ],
+            compiler_params=pltpu.CompilerParams(vmem_limit_bytes=VMEM_BYTES),
+            cost_estimate=pl.CostEstimate(
+                flops=32 * count * pairs * 2 * bins * lags, bytes_accessed=1024 * 1024, transcendentals=0
+            ),
+            name="stack",
+        )(*([owner_plan] if sums else []), table, locals_, sources, *sums)
+
     if sta == 2 and seg > 1:
-        steps = [(1, 0), (0, 1), (1, 1)]
-        spectra = join(held, *(exchange(held, ("seg", "sta"), step) for step in steps))
+        next_held, partner_held, across_held = (
+            exchange(held, ("seg", "sta"), step) for step in ((1, 0), (0, 1), (1, 1))
+        )
+        mine = join(held, next_held)
+        first = run(0, (0, 1, 0), mine, mine, [])
+        first, partner_held, across_held = lax.optimization_barrier((first, partner_held, across_held))
+        others = join(partner_held, across_held)
+        sums = [first, run(0, (1, 1, 0), mine, others, [])]
+        base = 0
     else:
         mine = join(held, exchange(held, "seg", 1)) if seg > 1 else held
         gathered = lax.all_gather(mine, "sta")
-        if sta == blocks:
-            spectra = join(*(gathered[lax.axis_index("sta") ^ k] for k in range(blocks)))
-        else:
-            spectra = join(mine, *(gathered[owner_plan[k]] for k in range(blocks)))
-
-    result = None
-    for distance in range(pol):
-        last = distance == pol - 1
-        out_shape = (STEPS, pairs, lags) if last else (2, blocks * pairs, half_lags)
-        flops = 2 * blocks * pairs * 2 * bins * lags
-        sums = [] if result is None else [result]
-        result = pl.pallas_call(
-            functools.partial(stack_kernel, sizes, distance),
-            out_shape=jax.ShapeDtypeStruct(out_shape, jnp.float32),
-            in_specs=[smem] * last + [vmem] * (2 + len(sums)),
-            out_specs=hbm if last else vmem,
-            scratch_shapes=[
-                pltpu.VMEM((blocks, pairs, lags), jnp.float32),
-                pltpu.VMEM((seg, blocks * pairs, LANES), jnp.float32),
-                pltpu.VMEM((seg, stations, 2, 8, LANES), jnp.float32),
-                pltpu.VMEM((blocks * pairs * 8, LANES), jnp.float32),
-                pltpu.VMEM((blocks * pairs * 8, LANES), jnp.float32),
-                pltpu.VMEM((2, blocks * pairs, bins), jnp.bfloat16),
-                pltpu.SemaphoreType.DMA((STEPS,)),
-            ],
-            compiler_params=pltpu.CompilerParams(vmem_limit_bytes=VMEM_BYTES),
-            cost_estimate=pl.CostEstimate(flops=16 * flops, bytes_accessed=1024 * 1024, transcendentals=0),
-            name="stack",
-        )(*([owner_plan] if last else []), table, exchange(spectra, "pol", distance), *sums)
+        others = join(*(gathered[lax.axis_index("sta") ^ k if sta == blocks else owner_plan[k]] for k in range(blocks)))
+        sums = [run(0, (0, blocks, 0), mine, others, [])]
+        base = seg
+    theirs = exchange(join(mine, others), "pol", 1)
+    result = run(1, (0, blocks, base), theirs, theirs, sums)
     return result.reshape(STEPS, stations, stations, lags)
 
 

time: 20.5 us -> 20.1 us (0.980)
  Pallas kernels: 6.18 us -> 5.93 us
    pallas_call x2 -> x3, Pallas kernels: 4.42 us -> 4.14 us  [run(): pl.pallas_call(functools.partial(stack_kernel, sizes, distance, held, len...]
  transfers between devices with their start and end apart: 5 -> 5, of which waited for: 3 -> 4; matrix products, arithmetic and copies ran while one was open for 0% -> 0% of each run, Pallas kernels for 9% -> 10%
where the time goes in v8:
time: 20.1 us; the launch traced here: 19.9 us
  starting transfers between devices  7.66 us (38%)
  Pallas kernels  5.93 us (30%)
  waiting for transfers between devices  3.82 us (19%)
  local copies, waits for them, and re-layouts  2.36 us (12%)
    ppermute x5, starting transfers between devices, exchange(): return lax.ppermute(value, axes, pairs)  7.66 us
    pallas_call x3, Pallas kernels, run(): pl.pallas_call(functools.partial(stack_kernel, sizes, distance, held, len...  4.14 us
    ppermute x5, waiting for transfers between devices, exchange(): return lax.ppermute(value, axes, pairs)  3.82 us
    unnamed x6, local copies, waits for them, and re-layouts  2.36 us
    pallas_call x1, Pallas kernels, shards(): pl.pallas_call(functools.partial(prepare_kernel, (stations, bands, sta, b...  1.54 us
  transfers between devices with their start and end apart: 5, of which 4 were waited for; matrix products, arithmetic and copies ran while one was open for 0% of the time, Pallas kernels for 10%

profile of v8, /device:TPU:0, one launch (start us, length us, event | category | flops | bytes accessed | tf_op | source)
XLA Modules:
  0.0 19.9 jit_solution(16983008456037131563)
XLA Ops:
  0.0 1.5 %prepare.1.payload_hbm = bf16[144,128]{1,0:T(8,128)(2,1)} custom-call(bf16[128,128]{1,0:T(8,128)(2,1)} %bitcast.13, s32[8,16]{1,0:T(8,128)} %bitcast.14, s32[1,16]{1,0:T(1,128)} %refs_2_.1), custom_call_target="tpu_custom_call" | custom-call | tf_op jit(solution)/shard_map/prepare/pallas_call | solution.py:252
  1.5 4.0 %collective-permute-start = (bf16[1,144,128]{2,1,0:T(8,128)(2,1)}, bf16[1,144,128]{2,1,0:T(8,128)(2,1)S(1)}, u32[]{:S(2)}, u32[]{:S(2)}) collective-permute-start(bf16[1,144,128]{2,1,0:T(8,128)(2,1)} %bitcast.11), channel_id=1, source_target_pairs={{8,0},{12,4},{0,8},{4,12},{9,1},{13,5},{1,9},{5,13},{10,2},{14,6},... | collective-permute-start | bytes 110600 | tf_op jit(solution)/shard_map/ppermute | solution.py:233
  5.6 0.0 copy-start
  5.6 1.6 %copy-done = bf16[2,2,1024,256]{3,2,1,0:T(8,128)(2,1)S(1)} copy-done((bf16[2,2,1024,256]{3,2,1,0:T(8,128)(2,1)S(1)}, bf16[2,2,1024,256]{3,2,1,0:T(8,128)(2,1)}, u32[]{:S(2)}) %copy-start) | copy-done | bytes 2097176
  7.2 0.0 copy-start.1
  7.2 0.8 %copy-done.1 = bf16[144,128]{1,0:T(8,128)(2,1)S(1)} copy-done((bf16[144,128]{1,0:T(8,128)(2,1)S(1)}, bf16[144,128]{1,0:T(8,128)(2,1)}, u32[]{:S(2)}) %copy-start.1) | copy-done | bytes 36888
  7.9 0.2 %fetch.1 = (bf16[2,2,1024,256]{3,2,1,0:T(8,128)(2,1)S(1)}, bf16[144,128]{1,0:T(8,128)(2,1)S(1)}) custom-call(bf16[2,2,1024,256]{3,2,1,0:T(8,128)(2,1)S(1)} %copy-done, bf16[144,128]{1,0:T(8,128)(2,1)S(1)} %copy-done.1), custom_call_target="tpu_custom_call" | custom-call | bytes 4194304 | tf_op jit(solution)/shard_map/fetch/pallas_call | solution.py:261
  8.1 0.0 collective-permute-done.refs_1_
  8.2 1.6 %collective-permute-start.1 = (bf16[2,144,128]{2,1,0:T(8,128)(2,1)S(1)}, bf16[2,144,128]{2,1,0:T(8,128)(2,1)S(1)}, u32[]{:S(2)}, u32[]{:S(2)}) collective-permute-start(bf16[2,144,128]{2,1,0:T(8,128)(2,1)S(1)} %join.4.refs_0_), channel_id=1, source_target_pairs={{4,0},{6,2},{0,4},{2,6},{12,8},{14,10},{8,12},{10,14},{5,1},{7,3},... | collective-permute-start | bytes 221192 | tf_op jit(solution)/shard_map/ppermute | solution.py:233
  9.8 1.5 %collective-permute-start.3 = (bf16[2,144,128]{2,1,0:T(8,128)(2,1)S(1)}, bf16[2,144,128]{2,1,0:T(8,128)(2,1)S(1)}, u32[]{:S(2)}, u32[]{:S(2)}) collective-permute-start(bf16[2,144,128]{2,1,0:T(8,128)(2,1)S(1)} %join.4.refs_0_), channel_id=1, source_target_pairs={{6,0},{4,2},{2,4},{0,6},{14,8},{12,10},{10,12},{8,14},{7,1},{5,3},... | collective-permute-start | bytes 221192 | tf_op jit(solution)/shard_map/ppermute | solution.py:233
  11.3 0.4 %collective-permute-start.2 = (bf16[2,144,128]{2,1,0:T(8,128)(2,1)S(1)}, bf16[2,144,128]{2,1,0:T(8,128)(2,1)S(1)}, u32[]{:S(2)}, u32[]{:S(2)}) collective-permute-start(bf16[2,144,128]{2,1,0:T(8,128)(2,1)S(1)} %join.4.refs_0_), channel_id=1, source_target_pairs={{2,0},{0,2},{6,4},{4,6},{10,8},{8,10},{14,12},{12,14},{3,1},{1,3},... | collective-permute-start | bytes 221192 | tf_op jit(solution)/shard_map/ppermute | solution.py:233
  11.7 0.9 %collective-permute-done.1.refs_1_ = bf16[2,144,128]{2,1,0:T(8,128)(2,1)S(1)} collective-permute-done((bf16[2,144,128]{2,1,0:T(8,128)(2,1)S(1)}, bf16[2,144,128]{2,1,0:T(8,128)(2,1)S(1)}, u32[]{:S(2)}, u32[]{:S(2)}) %collective-permute-start.1) | collective-permute-done | bytes 73760 | tf_op jit(solution)/shard_map/ppermute | solution.py:233
  12.6 0.9 %stack.3.refs_4_ = f32[2,64,256]{2,1,0:T(8,128)S(1)} custom-call(bf16[2,2,1024,256]{3,2,1,0:T(8,128)(2,1)S(1)} %get-tuple-element.10.refs_0_.refs_1_, bf16[4,144,128]{2,1,0:T(8,128)(2,1)S(1)} %join.5.refs_1_.refs_2_.refs_0_, bf16[4,144,128]{2,1,0:T(8,128)(2,1)S(1)} %join.5.refs_1_.refs_2_.refs_0_), custom_call_target="tpu_custom_call" | custom-call | flops 2147483648 | bytes 1048576 | tf_op jit(solution)/shard_map/stack/pallas_call | solution.py:281
  13.5 1.6 %collective-permute-done.3.refs_1_ = bf16[2,144,128]{2,1,0:T(8,128)(2,1)S(1)} collective-permute-done((bf16[2,144,128]{2,1,0:T(8,128)(2,1)S(1)}, bf16[2,144,128]{2,1,0:T(8,128)(2,1)S(1)}, u32[]{:S(2)}, u32[]{:S(2)}) %collective-permute-start.3) | collective-permute-done | bytes 73760 | tf_op jit(solution)/shard_map/ppermute | solution.py:233
  15.1 0.8 %collective-permute-done.2.refs_0_ = bf16[2,144,128]{2,1,0:T(8,128)(2,1)S(1)} collective-permute-done((bf16[2,144,128]{2,1,0:T(8,128)(2,1)S(1)}, bf16[2,144,128]{2,1,0:T(8,128)(2,1)S(1)}, u32[]{:S(2)}, u32[]{:S(2)}) %collective-permute-start.2) | collective-permute-done | bytes 73760 | tf_op jit(solution)/shard_map/ppermute | solution.py:233
  15.9 0.0 copy-start.2
  15.9 0.1 collective-permute-start.4
  16.0 0.9 %stack.4.refs_5_ = f32[2,64,256]{2,1,0:T(8,128)S(1)} custom-call(bf16[2,2,1024,256]{3,2,1,0:T(8,128)(2,1)S(1)} %get-tuple-element.10.refs_0_.refs_1_, bf16[4,144,128]{2,1,0:T(8,128)(2,1)S(1)} %join.5.refs_1_.refs_2_.refs_0_, bf16[4,144,128]{2,1,0:T(8,128)(2,1)S(1)} %join.6.refs_1_.refs_2_), custom_call_target="tpu_custom_call" | custom-call | flops 2147483648 | bytes 1048576 | tf_op jit(solution)/shard_map/stack/pallas_call | solution.py:281
  16.9 0.6 %collective-permute-done.4.refs_2_.refs_3_ = bf16[8,144,128]{2,1,0:T(8,128)(2,1)S(1)} collective-permute-done((bf16[8,144,128]{2,1,0:T(8,128)(2,1)S(1)}, bf16[8,144,128]{2,1,0:T(8,128)(2,1)S(1)}, u32[]{:S(2)}, u32[]{:S(2)}) %collective-permute-start.4) | collective-permute-done | bytes 294944 | tf_op jit(solution)/shard_map/ppermute | solution.py:233
  17.6 0.0 copy-done.2
  17.6 2.3 %stack.5 = f32[3,64,512]{2,1,0:T(8,128)} custom-call(s32[3]{0:T(128)S(1)} %copy-done.2, bf16[2,2,1024,256]{3,2,1,0:T(8,128)(2,1)S(1)} %get-tuple-element.10.refs_0_.refs_1_, bf16[8,144,128]{2,1,0:T(8,128)(2,1)S(1)} %collective-permute-done.4.refs_2_.refs_3_, bf16[8,144,128]{2,1,0:T(8,128)(2,1)S(1)} %collective-permute-done.4.refs_2_.refs_3_, ...), custom_call_target="tpu_custom_call" | custom-call | flops 4294967296 | bytes 1048576 | tf_op jit(solution)/shard_map/stack/pallas_call | solution.py:281
  (4 shorter events, 0.1 us)
Async XLA Ops:
  1.5 6.6 %collective-permute-start = (bf16[1,144,128]{2,1,0:T(8,128)(2,1)}, bf16[1,144,128]{2,1,0:T(8,128)(2,1)S(1)}, u32[]{:S(2)}, u32[]{:S(2)}) collective-permute-start(bf16[1,144,128]{2,1,0:T(8,128)(2,1)} %bitcast.11), channel_id=1, source_target_pairs={{8,0},{12,4},{0,8},{4,12},{9,1},{13,5},{1,9},{5,13},{10,2},{14,6},... | collective-permute-start | bytes 110600 | tf_op jit(solution)/shard_map/ppermute | solution.py:233
  5.6 1.6 %copy-start = (bf16[2,2,1024,256]{3,2,1,0:T(8,128)(2,1)S(1)}, bf16[2,2,1024,256]{3,2,1,0:T(8,128)(2,1)}, u32[]{:S(2)}) copy-start(bf16[2,2,1024,256]{3,2,1,0:T(8,128)(2,1)} %constant.2.clone.table_hbm) | copy-start | bytes 6291460
  7.2 0.8 %copy-start.1 = (bf16[144,128]{1,0:T(8,128)(2,1)S(1)}, bf16[144,128]{1,0:T(8,128)(2,1)}, u32[]{:S(2)}) copy-start(bf16[144,128]{1,0:T(8,128)(2,1)} %prepare.1.payload_hbm) | copy-start | bytes 110596
  8.2 4.4 %collective-permute-start.1 = (bf16[2,144,128]{2,1,0:T(8,128)(2,1)S(1)}, bf16[2,144,128]{2,1,0:T(8,128)(2,1)S(1)}, u32[]{:S(2)}, u32[]{:S(2)}) collective-permute-start(bf16[2,144,128]{2,1,0:T(8,128)(2,1)S(1)} %join.4.refs_0_), channel_id=1, source_target_pairs={{4,0},{6,2},{0,4},{2,6},{12,8},{14,10},{8,12},{10,14},{5,1},{7,3},... | collective-permute-start | bytes 221192 | tf_op jit(solution)/shard_map/ppermute | solution.py:233
  9.8 5.3 %collective-permute-start.3 = (bf16[2,144,128]{2,1,0:T(8,128)(2,1)S(1)}, bf16[2,144,128]{2,1,0:T(8,128)(2,1)S(1)}, u32[]{:S(2)}, u32[]{:S(2)}) collective-permute-start(bf16[2,144,128]{2,1,0:T(8,128)(2,1)S(1)} %join.4.refs_0_), channel_id=1, source_target_pairs={{6,0},{4,2},{2,4},{0,6},{14,8},{12,10},{10,12},{8,14},{7,1},{5,3},... | collective-permute-start | bytes 221192 | tf_op jit(solution)/shard_map/ppermute | solution.py:233
  11.3 4.6 %collective-permute-start.2 = (bf16[2,144,128]{2,1,0:T(8,128)(2,1)S(1)}, bf16[2,144,128]{2,1,0:T(8,128)(2,1)S(1)}, u32[]{:S(2)}, u32[]{:S(2)}) collective-permute-start(bf16[2,144,128]{2,1,0:T(8,128)(2,1)S(1)} %join.4.refs_0_), channel_id=1, source_target_pairs={{2,0},{0,2},{6,4},{4,6},{10,8},{8,10},{14,12},{12,14},{3,1},{1,3},... | collective-permute-start | bytes 221192 | tf_op jit(solution)/shard_map/ppermute | solution.py:233
  15.9 1.7 %copy-start.2 = (s32[3]{0:T(128)S(1)}, s32[3]{0:T(128)}, u32[]{:S(2)}) copy-start(s32[3]{0:T(128)} %refs_0_.1) | copy-start | bytes 40
  15.9 1.6 %collective-permute-start.4 = (bf16[8,144,128]{2,1,0:T(8,128)(2,1)S(1)}, bf16[8,144,128]{2,1,0:T(8,128)(2,1)S(1)}, u32[]{:S(2)}, u32[]{:S(2)}) collective-permute-start(bf16[8,144,128]{2,1,0:T(8,128)(2,1)S(1)} %join.7), channel_id=1, source_target_pairs={{1,0},{0,1},{3,2},{2,3},{5,4},{4,5},{7,6},{6,7},{9,8},{8,9},{11,10... | collective-permute-start | bytes 884744 | tf_op jit(solution)/shard_map/ppermute | solution.py:233

commit v9 on v8

--- a/solution.py
+++ b/solution.py
@@ -75,8 +75,8 @@
         rows.append(valid_row * (dot(quality, pick_source) * local_flags)[:1])
     rows.append(jnp.zeros((16 - blocks, LANES), jnp.float32))
     weights = jnp.concatenate(rows, axis=0).astype(jnp.bfloat16)
-    out_ref[pl.ds(0, 2 * count), :] = white
-    out_ref[pl.ds(2 * count, 16), :] = weights
+    out_ref[0, pl.ds(0, 2 * count), :] = white
+    out_ref[0, pl.ds(2 * count, 16), :] = weights
 
 
 def stack(sizes, half, held, locals_ref, sources_ref, wide_weight, local, real_x, imag_x, packed):
@@ -188,36 +188,33 @@
         copy.wait()
 
 
-def fetch_kernel(table_hbm, payload_hbm, table_ref, payload_ref, sems):
-    copies = [
-        pltpu.make_async_copy(table_hbm, table_ref, sems.at[0]),
-        pltpu.make_async_copy(payload_hbm, payload_ref, sems.at[1]),
-    ]
-    for copy in copies:
-        copy.start()
-    for copy in copies:
-        copy.wait()
-
-
-def join_kernel(*refs):
+def fetch_kernel(table_hbm, table_ref, sem):
+    copy = pltpu.make_async_copy(table_hbm, table_ref, sem)
+    copy.start()
+    copy.wait()
+
+
+def join_kernel(ranges, *refs):
     *pieces, out_ref = refs
-    first = 0
-    for piece in pieces:
-        out_ref[pl.ds(first, piece.shape[0])] = piece[...]
-        first += piece.shape[0]
+    at = 0
+    for piece, (first, count) in zip(pieces, ranges):
+        out_ref[pl.ds(at, count)] = piece[pl.ds(first, count)]
+        at += count
 
 
 def join(*pieces):
+    pieces = [piece if isinstance(piece, tuple) else (piece, 0, piece.shape[0]) for piece in pieces]
+    arrays = [piece[0] for piece in pieces]
+    ranges = [piece[1:] for piece in pieces]
     vmem = pl.BlockSpec(memory_space=pltpu.VMEM)
-    shape = (sum(piece.shape[0] for piece in pieces),) + pieces[0].shape[1:]
     return pl.pallas_call(
-        join_kernel,
-        out_shape=jax.ShapeDtypeStruct(shape, pieces[0].dtype),
-        in_specs=[vmem] * len(pieces),
+        functools.partial(join_kernel, ranges),
+        out_shape=pltpu.VMEM((sum(count for _, count in ranges),) + arrays[0].shape[1:], arrays[0].dtype),
+        in_specs=[vmem] * len(arrays),
         out_specs=vmem,
         compiler_params=pltpu.CompilerParams(vmem_limit_bytes=VMEM_BYTES),
         name="join",
-    )(*pieces)
+    )(*arrays)
 
 
 def exchange(value, axes, steps):
@@ -249,33 +246,29 @@
     smem = pl.BlockSpec(memory_space=pltpu.SMEM)
     hbm = pl.BlockSpec(memory_space=pltpu.HBM)
     plan = [] if sta == blocks else [owner_plan]
-    payload = pl.pallas_call(
+    in_hbm = functools.partial(pltpu.with_memory_space_constraint, memory_space=pltpu.HBM)
+    own = pl.pallas_call(
         functools.partial(prepare_kernel, (stations, bands, sta, blocks)),
-        out_shape=jax.ShapeDtypeStruct((rows, LANES), jnp.bfloat16),
+        out_shape=pltpu.VMEM((1, rows, LANES), jnp.bfloat16),
         in_specs=[smem] * len(plan) + [vmem, vmem, vmem],
         out_specs=vmem,
         scratch_shapes=[pltpu.VMEM((2 * stations * bands, LANES), jnp.float32)],
+        compiler_params=pltpu.CompilerParams(vmem_limit_bytes=VMEM_BYTES),
         name="prepare",
-    )(*plan, raw, jnp.transpose(pair_valid[0]), quality)
-
-    table, near = pl.pallas_call(
+    )(*plan, in_hbm(raw), in_hbm(jnp.transpose(pair_valid[0])), in_hbm(quality))
+
+    table = pl.pallas_call(
         fetch_kernel,
-        out_shape=[jax.ShapeDtypeStruct(x.shape, x.dtype) for x in (table, payload)],
-        in_specs=[hbm, hbm],
-        out_specs=[vmem, vmem],
-        scratch_shapes=[pltpu.SemaphoreType.DMA((2,))],
+        out_shape=pltpu.VMEM(table.shape, table.dtype),
+        in_specs=[hbm],
+        out_specs=vmem,
+        scratch_shapes=[pltpu.SemaphoreType.DMA(())],
         compiler_params=pltpu.CompilerParams(vmem_limit_bytes=VMEM_BYTES),
         cost_estimate=pl.CostEstimate(flops=0, bytes_accessed=2 * table.size * 2, transcendentals=0),
         name="fetch",
-    )(table, payload)
-
-    held = near[None]
-    distance = seg // 2
-    while distance > 1:
-        arrived = exchange(payload[None] if held.shape[0] == 1 else held, "seg", distance)
-        held = join(held, arrived)
-        distance //= 2
-    def run(distance, held, locals_, sources, sums):
+    )(in_hbm(table))
+
+    def run(table, distance, held, locals_, sources, sums):
         count = held[1]
         out_shape = (STEPS, pairs, lags) if sums else (2, count * pairs, half_lags)
         return pl.pallas_call(
@@ -300,24 +293,31 @@
             name="stack",
         )(*([owner_plan] if sums else []), table, locals_, sources, *sums)
 
-    if sta == 2 and seg > 1:
-        next_held, partner_held, across_held = (
-            exchange(held, ("seg", "sta"), step) for step in ((1, 0), (0, 1), (1, 1))
-        )
-        mine = join(held, next_held)
-        first = run(0, (0, 1, 0), mine, mine, [])
-        first, partner_held, across_held = lax.optimization_barrier((first, partner_held, across_held))
-        others = join(partner_held, across_held)
-        sums = [first, run(0, (1, 1, 0), mine, others, [])]
+    both = ("seg", "sta")
+    if sta == 2 and seg == 4:
+        far = exchange(own, "seg", 2)
+        partner = exchange(own, "sta", 1)
+        far, table = lax.optimization_barrier((far, table))
+        near = exchange(join(own, partner, far), "seg", 1)
+        far_partner = exchange(far, "sta", 1)
+        far_across = exchange(far, both, (1, 1))
+        mine = join(own, far, (near, 0, 1), (near, 2, 1))
+        first = run(table, 0, (0, 1, 0), mine, mine, [])
+        first, far_partner, far_across = lax.optimization_barrier((first, far_partner, far_across))
+        others = join(partner, far_partner, (near, 1, 1), far_across)
+        sums = [first, run(table, 0, (1, 1, 0), mine, others, [])]
         base = 0
     else:
-        mine = join(held, exchange(held, "seg", 1)) if seg > 1 else held
+        mine, distance = own, seg // 2
+        while distance:
+            mine = join(mine, exchange(mine, "seg", distance))
+            distance //= 2
         gathered = lax.all_gather(mine, "sta")
         others = join(*(gathered[lax.axis_index("sta") ^ k if sta == blocks else owner_plan[k]] for k in range(blocks)))
-        sums = [run(0, (0, blocks, 0), mine, others, [])]
+        sums = [run(table, 0, (0, blocks, 0), mine, others, [])]
         base = seg
     theirs = exchange(join(mine, others), "pol", 1)
-    result = run(1, (0, blocks, base), theirs, theirs, sums)
+    result = run(table, 1, (0, blocks, base), theirs, theirs, sums)
     return result.reshape(STEPS, stations, stations, lags)
 
 

time: 20.1 us -> 20.2 us (level)
  local copies, waits for them, and re-layouts: 2.36 us -> 0.01 us
  starting transfers between devices: 7.66 us -> 9.22 us
  Pallas kernels: 5.93 us -> 6.7 us
    unnamed x6 -> x2, local copies, waits for them, and re-layouts: 2.36 us -> 0.01 us
    ppermute x5 -> x6, starting transfers between devices: 7.66 us -> 9.22 us  [exchange(): return lax.ppermute(value, axes, pairs)]
    pallas_call x5, Pallas kernels: 0.25 us -> 1.65 us  [the longest x1 1.6 us: shards(): pl.pallas_call(fetch_kernel, out_shape=pltpu.VMEM(table.shape, table.dtyp...]
    pallas_call x1, Pallas kernels: 1.54 us -> 0.91 us  [shards(): pl.pallas_call(functools.partial(prepare_kernel, (stations, bands, sta, b...]
    ppermute x5 -> x6, waiting for transfers between devices: 3.82 us -> 3.97 us  [exchange(): return lax.ppermute(value, axes, pairs)]
  transfers between devices with their start and end apart: 5 -> 6, of which waited for: 4 -> 5; matrix products, arithmetic and copies ran while one was open for 0% -> 0% of each run, Pallas kernels for 10% -> 17%
where the time goes in v9:
time: 20.2 us; the launch traced here: 20 us
  starting transfers between devices  9.22 us (46%)
  Pallas kernels  6.7 us (33%)
  waiting for transfers between devices  3.97 us (20%)
    ppermute x6, starting transfers between devices, exchange(): return lax.ppermute(value, axes, pairs)  9.22 us
    pallas_call x3, Pallas kernels, run(): pl.pallas_call(functools.partial(stack_kernel, sizes, distance, held, len...  4.14 us
    ppermute x6, waiting for transfers between devices, exchange(): return lax.ppermute(value, axes, pairs)  3.97 us
    pallas_call x1, Pallas kernels, shards(): pl.pallas_call(fetch_kernel, out_shape=pltpu.VMEM(table.shape, table.dtyp...  1.6 us
    pallas_call x1, Pallas kernels, shards(): pl.pallas_call(functools.partial(prepare_kernel, (stations, bands, sta, b...  0.91 us
  transfers between devices with their start and end apart: 6, of which 5 were waited for; matrix products, arithmetic and copies ran while one was open for 0% of the time, Pallas kernels for 17%

profile of v9, /device:TPU:0, one launch (start us, length us, event | category | flops | bytes accessed | tf_op | source)
XLA Modules:
  0.0 20.0 jit_solution(12941149074335917865)
XLA Ops:
  0.0 0.9 %prepare.1.refs_0_ = bf16[1,144,128]{2,1,0:T(8,128)(2,1)S(1)} custom-call(bf16[128,128]{1,0:T(8,128)(2,1)} %bitcast.9, s32[8,16]{1,0:T(8,128)} %bitcast.10, s32[1,16]{1,0:T(1,128)} %refs_2_.1), custom_call_target="tpu_custom_call" | custom-call | tf_op jit(solution)/shard_map/prepare/pallas_call | solution.py:250
  0.9 4.1 %collective-permute-start = (bf16[1,144,128]{2,1,0:T(8,128)(2,1)S(1)}, bf16[1,144,128]{2,1,0:T(8,128)(2,1)S(1)}, u32[]{:S(2)}, u32[]{:S(2)}) collective-permute-start(bf16[1,144,128]{2,1,0:T(8,128)(2,1)S(1)} %prepare.1.refs_0_), channel_id=1, source_target_pairs={{8,0},{12,4},{0,8},{4,12},{9,1},{13,5},{1,9},{5,13},{10,2},{14,6},... | collective-permute-start | bytes 110600 | tf_op jit(solution)/shard_map/ppermute | solution.py:230
  5.0 1.5 %collective-permute-start.1 = (bf16[1,144,128]{2,1,0:T(8,128)(2,1)S(1)}, bf16[1,144,128]{2,1,0:T(8,128)(2,1)S(1)}, u32[]{:S(2)}, u32[]{:S(2)}) collective-permute-start(bf16[1,144,128]{2,1,0:T(8,128)(2,1)S(1)} %prepare.1.refs_0_), channel_id=1, source_target_pairs={{2,0},{0,2},{3,1},{1,3},{6,4},{4,6},{7,5},{5,7},{10,8},{8,10},{11,... | collective-permute-start | bytes 110600 | tf_op jit(solution)/shard_map/ppermute | solution.py:230
  6.5 1.6 %fetch.1.refs_0_.refs_1_ = bf16[2,2,1024,256]{3,2,1,0:T(8,128)(2,1)S(1)} custom-call(bf16[2,2,1024,256]{3,2,1,0:T(8,128)(2,1)} %constant.2.clone.table_hbm), custom_call_target="tpu_custom_call" | custom-call | bytes 4194304 | tf_op jit(solution)/shard_map/fetch/pallas_call | solution.py:260
  8.1 0.0 collective-permute-done.refs_2_.refs_1_
  8.1 0.8 %collective-permute-done.1.refs_1_.refs_0_ = bf16[1,144,128]{2,1,0:T(8,128)(2,1)S(1)} collective-permute-done((bf16[1,144,128]{2,1,0:T(8,128)(2,1)S(1)}, bf16[1,144,128]{2,1,0:T(8,128)(2,1)S(1)}, u32[]{:S(2)}, u32[]{:S(2)}) %collective-permute-start.1) | collective-permute-done | bytes 36896 | tf_op jit(solution)/shard_map/ppermute | solution.py:230
  9.0 1.6 %collective-permute-start.2 = (bf16[3,144,128]{2,1,0:T(8,128)(2,1)S(1)}, bf16[3,144,128]{2,1,0:T(8,128)(2,1)S(1)}, u32[]{:S(2)}, u32[]{:S(2)}) collective-permute-start(bf16[3,144,128]{2,1,0:T(8,128)(2,1)S(1)} %join.4), channel_id=1, source_target_pairs={{4,0},{0,4},{12,8},{8,12},{5,1},{1,5},{13,9},{9,13},{6,2},{2,6},{1... | collective-permute-start | bytes 331784 | tf_op jit(solution)/shard_map/ppermute | solution.py:230
  10.6 1.4 %collective-permute-start.4 = (bf16[1,144,128]{2,1,0:T(8,128)(2,1)S(1)}, bf16[1,144,128]{2,1,0:T(8,128)(2,1)S(1)}, u32[]{:S(2)}, u32[]{:S(2)}) collective-permute-start(bf16[1,144,128]{2,1,0:T(8,128)(2,1)S(1)} %collective-permute-done.refs_2_.refs_1_), channel_id=1, source_target_pairs={{6,0},{4,2},{2,4},{0,6},{14,8},{12,10},{10,12},{8,14},{7,1},{5,3},... | collective-permute-start | bytes 110600 | tf_op jit(solution)/shard_map/ppermute | solution.py:230
  12.0 0.5 %collective-permute-start.3 = (bf16[1,144,128]{2,1,0:T(8,128)(2,1)S(1)}, bf16[1,144,128]{2,1,0:T(8,128)(2,1)S(1)}, u32[]{:S(2)}, u32[]{:S(2)}) collective-permute-start(bf16[1,144,128]{2,1,0:T(8,128)(2,1)S(1)} %collective-permute-done.refs_2_.refs_1_), channel_id=1, source_target_pairs={{2,0},{0,2},{3,1},{1,3},{6,4},{4,6},{7,5},{5,7},{10,8},{8,10},{11,... | collective-permute-start | bytes 110600 | tf_op jit(solution)/shard_map/ppermute | solution.py:230
  12.5 1.3 %collective-permute-done.2.refs_2_.refs_3_ = bf16[3,144,128]{2,1,0:T(8,128)(2,1)S(1)} collective-permute-done((bf16[3,144,128]{2,1,0:T(8,128)(2,1)S(1)}, bf16[3,144,128]{2,1,0:T(8,128)(2,1)S(1)}, u32[]{:S(2)}, u32[]{:S(2)}) %collective-permute-start.2) | collective-permute-done | bytes 110624 | tf_op jit(solution)/shard_map/ppermute | solution.py:230
  13.9 0.9 %stack.3.refs_4_ = f32[2,64,256]{2,1,0:T(8,128)S(1)} custom-call(bf16[2,2,1024,256]{3,2,1,0:T(8,128)(2,1)S(1)} %fetch.1.refs_0_.refs_1_, bf16[4,144,128]{2,1,0:T(8,128)(2,1)S(1)} %join.5.refs_1_.refs_2_.refs_0_, bf16[4,144,128]{2,1,0:T(8,128)(2,1)S(1)} %join.5.refs_1_.refs_2_.refs_0_), custom_call_target="tpu_custom_call" | custom-call | flops 2147483648 | bytes 1048576 | tf_op jit(solution)/shard_map/stack/pallas_call | solution.py:274
  14.8 0.7 %collective-permute-done.4.refs_3_ = bf16[1,144,128]{2,1,0:T(8,128)(2,1)S(1)} collective-permute-done((bf16[1,144,128]{2,1,0:T(8,128)(2,1)S(1)}, bf16[1,144,128]{2,1,0:T(8,128)(2,1)S(1)}, u32[]{:S(2)}, u32[]{:S(2)}) %collective-permute-start.4) | collective-permute-done | bytes 36896 | tf_op jit(solution)/shard_map/ppermute | solution.py:230
  15.5 0.5 %collective-permute-done.3.refs_1_ = bf16[1,144,128]{2,1,0:T(8,128)(2,1)S(1)} collective-permute-done((bf16[1,144,128]{2,1,0:T(8,128)(2,1)S(1)}, bf16[1,144,128]{2,1,0:T(8,128)(2,1)S(1)}, u32[]{:S(2)}, u32[]{:S(2)}) %collective-permute-start.3) | collective-permute-done | bytes 36896 | tf_op jit(solution)/shard_map/ppermute | solution.py:230
  16.0 0.0 copy-start
  16.0 0.1 collective-permute-start.5
  16.1 0.9 %stack.4.refs_5_ = f32[2,64,256]{2,1,0:T(8,128)S(1)} custom-call(bf16[2,2,1024,256]{3,2,1,0:T(8,128)(2,1)S(1)} %fetch.1.refs_0_.refs_1_, bf16[4,144,128]{2,1,0:T(8,128)(2,1)S(1)} %join.5.refs_1_.refs_2_.refs_0_, bf16[4,144,128]{2,1,0:T(8,128)(2,1)S(1)} %join.6.refs_1_.refs_2_), custom_call_target="tpu_custom_call" | custom-call | flops 2147483648 | bytes 1048576 | tf_op jit(solution)/shard_map/stack/pallas_call | solution.py:274
  17.0 0.6 %collective-permute-done.5.refs_2_.refs_3_ = bf16[8,144,128]{2,1,0:T(8,128)(2,1)S(1)} collective-permute-done((bf16[8,144,128]{2,1,0:T(8,128)(2,1)S(1)}, bf16[8,144,128]{2,1,0:T(8,128)(2,1)S(1)}, u32[]{:S(2)}, u32[]{:S(2)}) %collective-permute-start.5) | collective-permute-done | bytes 294944 | tf_op jit(solution)/shard_map/ppermute | solution.py:230
  17.7 0.0 copy-done
  17.7 2.3 %stack.5 = f32[3,64,512]{2,1,0:T(8,128)} custom-call(s32[3]{0:T(128)S(1)} %copy-done, bf16[2,2,1024,256]{3,2,1,0:T(8,128)(2,1)S(1)} %fetch.1.refs_0_.refs_1_, bf16[8,144,128]{2,1,0:T(8,128)(2,1)S(1)} %collective-permute-done.5.refs_2_.refs_3_, bf16[8,144,128]{2,1,0:T(8,128)(2,1)S(1)} %collective-permute-done.5.refs_2_.refs_3_, ...), custom_call_target="tpu_custom_call" | custom-call | flops 4294967296 | bytes 1048576 | tf_op jit(solution)/shard_map/stack/pallas_call | solution.py:274
  (4 shorter events, 0.1 us)
Async XLA Ops:
  0.9 7.2 %collective-permute-start = (bf16[1,144,128]{2,1,0:T(8,128)(2,1)S(1)}, bf16[1,144,128]{2,1,0:T(8,128)(2,1)S(1)}, u32[]{:S(2)}, u32[]{:S(2)}) collective-permute-start(bf16[1,144,128]{2,1,0:T(8,128)(2,1)S(1)} %prepare.1.refs_0_), channel_id=1, source_target_pairs={{8,0},{12,4},{0,8},{4,12},{9,1},{13,5},{1,9},{5,13},{10,2},{14,6},... | collective-permute-start | bytes 110600 | tf_op jit(solution)/shard_map/ppermute | solution.py:230
  5.0 4.0 %collective-permute-start.1 = (bf16[1,144,128]{2,1,0:T(8,128)(2,1)S(1)}, bf16[1,144,128]{2,1,0:T(8,128)(2,1)S(1)}, u32[]{:S(2)}, u32[]{:S(2)}) collective-permute-start(bf16[1,144,128]{2,1,0:T(8,128)(2,1)S(1)} %prepare.1.refs_0_), channel_id=1, source_target_pairs={{2,0},{0,2},{3,1},{1,3},{6,4},{4,6},{7,5},{5,7},{10,8},{8,10},{11,... | collective-permute-start | bytes 110600 | tf_op jit(solution)/shard_map/ppermute | solution.py:230
  9.0 4.9 %collective-permute-start.2 = (bf16[3,144,128]{2,1,0:T(8,128)(2,1)S(1)}, bf16[3,144,128]{2,1,0:T(8,128)(2,1)S(1)}, u32[]{:S(2)}, u32[]{:S(2)}) collective-permute-start(bf16[3,144,128]{2,1,0:T(8,128)(2,1)S(1)} %join.4), channel_id=1, source_target_pairs={{4,0},{0,4},{12,8},{8,12},{5,1},{1,5},{13,9},{9,13},{6,2},{2,6},{1... | collective-permute-start | bytes 331784 | tf_op jit(solution)/shard_map/ppermute | solution.py:230
  10.6 4.9 %collective-permute-start.4 = (bf16[1,144,128]{2,1,0:T(8,128)(2,1)S(1)}, bf16[1,144,128]{2,1,0:T(8,128)(2,1)S(1)}, u32[]{:S(2)}, u32[]{:S(2)}) collective-permute-start(bf16[1,144,128]{2,1,0:T(8,128)(2,1)S(1)} %collective-permute-done.refs_2_.refs_1_), channel_id=1, source_target_pairs={{6,0},{4,2},{2,4},{0,6},{14,8},{12,10},{10,12},{8,14},{7,1},{5,3},... | collective-permute-start | bytes 110600 | tf_op jit(solution)/shard_map/ppermute | solution.py:230
  12.0 4.0 %collective-permute-start.3 = (bf16[1,144,128]{2,1,0:T(8,128)(2,1)S(1)}, bf16[1,144,128]{2,1,0:T(8,128)(2,1)S(1)}, u32[]{:S(2)}, u32[]{:S(2)}) collective-permute-start(bf16[1,144,128]{2,1,0:T(8,128)(2,1)S(1)} %collective-permute-done.refs_2_.refs_1_), channel_id=1, source_target_pairs={{2,0},{0,2},{3,1},{1,3},{6,4},{4,6},{7,5},{5,7},{10,8},{8,10},{11,... | collective-permute-start | bytes 110600 | tf_op jit(solution)/shard_map/ppermute | solution.py:230
  16.0 1.7 %copy-start = (s32[3]{0:T(128)S(1)}, s32[3]{0:T(128)}, u32[]{:S(2)}) copy-start(s32[3]{0:T(128)} %refs_0_.1) | copy-start | bytes 40
  16.0 1.6 %collective-permute-start.5 = (bf16[8,144,128]{2,1,0:T(8,128)(2,1)S(1)}, bf16[8,144,128]{2,1,0:T(8,128)(2,1)S(1)}, u32[]{:S(2)}, u32[]{:S(2)}) collective-permute-start(bf16[8,144,128]{2,1,0:T(8,128)(2,1)S(1)} %join.7), channel_id=1, source_target_pairs={{1,0},{0,1},{3,2},{2,3},{5,4},{4,5},{7,6},{6,7},{9,8},{8,9},{11,10... | collective-permute-start | bytes 884744 | tf_op jit(solution)/shard_map/ppermute | solution.py:230

commit v10 on v9

--- a/solution.py
+++ b/solution.py
@@ -157,35 +157,54 @@
     return jnp.concatenate(runs + [after], axis=1)
 
 
-def stack_kernel(sizes, distance, held, before, *refs):
+def stack_kernel(sizes, distance, held, mode, others, *refs):
     stations, bands, seg, sta, pol, blocks, lags = sizes
     refs = list(refs)
-    plan_any = refs.pop(0) if before else None
+    place = mode == "place"
+    plan_any = refs.pop(0) if place else None
     table, locals_ref, sources_ref = refs.pop(0), refs.pop(0), refs.pop(0)
-    sums = [refs.pop(0) for _ in range(before)]
+    sums = None if mode == "sum" else refs.pop(0)
+    others_ref = refs.pop(0) if others else None
     out_ref, result, wide_weight, local, real_x, imag_x, packed, plan_ref, sems = refs
-    if before:
+    if place:
         plan_copy = pltpu.make_async_copy(plan_any, plan_ref, sems.at[STEPS])
         plan_copy.start()
     half = lax.axis_index("pol") ^ distance
     stack(sizes, half, held, locals_ref, sources_ref, wide_weight, local, real_x, imag_x, packed)
+
+    first_block = held[0]
+    if place:
+        plan_copy.wait()
+        chosen = [plan_ref[step] ^ lax.axis_index("sta") if sta == blocks else step for step in range(STEPS)]
+
+        def copy_out(step, source):
+            return pltpu.make_async_copy(source, out_ref.at[step], sems.at[step])
+
+        for step in range(STEPS if others else 0):
+
+            @pl.when(chosen[step] < first_block)
+            def _():
+                copy_out(step, others_ref.at[chosen[step]]).start()
+
     even = jnp.dot(packed[0], table[half, 0], preferred_element_type=jnp.float32)
     odd = jnp.dot(packed[1], table[half, 1], preferred_element_type=jnp.float32)
-    if not before:
+    if mode == "sum":
         out_ref[0] = even
         out_ref[1] = odd
         return
-    even = even + jnp.concatenate([part[0] for part in sums], axis=0)
-    odd = odd + jnp.concatenate([part[1] for part in sums], axis=0)
-    result[...] = unfold(even, odd).reshape(blocks, stations * stations, lags)
-    plan_copy.wait()
-    copies = []
+    lag_sums = unfold(even + sums[0], odd + sums[1]).reshape(held[1], stations * stations, lags)
+    if not place:
+        out_ref[...] = lag_sums
+        return
+    result[...] = lag_sums
     for step in range(STEPS):
-        block = plan_ref[step] ^ lax.axis_index("sta") if sta == blocks else step
-        copies.append(pltpu.make_async_copy(result.at[block], out_ref.at[step], sems.at[step]))
-        copies[-1].start()
-    for copy in copies:
-        copy.wait()
+
+        @pl.when(chosen[step] >= first_block)
+        def _():
+            copy_out(step, result.at[chosen[step] - first_block]).start()
+
+    for step in range(STEPS):
+        copy_out(step, result.at[0]).wait()
 
 
 def fetch_kernel(table_hbm, table_ref, sem):
@@ -268,14 +287,20 @@
         name="fetch",
     )(in_hbm(table))
 
-    def run(table, distance, held, locals_, sources, sums):
+    def run(mode, distance, held, locals_, sources, sums=None, others=None):
         count = held[1]
-        out_shape = (STEPS, pairs, lags) if sums else (2, count * pairs, half_lags)
+        place = mode == "place"
+        if place:
+            out_shape = jax.ShapeDtypeStruct((STEPS, pairs, lags), jnp.float32)
+        else:
+            shape = (2, count * pairs, half_lags) if mode == "sum" else (count, pairs, lags)
+            out_shape = pltpu.VMEM(shape, jnp.float32)
+        before = [x for x in (sums, others) if x is not None]
         return pl.pallas_call(
-            functools.partial(stack_kernel, sizes, distance, held, len(sums)),
-            out_shape=jax.ShapeDtypeStruct(out_shape, jnp.float32),
-            in_specs=([hbm] if sums else []) + [vmem] * (3 + len(sums)),
-            out_specs=hbm if sums else vmem,
+            functools.partial(stack_kernel, sizes, distance, held, mode, others is not None),
+            out_shape=out_shape,
+            in_specs=([hbm] if place else []) + [vmem] * (3 + len(before)),
+            out_specs=hbm if place else vmem,
             scratch_shapes=[
                 pltpu.VMEM((count, pairs, lags), jnp.float32),
                 pltpu.VMEM((seg, count * pairs, LANES), jnp.float32),
@@ -290,23 +315,25 @@
             cost_estimate=pl.CostEstimate(
                 flops=32 * count * pairs * 2 * bins * lags, bytes_accessed=1024 * 1024, transcendentals=0
             ),
-            name="stack",
-        )(*([owner_plan] if sums else []), table, locals_, sources, *sums)
-
-    both = ("seg", "sta")
-    if sta == 2 and seg == 4:
-        far = exchange(own, "seg", 2)
-        partner = exchange(own, "sta", 1)
+            name="stack_" + mode,
+        )(*([in_hbm(owner_plan)] if place else []), table, locals_, sources, *before)
+
+    if sta == 2 and seg > 1:
+        far, distance = own, seg // 2
+        while distance > 1:
+            far = join(far, exchange(far, "seg", distance))
+            distance //= 2
         far, table = lax.optimization_barrier((far, table))
-        near = exchange(join(own, partner, far), "seg", 1)
-        far_partner = exchange(far, "sta", 1)
-        far_across = exchange(far, both, (1, 1))
-        mine = join(own, far, (near, 0, 1), (near, 2, 1))
-        first = run(table, 0, (0, 1, 0), mine, mine, [])
-        first, far_partner, far_across = lax.optimization_barrier((first, far_partner, far_across))
-        others = join(partner, far_partner, (near, 1, 1), far_across)
-        sums = [first, run(table, 0, (1, 1, 0), mine, others, [])]
-        base = 0
+        near, partner, across = (exchange(far, ("seg", "sta"), step) for step in ((1, 0), (0, 1), (1, 1)))
+        mine = join(far, near)
+        mine_too = exchange(mine, "pol", 1)
+        sums = run("sum", 0, (0, 1, 0), mine, mine)
+        first = run("fold", 1, (0, 1, 0), mine_too, mine_too, sums)
+        first, partner, across = lax.optimization_barrier((first, partner, across))
+        others = join(partner, across)
+        others_too = exchange(others, "pol", 1)
+        sums = run("sum", 0, (1, 1, 0), mine, others)
+        result = run("place", 1, (1, 1, 0), mine_too, others_too, sums, first)
     else:
         mine, distance = own, seg // 2
         while distance:
@@ -314,10 +341,9 @@
             distance //= 2
         gathered = lax.all_gather(mine, "sta")
         others = join(*(gathered[lax.axis_index("sta") ^ k if sta == blocks else owner_plan[k]] for k in range(blocks)))
-        sums = [run(table, 0, (0, blocks, 0), mine, others, [])]
-        base = seg
-    theirs = exchange(join(mine, others), "pol", 1)
-    result = run(table, 1, (0, blocks, base), theirs, theirs, sums)
+        sums = run("sum", 0, (0, blocks, 0), mine, others)
+        theirs = exchange(join(mine, others), "pol", 1)
+        result = run("place", 1, (0, blocks, seg), theirs, theirs, sums)
     return result.reshape(STEPS, stations, stations, lags)
 
 

time: 20.2 us -> 18.4 us (0.911)
  starting transfers between devices: 9.22 us -> 7.76 us
  waiting for transfers between devices: 3.97 us -> 3.18 us
  Pallas kernels: 6.7 us -> 7.18 us
    ppermute x6, starting transfers between devices: 9.22 us -> 7.76 us  [exchange(): return lax.ppermute(value, axes, pairs)]
    ppermute x6, waiting for transfers between devices: 3.97 us -> 3.18 us  [exchange(): return lax.ppermute(value, axes, pairs)]
    pallas_call x3 -> x4, Pallas kernels: 4.14 us -> 4.64 us  [run(): pl.pallas_call(functools.partial(stack_kernel, sizes, distance, held, mod...]
  transfers between devices with their start and end apart: 6 -> 6, of which waited for: 5 -> 5; matrix products, arithmetic and copies ran while one was open for 0% -> 0% of each run, Pallas kernels for 17% -> 24%
where the time goes in v10:
time: 18.4 us; the launch traced here: 18.2 us
  starting transfers between devices  7.76 us (42%)
  Pallas kernels  7.18 us (39%)
  waiting for transfers between devices  3.18 us (17%)
    ppermute x6, starting transfers between devices, exchange(): return lax.ppermute(value, axes, pairs)  7.76 us
    pallas_call x4, Pallas kernels, run(): pl.pallas_call(functools.partial(stack_kernel, sizes, distance, held, mod...  4.64 us
    ppermute x6, waiting for transfers between devices, exchange(): return lax.ppermute(value, axes, pairs)  3.18 us
    pallas_call x1, Pallas kernels, shards(): pl.pallas_call(fetch_kernel, out_shape=pltpu.VMEM(table.shape, table.dtyp...  1.6 us
    pallas_call x1, Pallas kernels, shards(): pl.pallas_call(functools.partial(prepare_kernel, (stations, bands, sta, b...  0.91 us
  transfers between devices with their start and end apart: 6, of which 5 were waited for; matrix products, arithmetic and copies ran while one was open for 0% of the time, Pallas kernels for 24%

profile of v10, /device:TPU:0, one launch (start us, length us, event | category | flops | bytes accessed | tf_op | source)
XLA Modules:
  0.0 18.2 jit_solution(337822274028484245)
XLA Ops:
  0.0 0.9 %prepare.1.refs_0_ = bf16[1,144,128]{2,1,0:T(8,128)(2,1)S(1)} custom-call(bf16[128,128]{1,0:T(8,128)(2,1)} %bitcast.9, s32[8,16]{1,0:T(8,128)} %bitcast.10, s32[1,16]{1,0:T(1,128)} %refs_2_.1), custom_call_target="tpu_custom_call" | custom-call | tf_op jit(solution)/shard_map/prepare/pallas_call | solution.py:269
  0.9 4.1 %collective-permute-start = (bf16[1,144,128]{2,1,0:T(8,128)(2,1)S(1)}, bf16[1,144,128]{2,1,0:T(8,128)(2,1)S(1)}, u32[]{:S(2)}, u32[]{:S(2)}) collective-permute-start(bf16[1,144,128]{2,1,0:T(8,128)(2,1)S(1)} %prepare.1.refs_0_), channel_id=1, source_target_pairs={{8,0},{12,4},{0,8},{4,12},{9,1},{13,5},{1,9},{5,13},{10,2},{14,6},... | collective-permute-start | bytes 110600 | tf_op jit(solution)/shard_map/ppermute | solution.py:249
  5.0 1.6 %fetch.1.refs_0_.refs_1_ = bf16[2,2,1024,256]{3,2,1,0:T(8,128)(2,1)S(1)} custom-call(bf16[2,2,1024,256]{3,2,1,0:T(8,128)(2,1)} %constant.2.clone.table_hbm), custom_call_target="tpu_custom_call" | custom-call | bytes 4194304 | tf_op jit(solution)/shard_map/fetch/pallas_call | solution.py:279
  6.6 0.7 %collective-permute-done.refs_1_ = bf16[1,144,128]{2,1,0:T(8,128)(2,1)S(1)} collective-permute-done((bf16[1,144,128]{2,1,0:T(8,128)(2,1)S(1)}, bf16[1,144,128]{2,1,0:T(8,128)(2,1)S(1)}, u32[]{:S(2)}, u32[]{:S(2)}) %collective-permute-start) | collective-permute-done | bytes 36896 | tf_op jit(solution)/shard_map/ppermute | solution.py:249
  7.4 1.5 %collective-permute-start.1 = (bf16[2,144,128]{2,1,0:T(8,128)(2,1)S(1)}, bf16[2,144,128]{2,1,0:T(8,128)(2,1)S(1)}, u32[]{:S(2)}, u32[]{:S(2)}) collective-permute-start(bf16[2,144,128]{2,1,0:T(8,128)(2,1)S(1)} %join.3.refs_0_), channel_id=1, source_target_pairs={{4,0},{6,2},{0,4},{2,6},{12,8},{14,10},{8,12},{10,14},{5,1},{7,3},... | collective-permute-start | bytes 221192 | tf_op jit(solution)/shard_map/ppermute | solution.py:249
  8.9 1.6 %collective-permute-start.4 = (bf16[2,144,128]{2,1,0:T(8,128)(2,1)S(1)}, bf16[2,144,128]{2,1,0:T(8,128)(2,1)S(1)}, u32[]{:S(2)}, u32[]{:S(2)}) collective-permute-start(bf16[2,144,128]{2,1,0:T(8,128)(2,1)S(1)} %join.3.refs_0_), channel_id=1, source_target_pairs={{6,0},{4,2},{2,4},{0,6},{14,8},{12,10},{10,12},{8,14},{7,1},{5,3},... | collective-permute-start | bytes 221192 | tf_op jit(solution)/shard_map/ppermute | solution.py:249
  10.5 0.3 %collective-permute-start.3 = (bf16[2,144,128]{2,1,0:T(8,128)(2,1)S(1)}, bf16[2,144,128]{2,1,0:T(8,128)(2,1)S(1)}, u32[]{:S(2)}, u32[]{:S(2)}) collective-permute-start(bf16[2,144,128]{2,1,0:T(8,128)(2,1)S(1)} %join.3.refs_0_), channel_id=1, source_target_pairs={{2,0},{0,2},{6,4},{4,6},{10,8},{8,10},{14,12},{12,14},{3,1},{1,3},... | collective-permute-start | bytes 221192 | tf_op jit(solution)/shard_map/ppermute | solution.py:249
  10.9 1.5 %collective-permute-done.1.refs_1_ = bf16[2,144,128]{2,1,0:T(8,128)(2,1)S(1)} collective-permute-done((bf16[2,144,128]{2,1,0:T(8,128)(2,1)S(1)}, bf16[2,144,128]{2,1,0:T(8,128)(2,1)S(1)}, u32[]{:S(2)}, u32[]{:S(2)}) %collective-permute-start.1) | collective-permute-done | bytes 73760 | tf_op jit(solution)/shard_map/ppermute | solution.py:249
  12.3 0.1 collective-permute-start.2
  12.4 0.9 %stack_sum.2.refs_3_ = f32[2,64,256]{2,1,0:T(8,128)S(1)} custom-call(bf16[2,2,1024,256]{3,2,1,0:T(8,128)(2,1)S(1)} %fetch.1.refs_0_.refs_1_, bf16[4,144,128]{2,1,0:T(8,128)(2,1)S(1)} %join.4.refs_1_.refs_2_, bf16[4,144,128]{2,1,0:T(8,128)(2,1)S(1)} %join.4.refs_1_.refs_2_), custom_call_target="tpu_custom_call" | custom-call | flops 2147483648 | bytes 1048576 | tf_op jit(solution)/shard_map/stack_sum/pallas_call | solution.py:299
  13.4 0.4 %collective-permute-done.2.refs_1_.refs_2_ = bf16[4,144,128]{2,1,0:T(8,128)(2,1)S(1)} collective-permute-done((bf16[4,144,128]{2,1,0:T(8,128)(2,1)S(1)}, bf16[4,144,128]{2,1,0:T(8,128)(2,1)S(1)}, u32[]{:S(2)}, u32[]{:S(2)}) %collective-permute-start.2) | collective-permute-done | bytes 147488 | tf_op jit(solution)/shard_map/ppermute | solution.py:249
  13.8 1.0 %stack_fold.1.refs_5_ = f32[1,64,512]{2,1,0:T(8,128)S(1)} custom-call(bf16[2,2,1024,256]{3,2,1,0:T(8,128)(2,1)S(1)} %fetch.1.refs_0_.refs_1_, bf16[4,144,128]{2,1,0:T(8,128)(2,1)S(1)} %collective-permute-done.2.refs_1_.refs_2_, bf16[4,144,128]{2,1,0:T(8,128)(2,1)S(1)} %collective-permute-done.2.refs_1_.refs_2_, f32[2,64,256]{2,1,0:T(8,128)S(1)} %stack_sum.2.refs_3_), custom_call_target="tpu_custom_call" | custom-call | flops 2147483648 | bytes 1048576 | tf_op jit(solution)/shard_map/stack_fold/pallas_call | solution.py:299
  14.8 0.0 collective-permute-done.4.refs_1_
  14.8 0.1 collective-permute-done.3.refs_0_
  14.9 0.1 collective-permute-start.5
  15.0 0.9 %stack_sum.3.refs_4_ = f32[2,64,256]{2,1,0:T(8,128)S(1)} custom-call(bf16[2,2,1024,256]{3,2,1,0:T(8,128)(2,1)S(1)} %fetch.1.refs_0_.refs_1_, bf16[4,144,128]{2,1,0:T(8,128)(2,1)S(1)} %join.4.refs_1_.refs_2_, bf16[4,144,128]{2,1,0:T(8,128)(2,1)S(1)} %join.5.refs_2_), custom_call_target="tpu_custom_call" | custom-call | flops 2147483648 | bytes 1048576 | tf_op jit(solution)/shard_map/stack_sum/pallas_call | solution.py:299
  16.0 0.4 %collective-permute-done.5.refs_3_ = bf16[4,144,128]{2,1,0:T(8,128)(2,1)S(1)} collective-permute-done((bf16[4,144,128]{2,1,0:T(8,128)(2,1)S(1)}, bf16[4,144,128]{2,1,0:T(8,128)(2,1)S(1)}, u32[]{:S(2)}, u32[]{:S(2)}) %collective-permute-start.5) | collective-permute-done | bytes 147488 | tf_op jit(solution)/shard_map/ppermute | solution.py:249
  16.4 1.8 %stack_place.1 = f32[3,64,512]{2,1,0:T(8,128)} custom-call(s32[3]{0:T(128)} %refs_0_.1, bf16[2,2,1024,256]{3,2,1,0:T(8,128)(2,1)S(1)} %fetch.1.refs_0_.refs_1_, bf16[4,144,128]{2,1,0:T(8,128)(2,1)S(1)} %collective-permute-done.2.refs_1_.refs_2_, bf16[4,144,128]{2,1,0:T(8,128)(2,1)S(1)} %collective-permute-done.5.refs_3_, ...), custom_call_target="tpu_custom_call" | custom-call | flops 2147483648 | bytes 1048576 | tf_op jit(solution)/shard_map/stack_place/pallas_call | solution.py:299
  (3 shorter events, 0.0 us)
Async XLA Ops:
  0.9 6.4 %collective-permute-start = (bf16[1,144,128]{2,1,0:T(8,128)(2,1)S(1)}, bf16[1,144,128]{2,1,0:T(8,128)(2,1)S(1)}, u32[]{:S(2)}, u32[]{:S(2)}) collective-permute-start(bf16[1,144,128]{2,1,0:T(8,128)(2,1)S(1)} %prepare.1.refs_0_), channel_id=1, source_target_pairs={{8,0},{12,4},{0,8},{4,12},{9,1},{13,5},{1,9},{5,13},{10,2},{14,6},... | collective-permute-start | bytes 110600 | tf_op jit(solution)/shard_map/ppermute | solution.py:249
  7.4 5.0 %collective-permute-start.1 = (bf16[2,144,128]{2,1,0:T(8,128)(2,1)S(1)}, bf16[2,144,128]{2,1,0:T(8,128)(2,1)S(1)}, u32[]{:S(2)}, u32[]{:S(2)}) collective-permute-start(bf16[2,144,128]{2,1,0:T(8,128)(2,1)S(1)} %join.3.refs_0_), channel_id=1, source_target_pairs={{4,0},{6,2},{0,4},{2,6},{12,8},{14,10},{8,12},{10,14},{5,1},{7,3},... | collective-permute-start | bytes 221192 | tf_op jit(solution)/shard_map/ppermute | solution.py:249
  8.9 5.9 %collective-permute-start.4 = (bf16[2,144,128]{2,1,0:T(8,128)(2,1)S(1)}, bf16[2,144,128]{2,1,0:T(8,128)(2,1)S(1)}, u32[]{:S(2)}, u32[]{:S(2)}) collective-permute-start(bf16[2,144,128]{2,1,0:T(8,128)(2,1)S(1)} %join.3.refs_0_), channel_id=1, source_target_pairs={{6,0},{4,2},{2,4},{0,6},{14,8},{12,10},{10,12},{8,14},{7,1},{5,3},... | collective-permute-start | bytes 221192 | tf_op jit(solution)/shard_map/ppermute | solution.py:249
  10.5 4.4 %collective-permute-start.3 = (bf16[2,144,128]{2,1,0:T(8,128)(2,1)S(1)}, bf16[2,144,128]{2,1,0:T(8,128)(2,1)S(1)}, u32[]{:S(2)}, u32[]{:S(2)}) collective-permute-start(bf16[2,144,128]{2,1,0:T(8,128)(2,1)S(1)} %join.3.refs_0_), channel_id=1, source_target_pairs={{2,0},{0,2},{6,4},{4,6},{10,8},{8,10},{14,12},{12,14},{3,1},{1,3},... | collective-permute-start | bytes 221192 | tf_op jit(solution)/shard_map/ppermute | solution.py:249
  12.3 1.4 %collective-permute-start.2 = (bf16[4,144,128]{2,1,0:T(8,128)(2,1)S(1)}, bf16[4,144,128]{2,1,0:T(8,128)(2,1)S(1)}, u32[]{:S(2)}, u32[]{:S(2)}) collective-permute-start(bf16[4,144,128]{2,1,0:T(8,128)(2,1)S(1)} %join.4.refs_1_.refs_2_), channel_id=1, source_target_pairs={{1,0},{0,1},{3,2},{2,3},{5,4},{4,5},{7,6},{6,7},{9,8},{8,9},{11,10... | collective-permute-start | bytes 442376 | tf_op jit(solution)/shard_map/ppermute | solution.py:249
  14.9 1.4 %collective-permute-start.5 = (bf16[4,144,128]{2,1,0:T(8,128)(2,1)S(1)}, bf16[4,144,128]{2,1,0:T(8,128)(2,1)S(1)}, u32[]{:S(2)}, u32[]{:S(2)}) collective-permute-start(bf16[4,144,128]{2,1,0:T(8,128)(2,1)S(1)} %join.5.refs_2_), channel_id=1, source_target_pairs={{1,0},{0,1},{3,2},{2,3},{5,4},{4,5},{7,6},{6,7},{9,8},{8,9},{11,10... | collective-permute-start | bytes 442376 | tf_op jit(solution)/shard_map/ppermute | solution.py:249

commit v11 on v9

--- a/solution.py
+++ b/solution.py
@@ -79,12 +79,9 @@
     out_ref[0, pl.ds(2 * count, 16), :] = weights
 
 
-def stack(sizes, half, held, locals_ref, sources_ref, wide_weight, local, real_x, imag_x, packed):
-    first_block, count, base = held
-    stations, bands, seg, sta, pol, blocks, lags = sizes
-    own_first = sta == blocks
+def spread_weights(sizes, first_block, locals_ref, wide):
+    stations, bands, seg, sta, pol, blocks, lags = sizes
     pairs = stations * stations
-    me = lax.axis_index("sta")
     row_index = lax.broadcasted_iota(jnp.int32, (16, LANES), 0)
     diagonal = lax.broadcasted_iota(jnp.int32, (pairs, LANES), 0) == lax.broadcasted_iota(
         jnp.int32, (pairs, LANES), 1
@@ -93,51 +90,184 @@
     for g in range(seg):
         flags = locals_ref[g, pl.ds(2 * stations * bands, 16), :].astype(jnp.float32)
         spread = []
-        for n in range(first_block, first_block + count):
-            block = me ^ n if own_first else n
+        for n in range(first_block, blocks):
+            block = lax.axis_index("sta") ^ n if sta == blocks else n
             row = jnp.sum(jnp.where(row_index == block, flags, 0.0), axis=0, keepdims=True)
             spread.append(jnp.where(diagonal, row, 0.0))
         spread = jnp.concatenate(spread, axis=0).astype(jnp.bfloat16)
-        wide_weight[g] = jnp.dot(spread, ones, preferred_element_type=jnp.float32)
-
+        wide[g] = jnp.dot(spread, ones, preferred_element_type=jnp.float32)
+
+
+def middle_phase(sizes, distance):
+    stations, bands, seg, sta, pol, blocks, lags = sizes
     lag_block = lax.axis_index("seg") * pol + lax.axis_index("pol")
+    half = lax.axis_index("pol") ^ distance
     row = half * bands + lax.broadcasted_iota(jnp.int32, (bands, LANES), 0)
     bin_index = row * LANES + lax.broadcasted_iota(jnp.int32, (bands, LANES), 1)
-    cosine, sine = turn(bin_index * (2 * lags * lag_block + lags - 1), 2 * lags * seg * pol)
+    return turn(bin_index * (2 * lags * lag_block + lags - 1), 2 * lags * seg * pol)
+
+
+def turn_locals(sizes, cosine, sine, locals_ref, local):
+    stations, bands, seg = sizes[:3]
     for g in range(seg):
         for j in range(stations):
             tile = locals_ref[g, pl.ds(j * 16, 16), :].astype(jnp.float32)
-            local[g, j, 0] = tile[:8] * cosine + tile[8:] * sine
-            local[g, j, 1] = tile[8:] * cosine - tile[:8] * sine
-
+            local[g, j, 0] = tile[:bands] * cosine + tile[bands:] * sine
+            local[g, j, 1] = tile[bands:] * cosine - tile[:bands] * sine
+
+
+def add_products(stations, count, segments, tile_of, weight_of, local_of, before, real_x, imag_x):
     def one_source(a, carry):
-        start = pl.multiple_of(a % stations * 16, 16)
-        begin = base + a // stations * seg
-        tiles = [sources_ref[begin + g, pl.ds(start, 16), :].astype(jnp.float32) for g in range(seg)]
+        tiles = [tile_of(n, a).astype(jnp.float32) for n in range(segments)]
         for j in range(stations):
             pair = a * stations + j
+            at = pl.ds(pair * 8 if isinstance(pair, int) else pl.multiple_of(pair * 8, 8), 8)
             real_sum = imag_sum = None
-            for g in range(seg):
-                weight = jnp.broadcast_to(wide_weight[g, pl.ds(pair, 1), :], (8, LANES))
-                real_src = tiles[g][:8] * weight
-                imag_src = tiles[g][8:] * weight
-                real_loc = local[g, j, 0]
-                imag_loc = local[g, j, 1]
+            if before is not None:
+                real_sum, imag_sum = before[0, at, :], before[1, at, :]
+            for n in range(segments):
+                weight = jnp.broadcast_to(weight_of(n, pair), (8, LANES))
+                real_src = tiles[n][:8] * weight
+                imag_src = tiles[n][8:] * weight
+                real_loc, imag_loc = local_of(n, j)
                 real_term = real_src * real_loc + imag_src * imag_loc
                 imag_term = imag_src * real_loc - real_src * imag_loc
-                real_sum = real_term if g == 0 else real_sum + real_term
-                imag_sum = imag_term if g == 0 else imag_sum + imag_term
-            at = pl.ds(pl.multiple_of(pair * 8, 8), 8)
+                real_sum = real_term if real_sum is None else real_sum + real_term
+                imag_sum = imag_term if imag_sum is None else imag_sum + imag_term
             real_x[at, :] = real_sum
             imag_x[at, :] = imag_sum
         return carry
 
-    lax.fori_loop(0, count * stations, one_source, 0, unroll=2)
+    if count <= 8:
+        for a in range(count):
+            one_source(a, 0)
+    else:
+        lax.fori_loop(0, count, one_source, 0, unroll=2)
+
+
+def pack(rows, bands, real_x, imag_x, packed):
     for band in range(bands):
         at = pl.ds(band * LANES, LANES)
-        rows = pl.ds(band, count * pairs, stride=8)
-        packed[0, :, at] = real_x[rows, :].astype(jnp.bfloat16)
-        packed[1, :, at] = imag_x[rows, :].astype(jnp.bfloat16)
+        strided = pl.ds(band, rows, stride=8)
+        packed[0, :, at] = real_x[strided, :].astype(jnp.bfloat16)
+        packed[1, :, at] = imag_x[strided, :].astype(jnp.bfloat16)
+
+
+def transform(packed, table):
+    dot = functools.partial(jnp.dot, preferred_element_type=jnp.float32)
+    return dot(packed[0], table[0]), dot(packed[1], table[1])
+
+
+def source_tile(sources_ref, base, count, stations):
+    def tile_of(n, a):
+        start = a % stations * 16
+        start = start if isinstance(a, int) else pl.multiple_of(start, 16)
+        return sources_ref[base + a // stations * count + n, pl.ds(start, 16), :]
+
+    return tile_of
+
+
+def place(sizes, plan_copy, plan_ref, others_ref, result, out_ref, sems):
+    stations, bands, seg, sta, pol, blocks, lags = sizes
+    first_block = others_ref.shape[0] if others_ref is not None else 0
+    plan_copy.wait()
+    chosen = [plan_ref[step] ^ lax.axis_index("sta") if sta == blocks else step for step in range(STEPS)]
+
+    def copy_out(step, source):
+        return pltpu.make_async_copy(source, out_ref.at[step], sems.at[step])
+
+    for step in range(STEPS if first_block else 0):
+
+        @pl.when(chosen[step] < first_block)
+        def _():
+            copy_out(step, others_ref.at[chosen[step]]).start()
+
+    def finish():
+        for step in range(STEPS):
+
+            @pl.when(chosen[step] >= first_block)
+            def _():
+                copy_out(step, result.at[chosen[step] - first_block]).start()
+
+        for step in range(STEPS):
+            copy_out(step, result.at[0]).wait()
+
+    return finish
+
+
+def own_first_kernel(
+    sizes, table, phase, mine_ref, sums_ref, local_ref, wide_ref, real_x, imag_x, packed
+):
+    stations, bands, seg, sta, pol, blocks, lags = sizes
+    spread_weights(sizes, 0, mine_ref, wide_ref)
+    turn_locals(sizes, phase[0, 0], phase[0, 1], mine_ref, local_ref)
+    add_products(
+        stations, stations, seg, source_tile(mine_ref, 0, seg, stations),
+        lambda n, pair: wide_ref[n, pl.ds(pair, 1), :],
+        lambda n, j: (local_ref[n, j, 0], local_ref[n, j, 1]),
+        None, real_x, imag_x,
+    )
+    pack(stations * stations, bands, real_x, imag_x, packed)
+    sums_ref[0], sums_ref[1] = transform(packed, table.at[lax.axis_index("pol")])
+
+
+def own_second_kernel(
+    sizes, table, phase, wide_ref, mine_ref, sums_ref, lags_ref, local_ref, real_x, imag_x, packed
+):
+    stations, bands, seg, sta, pol, blocks, lags = sizes
+    turn_locals(sizes, phase[1, 0], phase[1, 1], mine_ref, local_ref)
+    add_products(
+        stations, stations, seg, source_tile(mine_ref, 0, seg, stations),
+        lambda n, pair: wide_ref[n, pl.ds(pair, 1), :],
+        lambda n, j: (local_ref[n, j, 0], local_ref[n, j, 1]),
+        None, real_x, imag_x,
+    )
+    pack(stations * stations, bands, real_x, imag_x, packed)
+    even, odd = transform(packed, table.at[lax.axis_index("pol") ^ 1])
+    lags_ref[0] = unfold(even + sums_ref[0], odd + sums_ref[1])
+
+
+def other_products(sizes, first_segment, flip, wide_ref, local_refs, received, half, before, real_x, imag_x):
+    stations, seg = sizes[0], sizes[2]
+    pairs = stations * stations
+    count = seg // 2
+    add_products(
+        stations, stations, count, source_tile(received, (half ^ flip) * count, count, stations),
+        lambda n, pair: wide_ref[first_segment + n, pl.ds(pairs + pair, 1), :],
+        lambda n, j: (local_refs[half][first_segment + n, j, 0], local_refs[half][first_segment + n, j, 1]),
+        before, real_x, imag_x,
+    )
+
+
+def other_first_kernel(sizes, wide_ref, local_ref, local_too_ref, received, partial_ref):
+    first_segment = lax.axis_index("pol") * (sizes[2] // 2)
+    for half in range(2):
+        other_products(
+            sizes, first_segment, 0, wide_ref, (local_ref, local_too_ref), received, half,
+            None, partial_ref.at[half, 0], partial_ref.at[half, 1],
+        )
+
+
+def other_second_kernel(
+    sizes, plan_any, table, wide_ref, local_ref, local_too_ref, received, partial_ref, others_ref,
+    out_ref, result, real_x, imag_x, packed, plan_ref, sems,
+):
+    stations, bands, seg, sta, pol, blocks, lags = sizes
+    plan_copy = pltpu.make_async_copy(plan_any, plan_ref, sems.at[STEPS])
+    plan_copy.start()
+    first_segment = (1 - lax.axis_index("pol")) * (seg // 2)
+    even = odd = 0.0
+    for half in range(2):
+        other_products(
+            sizes, first_segment, 1, wide_ref, (local_ref, local_too_ref), received, half,
+            partial_ref.at[half], real_x.at[half], imag_x.at[half],
+        )
+        pack(stations * stations, bands, real_x.at[half], imag_x.at[half], packed.at[half])
+        even_term, odd_term = transform(packed.at[half], table.at[lax.axis_index("pol") ^ half])
+        even, odd = even + even_term, odd + odd_term
+    finish = place(sizes, plan_copy, plan_ref, others_ref, result, out_ref, sems)
+    result[0] = unfold(even, odd)
+    finish()
 
 
 def unfold(even, odd):
@@ -157,40 +287,48 @@
     return jnp.concatenate(runs + [after], axis=1)
 
 
-def stack_kernel(sizes, distance, held, before, *refs):
-    stations, bands, seg, sta, pol, blocks, lags = sizes
-    refs = list(refs)
-    plan_any = refs.pop(0) if before else None
-    table, locals_ref, sources_ref = refs.pop(0), refs.pop(0), refs.pop(0)
-    sums = [refs.pop(0) for _ in range(before)]
-    out_ref, result, wide_weight, local, real_x, imag_x, packed, plan_ref, sems = refs
-    if before:
+def half_kernel(sizes, distance, *refs):
+    stations, bands, seg, sta, pol, blocks, lags = sizes
+    pairs = stations * stations
+    if distance:
+        plan_any, table, mine_ref, sources_ref, sums_ref, out_ref, *rest = refs
+        plan_ref, sems = rest[-2:]
         plan_copy = pltpu.make_async_copy(plan_any, plan_ref, sems.at[STEPS])
         plan_copy.start()
-    half = lax.axis_index("pol") ^ distance
-    stack(sizes, half, held, locals_ref, sources_ref, wide_weight, local, real_x, imag_x, packed)
-    even = jnp.dot(packed[0], table[half, 0], preferred_element_type=jnp.float32)
-    odd = jnp.dot(packed[1], table[half, 1], preferred_element_type=jnp.float32)
-    if not before:
-        out_ref[0] = even
-        out_ref[1] = odd
+    else:
+        table, mine_ref, sources_ref, out_ref, *rest = refs
+    result, wide, local, real_x, imag_x, packed = rest[:6]
+    spread_weights(sizes, 0, mine_ref, wide)
+    turn_locals(sizes, *middle_phase(sizes, distance), mine_ref, local)
+    add_products(
+        stations, blocks * stations, seg, source_tile(sources_ref, 0, seg, stations),
+        lambda n, pair: wide[n, pl.ds(pair, 1), :],
+        lambda n, j: (local[n, j, 0], local[n, j, 1]),
+        None, real_x, imag_x,
+    )
+    pack(blocks * pairs, bands, real_x, imag_x, packed)
+    even, odd = transform(packed, table.at[lax.axis_index("pol") ^ distance])
+    if not distance:
+        out_ref[0], out_ref[1] = even, odd
         return
-    even = even + jnp.concatenate([part[0] for part in sums], axis=0)
-    odd = odd + jnp.concatenate([part[1] for part in sums], axis=0)
-    result[...] = unfold(even, odd).reshape(blocks, stations * stations, lags)
-    plan_copy.wait()
-    copies = []
-    for step in range(STEPS):
-        block = plan_ref[step] ^ lax.axis_index("sta") if sta == blocks else step
-        copies.append(pltpu.make_async_copy(result.at[block], out_ref.at[step], sems.at[step]))
-        copies[-1].start()
-    for copy in copies:
-        copy.wait()
-
-
-def fetch_kernel(table_hbm, table_ref, sem):
+    finish = place(sizes, plan_copy, plan_ref, None, result, out_ref, sems)
+    result[...] = unfold(even + sums_ref[0], odd + sums_ref[1]).reshape(blocks, pairs, lags)
+    finish()
+
+
+def first_half(sizes, *refs):
+    half_kernel(sizes, 0, *refs)
+
+
+def second_half(sizes, *refs):
+    half_kernel(sizes, 1, *refs)
+
+
+def fetch_kernel(sizes, table_hbm, table_ref, phase_ref, sem):
     copy = pltpu.make_async_copy(table_hbm, table_ref, sem)
     copy.start()
+    for distance in range(2):
+        phase_ref[distance, 0], phase_ref[distance, 1] = middle_phase(sizes, distance)
     copy.wait()
 
 
@@ -217,17 +355,17 @@
     )(*arrays)
 
 
-def exchange(value, axes, steps):
-    if isinstance(axes, str):
-        axes, steps = (axes,), (steps,)
-    if not any(steps):
-        return value
+def fetch_from(value, axes, source_of):
     sizes = tuple(lax.axis_size(axis) for axis in axes)
     pairs = []
     for index in np.ndindex(*sizes):
-        source = tuple(i ^ step for i, step in zip(index, steps))
+        source = source_of(*index)
         pairs.append((int(np.ravel_multi_index(source, sizes)), int(np.ravel_multi_index(index, sizes))))
     return lax.ppermute(value, axes, pairs)
+
+
+def exchange(value, axis, distance):
+    return fetch_from(value, (axis,), lambda i: (i ^ distance,))
 
 
 def shards(table, raw_spectra, owner_plan, pair_valid, quality):
@@ -257,67 +395,104 @@
         name="prepare",
     )(*plan, in_hbm(raw), in_hbm(jnp.transpose(pair_valid[0])), in_hbm(quality))
 
-    table = pl.pallas_call(
+    def call(kernel, out_shape, *args, out_specs=None, scratch=(), flops=0, moved=0, name=None):
+        many = isinstance(out_shape, (list, tuple))
+        return pl.pallas_call(
+            functools.partial(kernel, sizes),
+            out_shape=out_shape,
+            in_specs=[hbm if x is table_const or x is plan_const else vmem for x in args],
+            out_specs=out_specs or ([vmem] * len(out_shape) if many else vmem),
+            scratch_shapes=list(scratch),
+            compiler_params=pltpu.CompilerParams(vmem_limit_bytes=VMEM_BYTES),
+            cost_estimate=pl.CostEstimate(flops=flops, bytes_accessed=moved, transcendentals=0),
+            name=name,
+        )(*args)
+
+    f32 = jnp.float32
+    table_const, plan_const = in_hbm(table), in_hbm(owner_plan)
+    table, phase = call(
         fetch_kernel,
-        out_shape=pltpu.VMEM(table.shape, table.dtype),
-        in_specs=[hbm],
-        out_specs=vmem,
-        scratch_shapes=[pltpu.SemaphoreType.DMA(())],
-        compiler_params=pltpu.CompilerParams(vmem_limit_bytes=VMEM_BYTES),
-        cost_estimate=pl.CostEstimate(flops=0, bytes_accessed=2 * table.size * 2, transcendentals=0),
+        [pltpu.VMEM(table.shape, table.dtype), pltpu.VMEM((2, 2, bands, LANES), f32)],
+        table_const,
+        scratch=[pltpu.SemaphoreType.DMA(())],
+        moved=4 * table.size,
         name="fetch",
-    )(in_hbm(table))
-
-    def run(table, distance, held, locals_, sources, sums):
-        count = held[1]
-        out_shape = (STEPS, pairs, lags) if sums else (2, count * pairs, half_lags)
-        return pl.pallas_call(
-            functools.partial(stack_kernel, sizes, distance, held, len(sums)),
-            out_shape=jax.ShapeDtypeStruct(out_shape, jnp.float32),
-            in_specs=([hbm] if sums else []) + [vmem] * (3 + len(sums)),
-            out_specs=hbm if sums else vmem,
-            scratch_shapes=[
-                pltpu.VMEM((count, pairs, lags), jnp.float32),
-                pltpu.VMEM((seg, count * pairs, LANES), jnp.float32),
-                pltpu.VMEM((seg, stations, 2, 8, LANES), jnp.float32),
-                pltpu.VMEM((count * pairs * 8, LANES), jnp.float32),
-                pltpu.VMEM((count * pairs * 8, LANES), jnp.float32),
-                pltpu.VMEM((2, count * pairs, bins), jnp.bfloat16),
-                pltpu.SMEM((STEPS,), jnp.int32),
-                pltpu.SemaphoreType.DMA((STEPS + 1,)),
-            ],
-            compiler_params=pltpu.CompilerParams(vmem_limit_bytes=VMEM_BYTES),
-            cost_estimate=pl.CostEstimate(
-                flops=32 * count * pairs * 2 * bins * lags, bytes_accessed=1024 * 1024, transcendentals=0
-            ),
-            name="stack",
-        )(*([owner_plan] if sums else []), table, locals_, sources, *sums)
-
-    both = ("seg", "sta")
-    if sta == 2 and seg == 4:
-        far = exchange(own, "seg", 2)
-        partner = exchange(own, "sta", 1)
+    )
+
+    def products(count):
+        return [pltpu.VMEM((count * pairs * 8, LANES), f32)] * 2 + [pltpu.VMEM((2, count * pairs, bins), jnp.bfloat16)]
+
+    plan_scratch = [pltpu.SMEM((STEPS,), jnp.int32), pltpu.SemaphoreType.DMA((STEPS + 1,))]
+    quarter = 32 * pairs * 2 * bins * lags
+    placed_shape = jax.ShapeDtypeStruct((STEPS, pairs, lags), f32)
+    local_shape = pltpu.VMEM((seg, stations, 2, bands, LANES), f32)
+
+    if sta == 2 and pol == 2 and seg > 1:
+        far, distance = own, seg // 2
+        while distance > 1:
+            far = join(far, exchange(far, "seg", distance))
+            distance //= 2
         far, table = lax.optimization_barrier((far, table))
-        near = exchange(join(own, partner, far), "seg", 1)
-        far_partner = exchange(far, "sta", 1)
-        far_across = exchange(far, both, (1, 1))
-        mine = join(own, far, (near, 0, 1), (near, 2, 1))
-        first = run(table, 0, (0, 1, 0), mine, mine, [])
-        first, far_partner, far_across = lax.optimization_barrier((first, far_partner, far_across))
-        others = join(partner, far_partner, (near, 1, 1), far_across)
-        sums = [first, run(table, 0, (1, 1, 0), mine, others, [])]
-        base = 0
+        far_too = exchange(far, "pol", 1)
+        near = exchange(far, "seg", 1)
+        received = fetch_from(
+            join(far, far_too), ("seg", "sta", "pol"), lambda z, x, core: (z ^ core, x ^ 1, core)
+        )
+        near_too = exchange(near, "pol", 1)
+        mine, mine_too = join(far, near), join(far_too, near_too)
+        sums, local, wide = call(
+            own_first_kernel,
+            [pltpu.VMEM((2, pairs, half_lags), f32), local_shape, pltpu.VMEM((seg, blocks * pairs, LANES), f32)],
+            table, phase, mine,
+            scratch=products(1), flops=quarter, name="own_first",
+        )
+        own_lags, local_too = call(
+            own_second_kernel,
+            [pltpu.VMEM((1, pairs, lags), f32), local_shape],
+            table, phase, wide, mine_too, sums,
+            scratch=products(1), flops=quarter, name="own_second",
+        )
+        own_lags, received = lax.optimization_barrier((own_lags, received))
+        received_too = exchange(received, "pol", 1)
+        partial = call(
+            other_first_kernel,
+            pltpu.VMEM((2, 2, pairs * 8, LANES), f32),
+            wide, local, local_too, received,
+            flops=quarter, name="other_first",
+        )
+        result = call(
+            other_second_kernel, placed_shape,
+            plan_const, table, wide, local, local_too, received_too, partial, own_lags,
+            out_specs=hbm,
+            scratch=[pltpu.VMEM((1, pairs, lags), f32)]
+            + [pltpu.VMEM((2, pairs * 8, LANES), f32)] * 2
+            + [pltpu.VMEM((2, 2, pairs, bins), jnp.bfloat16)]
+            + plan_scratch,
+            flops=quarter, name="other_second",
+        )
     else:
         mine, distance = own, seg // 2
         while distance:
             mine = join(mine, exchange(mine, "seg", distance))
             distance //= 2
         gathered = lax.all_gather(mine, "sta")
-        others = join(*(gathered[lax.axis_index("sta") ^ k if sta == blocks else owner_plan[k]] for k in range(blocks)))
-        sums = [run(table, 0, (0, blocks, 0), mine, others, [])]
-        base = seg
-    theirs = exchange(join(mine, others), "pol", 1)
-    result = run(table, 1, (0, blocks, base), theirs, theirs, sums)
+        sources = join(*(gathered[lax.axis_index("sta") ^ k if sta == blocks else owner_plan[k]] for k in range(blocks)))
+        scratch = [
+            pltpu.VMEM((blocks, pairs, lags), f32),
+            pltpu.VMEM((seg, blocks * pairs, LANES), f32),
+            pltpu.VMEM((seg, stations, 2, bands, LANES), f32),
+            *products(blocks),
+        ]
+        sums = call(
+            first_half, pltpu.VMEM((2, blocks * pairs, half_lags), f32),
+            table, mine, sources,
+            scratch=scratch, flops=blocks * quarter, name="first_half",
+        )
+        result = call(
+            second_half, placed_shape,
+            plan_const, table, exchange(mine, "pol", 1), exchange(sources, "pol", 1), sums,
+            out_specs=hbm, scratch=scratch + plan_scratch, flops=blocks * quarter, name="second_half",
+        )
     return result.reshape(STEPS, stations, stations, lags)
 
 

time: 20.2 us -> 19.4 us (0.960)
  starting transfers between devices: 9.22 us -> 7.24 us
  waiting for transfers between devices: 3.97 us -> 5.33 us
    ppermute x6, starting transfers between devices: 9.22 us -> 7.24 us  [fetch_from(): return lax.ppermute(value, axes, pairs)]
    ppermute x6, waiting for transfers between devices: 3.97 us -> 5.33 us  [fetch_from(): return lax.ppermute(value, axes, pairs)]
    pallas_call x4 -> x5, Pallas kernels: 5.74 us -> 5.62 us  [call(): pl.pallas_call(functools.partial(kernel, sizes), out_shape=out_shape, in_...]
  transfers between devices with their start and end apart: 6 -> 6, of which waited for: 5 -> 5; matrix products, arithmetic and copies ran while one was open for 0% -> 0% of each run, Pallas kernels for 17% -> 19%
where the time goes in v11:
time: 19.4 us; the launch traced here: 19.2 us
  starting transfers between devices  7.24 us (37%)
  Pallas kernels  6.58 us (34%)
  waiting for transfers between devices  5.33 us (27%)
    ppermute x6, starting transfers between devices, fetch_from(): return lax.ppermute(value, axes, pairs)  7.24 us
    pallas_call x5, Pallas kernels, call(): pl.pallas_call(functools.partial(kernel, sizes), out_shape=out_shape, in_...  5.62 us
    ppermute x6, waiting for transfers between devices, fetch_from(): return lax.ppermute(value, axes, pairs)  5.33 us
    pallas_call x1, Pallas kernels, shards(): pl.pallas_call(functools.partial(prepare_kernel, (stations, bands, sta, b...  0.91 us
  transfers between devices with their start and end apart: 6, of which 5 were waited for; matrix products, arithmetic and copies ran while one was open for 0% of the time, Pallas kernels for 19%

profile of v11, /device:TPU:0, one launch (start us, length us, event | category | flops | bytes accessed | tf_op | source)
XLA Modules:
  0.0 19.2 jit_solution(3557879516572147950)
XLA Ops:
  0.0 0.9 %prepare.1.refs_0_ = bf16[1,144,128]{2,1,0:T(8,128)(2,1)S(1)} custom-call(bf16[128,128]{1,0:T(8,128)(2,1)} %bitcast.9, s32[8,16]{1,0:T(8,128)} %bitcast.10, s32[1,16]{1,0:T(1,128)} %refs_2_.1), custom_call_target="tpu_custom_call" | custom-call | tf_op jit(solution)/shard_map/prepare/pallas_call | solution.py:388
  0.9 4.1 %collective-permute-start = (bf16[1,144,128]{2,1,0:T(8,128)(2,1)S(1)}, bf16[1,144,128]{2,1,0:T(8,128)(2,1)S(1)}, u32[]{:S(2)}, u32[]{:S(2)}) collective-permute-start(bf16[1,144,128]{2,1,0:T(8,128)(2,1)S(1)} %prepare.1.refs_0_), channel_id=1, source_target_pairs={{8,0},{12,4},{0,8},{4,12},{9,1},{13,5},{1,9},{5,13},{10,2},{14,6},... | collective-permute-start | bytes 110600 | tf_op jit(solution)/shard_map/ppermute | solution.py:364
  5.0 1.6 %fetch.1 = (bf16[2,2,1024,256]{3,2,1,0:T(8,128)(2,1)S(1)}, f32[2,2,8,128]{3,2,1,0:T(8,128)S(1)}) custom-call(bf16[2,2,1024,256]{3,2,1,0:T(8,128)(2,1)} %constant.2.clone.table_hbm), custom_call_target="tpu_custom_call" | custom-call | bytes 4194304 | tf_op jit(solution)/shard_map/fetch/pallas_call | solution.py:400
  6.6 0.7 %collective-permute-done.refs_1_ = bf16[1,144,128]{2,1,0:T(8,128)(2,1)S(1)} collective-permute-done((bf16[1,144,128]{2,1,0:T(8,128)(2,1)S(1)}, bf16[1,144,128]{2,1,0:T(8,128)(2,1)S(1)}, u32[]{:S(2)}, u32[]{:S(2)}) %collective-permute-start) | collective-permute-done | bytes 36896 | tf_op jit(solution)/shard_map/ppermute | solution.py:364
  7.4 0.0 collective-permute-start.2
  7.4 1.6 %collective-permute-start.1 = (bf16[2,144,128]{2,1,0:T(8,128)(2,1)S(1)}, bf16[2,144,128]{2,1,0:T(8,128)(2,1)S(1)}, u32[]{:S(2)}, u32[]{:S(2)}) collective-permute-start(bf16[2,144,128]{2,1,0:T(8,128)(2,1)S(1)} %join.4.refs_0_), channel_id=1, source_target_pairs={{4,0},{0,4},{12,8},{8,12},{5,1},{1,5},{13,9},{9,13},{6,2},{2,6},{1... | collective-permute-start | bytes 221192 | tf_op jit(solution)/shard_map/ppermute | solution.py:364
  8.9 0.0 collective-permute-done.2.refs_0_.refs_1_
  9.0 1.6 %collective-permute-start.4 = (bf16[4,144,128]{2,1,0:T(8,128)(2,1)S(1)}, bf16[4,144,128]{2,1,0:T(8,128)(2,1)S(1)}, u32[]{:S(2)}, u32[]{:S(2)}) collective-permute-start(bf16[4,144,128]{2,1,0:T(8,128)(2,1)S(1)} %join.7), channel_id=1, source_target_pairs={{2,0},{7,1},{0,2},{5,3},{6,4},{3,5},{4,6},{1,7},{10,8},{15,9},{8,1... | collective-permute-start | bytes 442376 | tf_op jit(solution)/shard_map/ppermute | solution.py:364
  10.5 1.5 %collective-permute-done.1.refs_1_ = bf16[2,144,128]{2,1,0:T(8,128)(2,1)S(1)} collective-permute-done((bf16[2,144,128]{2,1,0:T(8,128)(2,1)S(1)}, bf16[2,144,128]{2,1,0:T(8,128)(2,1)S(1)}, u32[]{:S(2)}, u32[]{:S(2)}) %collective-permute-start.1) | collective-permute-done | bytes 73760 | tf_op jit(solution)/shard_map/ppermute | solution.py:364
  12.0 0.0 collective-permute-start.3
  12.1 0.8 %own_first.1 = (f32[2,64,256]{2,1,0:T(8,128)S(1)}, f32[4,8,2,8,128]{4,3,2,1,0:T(8,128)S(1)}, f32[4,128,128]{2,1,0:T(8,128)S(1)}) custom-call(bf16[2,2,1024,256]{3,2,1,0:T(8,128)(2,1)S(1)} %get-tuple-element.17.table, f32[2,2,8,128]{3,2,1,0:T(8,128)S(1)} %get-tuple-element.18.phase, bf16[4,144,128]{2,1,0:T(8,128)(2,1)S(1)} %join.5.mine_ref), custom_call_target="tpu_custom_call" | custom-call | flops 2147483648 | tf_op jit(solution)/shard_map/own_first/pallas_call | solution.py:400
  12.9 0.4 %collective-permute-done.3.refs_1_ = bf16[2,144,128]{2,1,0:T(8,128)(2,1)S(1)} collective-permute-done((bf16[2,144,128]{2,1,0:T(8,128)(2,1)S(1)}, bf16[2,144,128]{2,1,0:T(8,128)(2,1)S(1)}, u32[]{:S(2)}, u32[]{:S(2)}) %collective-permute-start.3) | collective-permute-done | bytes 73760 | tf_op jit(solution)/shard_map/ppermute | solution.py:364
  13.3 0.8 %own_second.1 = (f32[1,64,512]{2,1,0:T(8,128)S(1)}, f32[4,8,2,8,128]{4,3,2,1,0:T(8,128)S(1)}) custom-call(bf16[2,2,1024,256]{3,2,1,0:T(8,128)(2,1)S(1)} %get-tuple-element.17.table, f32[2,2,8,128]{3,2,1,0:T(8,128)S(1)} %get-tuple-element.18.phase, f32[4,128,128]{2,1,0:T(8,128)S(1)} %get-tuple-element.20.wide_ref, bf16[4,144,128]{2,1,0:T(8,128)(2,1)S(1)} %join.6.mine_ref, ...), custom_call_target="tpu_custom_call" | custom-call | flops 2147483648 | tf_op jit(solution)/shard_map/own_second/pallas_call | solution.py:400
  14.1 1.6 %collective-permute-done.4.received = bf16[4,144,128]{2,1,0:T(8,128)(2,1)S(1)} collective-permute-done((bf16[4,144,128]{2,1,0:T(8,128)(2,1)S(1)}, bf16[4,144,128]{2,1,0:T(8,128)(2,1)S(1)}, u32[]{:S(2)}, u32[]{:S(2)}) %collective-permute-start.4) | collective-permute-done | bytes 147488 | tf_op jit(solution)/shard_map/ppermute | solution.py:364
  15.8 0.0 collective-permute-start.5
  15.8 0.3 %other_first.1.partial_ref = f32[2,2,512,128]{3,2,1,0:T(8,128)S(1)} custom-call(f32[4,128,128]{2,1,0:T(8,128)S(1)} %get-tuple-element.20.wide_ref, f32[4,8,2,8,128]{4,3,2,1,0:T(8,128)S(1)} %get-tuple-element.21.local_ref, f32[4,8,2,8,128]{4,3,2,1,0:T(8,128)S(1)} %get-tuple-element.23.local_too_ref, bf16[4,144,128]{2,1,0:T(8,128)(2,1)S(1)} %collective-permute-done.4.received), custom_call_target="tpu_custom_call" | custom-call | flops 2147483648 | tf_op jit(solution)/shard_map/other_first/pallas_call | solution.py:400
  16.1 1.0 %collective-permute-done.5.received = bf16[4,144,128]{2,1,0:T(8,128)(2,1)S(1)} collective-permute-done((bf16[4,144,128]{2,1,0:T(8,128)(2,1)S(1)}, bf16[4,144,128]{2,1,0:T(8,128)(2,1)S(1)}, u32[]{:S(2)}, u32[]{:S(2)}) %collective-permute-start.5) | collective-permute-done | bytes 147488 | tf_op jit(solution)/shard_map/ppermute | solution.py:364
  17.1 2.1 %other_second.1 = f32[3,64,512]{2,1,0:T(8,128)} custom-call(s32[3]{0:T(128)} %plan_any.1, bf16[2,2,1024,256]{3,2,1,0:T(8,128)(2,1)S(1)} %get-tuple-element.17.table, f32[4,128,128]{2,1,0:T(8,128)S(1)} %get-tuple-element.20.wide_ref, f32[4,8,2,8,128]{4,3,2,1,0:T(8,128)S(1)} %get-tuple-element.21.local_ref, ...), custom_call_target="tpu_custom_call" | custom-call | flops 2147483648 | tf_op jit(solution)/shard_map/other_second/pallas_call | solution.py:400
  (4 shorter events, 0.0 us)
Async XLA Ops:
  0.9 6.4 %collective-permute-start = (bf16[1,144,128]{2,1,0:T(8,128)(2,1)S(1)}, bf16[1,144,128]{2,1,0:T(8,128)(2,1)S(1)}, u32[]{:S(2)}, u32[]{:S(2)}) collective-permute-start(bf16[1,144,128]{2,1,0:T(8,128)(2,1)S(1)} %prepare.1.refs_0_), channel_id=1, source_target_pairs={{8,0},{12,4},{0,8},{4,12},{9,1},{13,5},{1,9},{5,13},{10,2},{14,6},... | collective-permute-start | bytes 110600 | tf_op jit(solution)/shard_map/ppermute | solution.py:364
  7.4 1.6 %collective-permute-start.2 = (bf16[2,144,128]{2,1,0:T(8,128)(2,1)S(1)}, bf16[2,144,128]{2,1,0:T(8,128)(2,1)S(1)}, u32[]{:S(2)}, u32[]{:S(2)}) collective-permute-start(bf16[2,144,128]{2,1,0:T(8,128)(2,1)S(1)} %join.4.refs_0_), channel_id=1, source_target_pairs={{1,0},{0,1},{3,2},{2,3},{5,4},{4,5},{7,6},{6,7},{9,8},{8,9},{11,10... | collective-permute-start | bytes 221192 | tf_op jit(solution)/shard_map/ppermute | solution.py:364
  7.4 4.7 %collective-permute-start.1 = (bf16[2,144,128]{2,1,0:T(8,128)(2,1)S(1)}, bf16[2,144,128]{2,1,0:T(8,128)(2,1)S(1)}, u32[]{:S(2)}, u32[]{:S(2)}) collective-permute-start(bf16[2,144,128]{2,1,0:T(8,128)(2,1)S(1)} %join.4.refs_0_), channel_id=1, source_target_pairs={{4,0},{0,4},{12,8},{8,12},{5,1},{1,5},{13,9},{9,13},{6,2},{2,6},{1... | collective-permute-start | bytes 221192 | tf_op jit(solution)/shard_map/ppermute | solution.py:364
  9.0 6.8 %collective-permute-start.4 = (bf16[4,144,128]{2,1,0:T(8,128)(2,1)S(1)}, bf16[4,144,128]{2,1,0:T(8,128)(2,1)S(1)}, u32[]{:S(2)}, u32[]{:S(2)}) collective-permute-start(bf16[4,144,128]{2,1,0:T(8,128)(2,1)S(1)} %join.7), channel_id=1, source_target_pairs={{2,0},{7,1},{0,2},{5,3},{6,4},{3,5},{4,6},{1,7},{10,8},{15,9},{8,1... | collective-permute-start | bytes 442376 | tf_op jit(solution)/shard_map/ppermute | solution.py:364
  12.0 1.3 %collective-permute-start.3 = (bf16[2,144,128]{2,1,0:T(8,128)(2,1)S(1)}, bf16[2,144,128]{2,1,0:T(8,128)(2,1)S(1)}, u32[]{:S(2)}, u32[]{:S(2)}) collective-permute-start(bf16[2,144,128]{2,1,0:T(8,128)(2,1)S(1)} %collective-permute-done.1.refs_1_), channel_id=1, source_target_pairs={{1,0},{0,1},{3,2},{2,3},{5,4},{4,5},{7,6},{6,7},{9,8},{8,9},{11,10... | collective-permute-start | bytes 221192 | tf_op jit(solution)/shard_map/ppermute | solution.py:364
  15.8 1.4 %collective-permute-start.5 = (bf16[4,144,128]{2,1,0:T(8,128)(2,1)S(1)}, bf16[4,144,128]{2,1,0:T(8,128)(2,1)S(1)}, u32[]{:S(2)}, u32[]{:S(2)}) collective-permute-start(bf16[4,144,128]{2,1,0:T(8,128)(2,1)S(1)} %collective-permute-done.4.received), channel_id=1, source_target_pairs={{1,0},{0,1},{3,2},{2,3},{5,4},{4,5},{7,6},{6,7},{9,8},{8,9},{11,10... | collective-permute-start | bytes 442376 | tf_op jit(solution)/shard_map/ppermute | solution.py:364

commit v12 on v11

--- a/solution.py
+++ b/solution.py
@@ -167,6 +167,23 @@
     return tile_of
 
 
+def unfold(even, odd):
+    half = even.shape[1]
+    after = even - odd
+    before = even + odd
+    if half % LANES:
+        flip = lax.broadcasted_iota(jnp.int32, (half, half), 0) + lax.broadcasted_iota(
+            jnp.int32, (half, half), 1
+        )
+        flip = (flip == half - 1).astype(jnp.float32)
+        before = jnp.dot(before, flip, precision=lax.Precision.HIGHEST, preferred_element_type=jnp.float32)
+        return jnp.concatenate([before, after], axis=1)
+    index = LANES - 1 - lax.broadcasted_iota(jnp.int32, (even.shape[0], LANES), 1)
+    runs = [before[:, n * LANES : (n + 1) * LANES] for n in reversed(range(half // LANES))]
+    runs = [jnp.take_along_axis(run, index, axis=1, mode="promise_in_bounds") for run in runs]
+    return jnp.concatenate(runs + [after], axis=1)
+
+
 def place(sizes, plan_copy, plan_ref, others_ref, result, out_ref, sems):
     stations, bands, seg, sta, pol, blocks, lags = sizes
     first_block = others_ref.shape[0] if others_ref is not None else 0
@@ -227,64 +244,34 @@
     lags_ref[0] = unfold(even + sums_ref[0], odd + sums_ref[1])
 
 
-def other_products(sizes, first_segment, flip, wide_ref, local_refs, received, half, before, real_x, imag_x):
-    stations, seg = sizes[0], sizes[2]
+def other_products(sizes, sources_ref, wide_ref, local_ref, real_x, imag_x, packed):
+    stations, bands, seg = sizes[:3]
     pairs = stations * stations
-    count = seg // 2
     add_products(
-        stations, stations, count, source_tile(received, (half ^ flip) * count, count, stations),
-        lambda n, pair: wide_ref[first_segment + n, pl.ds(pairs + pair, 1), :],
-        lambda n, j: (local_refs[half][first_segment + n, j, 0], local_refs[half][first_segment + n, j, 1]),
-        before, real_x, imag_x,
-    )
-
-
-def other_first_kernel(sizes, wide_ref, local_ref, local_too_ref, received, partial_ref):
-    first_segment = lax.axis_index("pol") * (sizes[2] // 2)
-    for half in range(2):
-        other_products(
-            sizes, first_segment, 0, wide_ref, (local_ref, local_too_ref), received, half,
-            None, partial_ref.at[half, 0], partial_ref.at[half, 1],
-        )
+        stations, stations, seg, source_tile(sources_ref, 0, seg, stations),
+        lambda n, pair: wide_ref[n, pl.ds(pairs + pair, 1), :],
+        lambda n, j: (local_ref[n, j, 0], local_ref[n, j, 1]),
+        None, real_x, imag_x,
+    )
+    pack(pairs, bands, real_x, imag_x, packed)
+
+
+def other_first_kernel(sizes, table, wide_ref, local_ref, sources_ref, sums_ref, real_x, imag_x, packed):
+    other_products(sizes, sources_ref, wide_ref, local_ref, real_x, imag_x, packed)
+    sums_ref[0], sums_ref[1] = transform(packed, table.at[lax.axis_index("pol")])
 
 
 def other_second_kernel(
-    sizes, plan_any, table, wide_ref, local_ref, local_too_ref, received, partial_ref, others_ref,
+    sizes, plan_any, table, wide_ref, local_ref, sources_ref, sums_ref, others_ref,
     out_ref, result, real_x, imag_x, packed, plan_ref, sems,
 ):
-    stations, bands, seg, sta, pol, blocks, lags = sizes
     plan_copy = pltpu.make_async_copy(plan_any, plan_ref, sems.at[STEPS])
     plan_copy.start()
-    first_segment = (1 - lax.axis_index("pol")) * (seg // 2)
-    even = odd = 0.0
-    for half in range(2):
-        other_products(
-            sizes, first_segment, 1, wide_ref, (local_ref, local_too_ref), received, half,
-            partial_ref.at[half], real_x.at[half], imag_x.at[half],
-        )
-        pack(stations * stations, bands, real_x.at[half], imag_x.at[half], packed.at[half])
-        even_term, odd_term = transform(packed.at[half], table.at[lax.axis_index("pol") ^ half])
-        even, odd = even + even_term, odd + odd_term
+    other_products(sizes, sources_ref, wide_ref, local_ref, real_x, imag_x, packed)
     finish = place(sizes, plan_copy, plan_ref, others_ref, result, out_ref, sems)
-    result[0] = unfold(even, odd)
+    even, odd = transform(packed, table.at[lax.axis_index("pol") ^ 1])
+    result[0] = unfold(even + sums_ref[0], odd + sums_ref[1])
     finish()
-
-
-def unfold(even, odd):
-    half = even.shape[1]
-    after = even - odd
-    before = even + odd
-    if half % LANES:
-        flip = lax.broadcasted_iota(jnp.int32, (half, half), 0) + lax.broadcasted_iota(
-            jnp.int32, (half, half), 1
-        )
-        flip = (flip == half - 1).astype(jnp.float32)
-        before = jnp.dot(before, flip, precision=lax.Precision.HIGHEST, preferred_element_type=jnp.float32)
-        return jnp.concatenate([before, after], axis=1)
-    index = LANES - 1 - lax.broadcasted_iota(jnp.int32, (even.shape[0], LANES), 1)
-    runs = [before[:, n * LANES : (n + 1) * LANES] for n in reversed(range(half // LANES))]
-    runs = [jnp.take_along_axis(run, index, axis=1, mode="promise_in_bounds") for run in runs]
-    return jnp.concatenate(runs + [after], axis=1)
 
 
 def half_kernel(sizes, distance, *refs):
@@ -336,18 +323,20 @@
     *pieces, out_ref = refs
     at = 0
     for piece, (first, count) in zip(pieces, ranges):
-        out_ref[pl.ds(at, count)] = piece[pl.ds(first, count)]
+        out_ref[pl.ds(at, count)] = piece[pl.ds(first, count), pl.ds(0, out_ref.shape[1]), :]
         at += count
 
 
-def join(*pieces):
+def join(*pieces, rows=None):
     pieces = [piece if isinstance(piece, tuple) else (piece, 0, piece.shape[0]) for piece in pieces]
     arrays = [piece[0] for piece in pieces]
     ranges = [piece[1:] for piece in pieces]
     vmem = pl.BlockSpec(memory_space=pltpu.VMEM)
     return pl.pallas_call(
         functools.partial(join_kernel, ranges),
-        out_shape=pltpu.VMEM((sum(count for _, count in ranges),) + arrays[0].shape[1:], arrays[0].dtype),
+        out_shape=pltpu.VMEM(
+            (sum(count for _, count in ranges), rows or arrays[0].shape[1], LANES), arrays[0].dtype
+        ),
         in_specs=[vmem] * len(arrays),
         out_specs=vmem,
         compiler_params=pltpu.CompilerParams(vmem_limit_bytes=VMEM_BYTES),
@@ -433,13 +422,12 @@
             far = join(far, exchange(far, "seg", distance))
             distance //= 2
         far, table = lax.optimization_barrier((far, table))
-        far_too = exchange(far, "pol", 1)
         near = exchange(far, "seg", 1)
-        received = fetch_from(
-            join(far, far_too), ("seg", "sta", "pol"), lambda z, x, core: (z ^ core, x ^ 1, core)
-        )
-        near_too = exchange(near, "pol", 1)
-        mine, mine_too = join(far, near), join(far_too, near_too)
+        bare = join(far, rows=rows - 16)
+        partner = exchange(bare, "sta", 1)
+        across = fetch_from(bare, ("seg", "sta"), lambda z, x: (z ^ 1, x ^ 1))
+        mine = join(far, near)
+        mine_too = exchange(mine, "pol", 1)
         sums, local, wide = call(
             own_first_kernel,
             [pltpu.VMEM((2, pairs, half_lags), f32), local_shape, pltpu.VMEM((seg, blocks * pairs, LANES), f32)],
@@ -452,22 +440,20 @@
             table, phase, wide, mine_too, sums,
             scratch=products(1), flops=quarter, name="own_second",
         )
-        own_lags, received = lax.optimization_barrier((own_lags, received))
-        received_too = exchange(received, "pol", 1)
-        partial = call(
+        own_lags, partner, across = lax.optimization_barrier((own_lags, partner, across))
+        others = join(partner, across)
+        others_too = exchange(others, "pol", 1)
+        sums = call(
             other_first_kernel,
-            pltpu.VMEM((2, 2, pairs * 8, LANES), f32),
-            wide, local, local_too, received,
-            flops=quarter, name="other_first",
+            pltpu.VMEM((2, pairs, half_lags), f32),
+            table, wide, local, others,
+            scratch=products(1), flops=quarter, name="other_first",
         )
         result = call(
             other_second_kernel, placed_shape,
-            plan_const, table, wide, local, local_too, received_too, partial, own_lags,
+            plan_const, table, wide, local_too, others_too, sums, own_lags,
             out_specs=hbm,
-            scratch=[pltpu.VMEM((1, pairs, lags), f32)]
-            + [pltpu.VMEM((2, pairs * 8, LANES), f32)] * 2
-            + [pltpu.VMEM((2, 2, pairs, bins), jnp.bfloat16)]
-            + plan_scratch,
+            scratch=[pltpu.VMEM((1, pairs, lags), f32)] + products(1) + plan_scratch,
             flops=quarter, name="other_second",
         )
     else:

time: 19.4 us -> 19 us (0.979)
  waiting for transfers between devices: 5.33 us -> 4.29 us
  starting transfers between devices: 7.24 us -> 7.73 us
    ppermute x6, waiting for transfers between devices: 5.33 us -> 4.29 us  [fetch_from(): return lax.ppermute(value, axes, pairs)]
    ppermute x6, starting transfers between devices: 7.24 us -> 7.73 us  [fetch_from(): return lax.ppermute(value, axes, pairs)]
  transfers between devices with their start and end apart: 6 -> 6, of which waited for: 5 -> 5; matrix products, arithmetic and copies ran while one was open for 0% -> 0% of each run, Pallas kernels for 19% -> 21%
where the time goes in v12:
time: 19 us; the launch traced here: 18.7 us
  starting transfers between devices  7.73 us (41%)
  Pallas kernels  6.65 us (35%)
  waiting for transfers between devices  4.29 us (23%)
    ppermute x6, starting transfers between devices, fetch_from(): return lax.ppermute(value, axes, pairs)  7.73 us
    pallas_call x5, Pallas kernels, call(): pl.pallas_call(functools.partial(kernel, sizes), out_shape=out_shape, in_...  5.7 us
    ppermute x6, waiting for transfers between devices, fetch_from(): return lax.ppermute(value, axes, pairs)  4.29 us
    pallas_call x1, Pallas kernels, shards(): pl.pallas_call(functools.partial(prepare_kernel, (stations, bands, sta, b...  0.91 us
  transfers between devices with their start and end apart: 6, of which 5 were waited for; matrix products, arithmetic and copies ran while one was open for 0% of the time, Pallas kernels for 21%

profile of v12, /device:TPU:0, one launch (start us, length us, event | category | flops | bytes accessed | tf_op | source)
XLA Modules:
  0.0 18.7 jit_solution(13730031928957557462)
XLA Ops:
  0.0 0.9 %prepare.1.refs_0_ = bf16[1,144,128]{2,1,0:T(8,128)(2,1)S(1)} custom-call(bf16[128,128]{1,0:T(8,128)(2,1)} %bitcast.9, s32[8,16]{1,0:T(8,128)} %bitcast.10, s32[1,16]{1,0:T(1,128)} %refs_2_.1), custom_call_target="tpu_custom_call" | custom-call | tf_op jit(solution)/shard_map/prepare/pallas_call | solution.py:377
  0.9 4.1 %collective-permute-start = (bf16[1,144,128]{2,1,0:T(8,128)(2,1)S(1)}, bf16[1,144,128]{2,1,0:T(8,128)(2,1)S(1)}, u32[]{:S(2)}, u32[]{:S(2)}) collective-permute-start(bf16[1,144,128]{2,1,0:T(8,128)(2,1)S(1)} %prepare.1.refs_0_), channel_id=1, source_target_pairs={{8,0},{12,4},{0,8},{4,12},{9,1},{13,5},{1,9},{5,13},{10,2},{14,6},... | collective-permute-start | bytes 110600 | tf_op jit(solution)/shard_map/ppermute | solution.py:353
  5.0 1.6 %fetch.1 = (bf16[2,2,1024,256]{3,2,1,0:T(8,128)(2,1)S(1)}, f32[2,2,8,128]{3,2,1,0:T(8,128)S(1)}) custom-call(bf16[2,2,1024,256]{3,2,1,0:T(8,128)(2,1)} %constant.2.clone.table_hbm), custom_call_target="tpu_custom_call" | custom-call | bytes 4194304 | tf_op jit(solution)/shard_map/fetch/pallas_call | solution.py:389
  6.6 0.7 %collective-permute-done.refs_1_ = bf16[1,144,128]{2,1,0:T(8,128)(2,1)S(1)} collective-permute-done((bf16[1,144,128]{2,1,0:T(8,128)(2,1)S(1)}, bf16[1,144,128]{2,1,0:T(8,128)(2,1)S(1)}, u32[]{:S(2)}, u32[]{:S(2)}) %collective-permute-start) | collective-permute-done | bytes 36896 | tf_op jit(solution)/shard_map/ppermute | solution.py:353
  7.4 1.5 %collective-permute-start.1 = (bf16[2,144,128]{2,1,0:T(8,128)(2,1)S(1)}, bf16[2,144,128]{2,1,0:T(8,128)(2,1)S(1)}, u32[]{:S(2)}, u32[]{:S(2)}) collective-permute-start(bf16[2,144,128]{2,1,0:T(8,128)(2,1)S(1)} %join.4.refs_0_), channel_id=1, source_target_pairs={{4,0},{0,4},{12,8},{8,12},{5,1},{1,5},{13,9},{9,13},{6,2},{2,6},{1... | collective-permute-start | bytes 221192 | tf_op jit(solution)/shard_map/ppermute | solution.py:353
  8.9 1.5 %collective-permute-start.3 = (bf16[2,128,128]{2,1,0:T(8,128)(2,1)S(1)}, bf16[2,128,128]{2,1,0:T(8,128)(2,1)S(1)}, u32[]{:S(2)}, u32[]{:S(2)}) collective-permute-start(bf16[2,128,128]{2,1,0:T(8,128)(2,1)S(1)} %join.6), channel_id=1, source_target_pairs={{2,0},{0,2},{3,1},{1,3},{6,4},{4,6},{7,5},{5,7},{10,8},{8,10},{11,... | collective-permute-start | bytes 196616 | tf_op jit(solution)/shard_map/ppermute | solution.py:353
  10.4 0.5 %collective-permute-start.4 = (bf16[2,128,128]{2,1,0:T(8,128)(2,1)S(1)}, bf16[2,128,128]{2,1,0:T(8,128)(2,1)S(1)}, u32[]{:S(2)}, u32[]{:S(2)}) collective-permute-start(bf16[2,128,128]{2,1,0:T(8,128)(2,1)S(1)} %join.6), channel_id=1, source_target_pairs={{6,0},{4,2},{2,4},{0,6},{14,8},{12,10},{10,12},{8,14},{7,1},{5,3},... | collective-permute-start | bytes 196616 | tf_op jit(solution)/shard_map/ppermute | solution.py:353
  10.9 1.3 %collective-permute-done.1.refs_1_ = bf16[2,144,128]{2,1,0:T(8,128)(2,1)S(1)} collective-permute-done((bf16[2,144,128]{2,1,0:T(8,128)(2,1)S(1)}, bf16[2,144,128]{2,1,0:T(8,128)(2,1)S(1)}, u32[]{:S(2)}, u32[]{:S(2)}) %collective-permute-start.1) | collective-permute-done | bytes 73760 | tf_op jit(solution)/shard_map/ppermute | solution.py:353
  12.2 0.1 collective-permute-start.2
  12.2 0.8 %own_first.1 = (f32[2,64,256]{2,1,0:T(8,128)S(1)}, f32[4,8,2,8,128]{4,3,2,1,0:T(8,128)S(1)}, f32[4,128,128]{2,1,0:T(8,128)S(1)}) custom-call(bf16[2,2,1024,256]{3,2,1,0:T(8,128)(2,1)S(1)} %get-tuple-element.18.table, f32[2,2,8,128]{3,2,1,0:T(8,128)S(1)} %get-tuple-element.19.phase, bf16[4,144,128]{2,1,0:T(8,128)(2,1)S(1)} %join.5.mine_ref), custom_call_target="tpu_custom_call" | custom-call | flops 2147483648 | tf_op jit(solution)/shard_map/own_first/pallas_call | solution.py:389
  13.1 0.5 %collective-permute-done.2.mine_ref = bf16[4,144,128]{2,1,0:T(8,128)(2,1)S(1)} collective-permute-done((bf16[4,144,128]{2,1,0:T(8,128)(2,1)S(1)}, bf16[4,144,128]{2,1,0:T(8,128)(2,1)S(1)}, u32[]{:S(2)}, u32[]{:S(2)}) %collective-permute-start.2) | collective-permute-done | bytes 147488 | tf_op jit(solution)/shard_map/ppermute | solution.py:353
  13.6 0.8 %own_second.1 = (f32[1,64,512]{2,1,0:T(8,128)S(1)}, f32[4,8,2,8,128]{4,3,2,1,0:T(8,128)S(1)}) custom-call(bf16[2,2,1024,256]{3,2,1,0:T(8,128)(2,1)S(1)} %get-tuple-element.18.table, f32[2,2,8,128]{3,2,1,0:T(8,128)S(1)} %get-tuple-element.19.phase, f32[4,128,128]{2,1,0:T(8,128)S(1)} %get-tuple-element.21.wide_ref, ...), custom_call_target="tpu_custom_call" | custom-call | flops 2147483648 | tf_op jit(solution)/shard_map/own_second/pallas_call | solution.py:389
  14.4 0.0 collective-permute-done.3.refs_0_
  14.4 1.1 %collective-permute-done.4.refs_1_ = bf16[2,128,128]{2,1,0:T(8,128)(2,1)S(1)} collective-permute-done((bf16[2,128,128]{2,1,0:T(8,128)(2,1)S(1)}, bf16[2,128,128]{2,1,0:T(8,128)(2,1)S(1)}, u32[]{:S(2)}, u32[]{:S(2)}) %collective-permute-start.4) | collective-permute-done | bytes 65568 | tf_op jit(solution)/shard_map/ppermute | solution.py:353
  15.5 0.1 collective-permute-start.5
  15.6 0.7 %other_first.1.sums_ref = f32[2,64,256]{2,1,0:T(8,128)S(1)} custom-call(bf16[2,2,1024,256]{3,2,1,0:T(8,128)(2,1)S(1)} %get-tuple-element.18.table, f32[4,128,128]{2,1,0:T(8,128)S(1)} %get-tuple-element.21.wide_ref, f32[4,8,2,8,128]{4,3,2,1,0:T(8,128)S(1)} %get-tuple-element.27.local_ref, bf16[4,128,128]{2,1,0:T(8,128)(2,1)S(1)} %join.7.sources_ref), custom_call_target="tpu_custom_call" | custom-call | flops 2147483648 | tf_op jit(solution)/shard_map/other_first/pallas_call | solution.py:389
  16.3 0.6 %collective-permute-done.5.sources_ref = bf16[4,128,128]{2,1,0:T(8,128)(2,1)S(1)} collective-permute-done((bf16[4,128,128]{2,1,0:T(8,128)(2,1)S(1)}, bf16[4,128,128]{2,1,0:T(8,128)(2,1)S(1)}, u32[]{:S(2)}, u32[]{:S(2)}) %collective-permute-start.5) | collective-permute-done | bytes 131104 | tf_op jit(solution)/shard_map/ppermute | solution.py:353
  17.0 1.8 %other_second.1 = f32[3,64,512]{2,1,0:T(8,128)} custom-call(s32[3]{0:T(128)} %plan_any.1, bf16[2,2,1024,256]{3,2,1,0:T(8,128)(2,1)S(1)} %get-tuple-element.18.table, f32[4,128,128]{2,1,0:T(8,128)S(1)} %get-tuple-element.21.wide_ref, f32[4,8,2,8,128]{4,3,2,1,0:T(8,128)S(1)} %get-tuple-element.23.local_ref, ...), custom_call_target="tpu_custom_call" | custom-call | flops 2147483648 | tf_op jit(solution)/shard_map/other_second/pallas_call | solution.py:389
  (4 shorter events, 0.0 us)
Async XLA Ops:
  0.9 6.4 %collective-permute-start = (bf16[1,144,128]{2,1,0:T(8,128)(2,1)S(1)}, bf16[1,144,128]{2,1,0:T(8,128)(2,1)S(1)}, u32[]{:S(2)}, u32[]{:S(2)}) collective-permute-start(bf16[1,144,128]{2,1,0:T(8,128)(2,1)S(1)} %prepare.1.refs_0_), channel_id=1, source_target_pairs={{8,0},{12,4},{0,8},{4,12},{9,1},{13,5},{1,9},{5,13},{10,2},{14,6},... | collective-permute-start | bytes 110600 | tf_op jit(solution)/shard_map/ppermute | solution.py:353
  7.4 4.8 %collective-permute-start.1 = (bf16[2,144,128]{2,1,0:T(8,128)(2,1)S(1)}, bf16[2,144,128]{2,1,0:T(8,128)(2,1)S(1)}, u32[]{:S(2)}, u32[]{:S(2)}) collective-permute-start(bf16[2,144,128]{2,1,0:T(8,128)(2,1)S(1)} %join.4.refs_0_), channel_id=1, source_target_pairs={{4,0},{0,4},{12,8},{8,12},{5,1},{1,5},{13,9},{9,13},{6,2},{2,6},{1... | collective-permute-start | bytes 221192 | tf_op jit(solution)/shard_map/ppermute | solution.py:353
  8.9 5.5 %collective-permute-start.3 = (bf16[2,128,128]{2,1,0:T(8,128)(2,1)S(1)}, bf16[2,128,128]{2,1,0:T(8,128)(2,1)S(1)}, u32[]{:S(2)}, u32[]{:S(2)}) collective-permute-start(bf16[2,128,128]{2,1,0:T(8,128)(2,1)S(1)} %join.6), channel_id=1, source_target_pairs={{2,0},{0,2},{3,1},{1,3},{6,4},{4,6},{7,5},{5,7},{10,8},{8,10},{11,... | collective-permute-start | bytes 196616 | tf_op jit(solution)/shard_map/ppermute | solution.py:353
  10.4 5.2 %collective-permute-start.4 = (bf16[2,128,128]{2,1,0:T(8,128)(2,1)S(1)}, bf16[2,128,128]{2,1,0:T(8,128)(2,1)S(1)}, u32[]{:S(2)}, u32[]{:S(2)}) collective-permute-start(bf16[2,128,128]{2,1,0:T(8,128)(2,1)S(1)} %join.6), channel_id=1, source_target_pairs={{6,0},{4,2},{2,4},{0,6},{14,8},{12,10},{10,12},{8,14},{7,1},{5,3},... | collective-permute-start | bytes 196616 | tf_op jit(solution)/shard_map/ppermute | solution.py:353
  12.2 1.4 %collective-permute-start.2 = (bf16[4,144,128]{2,1,0:T(8,128)(2,1)S(1)}, bf16[4,144,128]{2,1,0:T(8,128)(2,1)S(1)}, u32[]{:S(2)}, u32[]{:S(2)}) collective-permute-start(bf16[4,144,128]{2,1,0:T(8,128)(2,1)S(1)} %join.5.mine_ref), channel_id=1, source_target_pairs={{1,0},{0,1},{3,2},{2,3},{5,4},{4,5},{7,6},{6,7},{9,8},{8,9},{11,10... | collective-permute-start | bytes 442376 | tf_op jit(solution)/shard_map/ppermute | solution.py:353
  15.5 1.4 %collective-permute-start.5 = (bf16[4,128,128]{2,1,0:T(8,128)(2,1)S(1)}, bf16[4,128,128]{2,1,0:T(8,128)(2,1)S(1)}, u32[]{:S(2)}, u32[]{:S(2)}) collective-permute-start(bf16[4,128,128]{2,1,0:T(8,128)(2,1)S(1)} %join.7.sources_ref), channel_id=1, source_target_pairs={{1,0},{0,1},{3,2},{2,3},{5,4},{4,5},{7,6},{6,7},{9,8},{8,9},{11,10... | collective-permute-start | bytes 393224 | tf_op jit(solution)/shard_map/ppermute | solution.py:353

commit v13 on v12

v13 whole, which is shorter than its diff:
```python
import functools
import math

import jax
import jax.numpy as jnp
import numpy as np
from jax import lax
from jax.experimental import pallas as pl
from jax.experimental.pallas import tpu as pltpu
from jax.sharding import PartitionSpec as P

STEPS = 3
BAND = 128
LANES = 128
VMEM_BYTES = 32 * 1024 * 1024


def lag_table(lags, bins, halves, scale):
    bin_index = np.arange(bins, dtype=np.int64)
    lag = 2 * np.arange(lags // 2, dtype=np.int64) + 1
    phase = (bin_index[:, None] * lag[None, :]) % (4 * bins)
    angle = phase * (2.0 * math.pi / (4 * bins))
    factor = np.where(bin_index == 0, 1.0, 2.0)[:, None] * scale
    parts = np.stack([np.cos(angle) * factor, np.sin(angle) * factor])
    parts = parts.reshape(2, halves, bins // halves, lags // 2).transpose(1, 0, 2, 3)
    return parts.astype(jnp.bfloat16)


def turn(count, period):
    count = count % period
    quarter = (count + period // 8) // (period // 4)
    x = (count - quarter * (period // 4)).astype(jnp.float32) * (2.0 * math.pi / period)
    y = x * x
    sine = x * (1.0 + y * (-1 / 6 + y * (1 / 120 + y * (-1 / 5040 + y * (1 / 362880)))))
    cosine = 1.0 + y * (-1 / 2 + y * (1 / 24 + y * (-1 / 720 + y * (1 / 40320))))
    quarter = quarter % 4
    odd = quarter % 2 == 1
    real = jnp.where(odd, sine, cosine)
    imag = jnp.where(odd, cosine, sine)
    real = jnp.where((quarter == 1) | (quarter == 2), -real, real)
    imag = jnp.where(quarter >= 2, -imag, imag)
    return real, imag


def prepare_kernel(sizes, *refs):
    stations, bands, sta, blocks = sizes
    *plan, raw_ref, valid_ref, quality_ref, out_ref, wide = refs
    total = stations * sta
    me = lax.axis_index("sta")
    wide[...] = raw_ref[...].astype(jnp.float32)
    count = stations * bands
    real = wide[pl.ds(0, count, stride=2), :]
    imag = wide[pl.ds(1, count, stride=2), :]
    power = jnp.sum(real * real + imag * imag, axis=1, keepdims=True) * (1.0 / (2 * BAND))
    inverse = 1.0 / jnp.sqrt(power + 1e-06)
    real = (real * inverse).reshape(stations, bands, LANES)
    imag = (imag * inverse).reshape(stations, bands, LANES)
    white = jnp.concatenate([real, imag], axis=1).reshape(2 * count, LANES).astype(jnp.bfloat16)

    valid = valid_ref[...].astype(jnp.float32).astype(jnp.bfloat16)
    quality = jnp.broadcast_to(quality_ref[...].astype(jnp.float32), (8, total)).astype(jnp.bfloat16)
    pair = lax.broadcasted_iota(jnp.int32, (total, LANES), 1)
    station = lax.broadcasted_iota(jnp.int32, (total, LANES), 0)
    mine = lax.broadcasted_iota(jnp.int32, (stations, LANES), 0) == (
        lax.broadcasted_iota(jnp.int32, (stations, LANES), 1) % stations
    )
    dot = functools.partial(jnp.dot, preferred_element_type=jnp.float32)
    pick_local = (station == me * stations + pair % stations).astype(jnp.float32).astype(jnp.bfloat16)
    local_flags = dot(quality, pick_local)
    rows = []
    for k in range(blocks):
        source = (plan[0][k] if plan else k) * stations + pair // stations
        pick_source = (station == source).astype(jnp.float32).astype(jnp.bfloat16)
        valid_row = jnp.sum(jnp.where(mine, dot(valid, pick_source), 0.0), axis=0, keepdims=True)
        rows.append(valid_row * (dot(quality, pick_source) * local_flags)[:1])
    rows.append(jnp.zeros((16 - blocks, LANES), jnp.float32))
    weights = jnp.concatenate(rows, axis=0).astype(jnp.bfloat16)
    out_ref[0, pl.ds(0, 2 * count), :] = white
    out_ref[0, pl.ds(2 * count, 16), :] = weights


def spread_weights(sizes, locals_ref, wide):
    stations, bands, seg, sta, pol, blocks, lags = sizes
    pairs = stations * stations
    row_index = lax.broadcasted_iota(jnp.int32, (16, LANES), 0)
    diagonal = lax.broadcasted_iota(jnp.int32, (pairs, LANES), 0) == lax.broadcasted_iota(
        jnp.int32, (pairs, LANES), 1
    )
    ones = jnp.ones((LANES, LANES), jnp.bfloat16)
    for g in range(seg):
        flags = locals_ref[g, pl.ds(2 * stations * bands, 16), :].astype(jnp.float32)
        spread = []
        for n in range(blocks):
            block = lax.axis_index("sta") ^ n if sta == 2 else n
            row = jnp.sum(jnp.where(row_index == block, flags, 0.0), axis=0, keepdims=True)
            spread.append(jnp.where(diagonal, row, 0.0))
        spread = jnp.concatenate(spread, axis=0).astype(jnp.bfloat16)
        wide[g] = jnp.dot(spread, ones, preferred_element_type=jnp.float32)


def middle_phase(sizes):
    stations, bands, seg, sta, pol, blocks, lags = sizes
    row = lax.axis_index("pol") * bands + lax.broadcasted_iota(jnp.int32, (bands, LANES), 0)
    bin_index = row * LANES + lax.broadcasted_iota(jnp.int32, (bands, LANES), 1)
    run = pol * lags
    return turn(bin_index * (2 * run * lax.axis_index("seg") + run - 1), 2 * run * seg)


def turn_locals(sizes, cosine, sine, locals_ref, local):
    stations, bands, seg = sizes[:3]
    for g in range(seg):
        for j in range(stations):
            tile = locals_ref[g, pl.ds(j * 16, 16), :].astype(jnp.float32)
            local[g, j, 0] = tile[:bands] * cosine + tile[bands:] * sine
            local[g, j, 1] = tile[bands:] * cosine - tile[:bands] * sine


def add_products(stations, count, segments, tile_of, weight_of, local_of, real_x, imag_x):
    def one_source(a, carry):
        tiles = [tile_of(n, a).astype(jnp.float32) for n in range(segments)]
        for j in range(stations):
            pair = a * stations + j
            at = pl.ds(pair * 8 if isinstance(pair, int) else pl.multiple_of(pair * 8, 8), 8)
            real_sum = imag_sum = None
            for n in range(segments):
                weight = jnp.broadcast_to(weight_of(n, pair), (8, LANES))
                real_src = tiles[n][:8] * weight
                imag_src = tiles[n][8:] * weight
                real_loc, imag_loc = local_of(n, j)
                real_term = real_src * real_loc + imag_src * imag_loc
                imag_term = imag_src * real_loc - real_src * imag_loc
                real_sum = real_term if real_sum is None else real_sum + real_term
                imag_sum = imag_term if imag_sum is None else imag_sum + imag_term
            real_x[at, :] = real_sum
            imag_x[at, :] = imag_sum
        return carry

    if count <= 8:
        for a in range(count):
            one_source(a, 0)
    else:
        lax.fori_loop(0, count, one_source, 0, unroll=2)


def pack(rows, bands, real_x, imag_x, packed):
    for band in range(bands):
        at = pl.ds(band * LANES, LANES)
        strided = pl.ds(band, rows, stride=8)
        packed[0, :, at] = real_x[strided, :].astype(jnp.bfloat16)
        packed[1, :, at] = imag_x[strided, :].astype(jnp.bfloat16)


def source_tile(sources_ref, base, count, stations):
    def tile_of(n, a):
        start = a % stations * 16
        start = start if isinstance(a, int) else pl.multiple_of(start, 16)
        return sources_ref[base + a // stations * count + n, pl.ds(start, 16), :]

    return tile_of


def block_sums(sizes, first_block, count, table, wide, local, sources_ref, kept_ref, sent_ref, real_x, imag_x, packed):
    stations, bands, seg = sizes[:3]
    pairs = stations * stations
    add_products(
        stations, count * stations, seg, source_tile(sources_ref, 0, seg, stations),
        lambda n, pair: wide[n, pl.ds(first_block * pairs + pair, 1), :],
        lambda n, j: (local[n, j, 0], local[n, j, 1]),
        real_x, imag_x,
    )
    pack(count * pairs, bands, real_x, imag_x, packed)
    dot = functools.partial(jnp.dot, preferred_element_type=jnp.float32)
    even, odd = dot(packed[0], table[0]), dot(packed[1], table[1])
    before = lax.axis_index("pol") == 0
    odd = jnp.where(before, odd, -odd)
    kept_ref[...] = even + odd
    sent_ref[...] = even - odd


def in_order(sizes, sums):
    before = lax.axis_index("pol") == 0
    lane = lax.broadcasted_iota(jnp.int32, (sums.shape[0], LANES), 1)
    index = jnp.where(before, LANES - 1 - lane, lane)
    runs = [sums[:, at : at + LANES] for at in range(0, sums.shape[1], LANES)]
    runs = [jnp.where(before, back, run) for run, back in zip(runs, runs[::-1])]
    runs = [jnp.take_along_axis(run, index, axis=1, mode="promise_in_bounds") for run in runs]
    return jnp.concatenate(runs, axis=1)


def all_blocks_kernel(sizes, table, phase, mine_ref, sources_ref, kept_ref, sent_ref, local, wide, *scratch):
    spread_weights(sizes, mine_ref, wide)
    turn_locals(sizes, phase[0], phase[1], mine_ref, local)
    block_sums(sizes, 0, sizes[5], table, wide, local, sources_ref, kept_ref, sent_ref, *scratch)


def own_block_kernel(sizes, table, phase, mine_ref, kept_ref, sent_ref, local_ref, wide_ref, *scratch):
    spread_weights(sizes, mine_ref, wide_ref)
    turn_locals(sizes, phase[0], phase[1], mine_ref, local_ref)
    block_sums(sizes, 0, 1, table, wide_ref, local_ref, mine_ref, kept_ref, sent_ref, *scratch)


def other_block_kernel(sizes, table, wide_ref, local_ref, sources_ref, kept_ref, sent_ref, *scratch):
    block_sums(sizes, 1, 1, table, wide_ref, local_ref, sources_ref, kept_ref, sent_ref, *scratch)


def combine_kernel(sizes, kept_ref, got_ref, lags_ref):
    lags_ref[...] = in_order(sizes, kept_ref[...] + got_ref[...])


def place_kernel(sizes, mask_ref, own_ref, kept_ref, got_ref, out_ref, steps, sems):
    other = in_order(sizes, kept_ref[...] + got_ref[...])
    own = own_ref[...]
    copies = []
    for step in range(STEPS):
        mask = jnp.broadcast_to(mask_ref[step, :1, :1], other.shape)
        steps[step] = jnp.where(mask > 0, own, other)
        copies.append(pltpu.make_async_copy(steps.at[step], out_ref.at[step], sems.at[step]))
        copies[-1].start()
    for copy in copies:
        copy.wait()


def fetch_kernel(sizes, table_hbm, plan_any, table_ref, phase_ref, mask_ref, plan_ref, sems):
    copies = [
        pltpu.make_async_copy(table_hbm.at[lax.axis_index("pol")], table_ref, sems.at[0]),
        pltpu.make_async_copy(plan_any, plan_ref, sems.at[1]),
    ]
    for copy in copies:
        copy.start()
    phase_ref[0], phase_ref[1] = middle_phase(sizes)
    copies[1].wait()
    for step in range(STEPS):
        own = (plan_ref[step] == lax.axis_index("sta")).astype(jnp.float32)
        mask_ref[step] = jnp.full(mask_ref.shape[1:], own, jnp.float32)
    copies[0].wait()


def join_kernel(ranges, *refs):
    *pieces, out_ref = refs
    at = 0
    for piece, (first, count) in zip(pieces, ranges):
        out_ref[pl.ds(at, count)] = piece[pl.ds(first, count), pl.ds(0, out_ref.shape[1]), :]
        at += count


def join(*pieces, rows=None):
    pieces = [piece if isinstance(piece, tuple) else (piece, 0, piece.shape[0]) for piece in pieces]
    arrays = [piece[0] for piece in pieces]
    ranges = [piece[1:] for piece in pieces]
    vmem = pl.BlockSpec(memory_space=pltpu.VMEM)
    return pl.pallas_call(
        functools.partial(join_kernel, ranges),
        out_shape=pltpu.VMEM(
            (sum(count for _, count in ranges), rows or arrays[0].shape[1], LANES), arrays[0].dtype
        ),
        in_specs=[vmem] * len(arrays),
        out_specs=vmem,
        compiler_params=pltpu.CompilerParams(vmem_limit_bytes=VMEM_BYTES),
        name="join",
    )(*arrays)


def fetch_from(value, axes, source_of):
    sizes = tuple(lax.axis_size(axis) for axis in axes)
    pairs = []
    for index in np.ndindex(*sizes):
        source = source_of(*index)
        pairs.append((int(np.ravel_multi_index(source, sizes)), int(np.ravel_multi_index(index, sizes))))
    return lax.ppermute(value, axes, pairs)


def exchange(value, axis, distance):
    return fetch_from(value, (axis,), lambda i: (i ^ distance,))


def shards(table, raw_spectra, owner_plan, pair_valid, quality):
    seg, sta, pol = (lax.axis_size(name) for name in ("seg", "sta", "pol"))
    _, stations, _, bins = raw_spectra.shape
    bands = bins // BAND
    fast = sta == 2 and pol == 2 and seg > 1
    blocks = 2 if fast else STEPS
    pairs = stations * stations
    lags = table.shape[3]
    rows = 2 * stations * bands + 16
    sizes = (stations, bands, seg, sta, pol, blocks, lags)

    raw = raw_spectra.reshape(stations, 2, bands, BAND).transpose(0, 2, 1, 3).reshape(-1, BAND)
    vmem = pl.BlockSpec(memory_space=pltpu.VMEM)
    smem = pl.BlockSpec(memory_space=pltpu.SMEM)
    hbm = pl.BlockSpec(memory_space=pltpu.HBM)
    plan = [] if fast else [owner_plan]
    in_hbm = functools.partial(pltpu.with_memory_space_constraint, memory_space=pltpu.HBM)
    own = pl.pallas_call(
        functools.partial(prepare_kernel, (stations, bands, sta, blocks)),
        out_shape=pltpu.VMEM((1, rows, LANES), jnp.bfloat16),
        in_specs=[smem] * len(plan) + [vmem, vmem, vmem],
        out_specs=vmem,
        scratch_shapes=[pltpu.VMEM((2 * stations * bands, LANES), jnp.float32)],
        compiler_params=pltpu.CompilerParams(vmem_limit_bytes=VMEM_BYTES),
        name="prepare",
    )(*plan, in_hbm(raw), in_hbm(jnp.transpose(pair_valid[0])), in_hbm(quality))

    def call(kernel, out_shape, *args, out_specs=None, scratch=(), flops=0, moved=0, name=None):
        many = isinstance(out_shape, (list, tuple))
        return pl.pallas_call(
            functools.partial(kernel, sizes),
            out_shape=out_shape,
            in_specs=[hbm if x is table_const or x is plan_const else vmem for x in args],
            out_specs=out_specs or ([vmem] * len(out_shape) if many else vmem),
            scratch_shapes=list(scratch),
            compiler_params=pltpu.CompilerParams(vmem_limit_bytes=VMEM_BYTES),
            cost_estimate=pl.CostEstimate(flops=flops, bytes_accessed=moved, transcendentals=0),
            name=name,
        )(*args)

    f32 = jnp.float32
    table_const, plan_const = in_hbm(table), in_hbm(owner_plan)
    table, phase, mask = call(
        fetch_kernel,
        [
            pltpu.VMEM(table.shape[1:], table.dtype),
            pltpu.VMEM((2, bands, LANES), f32),
            pltpu.VMEM((STEPS, 8, LANES), f32),
        ],
        table_const, plan_const,
        scratch=[pltpu.SMEM((STEPS,), jnp.int32), pltpu.SemaphoreType.DMA((2,))],
        moved=4 * table.size // pol,
        name="fetch",
    )

    def products(count):
        return [pltpu.VMEM((count * pairs * 8, LANES), f32)] * 2 + [pltpu.VMEM((2, count * pairs, bins), jnp.bfloat16)]

    quarter = 32 * pairs * 2 * bins * lags
    local_shape = pltpu.VMEM((seg, stations, 2, bands, LANES), f32)
    wide_shape = pltpu.VMEM((seg, blocks * pairs, LANES), f32)
    sums_shapes = [pltpu.VMEM((pairs, lags), f32)] * 2

    if fast:
        far, distance = own, seg // 2
        while distance > 1:
            far = join(far, exchange(far, "seg", distance))
            distance //= 2
        far, table = lax.optimization_barrier((far, table))
        near = exchange(far, "seg", 1)
        partner = exchange(far, "sta", 1)
        across = fetch_from(far, ("seg", "sta"), lambda z, x: (z ^ 1, x ^ 1))
        mine = join(far, near)
        own_kept, own_sent, local, wide = call(
            own_block_kernel, sums_shapes + [local_shape, wide_shape],
            table, phase, mine,
            scratch=products(1), flops=quarter, name="own_block",
        )
        own_kept, partner, across = lax.optimization_barrier((own_kept, partner, across))
        kept, sent = call(
            other_block_kernel, sums_shapes,
            table, wide, local, join(partner, across),
            scratch=products(1), flops=quarter, name="other_block",
        )
        own_lags = call(
            combine_kernel, pltpu.VMEM((pairs, lags), f32), own_kept, exchange(own_sent, "pol", 1), name="combine"
        )
        got = exchange(sent, "pol", 1)
        result = call(
            place_kernel, jax.ShapeDtypeStruct((STEPS, pairs, lags), f32),
            mask, own_lags, kept, got,
            out_specs=hbm,
            scratch=[pltpu.VMEM((STEPS, pairs, lags), f32), pltpu.SemaphoreType.DMA((STEPS,))],
            name="place",
        )
    else:
        mine, distance = own, seg // 2
        while distance:
            mine = join(mine, exchange(mine, "seg", distance))
            distance //= 2
        gathered = lax.all_gather(mine, "sta")
        sources = join(*(gathered[owner_plan[k]] for k in range(STEPS)))
        kept, sent = call(
            all_blocks_kernel, [pltpu.VMEM((blocks * pairs, lags), f32)] * 2,
            table, phase, mine, sources,
            scratch=[local_shape, wide_shape] + products(blocks), flops=blocks * quarter, name="all_blocks",
        )
        result = call(
            combine_kernel, jax.ShapeDtypeStruct((blocks * pairs, lags), f32),
            kept, exchange(sent, "pol", 1), name="combine",
        )
    return result.reshape(STEPS, stations, stations, lags)


def solution(mesh):
    placed = (
        P(("groups", "seg"), "sta", None, "pol"),
        P("groups"),
        P(("groups", "seg"), None, "sta"),
        P(("groups", "seg"), None),
    )

    def whole(raw_spectra, owner_plan, pair_valid, quality):
        seg, pol = mesh.shape["seg"], mesh.shape["pol"]
        bins = raw_spectra.shape[3]
        segments = raw_spectra.shape[0] // mesh.shape["groups"]
        table = lag_table(2 * bins // seg, bins, pol, 1.0 / math.sqrt(bins * segments))
        return jax.shard_map(
            shards,
            mesh=mesh,
            in_specs=(P(),) + placed,
            out_specs=P("groups", None, "sta", ("seg", "pol")),
            check_vma=False,
        )(jnp.asarray(table), raw_spectra, owner_plan, pair_valid, quality)

    return whole
```

time: 19 us -> 19.2 us (1.011)
  Pallas kernels: 6.65 us -> 5.51 us
  waiting for transfers between devices: 4.29 us -> 5.3 us
  starting transfers between devices: 7.73 us -> 8.17 us
    pallas_call x5, Pallas kernels: 5.7 us -> 4.57 us  [call(): pl.pallas_call(functools.partial(kernel, sizes), out_shape=out_shape, in_...]
    ppermute x6, waiting for transfers between devices: 4.29 us -> 5.3 us  [fetch_from(): return lax.ppermute(value, axes, pairs)]
    ppermute x6, starting transfers between devices: 7.73 us -> 8.17 us  [fetch_from(): return lax.ppermute(value, axes, pairs)]
  transfers between devices with their start and end apart: 6 -> 6, of which waited for: 5 -> 5; matrix products, arithmetic and copies ran while one was open for 0% -> 0% of each run, Pallas kernels for 21% -> 19%
where the time goes in v13:
time: 19.2 us; the launch traced here: 19 us
  starting transfers between devices  8.17 us (43%)
  Pallas kernels  5.51 us (29%)
  waiting for transfers between devices  5.3 us (28%)
    ppermute x6, starting transfers between devices, fetch_from(): return lax.ppermute(value, axes, pairs)  8.17 us
    ppermute x6, waiting for transfers between devices, fetch_from(): return lax.ppermute(value, axes, pairs)  5.3 us
    pallas_call x5, Pallas kernels, call(): pl.pallas_call(functools.partial(kernel, sizes), out_shape=out_shape, in_...  4.57 us
    pallas_call x1, Pallas kernels, shards(): pl.pallas_call(functools.partial(prepare_kernel, (stations, bands, sta, b...  0.91 us
  transfers between devices with their start and end apart: 6, of which 5 were waited for; matrix products, arithmetic and copies ran while one was open for 0% of the time, Pallas kernels for 19%

profile of v13, /device:TPU:0, one launch (start us, length us, event | category | flops | bytes accessed | tf_op | source)
XLA Modules:
  0.0 19.0 jit_solution(13656641092400508381)
XLA Ops:
  0.0 0.9 %prepare.1.refs_0_ = bf16[1,144,128]{2,1,0:T(8,128)(2,1)S(1)} custom-call(bf16[128,128]{1,0:T(8,128)(2,1)} %bitcast.9, s32[8,16]{1,0:T(8,128)} %bitcast.10, s32[1,16]{1,0:T(1,128)} %refs_2_.1), custom_call_target="tpu_custom_call" | custom-call | tf_op jit(solution)/shard_map/prepare/pallas_call | solution.py:293
  0.9 4.1 %collective-permute-start = (bf16[1,144,128]{2,1,0:T(8,128)(2,1)S(1)}, bf16[1,144,128]{2,1,0:T(8,128)(2,1)S(1)}, u32[]{:S(2)}, u32[]{:S(2)}) collective-permute-start(bf16[1,144,128]{2,1,0:T(8,128)(2,1)S(1)} %prepare.1.refs_0_), channel_id=1, source_target_pairs={{8,0},{12,4},{0,8},{4,12},{9,1},{13,5},{1,9},{5,13},{10,2},{14,6},... | collective-permute-start | bytes 110600 | tf_op jit(solution)/shard_map/ppermute | solution.py:269
  5.0 1.6 %fetch.1 = (bf16[2,1024,512]{2,1,0:T(8,128)(2,1)S(1)}, f32[2,8,128]{2,1,0:T(8,128)S(1)}, f32[3,8,128]{2,1,0:T(8,128)S(1)}) custom-call(bf16[2,2,1024,512]{3,2,1,0:T(8,128)(2,1)} %constant.2.clone.table_hbm, s32[3]{0:T(128)} %plan_any.1), custom_call_target="tpu_custom_call" | custom-call | bytes 4194304 | tf_op jit(solution)/shard_map/fetch/pallas_call | solution.py:305
  6.6 0.7 %collective-permute-done.refs_1_ = bf16[1,144,128]{2,1,0:T(8,128)(2,1)S(1)} collective-permute-done((bf16[1,144,128]{2,1,0:T(8,128)(2,1)S(1)}, bf16[1,144,128]{2,1,0:T(8,128)(2,1)S(1)}, u32[]{:S(2)}, u32[]{:S(2)}) %collective-permute-start) | collective-permute-done | bytes 36896 | tf_op jit(solution)/shard_map/ppermute | solution.py:269
  7.4 1.5 %collective-permute-start.1 = (bf16[2,144,128]{2,1,0:T(8,128)(2,1)S(1)}, bf16[2,144,128]{2,1,0:T(8,128)(2,1)S(1)}, u32[]{:S(2)}, u32[]{:S(2)}) collective-permute-start(bf16[2,144,128]{2,1,0:T(8,128)(2,1)S(1)} %join.3.refs_0_), channel_id=1, source_target_pairs={{4,0},{0,4},{12,8},{8,12},{5,1},{1,5},{13,9},{9,13},{6,2},{2,6},{1... | collective-permute-start | bytes 221192 | tf_op jit(solution)/shard_map/ppermute | solution.py:269
  8.9 1.5 %collective-permute-start.2 = (bf16[2,144,128]{2,1,0:T(8,128)(2,1)S(1)}, bf16[2,144,128]{2,1,0:T(8,128)(2,1)S(1)}, u32[]{:S(2)}, u32[]{:S(2)}) collective-permute-start(bf16[2,144,128]{2,1,0:T(8,128)(2,1)S(1)} %join.3.refs_0_), channel_id=1, source_target_pairs={{2,0},{0,2},{3,1},{1,3},{6,4},{4,6},{7,5},{5,7},{10,8},{8,10},{11,... | collective-permute-start | bytes 221192 | tf_op jit(solution)/shard_map/ppermute | solution.py:269
  10.4 0.5 %collective-permute-start.3 = (bf16[2,144,128]{2,1,0:T(8,128)(2,1)S(1)}, bf16[2,144,128]{2,1,0:T(8,128)(2,1)S(1)}, u32[]{:S(2)}, u32[]{:S(2)}) collective-permute-start(bf16[2,144,128]{2,1,0:T(8,128)(2,1)S(1)} %join.3.refs_0_), channel_id=1, source_target_pairs={{6,0},{4,2},{2,4},{0,6},{14,8},{12,10},{10,12},{8,14},{7,1},{5,3},... | collective-permute-start | bytes 221192 | tf_op jit(solution)/shard_map/ppermute | solution.py:269
  10.9 1.3 %collective-permute-done.1.refs_1_ = bf16[2,144,128]{2,1,0:T(8,128)(2,1)S(1)} collective-permute-done((bf16[2,144,128]{2,1,0:T(8,128)(2,1)S(1)}, bf16[2,144,128]{2,1,0:T(8,128)(2,1)S(1)}, u32[]{:S(2)}, u32[]{:S(2)}) %collective-permute-start.1) | collective-permute-done | bytes 73760 | tf_op jit(solution)/shard_map/ppermute | solution.py:269
  12.2 1.0 %own_block.1 = (f32[64,512]{1,0:T(8,128)S(1)}, f32[64,512]{1,0:T(8,128)S(1)}, f32[4,8,2,8,128]{4,3,2,1,0:T(8,128)S(1)}, f32[4,128,128]{2,1,0:T(8,128)S(1)}) custom-call(bf16[2,1024,512]{2,1,0:T(8,128)(2,1)S(1)} %get-tuple-element.21.table, f32[2,8,128]{2,1,0:T(8,128)S(1)} %get-tuple-element.22.phase, bf16[4,144,128]{2,1,0:T(8,128)(2,1)S(1)} %join.4.mine_ref), custom_call_target="tpu_custom_call" | custom-call | flops 2147483648 | tf_op jit(solution)/shard_map/own_block/pallas_call | solution.py:305
  13.2 0.7 %collective-permute-done.2.refs_0_ = bf16[2,144,128]{2,1,0:T(8,128)(2,1)S(1)} collective-permute-done((bf16[2,144,128]{2,1,0:T(8,128)(2,1)S(1)}, bf16[2,144,128]{2,1,0:T(8,128)(2,1)S(1)}, u32[]{:S(2)}, u32[]{:S(2)}) %collective-permute-start.2) | collective-permute-done | bytes 73760 | tf_op jit(solution)/shard_map/ppermute | solution.py:269
  13.9 1.7 %collective-permute-done.3.refs_1_ = bf16[2,144,128]{2,1,0:T(8,128)(2,1)S(1)} collective-permute-done((bf16[2,144,128]{2,1,0:T(8,128)(2,1)S(1)}, bf16[2,144,128]{2,1,0:T(8,128)(2,1)S(1)}, u32[]{:S(2)}, u32[]{:S(2)}) %collective-permute-start.3) | collective-permute-done | bytes 73760 | tf_op jit(solution)/shard_map/ppermute | solution.py:269
  15.6 0.0 collective-permute-start.4
  15.6 0.9 %other_block.1 = (f32[64,512]{1,0:T(8,128)S(1)}, f32[64,512]{1,0:T(8,128)S(1)}) custom-call(bf16[2,1024,512]{2,1,0:T(8,128)(2,1)S(1)} %get-tuple-element.21.table, f32[4,128,128]{2,1,0:T(8,128)S(1)} %get-tuple-element.27.wide_ref, f32[4,8,2,8,128]{4,3,2,1,0:T(8,128)S(1)} %get-tuple-element.28.local_ref, bf16[4,144,128]{2,1,0:T(8,128)(2,1)S(1)} %join.5.sources_ref), custom_call_target="tpu_custom_call" | custom-call | flops 2147483648 | tf_op jit(solution)/shard_map/other_block/pallas_call | solution.py:305
  16.6 0.6 %collective-permute-start.5 = (f32[64,512]{1,0:T(8,128)S(1)}, f32[64,512]{1,0:T(8,128)S(1)}, u32[]{:S(2)}, u32[]{:S(2)}) collective-permute-start(f32[64,512]{1,0:T(8,128)S(1)} %get-tuple-element.32), channel_id=1, source_target_pairs={{1,0},{0,1},{3,2},{2,3},{5,4},{4,5},{7,6},{6,7},{9,8},{8,9},{11,10... | collective-permute-start | bytes 393224 | tf_op jit(solution)/shard_map/ppermute | solution.py:269
  17.1 0.0 collective-permute-done.4.got_ref
  17.2 0.1 combine.1.own_ref
  17.3 0.9 %collective-permute-done.5.got_ref = f32[64,512]{1,0:T(8,128)S(1)} collective-permute-done((f32[64,512]{1,0:T(8,128)S(1)}, f32[64,512]{1,0:T(8,128)S(1)}, u32[]{:S(2)}, u32[]{:S(2)}) %collective-permute-start.5) | collective-permute-done | bytes 131104 | tf_op jit(solution)/shard_map/ppermute | solution.py:269
  18.1 0.9 %place.1 = f32[3,64,512]{2,1,0:T(8,128)} custom-call(f32[3,8,128]{2,1,0:T(8,128)S(1)} %get-tuple-element.19.mask_ref, f32[64,512]{1,0:T(8,128)S(1)} %combine.1.own_ref, f32[64,512]{1,0:T(8,128)S(1)} %get-tuple-element.31.kept_ref, f32[64,512]{1,0:T(8,128)S(1)} %collective-permute-done.5.got_ref), custom_call_target="tpu_custom_call" | custom-call | tf_op jit(solution)/shard_map/place/pallas_call | solution.py:305
  (3 shorter events, 0.0 us)
Async XLA Ops:
  0.9 6.4 %collective-permute-start = (bf16[1,144,128]{2,1,0:T(8,128)(2,1)S(1)}, bf16[1,144,128]{2,1,0:T(8,128)(2,1)S(1)}, u32[]{:S(2)}, u32[]{:S(2)}) collective-permute-start(bf16[1,144,128]{2,1,0:T(8,128)(2,1)S(1)} %prepare.1.refs_0_), channel_id=1, source_target_pairs={{8,0},{12,4},{0,8},{4,12},{9,1},{13,5},{1,9},{5,13},{10,2},{14,6},... | collective-permute-start | bytes 110600 | tf_op jit(solution)/shard_map/ppermute | solution.py:269
  7.4 4.8 %collective-permute-start.1 = (bf16[2,144,128]{2,1,0:T(8,128)(2,1)S(1)}, bf16[2,144,128]{2,1,0:T(8,128)(2,1)S(1)}, u32[]{:S(2)}, u32[]{:S(2)}) collective-permute-start(bf16[2,144,128]{2,1,0:T(8,128)(2,1)S(1)} %join.3.refs_0_), channel_id=1, source_target_pairs={{4,0},{0,4},{12,8},{8,12},{5,1},{1,5},{13,9},{9,13},{6,2},{2,6},{1... | collective-permute-start | bytes 221192 | tf_op jit(solution)/shard_map/ppermute | solution.py:269
  8.9 5.1 %collective-permute-start.2 = (bf16[2,144,128]{2,1,0:T(8,128)(2,1)S(1)}, bf16[2,144,128]{2,1,0:T(8,128)(2,1)S(1)}, u32[]{:S(2)}, u32[]{:S(2)}) collective-permute-start(bf16[2,144,128]{2,1,0:T(8,128)(2,1)S(1)} %join.3.refs_0_), channel_id=1, source_target_pairs={{2,0},{0,2},{3,1},{1,3},{6,4},{4,6},{7,5},{5,7},{10,8},{8,10},{11,... | collective-permute-start | bytes 221192 | tf_op jit(solution)/shard_map/ppermute | solution.py:269
  10.4 5.3 %collective-permute-start.3 = (bf16[2,144,128]{2,1,0:T(8,128)(2,1)S(1)}, bf16[2,144,128]{2,1,0:T(8,128)(2,1)S(1)}, u32[]{:S(2)}, u32[]{:S(2)}) collective-permute-start(bf16[2,144,128]{2,1,0:T(8,128)(2,1)S(1)} %join.3.refs_0_), channel_id=1, source_target_pairs={{6,0},{4,2},{2,4},{0,6},{14,8},{12,10},{10,12},{8,14},{7,1},{5,3},... | collective-permute-start | bytes 221192 | tf_op jit(solution)/shard_map/ppermute | solution.py:269
  15.6 1.5 %collective-permute-start.4 = (f32[64,512]{1,0:T(8,128)S(1)}, f32[64,512]{1,0:T(8,128)S(1)}, u32[]{:S(2)}, u32[]{:S(2)}) collective-permute-start(f32[64,512]{1,0:T(8,128)S(1)} %get-tuple-element.26), channel_id=1, source_target_pairs={{1,0},{0,1},{3,2},{2,3},{5,4},{4,5},{7,6},{6,7},{9,8},{8,9},{11,10... | collective-permute-start | bytes 393224 | tf_op jit(solution)/shard_map/ppermute | solution.py:269
  16.6 1.6 %collective-permute-start.5 = (f32[64,512]{1,0:T(8,128)S(1)}, f32[64,512]{1,0:T(8,128)S(1)}, u32[]{:S(2)}, u32[]{:S(2)}) collective-permute-start(f32[64,512]{1,0:T(8,128)S(1)} %get-tuple-element.32), channel_id=1, source_target_pairs={{1,0},{0,1},{3,2},{2,3},{5,4},{4,5},{7,6},{6,7},{9,8},{8,9},{11,10... | collective-permute-start | bytes 393224 | tf_op jit(solution)/shard_map/ppermute | solution.py:269

commit v14 on v13

--- a/solution.py
+++ b/solution.py
@@ -343,22 +343,22 @@
             distance //= 2
         far, table = lax.optimization_barrier((far, table))
         near = exchange(far, "seg", 1)
+        across = fetch_from(far, ("seg", "sta"), lambda z, x: (z ^ 1, x ^ 1))
         partner = exchange(far, "sta", 1)
-        across = fetch_from(far, ("seg", "sta"), lambda z, x: (z ^ 1, x ^ 1))
         mine = join(far, near)
         own_kept, own_sent, local, wide = call(
             own_block_kernel, sums_shapes + [local_shape, wide_shape],
             table, phase, mine,
             scratch=products(1), flops=quarter, name="own_block",
         )
-        own_kept, partner, across = lax.optimization_barrier((own_kept, partner, across))
+        own_lags = call(
+            combine_kernel, pltpu.VMEM((pairs, lags), f32), own_kept, exchange(own_sent, "pol", 1), name="combine"
+        )
+        own_lags, across, partner = lax.optimization_barrier((own_lags, across, partner))
         kept, sent = call(
             other_block_kernel, sums_shapes,
             table, wide, local, join(partner, across),
             scratch=products(1), flops=quarter, name="other_block",
-        )
-        own_lags = call(
-            combine_kernel, pltpu.VMEM((pairs, lags), f32), own_kept, exchange(own_sent, "pol", 1), name="combine"
         )
         got = exchange(sent, "pol", 1)
         result = call(

time: 19.2 us -> 23.5 us (1.22)
  waiting for transfers between devices: 5.3 us -> 8.9 us
  starting transfers between devices: 8.17 us -> 8.79 us
    ppermute x6, waiting for transfers between devices: 5.3 us -> 8.9 us  [fetch_from(): return lax.ppermute(value, axes, pairs)]
    ppermute x6, starting transfers between devices: 8.17 us -> 8.79 us  [fetch_from(): return lax.ppermute(value, axes, pairs)]
  transfers between devices with their start and end apart: 6 -> 6, of which waited for: 5 -> 5; matrix products, arithmetic and copies ran while one was open for 0% -> 0% of each run, Pallas kernels for 19% -> 7%
where the time goes in v14:
time: 23.5 us; the launch traced here: 23.3 us
  waiting for transfers between devices  8.9 us (38%)
  starting transfers between devices  8.79 us (37%)
  Pallas kernels  5.51 us (23%)
    ppermute x6, waiting for transfers between devices, fetch_from(): return lax.ppermute(value, axes, pairs)  8.9 us
    ppermute x6, starting transfers between devices, fetch_from(): return lax.ppermute(value, axes, pairs)  8.79 us
    pallas_call x5, Pallas kernels, call(): pl.pallas_call(functools.partial(kernel, sizes), out_shape=out_shape, in_...  4.57 us
    pallas_call x1, Pallas kernels, shards(): pl.pallas_call(functools.partial(prepare_kernel, (stations, bands, sta, b...  0.91 us
  transfers between devices with their start and end apart: 6, of which 5 were waited for; matrix products, arithmetic and copies ran while one was open for 0% of the time, Pallas kernels for 7%

profile of v14, /device:TPU:0, one launch (start us, length us, event | category | flops | bytes accessed | tf_op | source)
XLA Modules:
  0.0 23.3 jit_solution(4052336513160218972)
XLA Ops:
  0.0 0.9 %prepare.1.refs_0_ = bf16[1,144,128]{2,1,0:T(8,128)(2,1)S(1)} custom-call(bf16[128,128]{1,0:T(8,128)(2,1)} %bitcast.9, s32[8,16]{1,0:T(8,128)} %bitcast.10, s32[1,16]{1,0:T(1,128)} %refs_2_.1), custom_call_target="tpu_custom_call" | custom-call | tf_op jit(solution)/shard_map/prepare/pallas_call | solution.py:293
  0.9 4.1 %collective-permute-start = (bf16[1,144,128]{2,1,0:T(8,128)(2,1)S(1)}, bf16[1,144,128]{2,1,0:T(8,128)(2,1)S(1)}, u32[]{:S(2)}, u32[]{:S(2)}) collective-permute-start(bf16[1,144,128]{2,1,0:T(8,128)(2,1)S(1)} %prepare.1.refs_0_), channel_id=1, source_target_pairs={{8,0},{12,4},{0,8},{4,12},{9,1},{13,5},{1,9},{5,13},{10,2},{14,6},... | collective-permute-start | bytes 110600 | tf_op jit(solution)/shard_map/ppermute | solution.py:269
  5.0 1.6 %fetch.1 = (bf16[2,1024,512]{2,1,0:T(8,128)(2,1)S(1)}, f32[2,8,128]{2,1,0:T(8,128)S(1)}, f32[3,8,128]{2,1,0:T(8,128)S(1)}) custom-call(bf16[2,2,1024,512]{3,2,1,0:T(8,128)(2,1)} %constant.2.clone.table_hbm, s32[3]{0:T(128)} %plan_any.1), custom_call_target="tpu_custom_call" | custom-call | bytes 4194304 | tf_op jit(solution)/shard_map/fetch/pallas_call | solution.py:305
  6.6 0.7 %collective-permute-done.refs_1_ = bf16[1,144,128]{2,1,0:T(8,128)(2,1)S(1)} collective-permute-done((bf16[1,144,128]{2,1,0:T(8,128)(2,1)S(1)}, bf16[1,144,128]{2,1,0:T(8,128)(2,1)S(1)}, u32[]{:S(2)}, u32[]{:S(2)}) %collective-permute-start) | collective-permute-done | bytes 36896 | tf_op jit(solution)/shard_map/ppermute | solution.py:269
  7.4 1.5 %collective-permute-start.1 = (bf16[2,144,128]{2,1,0:T(8,128)(2,1)S(1)}, bf16[2,144,128]{2,1,0:T(8,128)(2,1)S(1)}, u32[]{:S(2)}, u32[]{:S(2)}) collective-permute-start(bf16[2,144,128]{2,1,0:T(8,128)(2,1)S(1)} %join.3.refs_0_), channel_id=1, source_target_pairs={{4,0},{0,4},{12,8},{8,12},{5,1},{1,5},{13,9},{9,13},{6,2},{2,6},{1... | collective-permute-start | bytes 221192 | tf_op jit(solution)/shard_map/ppermute | solution.py:269
  8.9 2.8 %collective-permute-done.1.refs_1_ = bf16[2,144,128]{2,1,0:T(8,128)(2,1)S(1)} collective-permute-done((bf16[2,144,128]{2,1,0:T(8,128)(2,1)S(1)}, bf16[2,144,128]{2,1,0:T(8,128)(2,1)S(1)}, u32[]{:S(2)}, u32[]{:S(2)}) %collective-permute-start.1) | collective-permute-done | bytes 73760 | tf_op jit(solution)/shard_map/ppermute | solution.py:269
  11.7 1.0 %own_block.1 = (f32[64,512]{1,0:T(8,128)S(1)}, f32[64,512]{1,0:T(8,128)S(1)}, f32[4,8,2,8,128]{4,3,2,1,0:T(8,128)S(1)}, f32[4,128,128]{2,1,0:T(8,128)S(1)}) custom-call(bf16[2,1024,512]{2,1,0:T(8,128)(2,1)S(1)} %get-tuple-element.21.table, f32[2,8,128]{2,1,0:T(8,128)S(1)} %get-tuple-element.22.phase, bf16[4,144,128]{2,1,0:T(8,128)(2,1)S(1)} %join.4.mine_ref), custom_call_target="tpu_custom_call" | custom-call | flops 2147483648 | tf_op jit(solution)/shard_map/own_block/pallas_call | solution.py:305
  12.8 0.1 collective-permute-start.2
  12.8 2.5 %collective-permute-start.3 = (bf16[2,144,128]{2,1,0:T(8,128)(2,1)S(1)}, bf16[2,144,128]{2,1,0:T(8,128)(2,1)S(1)}, u32[]{:S(2)}, u32[]{:S(2)}) collective-permute-start(bf16[2,144,128]{2,1,0:T(8,128)(2,1)S(1)} %join.3.refs_0_), channel_id=1, source_target_pairs={{6,0},{4,2},{2,4},{0,6},{14,8},{12,10},{10,12},{8,14},{7,1},{5,3},... | collective-permute-start | bytes 221192 | tf_op jit(solution)/shard_map/ppermute | solution.py:269
  15.4 0.5 %collective-permute-start.4 = (bf16[2,144,128]{2,1,0:T(8,128)(2,1)S(1)}, bf16[2,144,128]{2,1,0:T(8,128)(2,1)S(1)}, u32[]{:S(2)}, u32[]{:S(2)}) collective-permute-start(bf16[2,144,128]{2,1,0:T(8,128)(2,1)S(1)} %join.3.refs_0_), channel_id=1, source_target_pairs={{2,0},{0,2},{3,1},{1,3},{6,4},{4,6},{7,5},{5,7},{10,8},{8,10},{11,... | collective-permute-start | bytes 221192 | tf_op jit(solution)/shard_map/ppermute | solution.py:269
  15.9 0.0 collective-permute-done.2.got_ref
  15.9 0.1 combine.1.own_ref
  16.0 2.5 %collective-permute-done.3.refs_1_ = bf16[2,144,128]{2,1,0:T(8,128)(2,1)S(1)} collective-permute-done((bf16[2,144,128]{2,1,0:T(8,128)(2,1)S(1)}, bf16[2,144,128]{2,1,0:T(8,128)(2,1)S(1)}, u32[]{:S(2)}, u32[]{:S(2)}) %collective-permute-start.3) | collective-permute-done | bytes 73760 | tf_op jit(solution)/shard_map/ppermute | solution.py:269
  18.5 1.5 %collective-permute-done.4.refs_0_ = bf16[2,144,128]{2,1,0:T(8,128)(2,1)S(1)} collective-permute-done((bf16[2,144,128]{2,1,0:T(8,128)(2,1)S(1)}, bf16[2,144,128]{2,1,0:T(8,128)(2,1)S(1)}, u32[]{:S(2)}, u32[]{:S(2)}) %collective-permute-start.4) | collective-permute-done | bytes 73760 | tf_op jit(solution)/shard_map/ppermute | solution.py:269
  20.0 0.9 %other_block.1 = (f32[64,512]{1,0:T(8,128)S(1)}, f32[64,512]{1,0:T(8,128)S(1)}) custom-call(bf16[2,1024,512]{2,1,0:T(8,128)(2,1)S(1)} %get-tuple-element.21.table, f32[4,128,128]{2,1,0:T(8,128)S(1)} %get-tuple-element.27.wide_ref, f32[4,8,2,8,128]{4,3,2,1,0:T(8,128)S(1)} %get-tuple-element.28.local_ref, bf16[4,144,128]{2,1,0:T(8,128)(2,1)S(1)} %join.5.sources_ref), custom_call_target="tpu_custom_call" | custom-call | flops 2147483648 | tf_op jit(solution)/shard_map/other_block/pallas_call | solution.py:305
  21.0 0.1 collective-permute-start.5
  21.0 1.3 %collective-permute-done.5.got_ref = f32[64,512]{1,0:T(8,128)S(1)} collective-permute-done((f32[64,512]{1,0:T(8,128)S(1)}, f32[64,512]{1,0:T(8,128)S(1)}, u32[]{:S(2)}, u32[]{:S(2)}) %collective-permute-start.5) | collective-permute-done | bytes 131104 | tf_op jit(solution)/shard_map/ppermute | solution.py:269
  22.4 0.9 %place.1 = f32[3,64,512]{2,1,0:T(8,128)} custom-call(f32[3,8,128]{2,1,0:T(8,128)S(1)} %get-tuple-element.19.mask_ref, f32[64,512]{1,0:T(8,128)S(1)} %combine.1.own_ref, f32[64,512]{1,0:T(8,128)S(1)} %get-tuple-element.31.kept_ref, f32[64,512]{1,0:T(8,128)S(1)} %collective-permute-done.5.got_ref), custom_call_target="tpu_custom_call" | custom-call | tf_op jit(solution)/shard_map/place/pallas_call | solution.py:305
  (3 shorter events, 0.0 us)
Async XLA Ops:
  0.9 6.4 %collective-permute-start = (bf16[1,144,128]{2,1,0:T(8,128)(2,1)S(1)}, bf16[1,144,128]{2,1,0:T(8,128)(2,1)S(1)}, u32[]{:S(2)}, u32[]{:S(2)}) collective-permute-start(bf16[1,144,128]{2,1,0:T(8,128)(2,1)S(1)} %prepare.1.refs_0_), channel_id=1, source_target_pairs={{8,0},{12,4},{0,8},{4,12},{9,1},{13,5},{1,9},{5,13},{10,2},{14,6},... | collective-permute-start | bytes 110600 | tf_op jit(solution)/shard_map/ppermute | solution.py:269
  7.4 4.4 %collective-permute-start.1 = (bf16[2,144,128]{2,1,0:T(8,128)(2,1)S(1)}, bf16[2,144,128]{2,1,0:T(8,128)(2,1)S(1)}, u32[]{:S(2)}, u32[]{:S(2)}) collective-permute-start(bf16[2,144,128]{2,1,0:T(8,128)(2,1)S(1)} %join.3.refs_0_), channel_id=1, source_target_pairs={{4,0},{0,4},{12,8},{8,12},{5,1},{1,5},{13,9},{9,13},{6,2},{2,6},{1... | collective-permute-start | bytes 221192 | tf_op jit(solution)/shard_map/ppermute | solution.py:269
  12.8 3.1 %collective-permute-start.2 = (f32[64,512]{1,0:T(8,128)S(1)}, f32[64,512]{1,0:T(8,128)S(1)}, u32[]{:S(2)}, u32[]{:S(2)}) collective-permute-start(f32[64,512]{1,0:T(8,128)S(1)} %get-tuple-element.25), channel_id=1, source_target_pairs={{1,0},{0,1},{3,2},{2,3},{5,4},{4,5},{7,6},{6,7},{9,8},{8,9},{11,10... | collective-permute-start | bytes 393224 | tf_op jit(solution)/shard_map/ppermute | solution.py:269
  12.8 5.6 %collective-permute-start.3 = (bf16[2,144,128]{2,1,0:T(8,128)(2,1)S(1)}, bf16[2,144,128]{2,1,0:T(8,128)(2,1)S(1)}, u32[]{:S(2)}, u32[]{:S(2)}) collective-permute-start(bf16[2,144,128]{2,1,0:T(8,128)(2,1)S(1)} %join.3.refs_0_), channel_id=1, source_target_pairs={{6,0},{4,2},{2,4},{0,6},{14,8},{12,10},{10,12},{8,14},{7,1},{5,3},... | collective-permute-start | bytes 221192 | tf_op jit(solution)/shard_map/ppermute | solution.py:269
  15.4 4.7 %collective-permute-start.4 = (bf16[2,144,128]{2,1,0:T(8,128)(2,1)S(1)}, bf16[2,144,128]{2,1,0:T(8,128)(2,1)S(1)}, u32[]{:S(2)}, u32[]{:S(2)}) collective-permute-start(bf16[2,144,128]{2,1,0:T(8,128)(2,1)S(1)} %join.3.refs_0_), channel_id=1, source_target_pairs={{2,0},{0,2},{3,1},{1,3},{6,4},{4,6},{7,5},{5,7},{10,8},{8,10},{11,... | collective-permute-start | bytes 221192 | tf_op jit(solution)/shard_map/ppermute | solution.py:269
  21.0 1.4 %collective-permute-start.5 = (f32[64,512]{1,0:T(8,128)S(1)}, f32[64,512]{1,0:T(8,128)S(1)}, u32[]{:S(2)}, u32[]{:S(2)}) collective-permute-start(f32[64,512]{1,0:T(8,128)S(1)} %get-tuple-element.32), channel_id=1, source_target_pairs={{1,0},{0,1},{3,2},{2,3},{5,4},{4,5},{7,6},{6,7},{9,8},{8,9},{11,10... | collective-permute-start | bytes 393224 | tf_op jit(solution)/shard_map/ppermute | solution.py:269

commit v15 on v14

--- a/solution.py
+++ b/solution.py
@@ -123,10 +123,11 @@
             at = pl.ds(pair * 8 if isinstance(pair, int) else pl.multiple_of(pair * 8, 8), 8)
             real_sum = imag_sum = None
             for n in range(segments):
-                weight = jnp.broadcast_to(weight_of(n, pair), (8, LANES))
-                real_src = tiles[n][:8] * weight
-                imag_src = tiles[n][8:] * weight
-                real_loc, imag_loc = local_of(n, j)
+                real_src, imag_src = tiles[n][:8], tiles[n][8:]
+                if weight_of is not None:
+                    weight = jnp.broadcast_to(weight_of(n, pair), (8, LANES))
+                    real_src, imag_src = real_src * weight, imag_src * weight
+                real_loc, imag_loc = local_of(n, a, j)
                 real_term = real_src * real_loc + imag_src * imag_loc
                 imag_term = imag_src * real_loc - real_src * imag_loc
                 real_sum = real_term if real_sum is None else real_sum + real_term
@@ -165,10 +166,14 @@
     add_products(
         stations, count * stations, seg, source_tile(sources_ref, 0, seg, stations),
         lambda n, pair: wide[n, pl.ds(first_block * pairs + pair, 1), :],
-        lambda n, j: (local[n, j, 0], local[n, j, 1]),
+        lambda n, a, j: (local[n, j, 0], local[n, j, 1]),
         real_x, imag_x,
     )
-    pack(count * pairs, bands, real_x, imag_x, packed)
+    both_sums(sizes, count * pairs, table, kept_ref, sent_ref, real_x, imag_x, packed)
+
+
+def both_sums(sizes, rows, table, kept_ref, sent_ref, real_x, imag_x, packed):
+    pack(rows, sizes[1], real_x, imag_x, packed)
     dot = functools.partial(jnp.dot, preferred_element_type=jnp.float32)
     even, odd = dot(packed[0], table[0]), dot(packed[1], table[1])
     before = lax.axis_index("pol") == 0
@@ -199,8 +204,26 @@
     block_sums(sizes, 0, 1, table, wide_ref, local_ref, mine_ref, kept_ref, sent_ref, *scratch)
 
 
-def other_block_kernel(sizes, table, wide_ref, local_ref, sources_ref, kept_ref, sent_ref, *scratch):
-    block_sums(sizes, 1, 1, table, wide_ref, local_ref, sources_ref, kept_ref, sent_ref, *scratch)
+def weigh_kernel(sizes, wide_ref, local_ref, weighted_ref):
+    stations, bands, seg = sizes[:3]
+    for a in range(stations):
+        for j in range(stations):
+            pair = stations * stations + a * stations + j
+            for g in range(seg):
+                weight = jnp.broadcast_to(wide_ref[g, pl.ds(pair, 1), :], (bands, LANES))
+                weighted_ref[a, j, g, 0] = local_ref[g, j, 0] * weight
+                weighted_ref[a, j, g, 1] = local_ref[g, j, 1] * weight
+
+
+def other_block_kernel(sizes, table, weighted_ref, sources_ref, kept_ref, sent_ref, *scratch):
+    stations, bands, seg = sizes[:3]
+    add_products(
+        stations, stations, seg, source_tile(sources_ref, 0, seg, stations),
+        None,
+        lambda n, a, j: (weighted_ref[a, j, n, 0], weighted_ref[a, j, n, 1]),
+        *scratch[:2],
+    )
+    both_sums(sizes, stations * stations, table, kept_ref, sent_ref, *scratch)
 
 
 def combine_kernel(sizes, kept_ref, got_ref, lags_ref):
@@ -220,7 +243,8 @@
         copy.wait()
 
 
-def fetch_kernel(sizes, table_hbm, plan_any, table_ref, phase_ref, mask_ref, plan_ref, sems):
+def fetch_kernel(sizes, table_hbm, plan_any, after, table_ref, phase_ref, mask_ref, plan_ref, sems):
+    del after
     copies = [
         pltpu.make_async_copy(table_hbm.at[lax.axis_index("pol")], table_ref, sems.at[0]),
         pltpu.make_async_copy(plan_any, plan_ref, sems.at[1]),
@@ -277,7 +301,7 @@
     seg, sta, pol = (lax.axis_size(name) for name in ("seg", "sta", "pol"))
     _, stations, _, bins = raw_spectra.shape
     bands = bins // BAND
-    fast = sta == 2 and pol == 2 and seg > 1
+    fast = sta == 2 and pol == 2 and seg == 4
     blocks = 2 if fast else STEPS
     pairs = stations * stations
     lags = table.shape[3]
@@ -315,18 +339,20 @@
 
     f32 = jnp.float32
     table_const, plan_const = in_hbm(table), in_hbm(owner_plan)
-    table, phase, mask = call(
-        fetch_kernel,
-        [
-            pltpu.VMEM(table.shape[1:], table.dtype),
-            pltpu.VMEM((2, bands, LANES), f32),
-            pltpu.VMEM((STEPS, 8, LANES), f32),
-        ],
-        table_const, plan_const,
-        scratch=[pltpu.SMEM((STEPS,), jnp.int32), pltpu.SemaphoreType.DMA((2,))],
-        moved=4 * table.size // pol,
-        name="fetch",
-    )
+
+    def fetch(after):
+        return call(
+            fetch_kernel,
+            [
+                pltpu.VMEM(table.shape[1:], table.dtype),
+                pltpu.VMEM((2, bands, LANES), f32),
+                pltpu.VMEM((STEPS, 8, LANES), f32),
+            ],
+            table_const, plan_const, after,
+            scratch=[pltpu.SMEM((STEPS,), jnp.int32), pltpu.SemaphoreType.DMA((2,))],
+            moved=4 * table.size // pol,
+            name="fetch",
+        )
 
     def products(count):
         return [pltpu.VMEM((count * pairs * 8, LANES), f32)] * 2 + [pltpu.VMEM((2, count * pairs, bins), jnp.bfloat16)]
@@ -337,27 +363,31 @@
     sums_shapes = [pltpu.VMEM((pairs, lags), f32)] * 2
 
     if fast:
-        far, distance = own, seg // 2
-        while distance > 1:
-            far = join(far, exchange(far, "seg", distance))
-            distance //= 2
+        far = join(own, exchange(own, "seg", 2))
+        table, phase, mask = fetch(own)
         far, table = lax.optimization_barrier((far, table))
+        bare = join(far, rows=rows - 16)
         near = exchange(far, "seg", 1)
-        across = fetch_from(far, ("seg", "sta"), lambda z, x: (z ^ 1, x ^ 1))
-        partner = exchange(far, "sta", 1)
+        across = fetch_from(bare, ("seg", "sta"), lambda z, x: (z ^ 1, x ^ 1))
+        partner = exchange(bare, "sta", 1)
         mine = join(far, near)
         own_kept, own_sent, local, wide = call(
             own_block_kernel, sums_shapes + [local_shape, wide_shape],
             table, phase, mine,
-            scratch=products(1), flops=quarter, name="own_block",
-        )
-        own_lags = call(
-            combine_kernel, pltpu.VMEM((pairs, lags), f32), own_kept, exchange(own_sent, "pol", 1), name="combine"
-        )
+            scratch=products(1), flops=8 * quarter, name="own_block",
+        )
+        weighted = call(
+            weigh_kernel, pltpu.VMEM((stations, stations, seg, 2, bands, LANES), f32),
+            wide, local,
+            flops=8 * quarter, name="weigh",
+        )
+        own_got = exchange(own_sent, "pol", 1)
+        own_got, weighted = lax.optimization_barrier((own_got, weighted))
+        own_lags = call(combine_kernel, pltpu.VMEM((pairs, lags), f32), own_kept, own_got, name="combine")
         own_lags, across, partner = lax.optimization_barrier((own_lags, across, partner))
         kept, sent = call(
             other_block_kernel, sums_shapes,
-            table, wide, local, join(partner, across),
+            table, weighted, join(partner, across),
             scratch=products(1), flops=quarter, name="other_block",
         )
         got = exchange(sent, "pol", 1)
@@ -375,6 +405,7 @@
             distance //= 2
         gathered = lax.all_gather(mine, "sta")
         sources = join(*(gathered[owner_plan[k]] for k in range(STEPS)))
+        table, phase, _ = fetch(mine)
         kept, sent = call(
             all_blocks_kernel, [pltpu.VMEM((blocks * pairs, lags), f32)] * 2,
             table, phase, mine, sources,

time: 23.5 us -> 18.2 us (0.77)
  waiting for transfers between devices: 8.9 us -> 4.56 us
  starting transfers between devices: 8.79 us -> 7.87 us
    ppermute x6, waiting for transfers between devices: 8.9 us -> 4.56 us  [fetch_from(): return lax.ppermute(value, axes, pairs)]
    ppermute x6, starting transfers between devices: 8.79 us -> 7.87 us  [fetch_from(): return lax.ppermute(value, axes, pairs)]
    pallas_call x5 -> x6, Pallas kernels: 4.57 us -> 4.56 us  [call(): pl.pallas_call(functools.partial(kernel, sizes), out_shape=out_shape, in_...]
  transfers between devices with their start and end apart: 6 -> 6, of which waited for: 5 -> 4; matrix products, arithmetic and copies ran while one was open for 0% -> 0% of each run, Pallas kernels for 7% -> 16%
where the time goes in v15:
time: 18.2 us; the launch traced here: 18 us
  starting transfers between devices  7.87 us (43%)
  Pallas kernels  5.51 us (30%)
  waiting for transfers between devices  4.56 us (25%)
    ppermute x6, starting transfers between devices, fetch_from(): return lax.ppermute(value, axes, pairs)  7.87 us
    pallas_call x6, Pallas kernels, call(): pl.pallas_call(functools.partial(kernel, sizes), out_shape=out_shape, in_...  4.56 us
    ppermute x6, waiting for transfers between devices, fetch_from(): return lax.ppermute(value, axes, pairs)  4.56 us
    pallas_call x1, Pallas kernels, shards(): pl.pallas_call(functools.partial(prepare_kernel, (stations, bands, sta, b...  0.91 us
  transfers between devices with their start and end apart: 6, of which 4 were waited for; matrix products, arithmetic and copies ran while one was open for 0% of the time, Pallas kernels for 16%

profile of v15, /device:TPU:0, one launch (start us, length us, event | category | flops | bytes accessed | tf_op | source)
XLA Modules:
  0.0 18.0 jit_solution(17519161121961442682)
XLA Ops:
  0.0 0.9 %prepare.1.after.refs_0_ = bf16[1,144,128]{2,1,0:T(8,128)(2,1)S(1)} custom-call(bf16[128,128]{1,0:T(8,128)(2,1)} %bitcast.9, s32[8,16]{1,0:T(8,128)} %bitcast.10, s32[1,16]{1,0:T(1,128)} %refs_2_.1), custom_call_target="tpu_custom_call" | custom-call | tf_op jit(solution)/shard_map/prepare/pallas_call | solution.py:317
  0.9 4.1 %collective-permute-start = (bf16[1,144,128]{2,1,0:T(8,128)(2,1)S(1)}, bf16[1,144,128]{2,1,0:T(8,128)(2,1)S(1)}, u32[]{:S(2)}, u32[]{:S(2)}) collective-permute-start(bf16[1,144,128]{2,1,0:T(8,128)(2,1)S(1)} %prepare.1.after.refs_0_), channel_id=1, source_target_pairs={{8,0},{12,4},{0,8},{4,12},{9,1},{13,5},{1,9},{5,13},{10,2},{14,6},... | collective-permute-start | bytes 110600 | tf_op jit(solution)/shard_map/ppermute | solution.py:293
  5.0 1.6 %fetch.1 = (bf16[2,1024,512]{2,1,0:T(8,128)(2,1)S(1)}, f32[2,8,128]{2,1,0:T(8,128)S(1)}, f32[3,8,128]{2,1,0:T(8,128)S(1)}) custom-call(bf16[2,2,1024,512]{3,2,1,0:T(8,128)(2,1)} %constant.2.clone.table_hbm, s32[3]{0:T(128)} %plan_any.1, bf16[1,144,128]{2,1,0:T(8,128)(2,1)S(1)} %prepare.1.after.refs_0_), custom_call_target="tpu_custom_call" | custom-call | bytes 4194304 | tf_op jit(solution)/shard_map/fetch/pallas_call | solution.py:329
  6.6 0.7 %collective-permute-done.refs_1_ = bf16[1,144,128]{2,1,0:T(8,128)(2,1)S(1)} collective-permute-done((bf16[1,144,128]{2,1,0:T(8,128)(2,1)S(1)}, bf16[1,144,128]{2,1,0:T(8,128)(2,1)S(1)}, u32[]{:S(2)}, u32[]{:S(2)}) %collective-permute-start) | collective-permute-done | bytes 36896 | tf_op jit(solution)/shard_map/ppermute | solution.py:293
  7.4 1.5 %collective-permute-start.1 = (bf16[2,144,128]{2,1,0:T(8,128)(2,1)S(1)}, bf16[2,144,128]{2,1,0:T(8,128)(2,1)S(1)}, u32[]{:S(2)}, u32[]{:S(2)}) collective-permute-start(bf16[2,144,128]{2,1,0:T(8,128)(2,1)S(1)} %join.4.refs_0_), channel_id=1, source_target_pairs={{4,0},{0,4},{12,8},{8,12},{5,1},{1,5},{13,9},{9,13},{6,2},{2,6},{1... | collective-permute-start | bytes 221192 | tf_op jit(solution)/shard_map/ppermute | solution.py:293
  8.9 1.6 %collective-permute-start.3 = (bf16[2,128,128]{2,1,0:T(8,128)(2,1)S(1)}, bf16[2,128,128]{2,1,0:T(8,128)(2,1)S(1)}, u32[]{:S(2)}, u32[]{:S(2)}) collective-permute-start(bf16[2,128,128]{2,1,0:T(8,128)(2,1)S(1)} %join.6), channel_id=1, source_target_pairs={{6,0},{4,2},{2,4},{0,6},{14,8},{12,10},{10,12},{8,14},{7,1},{5,3},... | collective-permute-start | bytes 196616 | tf_op jit(solution)/shard_map/ppermute | solution.py:293
  10.5 0.3 %collective-permute-start.4 = (bf16[2,128,128]{2,1,0:T(8,128)(2,1)S(1)}, bf16[2,128,128]{2,1,0:T(8,128)(2,1)S(1)}, u32[]{:S(2)}, u32[]{:S(2)}) collective-permute-start(bf16[2,128,128]{2,1,0:T(8,128)(2,1)S(1)} %join.6), channel_id=1, source_target_pairs={{2,0},{0,2},{3,1},{1,3},{6,4},{4,6},{7,5},{5,7},{10,8},{8,10},{11,... | collective-permute-start | bytes 196616 | tf_op jit(solution)/shard_map/ppermute | solution.py:293
  10.9 1.5 %collective-permute-done.1.refs_1_ = bf16[2,144,128]{2,1,0:T(8,128)(2,1)S(1)} collective-permute-done((bf16[2,144,128]{2,1,0:T(8,128)(2,1)S(1)}, bf16[2,144,128]{2,1,0:T(8,128)(2,1)S(1)}, u32[]{:S(2)}, u32[]{:S(2)}) %collective-permute-start.1) | collective-permute-done | bytes 73760 | tf_op jit(solution)/shard_map/ppermute | solution.py:293
  12.3 1.0 %own_block.1 = (f32[64,512]{1,0:T(8,128)S(1)}, f32[64,512]{1,0:T(8,128)S(1)}, f32[4,8,2,8,128]{4,3,2,1,0:T(8,128)S(1)}, f32[4,128,128]{2,1,0:T(8,128)S(1)}) custom-call(bf16[2,1024,512]{2,1,0:T(8,128)(2,1)S(1)} %get-tuple-element.23.table, f32[2,8,128]{2,1,0:T(8,128)S(1)} %get-tuple-element.24.phase, bf16[4,144,128]{2,1,0:T(8,128)(2,1)S(1)} %join.5.mine_ref), custom_call_target="tpu_custom_call" | custom-call | flops 17179869184 | tf_op jit(solution)/shard_map/own_block/pallas_call | solution.py:329
  13.4 0.1 collective-permute-start.2
  13.5 0.2 weigh.1.weighted_ref
  13.6 1.2 %collective-permute-done.2.got_ref = f32[64,512]{1,0:T(8,128)S(1)} collective-permute-done((f32[64,512]{1,0:T(8,128)S(1)}, f32[64,512]{1,0:T(8,128)S(1)}, u32[]{:S(2)}, u32[]{:S(2)}) %collective-permute-start.2) | collective-permute-done | bytes 131104 | tf_op jit(solution)/shard_map/ppermute | solution.py:293
  14.8 0.1 combine.1.own_ref
  14.9 0.0 collective-permute-done.3.refs_1_
  14.9 0.0 collective-permute-done.4.refs_0_
  14.9 0.8 %other_block.1 = (f32[64,512]{1,0:T(8,128)S(1)}, f32[64,512]{1,0:T(8,128)S(1)}) custom-call(bf16[2,1024,512]{2,1,0:T(8,128)(2,1)S(1)} %get-tuple-element.23.table, f32[8,8,4,2,8,128]{5,4,3,2,1,0:T(8,128)S(1)} %weigh.1.weighted_ref, bf16[4,128,128]{2,1,0:T(8,128)(2,1)S(1)} %join.7.sources_ref), custom_call_target="tpu_custom_call" | custom-call | flops 2147483648 | tf_op jit(solution)/shard_map/other_block/pallas_call | solution.py:329
  15.7 0.2 %collective-permute-start.5 = (f32[64,512]{1,0:T(8,128)S(1)}, f32[64,512]{1,0:T(8,128)S(1)}, u32[]{:S(2)}, u32[]{:S(2)}) collective-permute-start(f32[64,512]{1,0:T(8,128)S(1)} %get-tuple-element.36), channel_id=1, source_target_pairs={{1,0},{0,1},{3,2},{2,3},{5,4},{4,5},{7,6},{6,7},{9,8},{8,9},{11,10... | collective-permute-start | bytes 393224 | tf_op jit(solution)/shard_map/ppermute | solution.py:293
  15.9 1.2 %collective-permute-done.5.got_ref = f32[64,512]{1,0:T(8,128)S(1)} collective-permute-done((f32[64,512]{1,0:T(8,128)S(1)}, f32[64,512]{1,0:T(8,128)S(1)}, u32[]{:S(2)}, u32[]{:S(2)}) %collective-permute-start.5) | collective-permute-done | bytes 131104 | tf_op jit(solution)/shard_map/ppermute | solution.py:293
  17.1 0.9 %place.1 = f32[3,64,512]{2,1,0:T(8,128)} custom-call(f32[3,8,128]{2,1,0:T(8,128)S(1)} %get-tuple-element.21.mask_ref, f32[64,512]{1,0:T(8,128)S(1)} %combine.1.own_ref, f32[64,512]{1,0:T(8,128)S(1)} %get-tuple-element.35.kept_ref, f32[64,512]{1,0:T(8,128)S(1)} %collective-permute-done.5.got_ref), custom_call_target="tpu_custom_call" | custom-call | tf_op jit(solution)/shard_map/place/pallas_call | solution.py:329
  (4 shorter events, 0.0 us)
Async XLA Ops:
  0.9 6.4 %collective-permute-start = (bf16[1,144,128]{2,1,0:T(8,128)(2,1)S(1)}, bf16[1,144,128]{2,1,0:T(8,128)(2,1)S(1)}, u32[]{:S(2)}, u32[]{:S(2)}) collective-permute-start(bf16[1,144,128]{2,1,0:T(8,128)(2,1)S(1)} %prepare.1.after.refs_0_), channel_id=1, source_target_pairs={{8,0},{12,4},{0,8},{4,12},{9,1},{13,5},{1,9},{5,13},{10,2},{14,6},... | collective-permute-start | bytes 110600 | tf_op jit(solution)/shard_map/ppermute | solution.py:293
  7.4 5.0 %collective-permute-start.1 = (bf16[2,144,128]{2,1,0:T(8,128)(2,1)S(1)}, bf16[2,144,128]{2,1,0:T(8,128)(2,1)S(1)}, u32[]{:S(2)}, u32[]{:S(2)}) collective-permute-start(bf16[2,144,128]{2,1,0:T(8,128)(2,1)S(1)} %join.4.refs_0_), channel_id=1, source_target_pairs={{4,0},{0,4},{12,8},{8,12},{5,1},{1,5},{13,9},{9,13},{6,2},{2,6},{1... | collective-permute-start | bytes 221192 | tf_op jit(solution)/shard_map/ppermute | solution.py:293
  8.9 6.0 %collective-permute-start.3 = (bf16[2,128,128]{2,1,0:T(8,128)(2,1)S(1)}, bf16[2,128,128]{2,1,0:T(8,128)(2,1)S(1)}, u32[]{:S(2)}, u32[]{:S(2)}) collective-permute-start(bf16[2,128,128]{2,1,0:T(8,128)(2,1)S(1)} %join.6), channel_id=1, source_target_pairs={{6,0},{4,2},{2,4},{0,6},{14,8},{12,10},{10,12},{8,14},{7,1},{5,3},... | collective-permute-start | bytes 196616 | tf_op jit(solution)/shard_map/ppermute | solution.py:293
  10.5 4.4 %collective-permute-start.4 = (bf16[2,128,128]{2,1,0:T(8,128)(2,1)S(1)}, bf16[2,128,128]{2,1,0:T(8,128)(2,1)S(1)}, u32[]{:S(2)}, u32[]{:S(2)}) collective-permute-start(bf16[2,128,128]{2,1,0:T(8,128)(2,1)S(1)} %join.6), channel_id=1, source_target_pairs={{2,0},{0,2},{3,1},{1,3},{6,4},{4,6},{7,5},{5,7},{10,8},{8,10},{11,... | collective-permute-start | bytes 196616 | tf_op jit(solution)/shard_map/ppermute | solution.py:293
  13.4 1.4 %collective-permute-start.2 = (f32[64,512]{1,0:T(8,128)S(1)}, f32[64,512]{1,0:T(8,128)S(1)}, u32[]{:S(2)}, u32[]{:S(2)}) collective-permute-start(f32[64,512]{1,0:T(8,128)S(1)} %get-tuple-element.27), channel_id=1, source_target_pairs={{1,0},{0,1},{3,2},{2,3},{5,4},{4,5},{7,6},{6,7},{9,8},{8,9},{11,10... | collective-permute-start | bytes 393224 | tf_op jit(solution)/shard_map/ppermute | solution.py:293
  15.7 1.4 %collective-permute-start.5 = (f32[64,512]{1,0:T(8,128)S(1)}, f32[64,512]{1,0:T(8,128)S(1)}, u32[]{:S(2)}, u32[]{:S(2)}) collective-permute-start(f32[64,512]{1,0:T(8,128)S(1)} %get-tuple-element.36), channel_id=1, source_target_pairs={{1,0},{0,1},{3,2},{2,3},{5,4},{4,5},{7,6},{6,7},{9,8},{8,9},{11,10... | collective-permute-start | bytes 393224 | tf_op jit(solution)/shard_map/ppermute | solution.py:293

commit v16 on v15

--- a/solution.py
+++ b/solution.py
@@ -172,36 +172,50 @@
     both_sums(sizes, count * pairs, table, kept_ref, sent_ref, real_x, imag_x, packed)
 
 
-def both_sums(sizes, rows, table, kept_ref, sent_ref, real_x, imag_x, packed):
+def both_sums(sizes, rows, table, real_x, imag_x, packed):
     pack(rows, sizes[1], real_x, imag_x, packed)
     dot = functools.partial(jnp.dot, preferred_element_type=jnp.float32)
     even, odd = dot(packed[0], table[0]), dot(packed[1], table[1])
-    before = lax.axis_index("pol") == 0
-    odd = jnp.where(before, odd, -odd)
-    kept_ref[...] = even + odd
-    sent_ref[...] = even - odd
-
-
-def in_order(sizes, sums):
-    before = lax.axis_index("pol") == 0
-    lane = lax.broadcasted_iota(jnp.int32, (sums.shape[0], LANES), 1)
-    index = jnp.where(before, LANES - 1 - lane, lane)
-    runs = [sums[:, at : at + LANES] for at in range(0, sums.shape[1], LANES)]
-    runs = [jnp.where(before, back, run) for run, back in zip(runs, runs[::-1])]
+    return even + odd, even - odd
+
+
+def turned_round(sums):
+    index = LANES - 1 - lax.broadcasted_iota(jnp.int32, (sums.shape[0], LANES), 1)
+    runs = [sums[:, at : at + LANES] for at in reversed(range(0, sums.shape[1], LANES))]
     runs = [jnp.take_along_axis(run, index, axis=1, mode="promise_in_bounds") for run in runs]
     return jnp.concatenate(runs, axis=1)
+
+
+def block_sums(sizes, first_block, count, table, wide, local, sources_ref, real_x, imag_x, packed):
+    stations, bands, seg = sizes[:3]
+    pairs = stations * stations
+    add_products(
+        stations, count * stations, seg, source_tile(sources_ref, 0, seg, stations),
+        lambda n, pair: wide[n, pl.ds(first_block * pairs + pair, 1), :],
+        lambda n, a, j: (local[n, j, 0], local[n, j, 1]),
+        real_x, imag_x,
+    )
+    return both_sums(sizes, count * pairs, table, real_x, imag_x, packed)
+
+
+def keep_and_send(before, after, kept_ref, sent_ref):
+    first_core = lax.axis_index("pol") == 0
+    kept_ref[...] = jnp.where(first_core, before, after)
+    sent_ref[...] = jnp.where(first_core, after, before).astype(sent_ref.dtype)
 
 
 def all_blocks_kernel(sizes, table, phase, mine_ref, sources_ref, kept_ref, sent_ref, local, wide, *scratch):
     spread_weights(sizes, mine_ref, wide)
     turn_locals(sizes, phase[0], phase[1], mine_ref, local)
-    block_sums(sizes, 0, sizes[5], table, wide, local, sources_ref, kept_ref, sent_ref, *scratch)
+    before, after = block_sums(sizes, 0, sizes[5], table, wide, local, sources_ref, *scratch)
+    keep_and_send(turned_round(before), after, kept_ref, sent_ref)
 
 
 def own_block_kernel(sizes, table, phase, mine_ref, kept_ref, sent_ref, local_ref, wide_ref, *scratch):
     spread_weights(sizes, mine_ref, wide_ref)
     turn_locals(sizes, phase[0], phase[1], mine_ref, local_ref)
-    block_sums(sizes, 0, 1, table, wide_ref, local_ref, mine_ref, kept_ref, sent_ref, *scratch)
+    before, after = block_sums(sizes, 0, 1, table, wide_ref, local_ref, mine_ref, *scratch)
+    keep_and_send(turned_round(before), after, kept_ref, sent_ref)
 
 
 def weigh_kernel(sizes, wide_ref, local_ref, weighted_ref):
@@ -215,24 +229,43 @@
                 weighted_ref[a, j, g, 1] = local_ref[g, j, 1] * weight
 
 
-def other_block_kernel(sizes, table, weighted_ref, sources_ref, kept_ref, sent_ref, *scratch):
+def other_block_kernel(sizes, table, weighted_ref, own_sent_ref, sources_ref, kept_ref, sent_ref, *scratch):
     stations, bands, seg = sizes[:3]
+    pairs = stations * stations
     add_products(
         stations, stations, seg, source_tile(sources_ref, 0, seg, stations),
         None,
         lambda n, a, j: (weighted_ref[a, j, n, 0], weighted_ref[a, j, n, 1]),
         *scratch[:2],
     )
-    both_sums(sizes, stations * stations, table, kept_ref, sent_ref, *scratch)
+    before, after = both_sums(sizes, pairs, table, *scratch)
+    sent_ref[pl.ds(0, pairs), :] = own_sent_ref[...]
+    first_core = lax.axis_index("pol") == 0
+
+    @pl.when(first_core)
+    def _():
+        kept_ref[...] = before
+        sent_ref[pl.ds(pairs, pairs), :] = after.astype(sent_ref.dtype)
+
+    @pl.when(jnp.logical_not(first_core))
+    def _():
+        kept_ref[...] = after
+        sent_ref[pl.ds(pairs, pairs), :] = turned_round(before).astype(sent_ref.dtype)
+
+
+def settle_kernel(sizes, kept_ref, settled_ref):
+    kept = kept_ref[...]
+    settled_ref[...] = jnp.where(lax.axis_index("pol") == 0, turned_round(kept), kept)
 
 
 def combine_kernel(sizes, kept_ref, got_ref, lags_ref):
-    lags_ref[...] = in_order(sizes, kept_ref[...] + got_ref[...])
-
-
-def place_kernel(sizes, mask_ref, own_ref, kept_ref, got_ref, out_ref, steps, sems):
-    other = in_order(sizes, kept_ref[...] + got_ref[...])
-    own = own_ref[...]
+    lags_ref[...] = kept_ref[...] + got_ref[...].astype(jnp.float32)
+
+
+def place_kernel(sizes, mask_ref, own_ref, other_ref, got_ref, out_ref, steps, sems):
+    pairs = sizes[0] * sizes[0]
+    own = own_ref[...] + got_ref[pl.ds(0, pairs), :].astype(jnp.float32)
+    other = other_ref[...] + got_ref[pl.ds(pairs, pairs), :].astype(jnp.float32)
     copies = []
     for step in range(STEPS):
         mask = jnp.broadcast_to(mask_ref[step, :1, :1], other.shape)
@@ -360,7 +393,7 @@
     quarter = 32 * pairs * 2 * bins * lags
     local_shape = pltpu.VMEM((seg, stations, 2, bands, LANES), f32)
     wide_shape = pltpu.VMEM((seg, blocks * pairs, LANES), f32)
-    sums_shapes = [pltpu.VMEM((pairs, lags), f32)] * 2
+    kept_shape = pltpu.VMEM((pairs, lags), f32)
 
     if fast:
         far = join(own, exchange(own, "seg", 2))
@@ -372,7 +405,7 @@
         partner = exchange(bare, "sta", 1)
         mine = join(far, near)
         own_kept, own_sent, local, wide = call(
-            own_block_kernel, sums_shapes + [local_shape, wide_shape],
+            own_block_kernel, [kept_shape, pltpu.VMEM((pairs, lags), jnp.bfloat16), local_shape, wide_shape],
             table, phase, mine,
             scratch=products(1), flops=8 * quarter, name="own_block",
         )
@@ -381,19 +414,17 @@
             wide, local,
             flops=8 * quarter, name="weigh",
         )
-        own_got = exchange(own_sent, "pol", 1)
-        own_got, weighted = lax.optimization_barrier((own_got, weighted))
-        own_lags = call(combine_kernel, pltpu.VMEM((pairs, lags), f32), own_kept, own_got, name="combine")
-        own_lags, across, partner = lax.optimization_barrier((own_lags, across, partner))
+        weighted, across, partner = lax.optimization_barrier((weighted, across, partner))
         kept, sent = call(
-            other_block_kernel, sums_shapes,
-            table, weighted, join(partner, across),
+            other_block_kernel, [kept_shape, pltpu.VMEM((2 * pairs, lags), jnp.bfloat16)],
+            table, weighted, own_sent, join(partner, across),
             scratch=products(1), flops=quarter, name="other_block",
         )
         got = exchange(sent, "pol", 1)
+        kept = call(settle_kernel, kept_shape, kept, flops=quarter, name="settle")
         result = call(
             place_kernel, jax.ShapeDtypeStruct((STEPS, pairs, lags), f32),
-            mask, own_lags, kept, got,
+            mask, own_kept, kept, got,
             out_specs=hbm,
             scratch=[pltpu.VMEM((STEPS, pairs, lags), f32), pltpu.SemaphoreType.DMA((STEPS,))],
             name="place",
@@ -407,7 +438,8 @@
         sources = join(*(gathered[owner_plan[k]] for k in range(STEPS)))
         table, phase, _ = fetch(mine)
         kept, sent = call(
-            all_blocks_kernel, [pltpu.VMEM((blocks * pairs, lags), f32)] * 2,
+            all_blocks_kernel,
+            [pltpu.VMEM((blocks * pairs, lags), f32), pltpu.VMEM((blocks * pairs, lags), jnp.bfloat16)],
             table, phase, mine, sources,
             scratch=[local_shape, wide_shape] + products(blocks), flops=blocks * quarter, name="all_blocks",
         )

time: 18.2 us -> 18 us (0.989)
  starting transfers between devices: 7.87 us -> 7.66 us
    ppermute x6 -> x5, starting transfers between devices: 7.87 us -> 7.66 us  [fetch_from(): return lax.ppermute(value, axes, pairs)]
    ppermute x6 -> x5, waiting for transfers between devices: 4.56 us -> 4.58 us  [fetch_from(): return lax.ppermute(value, axes, pairs)]
  transfers between devices with their start and end apart: 6 -> 5, of which waited for: 4 -> 5; matrix products, arithmetic and copies ran while one was open for 0% -> 0% of each run, Pallas kernels for 16% -> 17%
where the time goes in v16:
time: 18 us; the launch traced here: 17.8 us
  starting transfers between devices  7.66 us (43%)
  Pallas kernels  5.48 us (30%)
  waiting for transfers between devices  4.58 us (25%)
    ppermute x5, starting transfers between devices, fetch_from(): return lax.ppermute(value, axes, pairs)  7.66 us
    ppermute x5, waiting for transfers between devices, fetch_from(): return lax.ppermute(value, axes, pairs)  4.58 us
    pallas_call x6, Pallas kernels, call(): pl.pallas_call(functools.partial(kernel, sizes), out_shape=out_shape, in_...  4.54 us
    pallas_call x1, Pallas kernels, shards(): pl.pallas_call(functools.partial(prepare_kernel, (stations, bands, sta, b...  0.91 us
  transfers between devices with their start and end apart: 5, of which 5 were waited for; matrix products, arithmetic and copies ran while one was open for 0% of the time, Pallas kernels for 17%

profile of v16, /device:TPU:0, one launch (start us, length us, event | category | flops | bytes accessed | tf_op | source)
XLA Modules:
  0.0 17.8 jit_solution(6487964785743872230)
XLA Ops:
  0.0 0.9 %prepare.1.after.refs_0_ = bf16[1,144,128]{2,1,0:T(8,128)(2,1)S(1)} custom-call(bf16[128,128]{1,0:T(8,128)(2,1)} %bitcast.9, s32[8,16]{1,0:T(8,128)} %bitcast.10, s32[1,16]{1,0:T(1,128)} %refs_2_.1), custom_call_target="tpu_custom_call" | custom-call | tf_op jit(solution)/shard_map/prepare/pallas_call | solution.py:350
  0.9 4.1 %collective-permute-start = (bf16[1,144,128]{2,1,0:T(8,128)(2,1)S(1)}, bf16[1,144,128]{2,1,0:T(8,128)(2,1)S(1)}, u32[]{:S(2)}, u32[]{:S(2)}) collective-permute-start(bf16[1,144,128]{2,1,0:T(8,128)(2,1)S(1)} %prepare.1.after.refs_0_), channel_id=1, source_target_pairs={{8,0},{12,4},{0,8},{4,12},{9,1},{13,5},{1,9},{5,13},{10,2},{14,6},... | collective-permute-start | bytes 110600 | tf_op jit(solution)/shard_map/ppermute | solution.py:326
  5.0 1.6 %fetch.1 = (bf16[2,1024,512]{2,1,0:T(8,128)(2,1)S(1)}, f32[2,8,128]{2,1,0:T(8,128)S(1)}, f32[3,8,128]{2,1,0:T(8,128)S(1)}) custom-call(bf16[2,2,1024,512]{3,2,1,0:T(8,128)(2,1)} %constant.2.clone.table_hbm, s32[3]{0:T(128)} %plan_any.1, bf16[1,144,128]{2,1,0:T(8,128)(2,1)S(1)} %prepare.1.after.refs_0_), custom_call_target="tpu_custom_call" | custom-call | bytes 4194304 | tf_op jit(solution)/shard_map/fetch/pallas_call | solution.py:362
  6.6 0.7 %collective-permute-done.refs_1_ = bf16[1,144,128]{2,1,0:T(8,128)(2,1)S(1)} collective-permute-done((bf16[1,144,128]{2,1,0:T(8,128)(2,1)S(1)}, bf16[1,144,128]{2,1,0:T(8,128)(2,1)S(1)}, u32[]{:S(2)}, u32[]{:S(2)}) %collective-permute-start) | collective-permute-done | bytes 36896 | tf_op jit(solution)/shard_map/ppermute | solution.py:326
  7.4 1.5 %collective-permute-start.1 = (bf16[2,144,128]{2,1,0:T(8,128)(2,1)S(1)}, bf16[2,144,128]{2,1,0:T(8,128)(2,1)S(1)}, u32[]{:S(2)}, u32[]{:S(2)}) collective-permute-start(bf16[2,144,128]{2,1,0:T(8,128)(2,1)S(1)} %join.4.refs_0_), channel_id=1, source_target_pairs={{4,0},{0,4},{12,8},{8,12},{5,1},{1,5},{13,9},{9,13},{6,2},{2,6},{1... | collective-permute-start | bytes 221192 | tf_op jit(solution)/shard_map/ppermute | solution.py:326
  8.9 1.6 %collective-permute-start.2 = (bf16[2,128,128]{2,1,0:T(8,128)(2,1)S(1)}, bf16[2,128,128]{2,1,0:T(8,128)(2,1)S(1)}, u32[]{:S(2)}, u32[]{:S(2)}) collective-permute-start(bf16[2,128,128]{2,1,0:T(8,128)(2,1)S(1)} %join.6), channel_id=1, source_target_pairs={{6,0},{4,2},{2,4},{0,6},{14,8},{12,10},{10,12},{8,14},{7,1},{5,3},... | collective-permute-start | bytes 196616 | tf_op jit(solution)/shard_map/ppermute | solution.py:326
  10.5 0.3 %collective-permute-start.3 = (bf16[2,128,128]{2,1,0:T(8,128)(2,1)S(1)}, bf16[2,128,128]{2,1,0:T(8,128)(2,1)S(1)}, u32[]{:S(2)}, u32[]{:S(2)}) collective-permute-start(bf16[2,128,128]{2,1,0:T(8,128)(2,1)S(1)} %join.6), channel_id=1, source_target_pairs={{2,0},{0,2},{3,1},{1,3},{6,4},{4,6},{7,5},{5,7},{10,8},{8,10},{11,... | collective-permute-start | bytes 196616 | tf_op jit(solution)/shard_map/ppermute | solution.py:326
  10.9 1.5 %collective-permute-done.1.refs_1_ = bf16[2,144,128]{2,1,0:T(8,128)(2,1)S(1)} collective-permute-done((bf16[2,144,128]{2,1,0:T(8,128)(2,1)S(1)}, bf16[2,144,128]{2,1,0:T(8,128)(2,1)S(1)}, u32[]{:S(2)}, u32[]{:S(2)}) %collective-permute-start.1) | collective-permute-done | bytes 73760 | tf_op jit(solution)/shard_map/ppermute | solution.py:326
  12.3 1.1 %own_block.1 = (f32[64,512]{1,0:T(8,128)S(1)}, bf16[64,512]{1,0:T(8,128)(2,1)S(1)}, f32[4,8,2,8,128]{4,3,2,1,0:T(8,128)S(1)}, f32[4,128,128]{2,1,0:T(8,128)S(1)}) custom-call(bf16[2,1024,512]{2,1,0:T(8,128)(2,1)S(1)} %get-tuple-element.21.table, f32[2,8,128]{2,1,0:T(8,128)S(1)} %get-tuple-element.22.phase, bf16[4,144,128]{2,1,0:T(8,128)(2,1)S(1)} %join.5.mine_ref), custom_call_target="tpu_custom_call" | custom-call | flops 17179869184 | tf_op jit(solution)/shard_map/own_block/pallas_call | solution.py:362
  13.5 0.2 weigh.1.weighted_ref
  13.6 0.4 %collective-permute-done.2.refs_1_ = bf16[2,128,128]{2,1,0:T(8,128)(2,1)S(1)} collective-permute-done((bf16[2,128,128]{2,1,0:T(8,128)(2,1)S(1)}, bf16[2,128,128]{2,1,0:T(8,128)(2,1)S(1)}, u32[]{:S(2)}, u32[]{:S(2)}) %collective-permute-start.2) | collective-permute-done | bytes 65568 | tf_op jit(solution)/shard_map/ppermute | solution.py:326
  14.0 0.8 %collective-permute-done.3.refs_0_ = bf16[2,128,128]{2,1,0:T(8,128)(2,1)S(1)} collective-permute-done((bf16[2,128,128]{2,1,0:T(8,128)(2,1)S(1)}, bf16[2,128,128]{2,1,0:T(8,128)(2,1)S(1)}, u32[]{:S(2)}, u32[]{:S(2)}) %collective-permute-start.3) | collective-permute-done | bytes 65568 | tf_op jit(solution)/shard_map/ppermute | solution.py:326
  14.8 0.7 %other_block.1 = (f32[64,512]{1,0:T(8,128)S(1)}, bf16[128,512]{1,0:T(8,128)(2,1)S(1)}) custom-call(bf16[2,1024,512]{2,1,0:T(8,128)(2,1)S(1)} %get-tuple-element.21.table, f32[8,8,4,2,8,128]{5,4,3,2,1,0:T(8,128)S(1)} %weigh.1.weighted_ref, bf16[64,512]{1,0:T(8,128)(2,1)S(1)} %get-tuple-element.28.own_sent_ref, bf16[4,128,128]{2,1,0:T(8,128)(2,1)S(1)} %join.7.sources_ref), custom_call_target="tpu_custom_call" | custom-call | flops 2147483648 | tf_op jit(solution)/shard_map/other_block/pallas_call | solution.py:362
  15.6 0.1 collective-permute-start.4
  15.6 0.1 settle.1.other_ref
  15.7 1.2 %collective-permute-done.4.got_ref = bf16[128,512]{1,0:T(8,128)(2,1)S(1)} collective-permute-done((bf16[128,512]{1,0:T(8,128)(2,1)S(1)}, bf16[128,512]{1,0:T(8,128)(2,1)S(1)}, u32[]{:S(2)}, u32[]{:S(2)}) %collective-permute-start.4) | collective-permute-done | bytes 131104 | tf_op jit(solution)/shard_map/ppermute | solution.py:326
  17.0 0.8 %place.1 = f32[3,64,512]{2,1,0:T(8,128)} custom-call(f32[3,8,128]{2,1,0:T(8,128)S(1)} %get-tuple-element.19.mask_ref, f32[64,512]{1,0:T(8,128)S(1)} %get-tuple-element.24.own_ref, f32[64,512]{1,0:T(8,128)S(1)} %settle.1.other_ref, bf16[128,512]{1,0:T(8,128)(2,1)S(1)} %collective-permute-done.4.got_ref), custom_call_target="tpu_custom_call" | custom-call | tf_op jit(solution)/shard_map/place/pallas_call | solution.py:362
  (4 shorter events, 0.0 us)
Async XLA Ops:
  0.9 6.4 %collective-permute-start = (bf16[1,144,128]{2,1,0:T(8,128)(2,1)S(1)}, bf16[1,144,128]{2,1,0:T(8,128)(2,1)S(1)}, u32[]{:S(2)}, u32[]{:S(2)}) collective-permute-start(bf16[1,144,128]{2,1,0:T(8,128)(2,1)S(1)} %prepare.1.after.refs_0_), channel_id=1, source_target_pairs={{8,0},{12,4},{0,8},{4,12},{9,1},{13,5},{1,9},{5,13},{10,2},{14,6},... | collective-permute-start | bytes 110600 | tf_op jit(solution)/shard_map/ppermute | solution.py:326
  7.4 5.0 %collective-permute-start.1 = (bf16[2,144,128]{2,1,0:T(8,128)(2,1)S(1)}, bf16[2,144,128]{2,1,0:T(8,128)(2,1)S(1)}, u32[]{:S(2)}, u32[]{:S(2)}) collective-permute-start(bf16[2,144,128]{2,1,0:T(8,128)(2,1)S(1)} %join.4.refs_0_), channel_id=1, source_target_pairs={{4,0},{0,4},{12,8},{8,12},{5,1},{1,5},{13,9},{9,13},{6,2},{2,6},{1... | collective-permute-start | bytes 221192 | tf_op jit(solution)/shard_map/ppermute | solution.py:326
  8.9 5.2 %collective-permute-start.2 = (bf16[2,128,128]{2,1,0:T(8,128)(2,1)S(1)}, bf16[2,128,128]{2,1,0:T(8,128)(2,1)S(1)}, u32[]{:S(2)}, u32[]{:S(2)}) collective-permute-start(bf16[2,128,128]{2,1,0:T(8,128)(2,1)S(1)} %join.6), channel_id=1, source_target_pairs={{6,0},{4,2},{2,4},{0,6},{14,8},{12,10},{10,12},{8,14},{7,1},{5,3},... | collective-permute-start | bytes 196616 | tf_op jit(solution)/shard_map/ppermute | solution.py:326
  10.5 4.3 %collective-permute-start.3 = (bf16[2,128,128]{2,1,0:T(8,128)(2,1)S(1)}, bf16[2,128,128]{2,1,0:T(8,128)(2,1)S(1)}, u32[]{:S(2)}, u32[]{:S(2)}) collective-permute-start(bf16[2,128,128]{2,1,0:T(8,128)(2,1)S(1)} %join.6), channel_id=1, source_target_pairs={{2,0},{0,2},{3,1},{1,3},{6,4},{4,6},{7,5},{5,7},{10,8},{8,10},{11,... | collective-permute-start | bytes 196616 | tf_op jit(solution)/shard_map/ppermute | solution.py:326
  15.6 1.4 %collective-permute-start.4 = (bf16[128,512]{1,0:T(8,128)(2,1)S(1)}, bf16[128,512]{1,0:T(8,128)(2,1)S(1)}, u32[]{:S(2)}, u32[]{:S(2)}) collective-permute-start(bf16[128,512]{1,0:T(8,128)(2,1)S(1)} %get-tuple-element.32), channel_id=1, source_target_pairs={{1,0},{0,1},{3,2},{2,3},{5,4},{4,5},{7,6},{6,7},{9,8},{8,9},{11,10... | collective-permute-start | bytes 393224 | tf_op jit(solution)/shard_map/ppermute | solution.py:326

commit v17 on v16

--- a/solution.py
+++ b/solution.py
@@ -123,10 +123,8 @@
             at = pl.ds(pair * 8 if isinstance(pair, int) else pl.multiple_of(pair * 8, 8), 8)
             real_sum = imag_sum = None
             for n in range(segments):
-                real_src, imag_src = tiles[n][:8], tiles[n][8:]
-                if weight_of is not None:
-                    weight = jnp.broadcast_to(weight_of(n, pair), (8, LANES))
-                    real_src, imag_src = real_src * weight, imag_src * weight
+                weight = jnp.broadcast_to(weight_of(n, pair), (8, LANES))
+                real_src, imag_src = tiles[n][:8] * weight, tiles[n][8:] * weight
                 real_loc, imag_loc = local_of(n, a, j)
                 real_term = real_src * real_loc + imag_src * imag_loc
                 imag_term = imag_src * real_loc - real_src * imag_loc
@@ -211,46 +209,51 @@
     keep_and_send(turned_round(before), after, kept_ref, sent_ref)
 
 
-def own_block_kernel(sizes, table, phase, mine_ref, kept_ref, sent_ref, local_ref, wide_ref, *scratch):
-    spread_weights(sizes, mine_ref, wide_ref)
-    turn_locals(sizes, phase[0], phase[1], mine_ref, local_ref)
-    before, after = block_sums(sizes, 0, 1, table, wide_ref, local_ref, mine_ref, *scratch)
-    keep_and_send(turned_round(before), after, kept_ref, sent_ref)
-
-
-def weigh_kernel(sizes, wide_ref, local_ref, weighted_ref):
-    stations, bands, seg = sizes[:3]
-    for a in range(stations):
-        for j in range(stations):
-            pair = stations * stations + a * stations + j
-            for g in range(seg):
-                weight = jnp.broadcast_to(wide_ref[g, pl.ds(pair, 1), :], (bands, LANES))
-                weighted_ref[a, j, g, 0] = local_ref[g, j, 0] * weight
-                weighted_ref[a, j, g, 1] = local_ref[g, j, 1] * weight
-
-
-def other_block_kernel(sizes, table, weighted_ref, own_sent_ref, sources_ref, kept_ref, sent_ref, *scratch):
+def both_blocks_kernel(
+    sizes, table, phase, mine_ref, others_ref, kept_ref, sent_ref, local, wide, real_x, imag_x, packed
+):
     stations, bands, seg = sizes[:3]
     pairs = stations * stations
-    add_products(
-        stations, stations, seg, source_tile(sources_ref, 0, seg, stations),
-        None,
-        lambda n, a, j: (weighted_ref[a, j, n, 0], weighted_ref[a, j, n, 1]),
-        *scratch[:2],
-    )
-    before, after = both_sums(sizes, pairs, table, *scratch)
-    sent_ref[pl.ds(0, pairs), :] = own_sent_ref[...]
+    spread_weights(sizes, mine_ref, wide)
+    turn_locals(sizes, phase[0], phase[1], mine_ref, local)
+    for block, sources_ref in enumerate((mine_ref, others_ref)):
+        rows = pl.ds(block * pairs * 8, pairs * 8)
+        add_products(
+            stations, stations, seg, source_tile(sources_ref, 0, seg, stations),
+            lambda n, pair: wide[n, pl.ds(block * pairs + pair, 1), :],
+            lambda n, a, j: (local[n, j, 0], local[n, j, 1]),
+            real_x.at[rows], imag_x.at[rows],
+        )
+    before, after = both_sums(sizes, 2 * pairs, table, real_x, imag_x, packed)
     first_core = lax.axis_index("pol") == 0
 
     @pl.when(first_core)
     def _():
         kept_ref[...] = before
-        sent_ref[pl.ds(pairs, pairs), :] = after.astype(sent_ref.dtype)
+        sent_ref[...] = after.astype(sent_ref.dtype)
 
     @pl.when(jnp.logical_not(first_core))
     def _():
         kept_ref[...] = after
-        sent_ref[pl.ds(pairs, pairs), :] = turned_round(before).astype(sent_ref.dtype)
+        sent_ref[...] = turned_round(before).astype(sent_ref.dtype)
+
+
+def arrange_kernel(sizes, far_ref, across_ref, first_ref, second_ref, mine_ref, others_ref):
+    half = far_ref.shape[0]
+    rows = pl.ds(0, others_ref.shape[1])
+    mine_ref[pl.ds(0, half)] = far_ref[...]
+    others_ref[pl.ds(half, half)] = across_ref[:, rows, :]
+    first_core = lax.axis_index("pol") == 0
+
+    @pl.when(first_core)
+    def _():
+        mine_ref[pl.ds(half, half)] = first_ref[...]
+        others_ref[pl.ds(0, half)] = second_ref[:, rows, :]
+
+    @pl.when(jnp.logical_not(first_core))
+    def _():
+        mine_ref[pl.ds(half, half)] = second_ref[...]
+        others_ref[pl.ds(0, half)] = first_ref[:, rows, :]
 
 
 def settle_kernel(sizes, kept_ref, settled_ref):
@@ -262,10 +265,11 @@
     lags_ref[...] = kept_ref[...] + got_ref[...].astype(jnp.float32)
 
 
-def place_kernel(sizes, mask_ref, own_ref, other_ref, got_ref, out_ref, steps, sems):
+def place_kernel(sizes, mask_ref, kept_ref, got_ref, out_ref, steps, sems):
     pairs = sizes[0] * sizes[0]
-    own = own_ref[...] + got_ref[pl.ds(0, pairs), :].astype(jnp.float32)
-    other = other_ref[...] + got_ref[pl.ds(pairs, pairs), :].astype(jnp.float32)
+    own, other = (
+        kept_ref[rows, :] + got_ref[rows, :].astype(jnp.float32) for rows in (pl.ds(0, pairs), pl.ds(pairs, pairs))
+    )
     copies = []
     for step in range(STEPS):
         mask = jnp.broadcast_to(mask_ref[step, :1, :1], other.shape)
@@ -393,38 +397,33 @@
     quarter = 32 * pairs * 2 * bins * lags
     local_shape = pltpu.VMEM((seg, stations, 2, bands, LANES), f32)
     wide_shape = pltpu.VMEM((seg, blocks * pairs, LANES), f32)
-    kept_shape = pltpu.VMEM((pairs, lags), f32)
 
     if fast:
-        far = join(own, exchange(own, "seg", 2))
+        distant = exchange(own, "seg", 2)
         table, phase, mask = fetch(own)
-        far, table = lax.optimization_barrier((far, table))
-        bare = join(far, rows=rows - 16)
-        near = exchange(far, "seg", 1)
-        across = fetch_from(bare, ("seg", "sta"), lambda z, x: (z ^ 1, x ^ 1))
-        partner = exchange(bare, "sta", 1)
-        mine = join(far, near)
-        own_kept, own_sent, local, wide = call(
-            own_block_kernel, [kept_shape, pltpu.VMEM((pairs, lags), jnp.bfloat16), local_shape, wide_shape],
-            table, phase, mine,
-            scratch=products(1), flops=8 * quarter, name="own_block",
-        )
-        weighted = call(
-            weigh_kernel, pltpu.VMEM((stations, stations, seg, 2, bands, LANES), f32),
-            wide, local,
-            flops=8 * quarter, name="weigh",
-        )
-        weighted, across, partner = lax.optimization_barrier((weighted, across, partner))
+        distant, table = lax.optimization_barrier((distant, table))
+        far = join(own, distant)
+        axes = ("seg", "sta", "pol")
+        across = fetch_from(far, axes, lambda z, x, core: (z ^ 1, x ^ 1, core))
+        first = fetch_from(far, axes, lambda z, x, core: (z ^ 1 ^ core, x ^ core, core))
+        second = fetch_from(far, axes, lambda z, x, core: (z ^ core, x ^ 1 ^ core, core))
+        mine, others = call(
+            arrange_kernel,
+            [pltpu.VMEM((seg, r, LANES), jnp.bfloat16) for r in (rows, rows - 16)],
+            far, across, first, second,
+            name="arrange",
+        )
+        kept_shape = pltpu.VMEM((2 * pairs, lags), f32)
         kept, sent = call(
-            other_block_kernel, [kept_shape, pltpu.VMEM((2 * pairs, lags), jnp.bfloat16)],
-            table, weighted, own_sent, join(partner, across),
-            scratch=products(1), flops=quarter, name="other_block",
+            both_blocks_kernel, [kept_shape, pltpu.VMEM((2 * pairs, lags), jnp.bfloat16)],
+            table, phase, mine, others,
+            scratch=[local_shape, wide_shape] + products(2), flops=quarter, name="both_blocks",
         )
         got = exchange(sent, "pol", 1)
         kept = call(settle_kernel, kept_shape, kept, flops=quarter, name="settle")
         result = call(
             place_kernel, jax.ShapeDtypeStruct((STEPS, pairs, lags), f32),
-            mask, own_kept, kept, got,
+            mask, kept, got,
             out_specs=hbm,
             scratch=[pltpu.VMEM((STEPS, pairs, lags), f32), pltpu.SemaphoreType.DMA((STEPS,))],
             name="place",

time: 18 us -> 19.5 us (1.083)
  waiting for transfers between devices: 4.58 us -> 6.67 us
  Pallas kernels: 5.48 us -> 4.87 us
    ppermute x5, waiting for transfers between devices: 4.58 us -> 6.67 us  [fetch_from(): return lax.ppermute(value, axes, pairs)]
    pallas_call x6 -> x5, Pallas kernels: 4.54 us -> 3.95 us  [call(): pl.pallas_call(functools.partial(kernel, sizes), out_shape=out_shape, in_...]
  transfers between devices with their start and end apart: 5 -> 5, of which waited for: 5 -> 5; matrix products, arithmetic and copies ran while one was open for 0% -> 0% of each run, Pallas kernels for 17% -> 9%
where the time goes in v17:
time: 19.5 us; the launch traced here: 19.3 us
  starting transfers between devices  7.66 us (39%)
  waiting for transfers between devices  6.67 us (34%)
  Pallas kernels  4.87 us (25%)
    ppermute x5, starting transfers between devices, fetch_from(): return lax.ppermute(value, axes, pairs)  7.66 us
    ppermute x5, waiting for transfers between devices, fetch_from(): return lax.ppermute(value, axes, pairs)  6.67 us
    pallas_call x5, Pallas kernels, call(): pl.pallas_call(functools.partial(kernel, sizes), out_shape=out_shape, in_...  3.95 us
    pallas_call x1, Pallas kernels, shards(): pl.pallas_call(functools.partial(prepare_kernel, (stations, bands, sta, b...  0.91 us
  transfers between devices with their start and end apart: 5, of which 5 were waited for; matrix products, arithmetic and copies ran while one was open for 0% of the time, Pallas kernels for 9%

profile of v17, /device:TPU:0, one launch (start us, length us, event | category | flops | bytes accessed | tf_op | source)
XLA Modules:
  0.0 19.3 jit_solution(14317012478193725582)
XLA Ops:
  0.0 0.9 %prepare.1.after.refs_0_ = bf16[1,144,128]{2,1,0:T(8,128)(2,1)S(1)} custom-call(bf16[128,128]{1,0:T(8,128)(2,1)} %bitcast.9, s32[8,16]{1,0:T(8,128)} %bitcast.10, s32[1,16]{1,0:T(1,128)} %refs_2_.1), custom_call_target="tpu_custom_call" | custom-call | tf_op jit(solution)/shard_map/prepare/pallas_call | solution.py:354
  0.9 4.1 %collective-permute-start = (bf16[1,144,128]{2,1,0:T(8,128)(2,1)S(1)}, bf16[1,144,128]{2,1,0:T(8,128)(2,1)S(1)}, u32[]{:S(2)}, u32[]{:S(2)}) collective-permute-start(bf16[1,144,128]{2,1,0:T(8,128)(2,1)S(1)} %prepare.1.after.refs_0_), channel_id=1, source_target_pairs={{8,0},{12,4},{0,8},{4,12},{9,1},{13,5},{1,9},{5,13},{10,2},{14,6},... | collective-permute-start | bytes 110600 | tf_op jit(solution)/shard_map/ppermute | solution.py:330
  5.0 1.6 %fetch.1 = (bf16[2,1024,512]{2,1,0:T(8,128)(2,1)S(1)}, f32[2,8,128]{2,1,0:T(8,128)S(1)}, f32[3,8,128]{2,1,0:T(8,128)S(1)}) custom-call(bf16[2,2,1024,512]{3,2,1,0:T(8,128)(2,1)} %constant.2.clone.table_hbm, s32[3]{0:T(128)} %plan_any.1, bf16[1,144,128]{2,1,0:T(8,128)(2,1)S(1)} %prepare.1.after.refs_0_), custom_call_target="tpu_custom_call" | custom-call | bytes 4194304 | tf_op jit(solution)/shard_map/fetch/pallas_call | solution.py:366
  6.6 0.7 %collective-permute-done.refs_1_ = bf16[1,144,128]{2,1,0:T(8,128)(2,1)S(1)} collective-permute-done((bf16[1,144,128]{2,1,0:T(8,128)(2,1)S(1)}, bf16[1,144,128]{2,1,0:T(8,128)(2,1)S(1)}, u32[]{:S(2)}, u32[]{:S(2)}) %collective-permute-start) | collective-permute-done | bytes 36896 | tf_op jit(solution)/shard_map/ppermute | solution.py:330
  7.4 1.7 %collective-permute-start.3 = (bf16[2,144,128]{2,1,0:T(8,128)(2,1)S(1)}, bf16[2,144,128]{2,1,0:T(8,128)(2,1)S(1)}, u32[]{:S(2)}, u32[]{:S(2)}) collective-permute-start(bf16[2,144,128]{2,1,0:T(8,128)(2,1)S(1)} %join.1.far_ref), channel_id=1, source_target_pairs={{2,0},{5,1},{0,2},{7,3},{6,4},{1,5},{4,6},{3,7},{10,8},{13,9},{8,1... | collective-permute-start | bytes 221192 | tf_op jit(solution)/shard_map/ppermute | solution.py:330
  9.1 1.3 %collective-permute-start.2 = (bf16[2,144,128]{2,1,0:T(8,128)(2,1)S(1)}, bf16[2,144,128]{2,1,0:T(8,128)(2,1)S(1)}, u32[]{:S(2)}, u32[]{:S(2)}) collective-permute-start(bf16[2,144,128]{2,1,0:T(8,128)(2,1)S(1)} %join.1.far_ref), channel_id=1, source_target_pairs={{4,0},{3,1},{6,2},{1,3},{0,4},{7,5},{2,6},{5,7},{12,8},{11,9},{14,... | collective-permute-start | bytes 221192 | tf_op jit(solution)/shard_map/ppermute | solution.py:330
  10.4 0.5 %collective-permute-start.1 = (bf16[2,144,128]{2,1,0:T(8,128)(2,1)S(1)}, bf16[2,144,128]{2,1,0:T(8,128)(2,1)S(1)}, u32[]{:S(2)}, u32[]{:S(2)}) collective-permute-start(bf16[2,144,128]{2,1,0:T(8,128)(2,1)S(1)} %join.1.far_ref), channel_id=1, source_target_pairs={{6,0},{7,1},{4,2},{5,3},{2,4},{3,5},{0,6},{1,7},{14,8},{15,9},{12,... | collective-permute-start | bytes 221192 | tf_op jit(solution)/shard_map/ppermute | solution.py:330
  10.9 0.9 %collective-permute-done.3.second_ref = bf16[2,144,128]{2,1,0:T(8,128)(2,1)S(1)} collective-permute-done((bf16[2,144,128]{2,1,0:T(8,128)(2,1)S(1)}, bf16[2,144,128]{2,1,0:T(8,128)(2,1)S(1)}, u32[]{:S(2)}, u32[]{:S(2)}) %collective-permute-start.3) | collective-permute-done | bytes 73760 | tf_op jit(solution)/shard_map/ppermute | solution.py:330
  11.8 1.7 %collective-permute-done.2.first_ref = bf16[2,144,128]{2,1,0:T(8,128)(2,1)S(1)} collective-permute-done((bf16[2,144,128]{2,1,0:T(8,128)(2,1)S(1)}, bf16[2,144,128]{2,1,0:T(8,128)(2,1)S(1)}, u32[]{:S(2)}, u32[]{:S(2)}) %collective-permute-start.2) | collective-permute-done | bytes 73760 | tf_op jit(solution)/shard_map/ppermute | solution.py:330
  13.4 2.2 %collective-permute-done.1.across_ref = bf16[2,144,128]{2,1,0:T(8,128)(2,1)S(1)} collective-permute-done((bf16[2,144,128]{2,1,0:T(8,128)(2,1)S(1)}, bf16[2,144,128]{2,1,0:T(8,128)(2,1)S(1)}, u32[]{:S(2)}, u32[]{:S(2)}) %collective-permute-start.1) | collective-permute-done | bytes 73760 | tf_op jit(solution)/shard_map/ppermute | solution.py:330
  15.6 1.4 %both_blocks.1 = (f32[128,512]{1,0:T(8,128)S(1)}, bf16[128,512]{1,0:T(8,128)(2,1)S(1)}) custom-call(bf16[2,1024,512]{2,1,0:T(8,128)(2,1)S(1)} %get-tuple-element.16.table, f32[2,8,128]{2,1,0:T(8,128)S(1)} %get-tuple-element.17.phase, bf16[4,144,128]{2,1,0:T(8,128)(2,1)S(1)} %get-tuple-element.19.mine_ref, bf16[4,128,128]{2,1,0:T(8,128)(2,1)S(1)} %get-tuple-element.20.others_ref), custom_call_target="tpu_custom_call" | custom-call | flops 2147483648 | tf_op jit(solution)/shard_map/both_blocks/pallas_call | solution.py:366
  17.0 0.1 collective-permute-start.4
  17.1 0.1 settle.1.kept_ref
  17.3 1.2 %collective-permute-done.4.got_ref = bf16[128,512]{1,0:T(8,128)(2,1)S(1)} collective-permute-done((bf16[128,512]{1,0:T(8,128)(2,1)S(1)}, bf16[128,512]{1,0:T(8,128)(2,1)S(1)}, u32[]{:S(2)}, u32[]{:S(2)}) %collective-permute-start.4) | collective-permute-done | bytes 131104 | tf_op jit(solution)/shard_map/ppermute | solution.py:330
  18.4 0.8 %place.1 = f32[3,64,512]{2,1,0:T(8,128)} custom-call(f32[3,8,128]{2,1,0:T(8,128)S(1)} %get-tuple-element.14.mask_ref, f32[128,512]{1,0:T(8,128)S(1)} %settle.1.kept_ref, bf16[128,512]{1,0:T(8,128)(2,1)S(1)} %collective-permute-done.4.got_ref), custom_call_target="tpu_custom_call" | custom-call | tf_op jit(solution)/shard_map/place/pallas_call | solution.py:366
  (2 shorter events, 0.0 us)
Async XLA Ops:
  0.9 6.4 %collective-permute-start = (bf16[1,144,128]{2,1,0:T(8,128)(2,1)S(1)}, bf16[1,144,128]{2,1,0:T(8,128)(2,1)S(1)}, u32[]{:S(2)}, u32[]{:S(2)}) collective-permute-start(bf16[1,144,128]{2,1,0:T(8,128)(2,1)S(1)} %prepare.1.after.refs_0_), channel_id=1, source_target_pairs={{8,0},{12,4},{0,8},{4,12},{9,1},{13,5},{1,9},{5,13},{10,2},{14,6},... | collective-permute-start | bytes 110600 | tf_op jit(solution)/shard_map/ppermute | solution.py:330
  7.4 4.4 %collective-permute-start.3 = (bf16[2,144,128]{2,1,0:T(8,128)(2,1)S(1)}, bf16[2,144,128]{2,1,0:T(8,128)(2,1)S(1)}, u32[]{:S(2)}, u32[]{:S(2)}) collective-permute-start(bf16[2,144,128]{2,1,0:T(8,128)(2,1)S(1)} %join.1.far_ref), channel_id=1, source_target_pairs={{2,0},{5,1},{0,2},{7,3},{6,4},{1,5},{4,6},{3,7},{10,8},{13,9},{8,1... | collective-permute-start | bytes 221192 | tf_op jit(solution)/shard_map/ppermute | solution.py:330
  9.1 4.4 %collective-permute-start.2 = (bf16[2,144,128]{2,1,0:T(8,128)(2,1)S(1)}, bf16[2,144,128]{2,1,0:T(8,128)(2,1)S(1)}, u32[]{:S(2)}, u32[]{:S(2)}) collective-permute-start(bf16[2,144,128]{2,1,0:T(8,128)(2,1)S(1)} %join.1.far_ref), channel_id=1, source_target_pairs={{4,0},{3,1},{6,2},{1,3},{0,4},{7,5},{2,6},{5,7},{12,8},{11,9},{14,... | collective-permute-start | bytes 221192 | tf_op jit(solution)/shard_map/ppermute | solution.py:330
  10.4 5.3 %collective-permute-start.1 = (bf16[2,144,128]{2,1,0:T(8,128)(2,1)S(1)}, bf16[2,144,128]{2,1,0:T(8,128)(2,1)S(1)}, u32[]{:S(2)}, u32[]{:S(2)}) collective-permute-start(bf16[2,144,128]{2,1,0:T(8,128)(2,1)S(1)} %join.1.far_ref), channel_id=1, source_target_pairs={{6,0},{7,1},{4,2},{5,3},{2,4},{3,5},{0,6},{1,7},{14,8},{15,9},{12,... | collective-permute-start | bytes 221192 | tf_op jit(solution)/shard_map/ppermute | solution.py:330
  17.0 1.4 %collective-permute-start.4 = (bf16[128,512]{1,0:T(8,128)(2,1)S(1)}, bf16[128,512]{1,0:T(8,128)(2,1)S(1)}, u32[]{:S(2)}, u32[]{:S(2)}) collective-permute-start(bf16[128,512]{1,0:T(8,128)(2,1)S(1)} %get-tuple-element.22), channel_id=1, source_target_pairs={{1,0},{0,1},{3,2},{2,3},{5,4},{4,5},{7,6},{6,7},{9,8},{8,9},{11,10... | collective-permute-start | bytes 393224 | tf_op jit(solution)/shard_map/ppermute | solution.py:330

commit v18 on v16

--- a/solution.py
+++ b/solution.py
@@ -115,13 +115,15 @@
             local[g, j, 1] = tile[bands:] * cosine - tile[:bands] * sine
 
 
-def add_products(stations, count, segments, tile_of, weight_of, local_of, real_x, imag_x):
+def add_products(stations, count, segments, tile_of, weight_of, local_of, real_x, imag_x, before=None):
     def one_source(a, carry):
         tiles = [tile_of(n, a).astype(jnp.float32) for n in range(segments)]
         for j in range(stations):
             pair = a * stations + j
             at = pl.ds(pair * 8 if isinstance(pair, int) else pl.multiple_of(pair * 8, 8), 8)
             real_sum = imag_sum = None
+            if before is not None:
+                real_sum, imag_sum = before[0][at, :], before[1][at, :]
             for n in range(segments):
                 real_src, imag_src = tiles[n][:8], tiles[n][8:]
                 if weight_of is not None:
@@ -229,31 +231,43 @@
                 weighted_ref[a, j, g, 1] = local_ref[g, j, 1] * weight
 
 
-def other_block_kernel(sizes, table, weighted_ref, own_sent_ref, sources_ref, kept_ref, sent_ref, *scratch):
+def across_kernel(sizes, weighted_ref, across_ref, real_x, imag_x):
+    stations = sizes[0]
+    add_products(
+        stations, stations, 2,
+        lambda n, a: across_ref[n, pl.ds(a * 16, 16), :],
+        None,
+        lambda n, a, j: (weighted_ref[a, j, 2 + n, 0], weighted_ref[a, j, 2 + n, 1]),
+        real_x, imag_x,
+    )
+
+
+def other_block_kernel(sizes, table, weighted_ref, real_ref, imag_ref, partner_ref, kept_ref, sent_ref, *scratch):
     stations, bands, seg = sizes[:3]
-    pairs = stations * stations
     add_products(
-        stations, stations, seg, source_tile(sources_ref, 0, seg, stations),
+        stations, stations, 2,
+        lambda n, a: partner_ref[n, pl.ds(a * 16, 16), :],
         None,
         lambda n, a, j: (weighted_ref[a, j, n, 0], weighted_ref[a, j, n, 1]),
         *scratch[:2],
-    )
-    before, after = both_sums(sizes, pairs, table, *scratch)
-    sent_ref[pl.ds(0, pairs), :] = own_sent_ref[...]
+        before=(real_ref, imag_ref),
+    )
+    before, after = both_sums(sizes, stations * stations, table, *scratch)
     first_core = lax.axis_index("pol") == 0
 
     @pl.when(first_core)
     def _():
         kept_ref[...] = before
-        sent_ref[pl.ds(pairs, pairs), :] = after.astype(sent_ref.dtype)
+        sent_ref[...] = after.astype(sent_ref.dtype)
 
     @pl.when(jnp.logical_not(first_core))
     def _():
         kept_ref[...] = after
-        sent_ref[pl.ds(pairs, pairs), :] = turned_round(before).astype(sent_ref.dtype)
-
-
-def settle_kernel(sizes, kept_ref, settled_ref):
+        sent_ref[...] = turned_round(before).astype(sent_ref.dtype)
+
+
+def settle_kernel(sizes, own_kept_ref, own_got_ref, kept_ref, own_lags_ref, settled_ref):
+    own_lags_ref[...] = own_kept_ref[...] + own_got_ref[...]
     kept = kept_ref[...]
     settled_ref[...] = jnp.where(lax.axis_index("pol") == 0, turned_round(kept), kept)
 
@@ -263,9 +277,8 @@
 
 
 def place_kernel(sizes, mask_ref, own_ref, other_ref, got_ref, out_ref, steps, sems):
-    pairs = sizes[0] * sizes[0]
-    own = own_ref[...] + got_ref[pl.ds(0, pairs), :].astype(jnp.float32)
-    other = other_ref[...] + got_ref[pl.ds(pairs, pairs), :].astype(jnp.float32)
+    own = own_ref[...]
+    other = other_ref[...] + got_ref[...].astype(jnp.float32)
     copies = []
     for step in range(STEPS):
         mask = jnp.broadcast_to(mask_ref[step, :1, :1], other.shape)
@@ -405,7 +418,7 @@
         partner = exchange(bare, "sta", 1)
         mine = join(far, near)
         own_kept, own_sent, local, wide = call(
-            own_block_kernel, [kept_shape, pltpu.VMEM((pairs, lags), jnp.bfloat16), local_shape, wide_shape],
+            own_block_kernel, [kept_shape, kept_shape, local_shape, wide_shape],
             table, phase, mine,
             scratch=products(1), flops=8 * quarter, name="own_block",
         )
@@ -414,17 +427,26 @@
             wide, local,
             flops=8 * quarter, name="weigh",
         )
-        weighted, across, partner = lax.optimization_barrier((weighted, across, partner))
+        own_got = exchange(own_sent, "pol", 1)
+        weighted, across = lax.optimization_barrier((weighted, across))
+        partial = call(
+            across_kernel, [pltpu.VMEM((pairs * 8, LANES), f32)] * 2,
+            weighted, across,
+            name="across",
+        )
+        own_got, partial, partner = lax.optimization_barrier((own_got, partial, partner))
         kept, sent = call(
-            other_block_kernel, [kept_shape, pltpu.VMEM((2 * pairs, lags), jnp.bfloat16)],
-            table, weighted, own_sent, join(partner, across),
+            other_block_kernel, [kept_shape, pltpu.VMEM((pairs, lags), jnp.bfloat16)],
+            table, weighted, *partial, partner,
             scratch=products(1), flops=quarter, name="other_block",
         )
         got = exchange(sent, "pol", 1)
-        kept = call(settle_kernel, kept_shape, kept, flops=quarter, name="settle")
+        own_lags, kept = call(
+            settle_kernel, [kept_shape] * 2, own_kept, own_got, kept, flops=quarter, name="settle"
+        )
         result = call(
             place_kernel, jax.ShapeDtypeStruct((STEPS, pairs, lags), f32),
-            mask, own_kept, kept, got,
+            mask, own_lags, kept, got,
             out_specs=hbm,
             scratch=[pltpu.VMEM((STEPS, pairs, lags), f32), pltpu.SemaphoreType.DMA((STEPS,))],
             name="place",

time: 18 us -> 17.9 us (level)
  waiting for transfers between devices: 4.58 us -> 4.13 us
  starting transfers between devices: 7.66 us -> 7.95 us
    ppermute x5 -> x6, waiting for transfers between devices: 4.58 us -> 4.13 us  [fetch_from(): return lax.ppermute(value, axes, pairs)]
    ppermute x5 -> x6, starting transfers between devices: 7.66 us -> 7.95 us  [fetch_from(): return lax.ppermute(value, axes, pairs)]
    pallas_call x6 -> x7, Pallas kernels: 4.54 us -> 4.56 us  [call(): pl.pallas_call(functools.partial(kernel, sizes), out_shape=out_shape, in_...]
  transfers between devices with their start and end apart: 5 -> 6, of which waited for: 5 -> 6; matrix products, arithmetic and copies ran while one was open for 0% -> 0% of each run, Pallas kernels for 17% -> 18%
where the time goes in v18:
time: 17.9 us; the launch traced here: 17.6 us
  starting transfers between devices  7.95 us (44%)
  Pallas kernels  5.5 us (31%)
  waiting for transfers between devices  4.13 us (23%)
    ppermute x6, starting transfers between devices, fetch_from(): return lax.ppermute(value, axes, pairs)  7.95 us
    pallas_call x7, Pallas kernels, call(): pl.pallas_call(functools.partial(kernel, sizes), out_shape=out_shape, in_...  4.56 us
    ppermute x6, waiting for transfers between devices, fetch_from(): return lax.ppermute(value, axes, pairs)  4.13 us
    pallas_call x1, Pallas kernels, shards(): pl.pallas_call(functools.partial(prepare_kernel, (stations, bands, sta, b...  0.91 us
  transfers between devices with their start and end apart: 6, of which 6 were waited for; matrix products, arithmetic and copies ran while one was open for 0% of the time, Pallas kernels for 18%

profile of v18, /device:TPU:0, one launch (start us, length us, event | category | flops | bytes accessed | tf_op | source)
XLA Modules:
  0.0 17.6 jit_solution(10769321902022258810)
XLA Ops:
  0.0 0.9 %prepare.1.after.refs_0_ = bf16[1,144,128]{2,1,0:T(8,128)(2,1)S(1)} custom-call(bf16[128,128]{1,0:T(8,128)(2,1)} %bitcast.9, s32[8,16]{1,0:T(8,128)} %bitcast.10, s32[1,16]{1,0:T(1,128)} %refs_2_.1), custom_call_target="tpu_custom_call" | custom-call | tf_op jit(solution)/shard_map/prepare/pallas_call | solution.py:363
  0.9 4.1 %collective-permute-start = (bf16[1,144,128]{2,1,0:T(8,128)(2,1)S(1)}, bf16[1,144,128]{2,1,0:T(8,128)(2,1)S(1)}, u32[]{:S(2)}, u32[]{:S(2)}) collective-permute-start(bf16[1,144,128]{2,1,0:T(8,128)(2,1)S(1)} %prepare.1.after.refs_0_), channel_id=1, source_target_pairs={{8,0},{12,4},{0,8},{4,12},{9,1},{13,5},{1,9},{5,13},{10,2},{14,6},... | collective-permute-start | bytes 110600 | tf_op jit(solution)/shard_map/ppermute | solution.py:339
  5.0 1.6 %fetch.1 = (bf16[2,1024,512]{2,1,0:T(8,128)(2,1)S(1)}, f32[2,8,128]{2,1,0:T(8,128)S(1)}, f32[3,8,128]{2,1,0:T(8,128)S(1)}) custom-call(bf16[2,2,1024,512]{3,2,1,0:T(8,128)(2,1)} %constant.2.clone.table_hbm, s32[3]{0:T(128)} %plan_any.1, bf16[1,144,128]{2,1,0:T(8,128)(2,1)S(1)} %prepare.1.after.refs_0_), custom_call_target="tpu_custom_call" | custom-call | bytes 4194304 | tf_op jit(solution)/shard_map/fetch/pallas_call | solution.py:375
  6.6 0.7 %collective-permute-done.refs_1_ = bf16[1,144,128]{2,1,0:T(8,128)(2,1)S(1)} collective-permute-done((bf16[1,144,128]{2,1,0:T(8,128)(2,1)S(1)}, bf16[1,144,128]{2,1,0:T(8,128)(2,1)S(1)}, u32[]{:S(2)}, u32[]{:S(2)}) %collective-permute-start) | collective-permute-done | bytes 36896 | tf_op jit(solution)/shard_map/ppermute | solution.py:339
  7.4 1.5 %collective-permute-start.1 = (bf16[2,144,128]{2,1,0:T(8,128)(2,1)S(1)}, bf16[2,144,128]{2,1,0:T(8,128)(2,1)S(1)}, u32[]{:S(2)}, u32[]{:S(2)}) collective-permute-start(bf16[2,144,128]{2,1,0:T(8,128)(2,1)S(1)} %join.3.refs_0_), channel_id=1, source_target_pairs={{4,0},{0,4},{12,8},{8,12},{5,1},{1,5},{13,9},{9,13},{6,2},{2,6},{1... | collective-permute-start | bytes 221192 | tf_op jit(solution)/shard_map/ppermute | solution.py:339
  8.9 1.6 %collective-permute-start.3 = (bf16[2,128,128]{2,1,0:T(8,128)(2,1)S(1)}, bf16[2,128,128]{2,1,0:T(8,128)(2,1)S(1)}, u32[]{:S(2)}, u32[]{:S(2)}) collective-permute-start(bf16[2,128,128]{2,1,0:T(8,128)(2,1)S(1)} %join.5), channel_id=1, source_target_pairs={{6,0},{4,2},{2,4},{0,6},{14,8},{12,10},{10,12},{8,14},{7,1},{5,3},... | collective-permute-start | bytes 196616 | tf_op jit(solution)/shard_map/ppermute | solution.py:339
  10.5 0.3 %collective-permute-start.4 = (bf16[2,128,128]{2,1,0:T(8,128)(2,1)S(1)}, bf16[2,128,128]{2,1,0:T(8,128)(2,1)S(1)}, u32[]{:S(2)}, u32[]{:S(2)}) collective-permute-start(bf16[2,128,128]{2,1,0:T(8,128)(2,1)S(1)} %join.5), channel_id=1, source_target_pairs={{2,0},{0,2},{3,1},{1,3},{6,4},{4,6},{7,5},{5,7},{10,8},{8,10},{11,... | collective-permute-start | bytes 196616 | tf_op jit(solution)/shard_map/ppermute | solution.py:339
  10.9 1.5 %collective-permute-done.1.refs_1_ = bf16[2,144,128]{2,1,0:T(8,128)(2,1)S(1)} collective-permute-done((bf16[2,144,128]{2,1,0:T(8,128)(2,1)S(1)}, bf16[2,144,128]{2,1,0:T(8,128)(2,1)S(1)}, u32[]{:S(2)}, u32[]{:S(2)}) %collective-permute-start.1) | collective-permute-done | bytes 73760 | tf_op jit(solution)/shard_map/ppermute | solution.py:339
  12.3 1.1 %own_block.1 = (f32[64,512]{1,0:T(8,128)S(1)}, f32[64,512]{1,0:T(8,128)S(1)}, f32[4,8,2,8,128]{4,3,2,1,0:T(8,128)S(1)}, f32[4,128,128]{2,1,0:T(8,128)S(1)}) custom-call(bf16[2,1024,512]{2,1,0:T(8,128)(2,1)S(1)} %get-tuple-element.28.table, f32[2,8,128]{2,1,0:T(8,128)S(1)} %get-tuple-element.29.phase, bf16[4,144,128]{2,1,0:T(8,128)(2,1)S(1)} %join.4.mine_ref), custom_call_target="tpu_custom_call" | custom-call | flops 17179869184 | tf_op jit(solution)/shard_map/own_block/pallas_call | solution.py:375
  13.5 0.1 collective-permute-start.2
  13.5 0.2 weigh.1.weighted_ref
  13.7 0.4 %collective-permute-done.3.across_ref = bf16[2,128,128]{2,1,0:T(8,128)(2,1)S(1)} collective-permute-done((bf16[2,128,128]{2,1,0:T(8,128)(2,1)S(1)}, bf16[2,128,128]{2,1,0:T(8,128)(2,1)S(1)}, u32[]{:S(2)}, u32[]{:S(2)}) %collective-permute-start.3) | collective-permute-done | bytes 65568 | tf_op jit(solution)/shard_map/ppermute | solution.py:339
  14.0 0.1 across.1
  14.2 0.6 %collective-permute-done.4.partner_ref = bf16[2,128,128]{2,1,0:T(8,128)(2,1)S(1)} collective-permute-done((bf16[2,128,128]{2,1,0:T(8,128)(2,1)S(1)}, bf16[2,128,128]{2,1,0:T(8,128)(2,1)S(1)}, u32[]{:S(2)}, u32[]{:S(2)}) %collective-permute-start.4) | collective-permute-done | bytes 65568 | tf_op jit(solution)/shard_map/ppermute | solution.py:339
  14.8 0.1 collective-permute-done.2.own_got_ref
  14.9 0.6 %other_block.1 = (f32[64,512]{1,0:T(8,128)S(1)}, bf16[64,512]{1,0:T(8,128)(2,1)S(1)}) custom-call(bf16[2,1024,512]{2,1,0:T(8,128)(2,1)S(1)} %get-tuple-element.28.table, f32[8,8,4,2,8,128]{5,4,3,2,1,0:T(8,128)S(1)} %weigh.1.weighted_ref, f32[512,128]{1,0:T(8,128)S(1)} %get-tuple-element.40.real_ref, f32[512,128]{1,0:T(8,128)S(1)} %get-tuple-element.41.imag_ref, ...), custom_call_target="tpu_custom_call" | custom-call | flops 2147483648 | tf_op jit(solution)/shard_map/other_block/pallas_call | solution.py:375
  15.5 0.3 %collective-permute-start.5 = (bf16[64,512]{1,0:T(8,128)(2,1)S(1)}, bf16[64,512]{1,0:T(8,128)(2,1)S(1)}, u32[]{:S(2)}, u32[]{:S(2)}) collective-permute-start(bf16[64,512]{1,0:T(8,128)(2,1)S(1)} %get-tuple-element.46), channel_id=1, source_target_pairs={{1,0},{0,1},{3,2},{2,3},{5,4},{4,5},{7,6},{6,7},{9,8},{8,9},{11,10... | collective-permute-start | bytes 196616 | tf_op jit(solution)/shard_map/ppermute | solution.py:339
  15.8 0.1 settle.1
  15.9 0.9 %collective-permute-done.5.got_ref = bf16[64,512]{1,0:T(8,128)(2,1)S(1)} collective-permute-done((bf16[64,512]{1,0:T(8,128)(2,1)S(1)}, bf16[64,512]{1,0:T(8,128)(2,1)S(1)}, u32[]{:S(2)}, u32[]{:S(2)}) %collective-permute-start.5) | collective-permute-done | bytes 65568 | tf_op jit(solution)/shard_map/ppermute | solution.py:339
  16.8 0.8 %place.1 = f32[3,64,512]{2,1,0:T(8,128)} custom-call(f32[3,8,128]{2,1,0:T(8,128)S(1)} %get-tuple-element.26.mask_ref, f32[64,512]{1,0:T(8,128)S(1)} %get-tuple-element.44.own_ref, f32[64,512]{1,0:T(8,128)S(1)} %get-tuple-element.45.other_ref, bf16[64,512]{1,0:T(8,128)(2,1)S(1)} %collective-permute-done.5.got_ref), custom_call_target="tpu_custom_call" | custom-call | tf_op jit(solution)/shard_map/place/pallas_call | solution.py:375
  (3 shorter events, 0.0 us)
Async XLA Ops:
  0.9 6.4 %collective-permute-start = (bf16[1,144,128]{2,1,0:T(8,128)(2,1)S(1)}, bf16[1,144,128]{2,1,0:T(8,128)(2,1)S(1)}, u32[]{:S(2)}, u32[]{:S(2)}) collective-permute-start(bf16[1,144,128]{2,1,0:T(8,128)(2,1)S(1)} %prepare.1.after.refs_0_), channel_id=1, source_target_pairs={{8,0},{12,4},{0,8},{4,12},{9,1},{13,5},{1,9},{5,13},{10,2},{14,6},... | collective-permute-start | bytes 110600 | tf_op jit(solution)/shard_map/ppermute | solution.py:339
  7.4 5.0 %collective-permute-start.1 = (bf16[2,144,128]{2,1,0:T(8,128)(2,1)S(1)}, bf16[2,144,128]{2,1,0:T(8,128)(2,1)S(1)}, u32[]{:S(2)}, u32[]{:S(2)}) collective-permute-start(bf16[2,144,128]{2,1,0:T(8,128)(2,1)S(1)} %join.3.refs_0_), channel_id=1, source_target_pairs={{4,0},{0,4},{12,8},{8,12},{5,1},{1,5},{13,9},{9,13},{6,2},{2,6},{1... | collective-permute-start | bytes 221192 | tf_op jit(solution)/shard_map/ppermute | solution.py:339
  8.9 5.2 %collective-permute-start.3 = (bf16[2,128,128]{2,1,0:T(8,128)(2,1)S(1)}, bf16[2,128,128]{2,1,0:T(8,128)(2,1)S(1)}, u32[]{:S(2)}, u32[]{:S(2)}) collective-permute-start(bf16[2,128,128]{2,1,0:T(8,128)(2,1)S(1)} %join.5), channel_id=1, source_target_pairs={{6,0},{4,2},{2,4},{0,6},{14,8},{12,10},{10,12},{8,14},{7,1},{5,3},... | collective-permute-start | bytes 196616 | tf_op jit(solution)/shard_map/ppermute | solution.py:339
  10.5 4.3 %collective-permute-start.4 = (bf16[2,128,128]{2,1,0:T(8,128)(2,1)S(1)}, bf16[2,128,128]{2,1,0:T(8,128)(2,1)S(1)}, u32[]{:S(2)}, u32[]{:S(2)}) collective-permute-start(bf16[2,128,128]{2,1,0:T(8,128)(2,1)S(1)} %join.5), channel_id=1, source_target_pairs={{2,0},{0,2},{3,1},{1,3},{6,4},{4,6},{7,5},{5,7},{10,8},{8,10},{11,... | collective-permute-start | bytes 196616 | tf_op jit(solution)/shard_map/ppermute | solution.py:339
  13.5 1.4 %collective-permute-start.2 = (f32[64,512]{1,0:T(8,128)S(1)}, f32[64,512]{1,0:T(8,128)S(1)}, u32[]{:S(2)}, u32[]{:S(2)}) collective-permute-start(f32[64,512]{1,0:T(8,128)S(1)} %get-tuple-element.32), channel_id=1, source_target_pairs={{1,0},{0,1},{3,2},{2,3},{5,4},{4,5},{7,6},{6,7},{9,8},{8,9},{11,10... | collective-permute-start | bytes 393224 | tf_op jit(solution)/shard_map/ppermute | solution.py:339
  15.5 1.3 %collective-permute-start.5 = (bf16[64,512]{1,0:T(8,128)(2,1)S(1)}, bf16[64,512]{1,0:T(8,128)(2,1)S(1)}, u32[]{:S(2)}, u32[]{:S(2)}) collective-permute-start(bf16[64,512]{1,0:T(8,128)(2,1)S(1)} %get-tuple-element.46), channel_id=1, source_target_pairs={{1,0},{0,1},{3,2},{2,3},{5,4},{4,5},{7,6},{6,7},{9,8},{8,9},{11,10... | collective-permute-start | bytes 196616 | tf_op jit(solution)/shard_map/ppermute | solution.py:339

commit v19 on v18

--- a/solution.py
+++ b/solution.py
@@ -266,30 +266,33 @@
         sent_ref[...] = turned_round(before).astype(sent_ref.dtype)
 
 
-def settle_kernel(sizes, own_kept_ref, own_got_ref, kept_ref, own_lags_ref, settled_ref):
-    own_lags_ref[...] = own_kept_ref[...] + own_got_ref[...]
+def settle_kernel(sizes, own_kept_ref, own_got_ref, kept_ref, out_ref, settled_ref, own, sems):
+    own[...] = own_kept_ref[...] + own_got_ref[...]
+    copies = [pltpu.make_async_copy(own, out_ref.at[step], sems.at[step]) for step in range(STEPS)]
+    for copy in copies:
+        copy.start()
     kept = kept_ref[...]
     settled_ref[...] = jnp.where(lax.axis_index("pol") == 0, turned_round(kept), kept)
+    for copy in copies:
+        copy.wait()
 
 
 def combine_kernel(sizes, kept_ref, got_ref, lags_ref):
     lags_ref[...] = kept_ref[...] + got_ref[...].astype(jnp.float32)
 
 
-def place_kernel(sizes, mask_ref, own_ref, other_ref, got_ref, out_ref, steps, sems):
-    own = own_ref[...]
-    other = other_ref[...] + got_ref[...].astype(jnp.float32)
-    copies = []
-    for step in range(STEPS):
-        mask = jnp.broadcast_to(mask_ref[step, :1, :1], other.shape)
-        steps[step] = jnp.where(mask > 0, own, other)
-        copies.append(pltpu.make_async_copy(steps.at[step], out_ref.at[step], sems.at[step]))
-        copies[-1].start()
-    for copy in copies:
-        copy.wait()
-
-
-def fetch_kernel(sizes, table_hbm, plan_any, after, table_ref, phase_ref, mask_ref, plan_ref, sems):
+def place_kernel(sizes, is_own_ref, kept_ref, got_ref, steps_ref, out_ref, other, sems):
+    del steps_ref
+    other[...] = kept_ref[...] + got_ref[...].astype(jnp.float32)
+    for act in ("start", "wait"):
+        for step in range(STEPS):
+
+            @pl.when(is_own_ref[step] == 0)
+            def _():
+                getattr(pltpu.make_async_copy(other, out_ref.at[step], sems.at[step]), act)()
+
+
+def fetch_kernel(sizes, table_hbm, plan_any, after, table_ref, phase_ref, is_own_ref, plan_ref, sems):
     del after
     copies = [
         pltpu.make_async_copy(table_hbm.at[lax.axis_index("pol")], table_ref, sems.at[0]),
@@ -300,8 +303,7 @@
     phase_ref[0], phase_ref[1] = middle_phase(sizes)
     copies[1].wait()
     for step in range(STEPS):
-        own = (plan_ref[step] == lax.axis_index("sta")).astype(jnp.float32)
-        mask_ref[step] = jnp.full(mask_ref.shape[1:], own, jnp.float32)
+        is_own_ref[step] = (plan_ref[step] == lax.axis_index("sta")).astype(jnp.int32)
     copies[0].wait()
 
 
@@ -370,13 +372,19 @@
         name="prepare",
     )(*plan, in_hbm(raw), in_hbm(jnp.transpose(pair_valid[0])), in_hbm(quality))
 
-    def call(kernel, out_shape, *args, out_specs=None, scratch=(), flops=0, moved=0, name=None):
+    def call(kernel, out_shape, *args, aliases=None, scratch=(), flops=0, moved=0, name=None):
+        def spec(x):
+            if x is table_const or x is plan_const or x.shape == placed_shape.shape:
+                return hbm
+            return smem if x.shape == (STEPS,) else vmem
+
         many = isinstance(out_shape, (list, tuple))
         return pl.pallas_call(
             functools.partial(kernel, sizes),
             out_shape=out_shape,
-            in_specs=[hbm if x is table_const or x is plan_const else vmem for x in args],
-            out_specs=out_specs or ([vmem] * len(out_shape) if many else vmem),
+            in_specs=[spec(x) for x in args],
+            out_specs=[spec(x) for x in out_shape] if many else spec(out_shape),
+            input_output_aliases=aliases or {},
             scratch_shapes=list(scratch),
             compiler_params=pltpu.CompilerParams(vmem_limit_bytes=VMEM_BYTES),
             cost_estimate=pl.CostEstimate(flops=flops, bytes_accessed=moved, transcendentals=0),
@@ -384,6 +392,7 @@
         )(*args)
 
     f32 = jnp.float32
+    placed_shape = jax.ShapeDtypeStruct((STEPS, pairs, lags), f32)
     table_const, plan_const = in_hbm(table), in_hbm(owner_plan)
 
     def fetch(after):
@@ -392,7 +401,7 @@
             [
                 pltpu.VMEM(table.shape[1:], table.dtype),
                 pltpu.VMEM((2, bands, LANES), f32),
-                pltpu.VMEM((STEPS, 8, LANES), f32),
+                pltpu.SMEM((STEPS,), jnp.int32),
             ],
             table_const, plan_const, after,
             scratch=[pltpu.SMEM((STEPS,), jnp.int32), pltpu.SemaphoreType.DMA((2,))],
@@ -410,7 +419,7 @@
 
     if fast:
         far = join(own, exchange(own, "seg", 2))
-        table, phase, mask = fetch(own)
+        table, phase, is_own = fetch(own)
         far, table = lax.optimization_barrier((far, table))
         bare = join(far, rows=rows - 16)
         near = exchange(far, "seg", 1)
@@ -441,14 +450,15 @@
             scratch=products(1), flops=quarter, name="other_block",
         )
         got = exchange(sent, "pol", 1)
-        own_lags, kept = call(
-            settle_kernel, [kept_shape] * 2, own_kept, own_got, kept, flops=quarter, name="settle"
+        steps, kept = call(
+            settle_kernel, [placed_shape, kept_shape], own_kept, own_got, kept,
+            scratch=[pltpu.VMEM((pairs, lags), f32), pltpu.SemaphoreType.DMA((STEPS,))],
+            flops=quarter, name="settle",
         )
         result = call(
-            place_kernel, jax.ShapeDtypeStruct((STEPS, pairs, lags), f32),
-            mask, own_lags, kept, got,
-            out_specs=hbm,
-            scratch=[pltpu.VMEM((STEPS, pairs, lags), f32), pltpu.SemaphoreType.DMA((STEPS,))],
+            place_kernel, placed_shape, is_own, kept, got, steps,
+            aliases={3: 0},
+            scratch=[pltpu.VMEM((pairs, lags), f32), pltpu.SemaphoreType.DMA((STEPS,))],
             name="place",
         )
     else:

time: 17.9 us -> 17.8 us (level)
  waiting for transfers between devices: 4.13 us -> 3.45 us
  Pallas kernels: 5.5 us -> 6.07 us
    ppermute x6, waiting for transfers between devices: 4.13 us -> 3.45 us  [fetch_from(): return lax.ppermute(value, axes, pairs)]
    pallas_call x7, Pallas kernels: 4.56 us -> 5.14 us  [call(): pl.pallas_call(functools.partial(kernel, sizes), out_shape=out_shape, in_...]
  transfers between devices with their start and end apart: 6 -> 6, of which waited for: 6 -> 6; matrix products, arithmetic and copies ran while one was open for 0% -> 0% of each run, Pallas kernels for 18% -> 22%
where the time goes in v19:
time: 17.8 us; the launch traced here: 17.5 us
  starting transfers between devices  7.95 us (45%)
  Pallas kernels  6.07 us (34%)
  waiting for transfers between devices  3.45 us (19%)
    ppermute x6, starting transfers between devices, fetch_from(): return lax.ppermute(value, axes, pairs)  7.95 us
    pallas_call x7, Pallas kernels, call(): pl.pallas_call(functools.partial(kernel, sizes), out_shape=out_shape, in_...  5.14 us
    ppermute x6, waiting for transfers between devices, fetch_from(): return lax.ppermute(value, axes, pairs)  3.45 us
    pallas_call x1, Pallas kernels, shards(): pl.pallas_call(functools.partial(prepare_kernel, (stations, bands, sta, b...  0.91 us
  transfers between devices with their start and end apart: 6, of which 6 were waited for; matrix products, arithmetic and copies ran while one was open for 0% of the time, Pallas kernels for 22%

profile of v19, /device:TPU:0, one launch (start us, length us, event | category | flops | bytes accessed | tf_op | source)
XLA Modules:
  0.0 17.5 jit_solution(12797361223274052601)
XLA Ops:
  0.0 0.9 %prepare.1.after.refs_0_ = bf16[1,144,128]{2,1,0:T(8,128)(2,1)S(1)} custom-call(bf16[128,128]{1,0:T(8,128)(2,1)} %bitcast.9, s32[8,16]{1,0:T(8,128)} %bitcast.10, s32[1,16]{1,0:T(1,128)} %refs_2_.1), custom_call_target="tpu_custom_call" | custom-call | tf_op jit(solution)/shard_map/prepare/pallas_call | solution.py:365
  0.9 4.1 %collective-permute-start = (bf16[1,144,128]{2,1,0:T(8,128)(2,1)S(1)}, bf16[1,144,128]{2,1,0:T(8,128)(2,1)S(1)}, u32[]{:S(2)}, u32[]{:S(2)}) collective-permute-start(bf16[1,144,128]{2,1,0:T(8,128)(2,1)S(1)} %prepare.1.after.refs_0_), channel_id=1, source_target_pairs={{8,0},{12,4},{0,8},{4,12},{9,1},{13,5},{1,9},{5,13},{10,2},{14,6},... | collective-permute-start | bytes 110600 | tf_op jit(solution)/shard_map/ppermute | solution.py:341
  5.0 1.6 %fetch.1 = (bf16[2,1024,512]{2,1,0:T(8,128)(2,1)S(1)}, f32[2,8,128]{2,1,0:T(8,128)S(1)}, s32[3]{0:T(128)S(4)}) custom-call(bf16[2,2,1024,512]{3,2,1,0:T(8,128)(2,1)} %constant.2.clone.table_hbm, s32[3]{0:T(128)} %plan_any.1, bf16[1,144,128]{2,1,0:T(8,128)(2,1)S(1)} %prepare.1.after.refs_0_), custom_call_target="tpu_custom_call" | custom-call | bytes 4194304 | tf_op jit(solution)/shard_map/fetch/pallas_call | solution.py:382
  6.6 0.7 %collective-permute-done.refs_1_ = bf16[1,144,128]{2,1,0:T(8,128)(2,1)S(1)} collective-permute-done((bf16[1,144,128]{2,1,0:T(8,128)(2,1)S(1)}, bf16[1,144,128]{2,1,0:T(8,128)(2,1)S(1)}, u32[]{:S(2)}, u32[]{:S(2)}) %collective-permute-start) | collective-permute-done | bytes 36896 | tf_op jit(solution)/shard_map/ppermute | solution.py:341
  7.4 1.5 %collective-permute-start.1 = (bf16[2,144,128]{2,1,0:T(8,128)(2,1)S(1)}, bf16[2,144,128]{2,1,0:T(8,128)(2,1)S(1)}, u32[]{:S(2)}, u32[]{:S(2)}) collective-permute-start(bf16[2,144,128]{2,1,0:T(8,128)(2,1)S(1)} %join.3.refs_0_), channel_id=1, source_target_pairs={{4,0},{0,4},{12,8},{8,12},{5,1},{1,5},{13,9},{9,13},{6,2},{2,6},{1... | collective-permute-start | bytes 221192 | tf_op jit(solution)/shard_map/ppermute | solution.py:341
  8.9 1.6 %collective-permute-start.3 = (bf16[2,128,128]{2,1,0:T(8,128)(2,1)S(1)}, bf16[2,128,128]{2,1,0:T(8,128)(2,1)S(1)}, u32[]{:S(2)}, u32[]{:S(2)}) collective-permute-start(bf16[2,128,128]{2,1,0:T(8,128)(2,1)S(1)} %join.5), channel_id=1, source_target_pairs={{6,0},{4,2},{2,4},{0,6},{14,8},{12,10},{10,12},{8,14},{7,1},{5,3},... | collective-permute-start | bytes 196616 | tf_op jit(solution)/shard_map/ppermute | solution.py:341
  10.5 0.3 %collective-permute-start.4 = (bf16[2,128,128]{2,1,0:T(8,128)(2,1)S(1)}, bf16[2,128,128]{2,1,0:T(8,128)(2,1)S(1)}, u32[]{:S(2)}, u32[]{:S(2)}) collective-permute-start(bf16[2,128,128]{2,1,0:T(8,128)(2,1)S(1)} %join.5), channel_id=1, source_target_pairs={{2,0},{0,2},{3,1},{1,3},{6,4},{4,6},{7,5},{5,7},{10,8},{8,10},{11,... | collective-permute-start | bytes 196616 | tf_op jit(solution)/shard_map/ppermute | solution.py:341
  10.9 1.5 %collective-permute-done.1.refs_1_ = bf16[2,144,128]{2,1,0:T(8,128)(2,1)S(1)} collective-permute-done((bf16[2,144,128]{2,1,0:T(8,128)(2,1)S(1)}, bf16[2,144,128]{2,1,0:T(8,128)(2,1)S(1)}, u32[]{:S(2)}, u32[]{:S(2)}) %collective-permute-start.1) | collective-permute-done | bytes 73760 | tf_op jit(solution)/shard_map/ppermute | solution.py:341
  12.3 1.1 %own_block.1 = (f32[64,512]{1,0:T(8,128)S(1)}, f32[64,512]{1,0:T(8,128)S(1)}, f32[4,8,2,8,128]{4,3,2,1,0:T(8,128)S(1)}, f32[4,128,128]{2,1,0:T(8,128)S(1)}) custom-call(bf16[2,1024,512]{2,1,0:T(8,128)(2,1)S(1)} %get-tuple-element.28.table, f32[2,8,128]{2,1,0:T(8,128)S(1)} %get-tuple-element.29.phase, bf16[4,144,128]{2,1,0:T(8,128)(2,1)S(1)} %join.4.mine_ref), custom_call_target="tpu_custom_call" | custom-call | flops 17179869184 | tf_op jit(solution)/shard_map/own_block/pallas_call | solution.py:382
  13.5 0.1 collective-permute-start.2
  13.5 0.2 weigh.1.weighted_ref
  13.7 0.4 %collective-permute-done.3.across_ref = bf16[2,128,128]{2,1,0:T(8,128)(2,1)S(1)} collective-permute-done((bf16[2,128,128]{2,1,0:T(8,128)(2,1)S(1)}, bf16[2,128,128]{2,1,0:T(8,128)(2,1)S(1)}, u32[]{:S(2)}, u32[]{:S(2)}) %collective-permute-start.3) | collective-permute-done | bytes 65568 | tf_op jit(solution)/shard_map/ppermute | solution.py:341
  14.0 0.1 across.1
  14.2 0.6 %collective-permute-done.4.partner_ref = bf16[2,128,128]{2,1,0:T(8,128)(2,1)S(1)} collective-permute-done((bf16[2,128,128]{2,1,0:T(8,128)(2,1)S(1)}, bf16[2,128,128]{2,1,0:T(8,128)(2,1)S(1)}, u32[]{:S(2)}, u32[]{:S(2)}) %collective-permute-start.4) | collective-permute-done | bytes 65568 | tf_op jit(solution)/shard_map/ppermute | solution.py:341
  14.8 0.1 collective-permute-done.2.own_got_ref
  14.9 0.6 %other_block.1 = (f32[64,512]{1,0:T(8,128)S(1)}, bf16[64,512]{1,0:T(8,128)(2,1)S(1)}) custom-call(bf16[2,1024,512]{2,1,0:T(8,128)(2,1)S(1)} %get-tuple-element.28.table, f32[8,8,4,2,8,128]{5,4,3,2,1,0:T(8,128)S(1)} %weigh.1.weighted_ref, f32[512,128]{1,0:T(8,128)S(1)} %get-tuple-element.40.real_ref, f32[512,128]{1,0:T(8,128)S(1)} %get-tuple-element.41.imag_ref, ...), custom_call_target="tpu_custom_call" | custom-call | flops 2147483648 | tf_op jit(solution)/shard_map/other_block/pallas_call | solution.py:382
  15.5 0.3 %collective-permute-start.5 = (bf16[64,512]{1,0:T(8,128)(2,1)S(1)}, bf16[64,512]{1,0:T(8,128)(2,1)S(1)}, u32[]{:S(2)}, u32[]{:S(2)}) collective-permute-start(bf16[64,512]{1,0:T(8,128)(2,1)S(1)} %get-tuple-element.45), channel_id=1, source_target_pairs={{1,0},{0,1},{3,2},{2,3},{5,4},{4,5},{7,6},{6,7},{9,8},{8,9},{11,10... | collective-permute-start | bytes 196616 | tf_op jit(solution)/shard_map/ppermute | solution.py:341
  15.8 0.8 %settle.1 = (f32[3,64,512]{2,1,0:T(8,128)}, f32[64,512]{1,0:T(8,128)S(1)}) custom-call(f32[64,512]{1,0:T(8,128)S(1)} %get-tuple-element.31.own_kept_ref, f32[64,512]{1,0:T(8,128)S(1)} %collective-permute-done.2.own_got_ref, f32[64,512]{1,0:T(8,128)S(1)} %get-tuple-element.43.kept_ref), custom_call_target="tpu_custom_call" | custom-call | flops 2147483648 | tf_op jit(solution)/shard_map/settle/pallas_call | solution.py:382
  16.6 0.2 %collective-permute-done.5.got_ref = bf16[64,512]{1,0:T(8,128)(2,1)S(1)} collective-permute-done((bf16[64,512]{1,0:T(8,128)(2,1)S(1)}, bf16[64,512]{1,0:T(8,128)(2,1)S(1)}, u32[]{:S(2)}, u32[]{:S(2)}) %collective-permute-start.5) | collective-permute-done | bytes 65568 | tf_op jit(solution)/shard_map/ppermute | solution.py:341
  16.8 0.7 %place.1 = f32[3,64,512]{2,1,0:T(8,128)} custom-call(s32[3]{0:T(128)S(4)} %get-tuple-element.26.is_own_ref, f32[64,512]{1,0:T(8,128)S(1)} %get-tuple-element.44.kept_ref, bf16[64,512]{1,0:T(8,128)(2,1)S(1)} %collective-permute-done.5.got_ref, f32[3,64,512]{2,1,0:T(8,128)} %get-tuple-element.46.steps_ref), custom_call_target="tpu_custom_call", output_to_operand_aliasing={{}: (3, {})} | custom-call | tf_op jit(solution)/shard_map/place/pallas_call | solution.py:382
  (3 shorter events, 0.0 us)
Async XLA Ops:
  0.9 6.4 %collective-permute-start = (bf16[1,144,128]{2,1,0:T(8,128)(2,1)S(1)}, bf16[1,144,128]{2,1,0:T(8,128)(2,1)S(1)}, u32[]{:S(2)}, u32[]{:S(2)}) collective-permute-start(bf16[1,144,128]{2,1,0:T(8,128)(2,1)S(1)} %prepare.1.after.refs_0_), channel_id=1, source_target_pairs={{8,0},{12,4},{0,8},{4,12},{9,1},{13,5},{1,9},{5,13},{10,2},{14,6},... | collective-permute-start | bytes 110600 | tf_op jit(solution)/shard_map/ppermute | solution.py:341
  7.4 5.0 %collective-permute-start.1 = (bf16[2,144,128]{2,1,0:T(8,128)(2,1)S(1)}, bf16[2,144,128]{2,1,0:T(8,128)(2,1)S(1)}, u32[]{:S(2)}, u32[]{:S(2)}) collective-permute-start(bf16[2,144,128]{2,1,0:T(8,128)(2,1)S(1)} %join.3.refs_0_), channel_id=1, source_target_pairs={{4,0},{0,4},{12,8},{8,12},{5,1},{1,5},{13,9},{9,13},{6,2},{2,6},{1... | collective-permute-start | bytes 221192 | tf_op jit(solution)/shard_map/ppermute | solution.py:341
  8.9 5.2 %collective-permute-start.3 = (bf16[2,128,128]{2,1,0:T(8,128)(2,1)S(1)}, bf16[2,128,128]{2,1,0:T(8,128)(2,1)S(1)}, u32[]{:S(2)}, u32[]{:S(2)}) collective-permute-start(bf16[2,128,128]{2,1,0:T(8,128)(2,1)S(1)} %join.5), channel_id=1, source_target_pairs={{6,0},{4,2},{2,4},{0,6},{14,8},{12,10},{10,12},{8,14},{7,1},{5,3},... | collective-permute-start | bytes 196616 | tf_op jit(solution)/shard_map/ppermute | solution.py:341
  10.5 4.3 %collective-permute-start.4 = (bf16[2,128,128]{2,1,0:T(8,128)(2,1)S(1)}, bf16[2,128,128]{2,1,0:T(8,128)(2,1)S(1)}, u32[]{:S(2)}, u32[]{:S(2)}) collective-permute-start(bf16[2,128,128]{2,1,0:T(8,128)(2,1)S(1)} %join.5), channel_id=1, source_target_pairs={{2,0},{0,2},{3,1},{1,3},{6,4},{4,6},{7,5},{5,7},{10,8},{8,10},{11,... | collective-permute-start | bytes 196616 | tf_op jit(solution)/shard_map/ppermute | solution.py:341
  13.5 1.4 %collective-permute-start.2 = (f32[64,512]{1,0:T(8,128)S(1)}, f32[64,512]{1,0:T(8,128)S(1)}, u32[]{:S(2)}, u32[]{:S(2)}) collective-permute-start(f32[64,512]{1,0:T(8,128)S(1)} %get-tuple-element.32), channel_id=1, source_target_pairs={{1,0},{0,1},{3,2},{2,3},{5,4},{4,5},{7,6},{6,7},{9,8},{8,9},{11,10... | collective-permute-start | bytes 393224 | tf_op jit(solution)/shard_map/ppermute | solution.py:341
  15.5 1.3 %collective-permute-start.5 = (bf16[64,512]{1,0:T(8,128)(2,1)S(1)}, bf16[64,512]{1,0:T(8,128)(2,1)S(1)}, u32[]{:S(2)}, u32[]{:S(2)}) collective-permute-start(bf16[64,512]{1,0:T(8,128)(2,1)S(1)} %get-tuple-element.45), channel_id=1, source_target_pairs={{1,0},{0,1},{3,2},{2,3},{5,4},{4,5},{7,6},{6,7},{9,8},{8,9},{11,10... | collective-permute-start | bytes 196616 | tf_op jit(solution)/shard_map/ppermute | solution.py:341

commit v20 on v19

--- a/solution.py
+++ b/solution.py
@@ -52,27 +52,30 @@
     real = wide[pl.ds(0, count, stride=2), :]
     imag = wide[pl.ds(1, count, stride=2), :]
     power = jnp.sum(real * real + imag * imag, axis=1, keepdims=True) * (1.0 / (2 * BAND))
-    inverse = 1.0 / jnp.sqrt(power + 1e-06)
+    inverse = lax.rsqrt(power + 1e-06)
     real = (real * inverse).reshape(stations, bands, LANES)
     imag = (imag * inverse).reshape(stations, bands, LANES)
     white = jnp.concatenate([real, imag], axis=1).reshape(2 * count, LANES).astype(jnp.bfloat16)
 
-    valid = valid_ref[...].astype(jnp.float32).astype(jnp.bfloat16)
-    quality = jnp.broadcast_to(quality_ref[...].astype(jnp.float32), (8, total)).astype(jnp.bfloat16)
+    flags = jnp.concatenate([valid_ref[...], jnp.broadcast_to(quality_ref[...], (8, total))], axis=0)
     pair = lax.broadcasted_iota(jnp.int32, (total, LANES), 1)
     station = lax.broadcasted_iota(jnp.int32, (total, LANES), 0)
+    wanted = [(plan[0][k] if plan else k) * stations + pair // stations for k in range(blocks)]
+    wanted.append(me * stations + pair % stations)
+    picks = jnp.concatenate([(station == x).astype(jnp.float32) for x in wanted], axis=1)
+    picked = jnp.dot(
+        flags.astype(jnp.float32).astype(jnp.bfloat16), picks.astype(jnp.bfloat16),
+        preferred_element_type=jnp.float32,
+    )
     mine = lax.broadcasted_iota(jnp.int32, (stations, LANES), 0) == (
         lax.broadcasted_iota(jnp.int32, (stations, LANES), 1) % stations
     )
-    dot = functools.partial(jnp.dot, preferred_element_type=jnp.float32)
-    pick_local = (station == me * stations + pair % stations).astype(jnp.float32).astype(jnp.bfloat16)
-    local_flags = dot(quality, pick_local)
+    local_flags = picked[stations : stations + 1, blocks * LANES :]
     rows = []
     for k in range(blocks):
-        source = (plan[0][k] if plan else k) * stations + pair // stations
-        pick_source = (station == source).astype(jnp.float32).astype(jnp.bfloat16)
-        valid_row = jnp.sum(jnp.where(mine, dot(valid, pick_source), 0.0), axis=0, keepdims=True)
-        rows.append(valid_row * (dot(quality, pick_source) * local_flags)[:1])
+        part = picked[:, k * LANES : (k + 1) * LANES]
+        valid_row = jnp.sum(jnp.where(mine, part[:stations], 0.0), axis=0, keepdims=True)
+        rows.append(valid_row * part[stations : stations + 1] * local_flags)
     rows.append(jnp.zeros((16 - blocks, LANES), jnp.float32))
     weights = jnp.concatenate(rows, axis=0).astype(jnp.bfloat16)
     out_ref[0, pl.ds(0, 2 * count), :] = white

time: 17.8 us -> 17.8 us (level)
  no operation moved by 1% of the time
where the time goes in v20:
time: 17.8 us; the launch traced here: 17.6 us
  starting transfers between devices  7.95 us (45%)
  Pallas kernels  6.11 us (34%)
  waiting for transfers between devices  3.45 us (19%)
    ppermute x6, starting transfers between devices, fetch_from(): return lax.ppermute(value, axes, pairs)  7.95 us
    pallas_call x7, Pallas kernels, call(): pl.pallas_call(functools.partial(kernel, sizes), out_shape=out_shape, in_...  5.18 us
    ppermute x6, waiting for transfers between devices, fetch_from(): return lax.ppermute(value, axes, pairs)  3.45 us
    pallas_call x1, Pallas kernels, shards(): pl.pallas_call(functools.partial(prepare_kernel, (stations, bands, sta, b...  0.91 us
  transfers between devices with their start and end apart: 6, of which 6 were waited for; matrix products, arithmetic and copies ran while one was open for 0% of the time, Pallas kernels for 22%

profile of v20, /device:TPU:0, one launch (start us, length us, event | category | flops | bytes accessed | tf_op | source)
XLA Modules:
  0.0 17.6 jit_solution(7369661623352467438)
XLA Ops:
  0.0 0.9 %prepare.1.after.refs_0_ = bf16[1,144,128]{2,1,0:T(8,128)(2,1)S(1)} custom-call(bf16[128,128]{1,0:T(8,128)(2,1)} %bitcast.9, s32[8,16]{1,0:T(8,128)} %bitcast.10, s32[1,16]{1,0:T(1,128)} %refs_2_.1), custom_call_target="tpu_custom_call" | custom-call | tf_op jit(solution)/shard_map/prepare/pallas_call | solution.py:368
  0.9 4.1 %collective-permute-start = (bf16[1,144,128]{2,1,0:T(8,128)(2,1)S(1)}, bf16[1,144,128]{2,1,0:T(8,128)(2,1)S(1)}, u32[]{:S(2)}, u32[]{:S(2)}) collective-permute-start(bf16[1,144,128]{2,1,0:T(8,128)(2,1)S(1)} %prepare.1.after.refs_0_), channel_id=1, source_target_pairs={{8,0},{12,4},{0,8},{4,12},{9,1},{13,5},{1,9},{5,13},{10,2},{14,6},... | collective-permute-start | bytes 110600 | tf_op jit(solution)/shard_map/ppermute | solution.py:344
  5.0 1.6 %fetch.1 = (bf16[2,1024,512]{2,1,0:T(8,128)(2,1)S(1)}, f32[2,8,128]{2,1,0:T(8,128)S(1)}, s32[3]{0:T(128)S(4)}) custom-call(bf16[2,2,1024,512]{3,2,1,0:T(8,128)(2,1)} %constant.2.clone.table_hbm, s32[3]{0:T(128)} %plan_any.1, bf16[1,144,128]{2,1,0:T(8,128)(2,1)S(1)} %prepare.1.after.refs_0_), custom_call_target="tpu_custom_call" | custom-call | bytes 4194304 | tf_op jit(solution)/shard_map/fetch/pallas_call | solution.py:385
  6.6 0.7 %collective-permute-done.refs_1_ = bf16[1,144,128]{2,1,0:T(8,128)(2,1)S(1)} collective-permute-done((bf16[1,144,128]{2,1,0:T(8,128)(2,1)S(1)}, bf16[1,144,128]{2,1,0:T(8,128)(2,1)S(1)}, u32[]{:S(2)}, u32[]{:S(2)}) %collective-permute-start) | collective-permute-done | bytes 36896 | tf_op jit(solution)/shard_map/ppermute | solution.py:344
  7.4 1.5 %collective-permute-start.1 = (bf16[2,144,128]{2,1,0:T(8,128)(2,1)S(1)}, bf16[2,144,128]{2,1,0:T(8,128)(2,1)S(1)}, u32[]{:S(2)}, u32[]{:S(2)}) collective-permute-start(bf16[2,144,128]{2,1,0:T(8,128)(2,1)S(1)} %join.3.refs_0_), channel_id=1, source_target_pairs={{4,0},{0,4},{12,8},{8,12},{5,1},{1,5},{13,9},{9,13},{6,2},{2,6},{1... | collective-permute-start | bytes 221192 | tf_op jit(solution)/shard_map/ppermute | solution.py:344
  8.9 1.6 %collective-permute-start.3 = (bf16[2,128,128]{2,1,0:T(8,128)(2,1)S(1)}, bf16[2,128,128]{2,1,0:T(8,128)(2,1)S(1)}, u32[]{:S(2)}, u32[]{:S(2)}) collective-permute-start(bf16[2,128,128]{2,1,0:T(8,128)(2,1)S(1)} %join.5), channel_id=1, source_target_pairs={{6,0},{4,2},{2,4},{0,6},{14,8},{12,10},{10,12},{8,14},{7,1},{5,3},... | collective-permute-start | bytes 196616 | tf_op jit(solution)/shard_map/ppermute | solution.py:344
  10.5 0.3 %collective-permute-start.4 = (bf16[2,128,128]{2,1,0:T(8,128)(2,1)S(1)}, bf16[2,128,128]{2,1,0:T(8,128)(2,1)S(1)}, u32[]{:S(2)}, u32[]{:S(2)}) collective-permute-start(bf16[2,128,128]{2,1,0:T(8,128)(2,1)S(1)} %join.5), channel_id=1, source_target_pairs={{2,0},{0,2},{3,1},{1,3},{6,4},{4,6},{7,5},{5,7},{10,8},{8,10},{11,... | collective-permute-start | bytes 196616 | tf_op jit(solution)/shard_map/ppermute | solution.py:344
  10.9 1.5 %collective-permute-done.1.refs_1_ = bf16[2,144,128]{2,1,0:T(8,128)(2,1)S(1)} collective-permute-done((bf16[2,144,128]{2,1,0:T(8,128)(2,1)S(1)}, bf16[2,144,128]{2,1,0:T(8,128)(2,1)S(1)}, u32[]{:S(2)}, u32[]{:S(2)}) %collective-permute-start.1) | collective-permute-done | bytes 73760 | tf_op jit(solution)/shard_map/ppermute | solution.py:344
  12.3 1.1 %own_block.1 = (f32[64,512]{1,0:T(8,128)S(1)}, f32[64,512]{1,0:T(8,128)S(1)}, f32[4,8,2,8,128]{4,3,2,1,0:T(8,128)S(1)}, f32[4,128,128]{2,1,0:T(8,128)S(1)}) custom-call(bf16[2,1024,512]{2,1,0:T(8,128)(2,1)S(1)} %get-tuple-element.28.table, f32[2,8,128]{2,1,0:T(8,128)S(1)} %get-tuple-element.29.phase, bf16[4,144,128]{2,1,0:T(8,128)(2,1)S(1)} %join.4.mine_ref), custom_call_target="tpu_custom_call" | custom-call | flops 17179869184 | tf_op jit(solution)/shard_map/own_block/pallas_call | solution.py:385
  13.4 0.1 collective-permute-start.2
  13.5 0.2 weigh.1.weighted_ref
  13.7 0.4 %collective-permute-done.3.across_ref = bf16[2,128,128]{2,1,0:T(8,128)(2,1)S(1)} collective-permute-done((bf16[2,128,128]{2,1,0:T(8,128)(2,1)S(1)}, bf16[2,128,128]{2,1,0:T(8,128)(2,1)S(1)}, u32[]{:S(2)}, u32[]{:S(2)}) %collective-permute-start.3) | collective-permute-done | bytes 65568 | tf_op jit(solution)/shard_map/ppermute | solution.py:344
  14.0 0.1 across.1
  14.2 0.6 %collective-permute-done.4.partner_ref = bf16[2,128,128]{2,1,0:T(8,128)(2,1)S(1)} collective-permute-done((bf16[2,128,128]{2,1,0:T(8,128)(2,1)S(1)}, bf16[2,128,128]{2,1,0:T(8,128)(2,1)S(1)}, u32[]{:S(2)}, u32[]{:S(2)}) %collective-permute-start.4) | collective-permute-done | bytes 65568 | tf_op jit(solution)/shard_map/ppermute | solution.py:344
  14.8 0.1 collective-permute-done.2.own_got_ref
  14.9 0.6 %other_block.1 = (f32[64,512]{1,0:T(8,128)S(1)}, bf16[64,512]{1,0:T(8,128)(2,1)S(1)}) custom-call(bf16[2,1024,512]{2,1,0:T(8,128)(2,1)S(1)} %get-tuple-element.28.table, f32[8,8,4,2,8,128]{5,4,3,2,1,0:T(8,128)S(1)} %weigh.1.weighted_ref, f32[512,128]{1,0:T(8,128)S(1)} %get-tuple-element.40.real_ref, f32[512,128]{1,0:T(8,128)S(1)} %get-tuple-element.41.imag_ref, ...), custom_call_target="tpu_custom_call" | custom-call | flops 2147483648 | tf_op jit(solution)/shard_map/other_block/pallas_call | solution.py:385
  15.5 0.3 %collective-permute-start.5 = (bf16[64,512]{1,0:T(8,128)(2,1)S(1)}, bf16[64,512]{1,0:T(8,128)(2,1)S(1)}, u32[]{:S(2)}, u32[]{:S(2)}) collective-permute-start(bf16[64,512]{1,0:T(8,128)(2,1)S(1)} %get-tuple-element.45), channel_id=1, source_target_pairs={{1,0},{0,1},{3,2},{2,3},{5,4},{4,5},{7,6},{6,7},{9,8},{8,9},{11,10... | collective-permute-start | bytes 196616 | tf_op jit(solution)/shard_map/ppermute | solution.py:344
  15.8 0.8 %settle.1 = (f32[3,64,512]{2,1,0:T(8,128)}, f32[64,512]{1,0:T(8,128)S(1)}) custom-call(f32[64,512]{1,0:T(8,128)S(1)} %get-tuple-element.31.own_kept_ref, f32[64,512]{1,0:T(8,128)S(1)} %collective-permute-done.2.own_got_ref, f32[64,512]{1,0:T(8,128)S(1)} %get-tuple-element.43.kept_ref), custom_call_target="tpu_custom_call" | custom-call | flops 2147483648 | tf_op jit(solution)/shard_map/settle/pallas_call | solution.py:385
  16.6 0.2 %collective-permute-done.5.got_ref = bf16[64,512]{1,0:T(8,128)(2,1)S(1)} collective-permute-done((bf16[64,512]{1,0:T(8,128)(2,1)S(1)}, bf16[64,512]{1,0:T(8,128)(2,1)S(1)}, u32[]{:S(2)}, u32[]{:S(2)}) %collective-permute-start.5) | collective-permute-done | bytes 65568 | tf_op jit(solution)/shard_map/ppermute | solution.py:344
  16.8 0.7 %place.1 = f32[3,64,512]{2,1,0:T(8,128)} custom-call(s32[3]{0:T(128)S(4)} %get-tuple-element.26.is_own_ref, f32[64,512]{1,0:T(8,128)S(1)} %get-tuple-element.44.kept_ref, bf16[64,512]{1,0:T(8,128)(2,1)S(1)} %collective-permute-done.5.got_ref, f32[3,64,512]{2,1,0:T(8,128)} %get-tuple-element.46.steps_ref), custom_call_target="tpu_custom_call", output_to_operand_aliasing={{}: (3, {})} | custom-call | tf_op jit(solution)/shard_map/place/pallas_call | solution.py:385
  (3 shorter events, 0.0 us)
Async XLA Ops:
  0.9 6.4 %collective-permute-start = (bf16[1,144,128]{2,1,0:T(8,128)(2,1)S(1)}, bf16[1,144,128]{2,1,0:T(8,128)(2,1)S(1)}, u32[]{:S(2)}, u32[]{:S(2)}) collective-permute-start(bf16[1,144,128]{2,1,0:T(8,128)(2,1)S(1)} %prepare.1.after.refs_0_), channel_id=1, source_target_pairs={{8,0},{12,4},{0,8},{4,12},{9,1},{13,5},{1,9},{5,13},{10,2},{14,6},... | collective-permute-start | bytes 110600 | tf_op jit(solution)/shard_map/ppermute | solution.py:344
  7.4 5.0 %collective-permute-start.1 = (bf16[2,144,128]{2,1,0:T(8,128)(2,1)S(1)}, bf16[2,144,128]{2,1,0:T(8,128)(2,1)S(1)}, u32[]{:S(2)}, u32[]{:S(2)}) collective-permute-start(bf16[2,144,128]{2,1,0:T(8,128)(2,1)S(1)} %join.3.refs_0_), channel_id=1, source_target_pairs={{4,0},{0,4},{12,8},{8,12},{5,1},{1,5},{13,9},{9,13},{6,2},{2,6},{1... | collective-permute-start | bytes 221192 | tf_op jit(solution)/shard_map/ppermute | solution.py:344
  8.9 5.2 %collective-permute-start.3 = (bf16[2,128,128]{2,1,0:T(8,128)(2,1)S(1)}, bf16[2,128,128]{2,1,0:T(8,128)(2,1)S(1)}, u32[]{:S(2)}, u32[]{:S(2)}) collective-permute-start(bf16[2,128,128]{2,1,0:T(8,128)(2,1)S(1)} %join.5), channel_id=1, source_target_pairs={{6,0},{4,2},{2,4},{0,6},{14,8},{12,10},{10,12},{8,14},{7,1},{5,3},... | collective-permute-start | bytes 196616 | tf_op jit(solution)/shard_map/ppermute | solution.py:344
  10.5 4.3 %collective-permute-start.4 = (bf16[2,128,128]{2,1,0:T(8,128)(2,1)S(1)}, bf16[2,128,128]{2,1,0:T(8,128)(2,1)S(1)}, u32[]{:S(2)}, u32[]{:S(2)}) collective-permute-start(bf16[2,128,128]{2,1,0:T(8,128)(2,1)S(1)} %join.5), channel_id=1, source_target_pairs={{2,0},{0,2},{3,1},{1,3},{6,4},{4,6},{7,5},{5,7},{10,8},{8,10},{11,... | collective-permute-start | bytes 196616 | tf_op jit(solution)/shard_map/ppermute | solution.py:344
  13.4 1.4 %collective-permute-start.2 = (f32[64,512]{1,0:T(8,128)S(1)}, f32[64,512]{1,0:T(8,128)S(1)}, u32[]{:S(2)}, u32[]{:S(2)}) collective-permute-start(f32[64,512]{1,0:T(8,128)S(1)} %get-tuple-element.32), channel_id=1, source_target_pairs={{1,0},{0,1},{3,2},{2,3},{5,4},{4,5},{7,6},{6,7},{9,8},{8,9},{11,10... | collective-permute-start | bytes 393224 | tf_op jit(solution)/shard_map/ppermute | solution.py:344
  15.5 1.3 %collective-permute-start.5 = (bf16[64,512]{1,0:T(8,128)(2,1)S(1)}, bf16[64,512]{1,0:T(8,128)(2,1)S(1)}, u32[]{:S(2)}, u32[]{:S(2)}) collective-permute-start(bf16[64,512]{1,0:T(8,128)(2,1)S(1)} %get-tuple-element.45), channel_id=1, source_target_pairs={{1,0},{0,1},{3,2},{2,3},{5,4},{4,5},{7,6},{6,7},{9,8},{8,9},{11,10... | collective-permute-start | bytes 196616 | tf_op jit(solution)/shard_map/ppermute | solution.py:344

commit v21 on v20

--- a/solution.py
+++ b/solution.py
@@ -446,11 +446,11 @@
             weighted, across,
             name="across",
         )
-        own_got, partial, partner = lax.optimization_barrier((own_got, partial, partner))
+        partial, partner = lax.optimization_barrier((partial, partner))
         kept, sent = call(
             other_block_kernel, [kept_shape, pltpu.VMEM((pairs, lags), jnp.bfloat16)],
             table, weighted, *partial, partner,
-            scratch=products(1), flops=quarter, name="other_block",
+            scratch=products(1), name="other_block",
         )
         got = exchange(sent, "pol", 1)
         steps, kept = call(

time: 17.8 us -> 18.6 us (1.045)
  waiting for transfers between devices: 3.45 us -> 4.47 us
  starting transfers between devices: 7.95 us -> 7.73 us
    ppermute x6, waiting for transfers between devices: 3.45 us -> 4.47 us  [fetch_from(): return lax.ppermute(value, axes, pairs)]
    ppermute x6, starting transfers between devices: 7.95 us -> 7.73 us  [fetch_from(): return lax.ppermute(value, axes, pairs)]
  transfers between devices with their start and end apart: 6 -> 6, of which waited for: 6 -> 4; matrix products, arithmetic and copies ran while one was open for 0% -> 0% of each run, Pallas kernels for 22% -> 24%
where the time goes in v21:
time: 18.6 us; the launch traced here: 18.4 us
  starting transfers between devices  7.73 us (42%)
  Pallas kernels  6.07 us (33%)
  waiting for transfers between devices  4.47 us (24%)
    ppermute x6, starting transfers between devices, fetch_from(): return lax.ppermute(value, axes, pairs)  7.73 us
    pallas_call x7, Pallas kernels, call(): pl.pallas_call(functools.partial(kernel, sizes), out_shape=out_shape, in_...  5.14 us
    ppermute x6, waiting for transfers between devices, fetch_from(): return lax.ppermute(value, axes, pairs)  4.47 us
    pallas_call x1, Pallas kernels, shards(): pl.pallas_call(functools.partial(prepare_kernel, (stations, bands, sta, b...  0.91 us
  transfers between devices with their start and end apart: 6, of which 4 were waited for; matrix products, arithmetic and copies ran while one was open for 0% of the time, Pallas kernels for 24%

profile of v21, /device:TPU:0, one launch (start us, length us, event | category | flops | bytes accessed | tf_op | source)
XLA Modules:
  0.0 18.4 jit_solution(9607616107570587894)
XLA Ops:
  0.0 0.9 %prepare.1.after.refs_0_ = bf16[1,144,128]{2,1,0:T(8,128)(2,1)S(1)} custom-call(bf16[128,128]{1,0:T(8,128)(2,1)} %bitcast.9, s32[8,16]{1,0:T(8,128)} %bitcast.10, s32[1,16]{1,0:T(1,128)} %refs_2_.1), custom_call_target="tpu_custom_call" | custom-call | tf_op jit(solution)/shard_map/prepare/pallas_call | solution.py:368
  0.9 4.1 %collective-permute-start = (bf16[1,144,128]{2,1,0:T(8,128)(2,1)S(1)}, bf16[1,144,128]{2,1,0:T(8,128)(2,1)S(1)}, u32[]{:S(2)}, u32[]{:S(2)}) collective-permute-start(bf16[1,144,128]{2,1,0:T(8,128)(2,1)S(1)} %prepare.1.after.refs_0_), channel_id=1, source_target_pairs={{8,0},{12,4},{0,8},{4,12},{9,1},{13,5},{1,9},{5,13},{10,2},{14,6},... | collective-permute-start | bytes 110600 | tf_op jit(solution)/shard_map/ppermute | solution.py:344
  5.0 1.6 %fetch.1 = (bf16[2,1024,512]{2,1,0:T(8,128)(2,1)S(1)}, f32[2,8,128]{2,1,0:T(8,128)S(1)}, s32[3]{0:T(128)S(4)}) custom-call(bf16[2,2,1024,512]{3,2,1,0:T(8,128)(2,1)} %constant.2.clone.table_hbm, s32[3]{0:T(128)} %plan_any.1, bf16[1,144,128]{2,1,0:T(8,128)(2,1)S(1)} %prepare.1.after.refs_0_), custom_call_target="tpu_custom_call" | custom-call | bytes 4194304 | tf_op jit(solution)/shard_map/fetch/pallas_call | solution.py:385
  6.6 0.7 %collective-permute-done.refs_1_ = bf16[1,144,128]{2,1,0:T(8,128)(2,1)S(1)} collective-permute-done((bf16[1,144,128]{2,1,0:T(8,128)(2,1)S(1)}, bf16[1,144,128]{2,1,0:T(8,128)(2,1)S(1)}, u32[]{:S(2)}, u32[]{:S(2)}) %collective-permute-start) | collective-permute-done | bytes 36896 | tf_op jit(solution)/shard_map/ppermute | solution.py:344
  7.4 1.5 %collective-permute-start.1 = (bf16[2,144,128]{2,1,0:T(8,128)(2,1)S(1)}, bf16[2,144,128]{2,1,0:T(8,128)(2,1)S(1)}, u32[]{:S(2)}, u32[]{:S(2)}) collective-permute-start(bf16[2,144,128]{2,1,0:T(8,128)(2,1)S(1)} %join.3.refs_0_), channel_id=1, source_target_pairs={{4,0},{0,4},{12,8},{8,12},{5,1},{1,5},{13,9},{9,13},{6,2},{2,6},{1... | collective-permute-start | bytes 221192 | tf_op jit(solution)/shard_map/ppermute | solution.py:344
  8.9 1.5 %collective-permute-start.4 = (bf16[2,128,128]{2,1,0:T(8,128)(2,1)S(1)}, bf16[2,128,128]{2,1,0:T(8,128)(2,1)S(1)}, u32[]{:S(2)}, u32[]{:S(2)}) collective-permute-start(bf16[2,128,128]{2,1,0:T(8,128)(2,1)S(1)} %join.5), channel_id=1, source_target_pairs={{2,0},{0,2},{3,1},{1,3},{6,4},{4,6},{7,5},{5,7},{10,8},{8,10},{11,... | collective-permute-start | bytes 196616 | tf_op jit(solution)/shard_map/ppermute | solution.py:344
  10.4 0.5 %collective-permute-start.3 = (bf16[2,128,128]{2,1,0:T(8,128)(2,1)S(1)}, bf16[2,128,128]{2,1,0:T(8,128)(2,1)S(1)}, u32[]{:S(2)}, u32[]{:S(2)}) collective-permute-start(bf16[2,128,128]{2,1,0:T(8,128)(2,1)S(1)} %join.5), channel_id=1, source_target_pairs={{6,0},{4,2},{2,4},{0,6},{14,8},{12,10},{10,12},{8,14},{7,1},{5,3},... | collective-permute-start | bytes 196616 | tf_op jit(solution)/shard_map/ppermute | solution.py:344
  10.9 1.3 %collective-permute-done.1.refs_1_ = bf16[2,144,128]{2,1,0:T(8,128)(2,1)S(1)} collective-permute-done((bf16[2,144,128]{2,1,0:T(8,128)(2,1)S(1)}, bf16[2,144,128]{2,1,0:T(8,128)(2,1)S(1)}, u32[]{:S(2)}, u32[]{:S(2)}) %collective-permute-start.1) | collective-permute-done | bytes 73760 | tf_op jit(solution)/shard_map/ppermute | solution.py:344
  12.2 1.1 %own_block.1 = (f32[64,512]{1,0:T(8,128)S(1)}, f32[64,512]{1,0:T(8,128)S(1)}, f32[4,8,2,8,128]{4,3,2,1,0:T(8,128)S(1)}, f32[4,128,128]{2,1,0:T(8,128)S(1)}) custom-call(bf16[2,1024,512]{2,1,0:T(8,128)(2,1)S(1)} %get-tuple-element.27.table, f32[2,8,128]{2,1,0:T(8,128)S(1)} %get-tuple-element.28.phase, bf16[4,144,128]{2,1,0:T(8,128)(2,1)S(1)} %join.4.mine_ref), custom_call_target="tpu_custom_call" | custom-call | flops 17179869184 | tf_op jit(solution)/shard_map/own_block/pallas_call | solution.py:385
  13.3 0.1 collective-permute-start.2
  13.3 0.2 weigh.1.weighted_ref
  13.5 2.0 %collective-permute-done.3.across_ref = bf16[2,128,128]{2,1,0:T(8,128)(2,1)S(1)} collective-permute-done((bf16[2,128,128]{2,1,0:T(8,128)(2,1)S(1)}, bf16[2,128,128]{2,1,0:T(8,128)(2,1)S(1)}, u32[]{:S(2)}, u32[]{:S(2)}) %collective-permute-start.3) | collective-permute-done | bytes 65568 | tf_op jit(solution)/shard_map/ppermute | solution.py:344
  15.5 0.1 across.1
  15.7 0.0 collective-permute-done.4.partner_ref
  15.7 0.6 %other_block.1 = (f32[64,512]{1,0:T(8,128)S(1)}, bf16[64,512]{1,0:T(8,128)(2,1)S(1)}) custom-call(bf16[2,1024,512]{2,1,0:T(8,128)(2,1)S(1)} %get-tuple-element.27.table, f32[8,8,4,2,8,128]{5,4,3,2,1,0:T(8,128)S(1)} %weigh.1.weighted_ref, f32[512,128]{1,0:T(8,128)S(1)} %get-tuple-element.38.real_ref, f32[512,128]{1,0:T(8,128)S(1)} %get-tuple-element.39.imag_ref, ...), custom_call_target="tpu_custom_call" | custom-call | tf_op jit(solution)/shard_map/other_block/pallas_call | solution.py:385
  16.3 0.1 collective-permute-start.5
  16.4 0.0 collective-permute-done.2.own_got_ref
  16.4 0.8 %settle.1 = (f32[3,64,512]{2,1,0:T(8,128)}, f32[64,512]{1,0:T(8,128)S(1)}) custom-call(f32[64,512]{1,0:T(8,128)S(1)} %get-tuple-element.30.own_kept_ref, f32[64,512]{1,0:T(8,128)S(1)} %collective-permute-done.2.own_got_ref, f32[64,512]{1,0:T(8,128)S(1)} %get-tuple-element.41.kept_ref), custom_call_target="tpu_custom_call" | custom-call | flops 2147483648 | tf_op jit(solution)/shard_map/settle/pallas_call | solution.py:385
  17.2 0.4 %collective-permute-done.5.got_ref = bf16[64,512]{1,0:T(8,128)(2,1)S(1)} collective-permute-done((bf16[64,512]{1,0:T(8,128)(2,1)S(1)}, bf16[64,512]{1,0:T(8,128)(2,1)S(1)}, u32[]{:S(2)}, u32[]{:S(2)}) %collective-permute-start.5) | collective-permute-done | bytes 65568 | tf_op jit(solution)/shard_map/ppermute | solution.py:344
  17.6 0.7 %place.1 = f32[3,64,512]{2,1,0:T(8,128)} custom-call(s32[3]{0:T(128)S(4)} %get-tuple-element.25.is_own_ref, f32[64,512]{1,0:T(8,128)S(1)} %get-tuple-element.42.kept_ref, bf16[64,512]{1,0:T(8,128)(2,1)S(1)} %collective-permute-done.5.got_ref, f32[3,64,512]{2,1,0:T(8,128)} %get-tuple-element.44.steps_ref), custom_call_target="tpu_custom_call", output_to_operand_aliasing={{}: (3, {})} | custom-call | tf_op jit(solution)/shard_map/place/pallas_call | solution.py:385
  (3 shorter events, 0.0 us)
Async XLA Ops:
  0.9 6.4 %collective-permute-start = (bf16[1,144,128]{2,1,0:T(8,128)(2,1)S(1)}, bf16[1,144,128]{2,1,0:T(8,128)(2,1)S(1)}, u32[]{:S(2)}, u32[]{:S(2)}) collective-permute-start(bf16[1,144,128]{2,1,0:T(8,128)(2,1)S(1)} %prepare.1.after.refs_0_), channel_id=1, source_target_pairs={{8,0},{12,4},{0,8},{4,12},{9,1},{13,5},{1,9},{5,13},{10,2},{14,6},... | collective-permute-start | bytes 110600 | tf_op jit(solution)/shard_map/ppermute | solution.py:344
  7.4 4.8 %collective-permute-start.1 = (bf16[2,144,128]{2,1,0:T(8,128)(2,1)S(1)}, bf16[2,144,128]{2,1,0:T(8,128)(2,1)S(1)}, u32[]{:S(2)}, u32[]{:S(2)}) collective-permute-start(bf16[2,144,128]{2,1,0:T(8,128)(2,1)S(1)} %join.3.refs_0_), channel_id=1, source_target_pairs={{4,0},{0,4},{12,8},{8,12},{5,1},{1,5},{13,9},{9,13},{6,2},{2,6},{1... | collective-permute-start | bytes 221192 | tf_op jit(solution)/shard_map/ppermute | solution.py:344
  8.9 6.8 %collective-permute-start.4 = (bf16[2,128,128]{2,1,0:T(8,128)(2,1)S(1)}, bf16[2,128,128]{2,1,0:T(8,128)(2,1)S(1)}, u32[]{:S(2)}, u32[]{:S(2)}) collective-permute-start(bf16[2,128,128]{2,1,0:T(8,128)(2,1)S(1)} %join.5), channel_id=1, source_target_pairs={{2,0},{0,2},{3,1},{1,3},{6,4},{4,6},{7,5},{5,7},{10,8},{8,10},{11,... | collective-permute-start | bytes 196616 | tf_op jit(solution)/shard_map/ppermute | solution.py:344
  10.4 5.2 %collective-permute-start.3 = (bf16[2,128,128]{2,1,0:T(8,128)(2,1)S(1)}, bf16[2,128,128]{2,1,0:T(8,128)(2,1)S(1)}, u32[]{:S(2)}, u32[]{:S(2)}) collective-permute-start(bf16[2,128,128]{2,1,0:T(8,128)(2,1)S(1)} %join.5), channel_id=1, source_target_pairs={{6,0},{4,2},{2,4},{0,6},{14,8},{12,10},{10,12},{8,14},{7,1},{5,3},... | collective-permute-start | bytes 196616 | tf_op jit(solution)/shard_map/ppermute | solution.py:344
  13.3 3.1 %collective-permute-start.2 = (f32[64,512]{1,0:T(8,128)S(1)}, f32[64,512]{1,0:T(8,128)S(1)}, u32[]{:S(2)}, u32[]{:S(2)}) collective-permute-start(f32[64,512]{1,0:T(8,128)S(1)} %get-tuple-element.31), channel_id=1, source_target_pairs={{1,0},{0,1},{3,2},{2,3},{5,4},{4,5},{7,6},{6,7},{9,8},{8,9},{11,10... | collective-permute-start | bytes 393224 | tf_op jit(solution)/shard_map/ppermute | solution.py:344
  16.3 1.3 %collective-permute-start.5 = (bf16[64,512]{1,0:T(8,128)(2,1)S(1)}, bf16[64,512]{1,0:T(8,128)(2,1)S(1)}, u32[]{:S(2)}, u32[]{:S(2)}) collective-permute-start(bf16[64,512]{1,0:T(8,128)(2,1)S(1)} %get-tuple-element.43), channel_id=1, source_target_pairs={{1,0},{0,1},{3,2},{2,3},{5,4},{4,5},{7,6},{6,7},{9,8},{8,9},{11,10... | collective-permute-start | bytes 196616 | tf_op jit(solution)/shard_map/ppermute | solution.py:344

commit v22 on v21

--- a/solution.py
+++ b/solution.py
@@ -426,7 +426,7 @@
         far, table = lax.optimization_barrier((far, table))
         bare = join(far, rows=rows - 16)
         near = exchange(far, "seg", 1)
-        across = fetch_from(bare, ("seg", "sta"), lambda z, x: (z ^ 1, x ^ 1))
+        across = fetch_from(far, ("seg", "sta"), lambda z, x: (z ^ 1, x ^ 1))
         partner = exchange(bare, "sta", 1)
         mine = join(far, near)
         own_kept, own_sent, local, wide = call(

time: 18.6 us -> 17.7 us (0.952)
  waiting for transfers between devices: 4.47 us -> 3.64 us
    ppermute x6, waiting for transfers between devices: 4.47 us -> 3.64 us  [fetch_from(): return lax.ppermute(value, axes, pairs)]
  transfers between devices with their start and end apart: 6 -> 6, of which waited for: 4 -> 5; matrix products, arithmetic and copies ran while one was open for 0% -> 0% of each run, Pallas kernels for 24% -> 25%
where the time goes in v22:
time: 17.7 us; the launch traced here: 17.5 us
  starting transfers between devices  7.73 us (44%)
  Pallas kernels  6.08 us (34%)
  waiting for transfers between devices  3.64 us (21%)
    ppermute x6, starting transfers between devices, fetch_from(): return lax.ppermute(value, axes, pairs)  7.73 us
    pallas_call x7, Pallas kernels, call(): pl.pallas_call(functools.partial(kernel, sizes), out_shape=out_shape, in_...  5.15 us
    ppermute x6, waiting for transfers between devices, fetch_from(): return lax.ppermute(value, axes, pairs)  3.64 us
    pallas_call x1, Pallas kernels, shards(): pl.pallas_call(functools.partial(prepare_kernel, (stations, bands, sta, b...  0.91 us
  transfers between devices with their start and end apart: 6, of which 5 were waited for; matrix products, arithmetic and copies ran while one was open for 0% of the time, Pallas kernels for 25%

profile of v22, /device:TPU:0, one launch (start us, length us, event | category | flops | bytes accessed | tf_op | source)
XLA Modules:
  0.0 17.5 jit_solution(15506835627526169164)
XLA Ops:
  0.0 0.9 %prepare.1.after.refs_0_ = bf16[1,144,128]{2,1,0:T(8,128)(2,1)S(1)} custom-call(bf16[128,128]{1,0:T(8,128)(2,1)} %bitcast.9, s32[8,16]{1,0:T(8,128)} %bitcast.10, s32[1,16]{1,0:T(1,128)} %refs_2_.1), custom_call_target="tpu_custom_call" | custom-call | tf_op jit(solution)/shard_map/prepare/pallas_call | solution.py:368
  0.9 4.1 %collective-permute-start = (bf16[1,144,128]{2,1,0:T(8,128)(2,1)S(1)}, bf16[1,144,128]{2,1,0:T(8,128)(2,1)S(1)}, u32[]{:S(2)}, u32[]{:S(2)}) collective-permute-start(bf16[1,144,128]{2,1,0:T(8,128)(2,1)S(1)} %prepare.1.after.refs_0_), channel_id=1, source_target_pairs={{8,0},{12,4},{0,8},{4,12},{9,1},{13,5},{1,9},{5,13},{10,2},{14,6},... | collective-permute-start | bytes 110600 | tf_op jit(solution)/shard_map/ppermute | solution.py:344
  5.0 1.6 %fetch.1 = (bf16[2,1024,512]{2,1,0:T(8,128)(2,1)S(1)}, f32[2,8,128]{2,1,0:T(8,128)S(1)}, s32[3]{0:T(128)S(4)}) custom-call(bf16[2,2,1024,512]{3,2,1,0:T(8,128)(2,1)} %constant.2.clone.table_hbm, s32[3]{0:T(128)} %plan_any.1, bf16[1,144,128]{2,1,0:T(8,128)(2,1)S(1)} %prepare.1.after.refs_0_), custom_call_target="tpu_custom_call" | custom-call | bytes 4194304 | tf_op jit(solution)/shard_map/fetch/pallas_call | solution.py:385
  6.6 0.7 %collective-permute-done.refs_1_ = bf16[1,144,128]{2,1,0:T(8,128)(2,1)S(1)} collective-permute-done((bf16[1,144,128]{2,1,0:T(8,128)(2,1)S(1)}, bf16[1,144,128]{2,1,0:T(8,128)(2,1)S(1)}, u32[]{:S(2)}, u32[]{:S(2)}) %collective-permute-start) | collective-permute-done | bytes 36896 | tf_op jit(solution)/shard_map/ppermute | solution.py:344
  7.4 1.5 %collective-permute-start.1 = (bf16[2,144,128]{2,1,0:T(8,128)(2,1)S(1)}, bf16[2,144,128]{2,1,0:T(8,128)(2,1)S(1)}, u32[]{:S(2)}, u32[]{:S(2)}) collective-permute-start(bf16[2,144,128]{2,1,0:T(8,128)(2,1)S(1)} %join.3.refs_0_), channel_id=1, source_target_pairs={{4,0},{0,4},{12,8},{8,12},{5,1},{1,5},{13,9},{9,13},{6,2},{2,6},{1... | collective-permute-start | bytes 221192 | tf_op jit(solution)/shard_map/ppermute | solution.py:344
  8.9 1.6 %collective-permute-start.3 = (bf16[2,144,128]{2,1,0:T(8,128)(2,1)S(1)}, bf16[2,144,128]{2,1,0:T(8,128)(2,1)S(1)}, u32[]{:S(2)}, u32[]{:S(2)}) collective-permute-start(bf16[2,144,128]{2,1,0:T(8,128)(2,1)S(1)} %join.3.refs_0_), channel_id=1, source_target_pairs={{6,0},{4,2},{2,4},{0,6},{14,8},{12,10},{10,12},{8,14},{7,1},{5,3},... | collective-permute-start | bytes 221192 | tf_op jit(solution)/shard_map/ppermute | solution.py:344
  10.5 0.3 %collective-permute-start.4 = (bf16[2,128,128]{2,1,0:T(8,128)(2,1)S(1)}, bf16[2,128,128]{2,1,0:T(8,128)(2,1)S(1)}, u32[]{:S(2)}, u32[]{:S(2)}) collective-permute-start(bf16[2,128,128]{2,1,0:T(8,128)(2,1)S(1)} %join.5), channel_id=1, source_target_pairs={{2,0},{0,2},{3,1},{1,3},{6,4},{4,6},{7,5},{5,7},{10,8},{8,10},{11,... | collective-permute-start | bytes 196616 | tf_op jit(solution)/shard_map/ppermute | solution.py:344
  10.9 1.5 %collective-permute-done.1.refs_1_ = bf16[2,144,128]{2,1,0:T(8,128)(2,1)S(1)} collective-permute-done((bf16[2,144,128]{2,1,0:T(8,128)(2,1)S(1)}, bf16[2,144,128]{2,1,0:T(8,128)(2,1)S(1)}, u32[]{:S(2)}, u32[]{:S(2)}) %collective-permute-start.1) | collective-permute-done | bytes 73760 | tf_op jit(solution)/shard_map/ppermute | solution.py:344
  12.3 1.1 %own_block.1 = (f32[64,512]{1,0:T(8,128)S(1)}, f32[64,512]{1,0:T(8,128)S(1)}, f32[4,8,2,8,128]{4,3,2,1,0:T(8,128)S(1)}, f32[4,128,128]{2,1,0:T(8,128)S(1)}) custom-call(bf16[2,1024,512]{2,1,0:T(8,128)(2,1)S(1)} %get-tuple-element.27.table, f32[2,8,128]{2,1,0:T(8,128)S(1)} %get-tuple-element.28.phase, bf16[4,144,128]{2,1,0:T(8,128)(2,1)S(1)} %join.4.mine_ref), custom_call_target="tpu_custom_call" | custom-call | flops 17179869184 | tf_op jit(solution)/shard_map/own_block/pallas_call | solution.py:385
  13.4 0.1 collective-permute-start.2
  13.5 0.2 weigh.1.weighted_ref
  13.7 0.5 %collective-permute-done.3.across_ref = bf16[2,144,128]{2,1,0:T(8,128)(2,1)S(1)} collective-permute-done((bf16[2,144,128]{2,1,0:T(8,128)(2,1)S(1)}, bf16[2,144,128]{2,1,0:T(8,128)(2,1)S(1)}, u32[]{:S(2)}, u32[]{:S(2)}) %collective-permute-start.3) | collective-permute-done | bytes 73760 | tf_op jit(solution)/shard_map/ppermute | solution.py:344
  14.1 0.1 across.1
  14.3 0.6 %collective-permute-done.4.partner_ref = bf16[2,128,128]{2,1,0:T(8,128)(2,1)S(1)} collective-permute-done((bf16[2,128,128]{2,1,0:T(8,128)(2,1)S(1)}, bf16[2,128,128]{2,1,0:T(8,128)(2,1)S(1)}, u32[]{:S(2)}, u32[]{:S(2)}) %collective-permute-start.4) | collective-permute-done | bytes 65568 | tf_op jit(solution)/shard_map/ppermute | solution.py:344
  14.8 0.6 %other_block.1 = (f32[64,512]{1,0:T(8,128)S(1)}, bf16[64,512]{1,0:T(8,128)(2,1)S(1)}) custom-call(bf16[2,1024,512]{2,1,0:T(8,128)(2,1)S(1)} %get-tuple-element.27.table, f32[8,8,4,2,8,128]{5,4,3,2,1,0:T(8,128)S(1)} %weigh.1.weighted_ref, f32[512,128]{1,0:T(8,128)S(1)} %get-tuple-element.38.real_ref, f32[512,128]{1,0:T(8,128)S(1)} %get-tuple-element.39.imag_ref, ...), custom_call_target="tpu_custom_call" | custom-call | tf_op jit(solution)/shard_map/other_block/pallas_call | solution.py:385
  15.5 0.1 collective-permute-start.5
  15.6 0.0 collective-permute-done.2.own_got_ref
  15.6 0.8 %settle.1 = (f32[3,64,512]{2,1,0:T(8,128)}, f32[64,512]{1,0:T(8,128)S(1)}) custom-call(f32[64,512]{1,0:T(8,128)S(1)} %get-tuple-element.30.own_kept_ref, f32[64,512]{1,0:T(8,128)S(1)} %collective-permute-done.2.own_got_ref, f32[64,512]{1,0:T(8,128)S(1)} %get-tuple-element.41.kept_ref), custom_call_target="tpu_custom_call" | custom-call | flops 2147483648 | tf_op jit(solution)/shard_map/settle/pallas_call | solution.py:385
  16.4 0.4 %collective-permute-done.5.got_ref = bf16[64,512]{1,0:T(8,128)(2,1)S(1)} collective-permute-done((bf16[64,512]{1,0:T(8,128)(2,1)S(1)}, bf16[64,512]{1,0:T(8,128)(2,1)S(1)}, u32[]{:S(2)}, u32[]{:S(2)}) %collective-permute-start.5) | collective-permute-done | bytes 65568 | tf_op jit(solution)/shard_map/ppermute | solution.py:344
  16.8 0.7 %place.1 = f32[3,64,512]{2,1,0:T(8,128)} custom-call(s32[3]{0:T(128)S(4)} %get-tuple-element.25.is_own_ref, f32[64,512]{1,0:T(8,128)S(1)} %get-tuple-element.42.kept_ref, bf16[64,512]{1,0:T(8,128)(2,1)S(1)} %collective-permute-done.5.got_ref, f32[3,64,512]{2,1,0:T(8,128)} %get-tuple-element.44.steps_ref), custom_call_target="tpu_custom_call", output_to_operand_aliasing={{}: (3, {})} | custom-call | tf_op jit(solution)/shard_map/place/pallas_call | solution.py:385
  (3 shorter events, 0.0 us)
Async XLA Ops:
  0.9 6.4 %collective-permute-start = (bf16[1,144,128]{2,1,0:T(8,128)(2,1)S(1)}, bf16[1,144,128]{2,1,0:T(8,128)(2,1)S(1)}, u32[]{:S(2)}, u32[]{:S(2)}) collective-permute-start(bf16[1,144,128]{2,1,0:T(8,128)(2,1)S(1)} %prepare.1.after.refs_0_), channel_id=1, source_target_pairs={{8,0},{12,4},{0,8},{4,12},{9,1},{13,5},{1,9},{5,13},{10,2},{14,6},... | collective-permute-start | bytes 110600 | tf_op jit(solution)/shard_map/ppermute | solution.py:344
  7.4 5.0 %collective-permute-start.1 = (bf16[2,144,128]{2,1,0:T(8,128)(2,1)S(1)}, bf16[2,144,128]{2,1,0:T(8,128)(2,1)S(1)}, u32[]{:S(2)}, u32[]{:S(2)}) collective-permute-start(bf16[2,144,128]{2,1,0:T(8,128)(2,1)S(1)} %join.3.refs_0_), channel_id=1, source_target_pairs={{4,0},{0,4},{12,8},{8,12},{5,1},{1,5},{13,9},{9,13},{6,2},{2,6},{1... | collective-permute-start | bytes 221192 | tf_op jit(solution)/shard_map/ppermute | solution.py:344
  8.9 5.3 %collective-permute-start.3 = (bf16[2,144,128]{2,1,0:T(8,128)(2,1)S(1)}, bf16[2,144,128]{2,1,0:T(8,128)(2,1)S(1)}, u32[]{:S(2)}, u32[]{:S(2)}) collective-permute-start(bf16[2,144,128]{2,1,0:T(8,128)(2,1)S(1)} %join.3.refs_0_), channel_id=1, source_target_pairs={{6,0},{4,2},{2,4},{0,6},{14,8},{12,10},{10,12},{8,14},{7,1},{5,3},... | collective-permute-start | bytes 221192 | tf_op jit(solution)/shard_map/ppermute | solution.py:344
  10.5 4.3 %collective-permute-start.4 = (bf16[2,128,128]{2,1,0:T(8,128)(2,1)S(1)}, bf16[2,128,128]{2,1,0:T(8,128)(2,1)S(1)}, u32[]{:S(2)}, u32[]{:S(2)}) collective-permute-start(bf16[2,128,128]{2,1,0:T(8,128)(2,1)S(1)} %join.5), channel_id=1, source_target_pairs={{2,0},{0,2},{3,1},{1,3},{6,4},{4,6},{7,5},{5,7},{10,8},{8,10},{11,... | collective-permute-start | bytes 196616 | tf_op jit(solution)/shard_map/ppermute | solution.py:344
  13.4 2.1 %collective-permute-start.2 = (f32[64,512]{1,0:T(8,128)S(1)}, f32[64,512]{1,0:T(8,128)S(1)}, u32[]{:S(2)}, u32[]{:S(2)}) collective-permute-start(f32[64,512]{1,0:T(8,128)S(1)} %get-tuple-element.31), channel_id=1, source_target_pairs={{1,0},{0,1},{3,2},{2,3},{5,4},{4,5},{7,6},{6,7},{9,8},{8,9},{11,10... | collective-permute-start | bytes 393224 | tf_op jit(solution)/shard_map/ppermute | solution.py:344
  15.5 1.3 %collective-permute-start.5 = (bf16[64,512]{1,0:T(8,128)(2,1)S(1)}, bf16[64,512]{1,0:T(8,128)(2,1)S(1)}, u32[]{:S(2)}, u32[]{:S(2)}) collective-permute-start(bf16[64,512]{1,0:T(8,128)(2,1)S(1)} %get-tuple-element.43), channel_id=1, source_target_pairs={{1,0},{0,1},{3,2},{2,3},{5,4},{4,5},{7,6},{6,7},{9,8},{8,9},{11,10... | collective-permute-start | bytes 196616 | tf_op jit(solution)/shard_map/ppermute | solution.py:344

commit v23 on v22

--- a/solution.py
+++ b/solution.py
@@ -234,24 +234,24 @@
                 weighted_ref[a, j, g, 1] = local_ref[g, j, 1] * weight
 
 
-def across_kernel(sizes, weighted_ref, across_ref, real_x, imag_x):
+def partner_kernel(sizes, weighted_ref, first_ref, second_ref, real_x, imag_x):
     stations = sizes[0]
+    add_products(
+        stations, stations, 2,
+        lambda n, a: (first_ref, second_ref)[n][0, pl.ds(a * 16, 16), :],
+        None,
+        lambda n, a, j: (weighted_ref[a, j, n, 0], weighted_ref[a, j, n, 1]),
+        real_x, imag_x,
+    )
+
+
+def other_block_kernel(sizes, table, weighted_ref, real_ref, imag_ref, across_ref, kept_ref, sent_ref, *scratch):
+    stations, bands, seg = sizes[:3]
     add_products(
         stations, stations, 2,
         lambda n, a: across_ref[n, pl.ds(a * 16, 16), :],
         None,
         lambda n, a, j: (weighted_ref[a, j, 2 + n, 0], weighted_ref[a, j, 2 + n, 1]),
-        real_x, imag_x,
-    )
-
-
-def other_block_kernel(sizes, table, weighted_ref, real_ref, imag_ref, partner_ref, kept_ref, sent_ref, *scratch):
-    stations, bands, seg = sizes[:3]
-    add_products(
-        stations, stations, 2,
-        lambda n, a: partner_ref[n, pl.ds(a * 16, 16), :],
-        None,
-        lambda n, a, j: (weighted_ref[a, j, n, 0], weighted_ref[a, j, n, 1]),
         *scratch[:2],
         before=(real_ref, imag_ref),
     )
@@ -295,7 +295,12 @@
                 getattr(pltpu.make_async_copy(other, out_ref.at[step], sems.at[step]), act)()
 
 
-def fetch_kernel(sizes, table_hbm, plan_any, after, table_ref, phase_ref, is_own_ref, plan_ref, sems):
+def phase_kernel(sizes, after, phase_ref):
+    del after
+    phase_ref[0], phase_ref[1] = middle_phase(sizes)
+
+
+def fetch_kernel(sizes, table_hbm, plan_any, after, table_ref, is_own_ref, plan_ref, sems):
     del after
     copies = [
         pltpu.make_async_copy(table_hbm.at[lax.axis_index("pol")], table_ref, sems.at[0]),
@@ -303,7 +308,6 @@
     ]
     for copy in copies:
         copy.start()
-    phase_ref[0], phase_ref[1] = middle_phase(sizes)
     copies[1].wait()
     for step in range(STEPS):
         is_own_ref[step] = (plan_ref[step] == lax.axis_index("sta")).astype(jnp.int32)
@@ -398,36 +402,39 @@
     placed_shape = jax.ShapeDtypeStruct((STEPS, pairs, lags), f32)
     table_const, plan_const = in_hbm(table), in_hbm(owner_plan)
 
+    quarter = 32 * pairs * 2 * bins * lags
+
     def fetch(after):
         return call(
             fetch_kernel,
             [
                 pltpu.VMEM(table.shape[1:], table.dtype),
-                pltpu.VMEM((2, bands, LANES), f32),
                 pltpu.SMEM((STEPS,), jnp.int32),
             ],
             table_const, plan_const, after,
             scratch=[pltpu.SMEM((STEPS,), jnp.int32), pltpu.SemaphoreType.DMA((2,))],
-            moved=4 * table.size // pol,
-            name="fetch",
+            flops=64 * quarter, name="fetch",
         )
 
     def products(count):
         return [pltpu.VMEM((count * pairs * 8, LANES), f32)] * 2 + [pltpu.VMEM((2, count * pairs, bins), jnp.bfloat16)]
 
-    quarter = 32 * pairs * 2 * bins * lags
     local_shape = pltpu.VMEM((seg, stations, 2, bands, LANES), f32)
     wide_shape = pltpu.VMEM((seg, blocks * pairs, LANES), f32)
     kept_shape = pltpu.VMEM((pairs, lags), f32)
 
     if fast:
-        far = join(own, exchange(own, "seg", 2))
-        table, phase, is_own = fetch(own)
-        far, table = lax.optimization_barrier((far, table))
-        bare = join(far, rows=rows - 16)
+        bare = rows - 16
+        distant = exchange(own, "seg", 2)
+        partner_own = exchange(join(own, rows=bare), "sta", 1)
+        phase = call(phase_kernel, pltpu.VMEM((2, bands, LANES), f32), own, flops=64 * quarter, name="phase")
+        distant, phase = lax.optimization_barrier((distant, phase))
+        far = join(own, distant)
         near = exchange(far, "seg", 1)
         across = fetch_from(far, ("seg", "sta"), lambda z, x: (z ^ 1, x ^ 1))
-        partner = exchange(bare, "sta", 1)
+        partner_far = exchange(join(distant, rows=bare), "sta", 1)
+        table, is_own = fetch(far)
+        near, table = lax.optimization_barrier((near, table))
         mine = join(far, near)
         own_kept, own_sent, local, wide = call(
             own_block_kernel, [kept_shape, kept_shape, local_shape, wide_shape],
@@ -440,23 +447,23 @@
             flops=8 * quarter, name="weigh",
         )
         own_got = exchange(own_sent, "pol", 1)
-        weighted, across = lax.optimization_barrier((weighted, across))
+        weighted, partner_own, partner_far = lax.optimization_barrier((weighted, partner_own, partner_far))
         partial = call(
-            across_kernel, [pltpu.VMEM((pairs * 8, LANES), f32)] * 2,
-            weighted, across,
-            name="across",
-        )
-        partial, partner = lax.optimization_barrier((partial, partner))
+            partner_kernel, [pltpu.VMEM((pairs * 8, LANES), f32)] * 2,
+            weighted, partner_own, partner_far,
+            name="partner",
+        )
+        partial, across = lax.optimization_barrier((partial, across))
         kept, sent = call(
             other_block_kernel, [kept_shape, pltpu.VMEM((pairs, lags), jnp.bfloat16)],
-            table, weighted, *partial, partner,
+            table, weighted, *partial, across,
             scratch=products(1), name="other_block",
         )
         got = exchange(sent, "pol", 1)
         steps, kept = call(
             settle_kernel, [placed_shape, kept_shape], own_kept, own_got, kept,
             scratch=[pltpu.VMEM((pairs, lags), f32), pltpu.SemaphoreType.DMA((STEPS,))],
-            flops=quarter, name="settle",
+            name="settle",
         )
         result = call(
             place_kernel, placed_shape, is_own, kept, got, steps,
@@ -471,7 +478,8 @@
             distance //= 2
         gathered = lax.all_gather(mine, "sta")
         sources = join(*(gathered[owner_plan[k]] for k in range(STEPS)))
-        table, phase, _ = fetch(mine)
+        table, _ = fetch(mine)
+        phase = call(phase_kernel, pltpu.VMEM((2, bands, LANES), f32), mine, name="phase")
         kept, sent = call(
             all_blocks_kernel,
             [pltpu.VMEM((blocks * pairs, lags), f32), pltpu.VMEM((blocks * pairs, lags), jnp.bfloat16)],

time: 17.7 us -> 23 us (1.30); the launches traced: 17.5 us -> 22.6 us
  Pallas kernels: 6.08 us -> 11.4 us
  waiting for transfers between devices: 3.64 us -> 1.31 us
  starting transfers between devices: 7.73 us -> 9.79 us
    pallas_call x3 -> x4, Pallas kernels: 0.02 us -> 2.76 us  [join(): pl.pallas_call(functools.partial(join_kernel, ranges), out_shape=pltpu.VM...]
    pallas_call x7 -> x8, Pallas kernels: 5.15 us -> 7.71 us  [call(): pl.pallas_call(functools.partial(kernel, sizes), out_shape=out_shape, in_...]
    ppermute x6 -> x7, waiting for transfers between devices: 3.64 us -> 1.31 us  [fetch_from(): return lax.ppermute(value, axes, pairs)]
    ppermute x6 -> x7, starting transfers between devices: 7.73 us -> 9.79 us  [fetch_from(): return lax.ppermute(value, axes, pairs)]
  transfers between devices with their start and end apart: 6 -> 7, of which waited for: 5 -> 3; matrix products, arithmetic and copies ran while one was open for 0% -> 0% of each run, Pallas kernels for 25% -> 43%
where the time goes in v23:
time: 23 us; the launch traced here: 22.6 us
  Pallas kernels  11.4 us (50%)
  starting transfers between devices  9.79 us (43%)
  waiting for transfers between devices  1.31 us (6%)
    ppermute x7, starting transfers between devices, fetch_from(): return lax.ppermute(value, axes, pairs)  9.79 us
    pallas_call x8, Pallas kernels, call(): pl.pallas_call(functools.partial(kernel, sizes), out_shape=out_shape, in_...  7.71 us
    pallas_call x4, Pallas kernels, join(): pl.pallas_call(functools.partial(join_kernel, ranges), out_shape=pltpu.VM...  2.76 us
    ppermute x7, waiting for transfers between devices, fetch_from(): return lax.ppermute(value, axes, pairs)  1.31 us
    pallas_call x1, Pallas kernels, shards(): pl.pallas_call(functools.partial(prepare_kernel, (stations, bands, sta, b...  0.91 us
  transfers between devices with their start and end apart: 7, of which 3 were waited for; matrix products, arithmetic and copies ran while one was open for 0% of the time, Pallas kernels for 43%

profile of v23, /device:TPU:0, one launch (start us, length us, event | category | flops | bytes accessed | tf_op | source)
XLA Modules:
  0.0 22.6 jit_solution(12066228480151922597)
XLA Ops:
  0.0 0.9 %prepare.1.after.refs_0_ = bf16[1,144,128]{2,1,0:T(8,128)(2,1)S(1)} custom-call(bf16[128,128]{1,0:T(8,128)(2,1)} %bitcast.9, s32[8,16]{1,0:T(8,128)} %bitcast.10, s32[1,16]{1,0:T(1,128)} %refs_2_.1), custom_call_target="tpu_custom_call" | custom-call | tf_op jit(solution)/shard_map/prepare/pallas_call | solution.py:372
  0.9 4.1 %collective-permute-start = (bf16[1,144,128]{2,1,0:T(8,128)(2,1)S(1)}, bf16[1,144,128]{2,1,0:T(8,128)(2,1)S(1)}, u32[]{:S(2)}, u32[]{:S(2)}) collective-permute-start(bf16[1,144,128]{2,1,0:T(8,128)(2,1)S(1)} %prepare.1.after.refs_0_), channel_id=1, source_target_pairs={{8,0},{12,4},{0,8},{4,12},{9,1},{13,5},{1,9},{5,13},{10,2},{14,6},... | collective-permute-start | bytes 110600 | tf_op jit(solution)/shard_map/ppermute | solution.py:348
  5.0 0.6 %join.6 = bf16[1,128,128]{2,1,0:T(8,128)(2,1)} custom-call(bf16[1,144,128]{2,1,0:T(8,128)(2,1)S(1)} %prepare.1.after.refs_0_), custom_call_target="tpu_custom_call" | custom-call | tf_op jit(solution)/shard_map/join/pallas_call | solution.py:330
  5.6 1.5 %collective-permute-start.3 = (bf16[1,128,128]{2,1,0:T(8,128)(2,1)}, bf16[1,128,128]{2,1,0:T(8,128)(2,1)}, u32[]{:S(2)}, u32[]{:S(2)}) collective-permute-start(bf16[1,128,128]{2,1,0:T(8,128)(2,1)} %join.6), channel_id=1, source_target_pairs={{2,0},{0,2},{3,1},{1,3},{6,4},{4,6},{7,5},{5,7},{10,8},{8,10},{11,... | collective-permute-start | bytes 98312 | tf_op jit(solution)/shard_map/ppermute | solution.py:348
  7.2 0.2 collective-permute-done.refs_1_.refs_0_
  7.4 0.6 %join.7 = bf16[1,128,128]{2,1,0:T(8,128)(2,1)} custom-call(bf16[1,144,128]{2,1,0:T(8,128)(2,1)S(1)} %collective-permute-done.refs_1_.refs_0_), custom_call_target="tpu_custom_call" | custom-call | tf_op jit(solution)/shard_map/join/pallas_call | solution.py:330
  8.0 0.6 %join.4.after.refs_0_ = bf16[2,144,128]{2,1,0:T(8,128)(2,1)} custom-call(bf16[1,144,128]{2,1,0:T(8,128)(2,1)S(1)} %prepare.1.after.refs_0_, bf16[1,144,128]{2,1,0:T(8,128)(2,1)S(1)} %collective-permute-done.refs_1_.refs_0_), custom_call_target="tpu_custom_call" | custom-call | tf_op jit(solution)/shard_map/join/pallas_call | solution.py:330
  8.6 2.4 %collective-permute-start.5 = (bf16[2,144,128]{2,1,0:T(8,128)(2,1)}, bf16[2,144,128]{2,1,0:T(8,128)(2,1)}, u32[]{:S(2)}, u32[]{:S(2)}) collective-permute-start(bf16[2,144,128]{2,1,0:T(8,128)(2,1)} %join.4.after.refs_0_), channel_id=1, source_target_pairs={{6,0},{4,2},{2,4},{0,6},{14,8},{12,10},{10,12},{8,14},{7,1},{5,3},... | collective-permute-start | bytes 221192 | tf_op jit(solution)/shard_map/ppermute | solution.py:348
  11.0 0.7 %collective-permute-start.1 = (bf16[2,144,128]{2,1,0:T(8,128)(2,1)}, bf16[2,144,128]{2,1,0:T(8,128)(2,1)S(1)}, u32[]{:S(2)}, u32[]{:S(2)}) collective-permute-start(bf16[2,144,128]{2,1,0:T(8,128)(2,1)} %join.4.after.refs_0_), channel_id=1, source_target_pairs={{4,0},{0,4},{12,8},{8,12},{5,1},{1,5},{13,9},{9,13},{6,2},{2,6},{1... | collective-permute-start | bytes 221192 | tf_op jit(solution)/shard_map/ppermute | solution.py:348
  11.8 0.3 %collective-permute-start.4 = (bf16[1,128,128]{2,1,0:T(8,128)(2,1)}, bf16[1,128,128]{2,1,0:T(8,128)(2,1)}, u32[]{:S(2)}, u32[]{:S(2)}) collective-permute-start(bf16[1,128,128]{2,1,0:T(8,128)(2,1)} %join.7), channel_id=1, source_target_pairs={{2,0},{0,2},{3,1},{1,3},{6,4},{4,6},{7,5},{5,7},{10,8},{8,10},{11,... | collective-permute-start | bytes 98312 | tf_op jit(solution)/shard_map/ppermute | solution.py:348
  12.1 2.5 %fetch.1 = (bf16[2,1024,512]{2,1,0:T(8,128)(2,1)S(1)}, s32[3]{0:T(128)S(4)}) custom-call(bf16[2,2,1024,512]{3,2,1,0:T(8,128)(2,1)} %constant.2.clone.table_hbm, s32[3]{0:T(128)} %plan_any.1, bf16[2,144,128]{2,1,0:T(8,128)(2,1)} %join.4.after.refs_0_), custom_call_target="tpu_custom_call" | custom-call | flops 137438953472 | tf_op jit(solution)/shard_map/fetch/pallas_call | solution.py:389
  14.6 1.0 %collective-permute-done.1.refs_1_ = bf16[2,144,128]{2,1,0:T(8,128)(2,1)S(1)} collective-permute-done((bf16[2,144,128]{2,1,0:T(8,128)(2,1)}, bf16[2,144,128]{2,1,0:T(8,128)(2,1)S(1)}, u32[]{:S(2)}, u32[]{:S(2)}) %collective-permute-start.1) | collective-permute-done | bytes 73760 | tf_op jit(solution)/shard_map/ppermute | solution.py:348
  15.6 0.9 %join.5.mine_ref = bf16[4,144,128]{2,1,0:T(8,128)(2,1)S(1)} custom-call(bf16[2,144,128]{2,1,0:T(8,128)(2,1)} %join.4.after.refs_0_, bf16[2,144,128]{2,1,0:T(8,128)(2,1)S(1)} %collective-permute-done.1.refs_1_), custom_call_target="tpu_custom_call" | custom-call | tf_op jit(solution)/shard_map/join/pallas_call | solution.py:330
  16.5 1.1 %own_block.1 = (f32[64,512]{1,0:T(8,128)S(1)}, f32[64,512]{1,0:T(8,128)S(1)}, f32[4,8,2,8,128]{4,3,2,1,0:T(8,128)S(1)}, f32[4,128,128]{2,1,0:T(8,128)S(1)}) custom-call(bf16[2,1024,512]{2,1,0:T(8,128)(2,1)S(1)} %get-tuple-element.30.table, f32[2,8,128]{2,1,0:T(8,128)S(1)} %phase.1, bf16[4,144,128]{2,1,0:T(8,128)(2,1)S(1)} %join.5.mine_ref), custom_call_target="tpu_custom_call" | custom-call | flops 17179869184 | tf_op jit(solution)/shard_map/own_block/pallas_call | solution.py:389
  17.6 0.1 collective-permute-start.2
  17.7 0.2 weigh.1.weighted_ref
  17.8 0.0 collective-permute-done.3.first_ref
  17.9 0.0 collective-permute-done.4.second_ref
  17.9 0.9 %partner.1 = (f32[512,128]{1,0:T(8,128)S(1)}, f32[512,128]{1,0:T(8,128)S(1)}) custom-call(f32[8,8,4,2,8,128]{5,4,3,2,1,0:T(8,128)S(1)} %weigh.1.weighted_ref, bf16[1,128,128]{2,1,0:T(8,128)(2,1)} %collective-permute-done.3.first_ref, bf16[1,128,128]{2,1,0:T(8,128)(2,1)} %collective-permute-done.4.second_ref), custom_call_target="tpu_custom_call" | custom-call | tf_op jit(solution)/shard_map/partner/pallas_call | solution.py:389
  18.8 1.5 %other_block.1 = (f32[64,512]{1,0:T(8,128)S(1)}, bf16[64,512]{1,0:T(8,128)(2,1)S(1)}) custom-call(bf16[2,1024,512]{2,1,0:T(8,128)(2,1)S(1)} %get-tuple-element.30.table, f32[8,8,4,2,8,128]{5,4,3,2,1,0:T(8,128)S(1)} %weigh.1.weighted_ref, f32[512,128]{1,0:T(8,128)S(1)} %get-tuple-element.42.real_ref, f32[512,128]{1,0:T(8,128)S(1)} %get-tuple-element.43.imag_ref, ...), custom_call_target="tpu_custom_call" | custom-call | tf_op jit(solution)/shard_map/other_block/pallas_call | solution.py:389
  20.3 0.6 %collective-permute-start.6 = (bf16[64,512]{1,0:T(8,128)(2,1)S(1)}, bf16[64,512]{1,0:T(8,128)(2,1)S(1)}, u32[]{:S(2)}, u32[]{:S(2)}) collective-permute-start(bf16[64,512]{1,0:T(8,128)(2,1)S(1)} %get-tuple-element.47), channel_id=1, source_target_pairs={{1,0},{0,1},{3,2},{2,3},{5,4},{4,5},{7,6},{6,7},{9,8},{8,9},{11,10... | collective-permute-start | bytes 196616 | tf_op jit(solution)/shard_map/ppermute | solution.py:348
  21.0 0.8 %settle.1 = (f32[3,64,512]{2,1,0:T(8,128)}, f32[64,512]{1,0:T(8,128)S(1)}) custom-call(f32[64,512]{1,0:T(8,128)S(1)} %get-tuple-element.33.own_kept_ref, f32[64,512]{1,0:T(8,128)S(1)} %collective-permute-done.2.own_got_ref, f32[64,512]{1,0:T(8,128)S(1)} %get-tuple-element.45.kept_ref), custom_call_target="tpu_custom_call" | custom-call | tf_op jit(solution)/shard_map/settle/pallas_call | solution.py:389
  21.8 0.1 collective-permute-done.6.got_ref
  21.9 0.7 %place.1 = f32[3,64,512]{2,1,0:T(8,128)} custom-call(s32[3]{0:T(128)S(4)} %get-tuple-element.28.is_own_ref, f32[64,512]{1,0:T(8,128)S(1)} %get-tuple-element.46.kept_ref, bf16[64,512]{1,0:T(8,128)(2,1)S(1)} %collective-permute-done.6.got_ref, f32[3,64,512]{2,1,0:T(8,128)} %get-tuple-element.48.steps_ref), custom_call_target="tpu_custom_call", output_to_operand_aliasing={{}: (3, {})} | custom-call | tf_op jit(solution)/shard_map/place/pallas_call | solution.py:389
  (3 shorter events, 0.0 us)
Async XLA Ops:
  0.9 6.4 %collective-permute-start = (bf16[1,144,128]{2,1,0:T(8,128)(2,1)S(1)}, bf16[1,144,128]{2,1,0:T(8,128)(2,1)S(1)}, u32[]{:S(2)}, u32[]{:S(2)}) collective-permute-start(bf16[1,144,128]{2,1,0:T(8,128)(2,1)S(1)} %prepare.1.after.refs_0_), channel_id=1, source_target_pairs={{8,0},{12,4},{0,8},{4,12},{9,1},{13,5},{1,9},{5,13},{10,2},{14,6},... | collective-permute-start | bytes 110600 | tf_op jit(solution)/shard_map/ppermute | solution.py:348
  5.6 12.2 %collective-permute-start.3 = (bf16[1,128,128]{2,1,0:T(8,128)(2,1)}, bf16[1,128,128]{2,1,0:T(8,128)(2,1)}, u32[]{:S(2)}, u32[]{:S(2)}) collective-permute-start(bf16[1,128,128]{2,1,0:T(8,128)(2,1)} %join.6), channel_id=1, source_target_pairs={{2,0},{0,2},{3,1},{1,3},{6,4},{4,6},{7,5},{5,7},{10,8},{8,10},{11,... | collective-permute-start | bytes 98312 | tf_op jit(solution)/shard_map/ppermute | solution.py:348
  8.6 10.2 %collective-permute-start.5 = (bf16[2,144,128]{2,1,0:T(8,128)(2,1)}, bf16[2,144,128]{2,1,0:T(8,128)(2,1)}, u32[]{:S(2)}, u32[]{:S(2)}) collective-permute-start(bf16[2,144,128]{2,1,0:T(8,128)(2,1)} %join.4.after.refs_0_), channel_id=1, source_target_pairs={{6,0},{4,2},{2,4},{0,6},{14,8},{12,10},{10,12},{8,14},{7,1},{5,3},... | collective-permute-start | bytes 221192 | tf_op jit(solution)/shard_map/ppermute | solution.py:348
  11.0 4.6 %collective-permute-start.1 = (bf16[2,144,128]{2,1,0:T(8,128)(2,1)}, bf16[2,144,128]{2,1,0:T(8,128)(2,1)S(1)}, u32[]{:S(2)}, u32[]{:S(2)}) collective-permute-start(bf16[2,144,128]{2,1,0:T(8,128)(2,1)} %join.4.after.refs_0_), channel_id=1, source_target_pairs={{4,0},{0,4},{12,8},{8,12},{5,1},{1,5},{13,9},{9,13},{6,2},{2,6},{1... | collective-permute-start | bytes 221192 | tf_op jit(solution)/shard_map/ppermute | solution.py:348
  11.8 6.1 %collective-permute-start.4 = (bf16[1,128,128]{2,1,0:T(8,128)(2,1)}, bf16[1,128,128]{2,1,0:T(8,128)(2,1)}, u32[]{:S(2)}, u32[]{:S(2)}) collective-permute-start(bf16[1,128,128]{2,1,0:T(8,128)(2,1)} %join.7), channel_id=1, source_target_pairs={{2,0},{0,2},{3,1},{1,3},{6,4},{4,6},{7,5},{5,7},{10,8},{8,10},{11,... | collective-permute-start | bytes 98312 | tf_op jit(solution)/shard_map/ppermute | solution.py:348
  17.6 3.4 %collective-permute-start.2 = (f32[64,512]{1,0:T(8,128)S(1)}, f32[64,512]{1,0:T(8,128)S(1)}, u32[]{:S(2)}, u32[]{:S(2)}) collective-permute-start(f32[64,512]{1,0:T(8,128)S(1)} %get-tuple-element.34), channel_id=1, source_target_pairs={{1,0},{0,1},{3,2},{2,3},{5,4},{4,5},{7,6},{6,7},{9,8},{8,9},{11,10... | collective-permute-start | bytes 393224 | tf_op jit(solution)/shard_map/ppermute | solution.py:348
  20.3 1.5 %collective-permute-start.6 = (bf16[64,512]{1,0:T(8,128)(2,1)S(1)}, bf16[64,512]{1,0:T(8,128)(2,1)S(1)}, u32[]{:S(2)}, u32[]{:S(2)}) collective-permute-start(bf16[64,512]{1,0:T(8,128)(2,1)S(1)} %get-tuple-element.47), channel_id=1, source_target_pairs={{1,0},{0,1},{3,2},{2,3},{5,4},{4,5},{7,6},{6,7},{9,8},{8,9},{11,10... | collective-permute-start | bytes 196616 | tf_op jit(solution)/shard_map/ppermute | solution.py:348

commit v24 on v23

--- a/solution.py
+++ b/solution.py
@@ -413,7 +413,7 @@
             ],
             table_const, plan_const, after,
             scratch=[pltpu.SMEM((STEPS,), jnp.int32), pltpu.SemaphoreType.DMA((2,))],
-            flops=64 * quarter, name="fetch",
+            flops=4 * quarter, name="fetch",
         )
 
     def products(count):
@@ -427,7 +427,7 @@
         bare = rows - 16
         distant = exchange(own, "seg", 2)
         partner_own = exchange(join(own, rows=bare), "sta", 1)
-        phase = call(phase_kernel, pltpu.VMEM((2, bands, LANES), f32), own, flops=64 * quarter, name="phase")
+        phase = call(phase_kernel, pltpu.VMEM((2, bands, LANES), f32), own, flops=4 * quarter, name="phase")
         distant, phase = lax.optimization_barrier((distant, phase))
         far = join(own, distant)
         near = exchange(far, "seg", 1)

time: 23 us -> 18.9 us (0.82)
  Pallas kernels: 11.4 us -> 6.14 us
  waiting for transfers between devices: 1.31 us -> 2.59 us
    pallas_call x4, Pallas kernels: 2.76 us -> 0.02 us  [join(): pl.pallas_call(functools.partial(join_kernel, ranges), out_shape=pltpu.VM...]
    pallas_call x8, Pallas kernels: 7.71 us -> 5.21 us  [call(): pl.pallas_call(functools.partial(kernel, sizes), out_shape=out_shape, in_...]
    ppermute x7, waiting for transfers between devices: 1.31 us -> 2.59 us  [fetch_from(): return lax.ppermute(value, axes, pairs)]
  transfers between devices with their start and end apart: 7 -> 7, of which waited for: 3 -> 3; matrix products, arithmetic and copies ran while one was open for 0% -> 0% of each run, Pallas kernels for 43% -> 24%
where the time goes in v24:
time: 18.9 us; the launch traced here: 18.7 us
  starting transfers between devices  9.85 us (52%)
  Pallas kernels  6.14 us (32%)
  waiting for transfers between devices  2.59 us (14%)
    ppermute x7, starting transfers between devices, fetch_from(): return lax.ppermute(value, axes, pairs)  9.85 us
    pallas_call x8, Pallas kernels, call(): pl.pallas_call(functools.partial(kernel, sizes), out_shape=out_shape, in_...  5.21 us
    ppermute x7, waiting for transfers between devices, fetch_from(): return lax.ppermute(value, axes, pairs)  2.59 us
    pallas_call x1, Pallas kernels, shards(): pl.pallas_call(functools.partial(prepare_kernel, (stations, bands, sta, b...  0.91 us
  transfers between devices with their start and end apart: 7, of which 3 were waited for; matrix products, arithmetic and copies ran while one was open for 0% of the time, Pallas kernels for 24%

profile of v24, /device:TPU:0, one launch (start us, length us, event | category | flops | bytes accessed | tf_op | source)
XLA Modules:
  0.0 18.7 jit_solution(3627867731567307738)
XLA Ops:
  0.0 0.9 %prepare.1.after.refs_0_ = bf16[1,144,128]{2,1,0:T(8,128)(2,1)S(1)} custom-call(bf16[128,128]{1,0:T(8,128)(2,1)} %bitcast.9, s32[8,16]{1,0:T(8,128)} %bitcast.10, s32[1,16]{1,0:T(1,128)} %refs_2_.1), custom_call_target="tpu_custom_call" | custom-call | tf_op jit(solution)/shard_map/prepare/pallas_call | solution.py:372
  0.9 4.1 %collective-permute-start = (bf16[1,144,128]{2,1,0:T(8,128)(2,1)S(1)}, bf16[1,144,128]{2,1,0:T(8,128)(2,1)S(1)}, u32[]{:S(2)}, u32[]{:S(2)}) collective-permute-start(bf16[1,144,128]{2,1,0:T(8,128)(2,1)S(1)} %prepare.1.after.refs_0_), channel_id=1, source_target_pairs={{8,0},{12,4},{0,8},{4,12},{9,1},{13,5},{1,9},{5,13},{10,2},{14,6},... | collective-permute-start | bytes 110600 | tf_op jit(solution)/shard_map/ppermute | solution.py:348
  5.0 1.5 %collective-permute-start.3 = (bf16[1,128,128]{2,1,0:T(8,128)(2,1)S(1)}, bf16[1,128,128]{2,1,0:T(8,128)(2,1)S(1)}, u32[]{:S(2)}, u32[]{:S(2)}) collective-permute-start(bf16[1,128,128]{2,1,0:T(8,128)(2,1)S(1)} %join.6), channel_id=1, source_target_pairs={{2,0},{0,2},{3,1},{1,3},{6,4},{4,6},{7,5},{5,7},{10,8},{8,10},{11,... | collective-permute-start | bytes 98312 | tf_op jit(solution)/shard_map/ppermute | solution.py:348
  6.6 0.8 %collective-permute-done.refs_1_.refs_0_ = bf16[1,144,128]{2,1,0:T(8,128)(2,1)S(1)} collective-permute-done((bf16[1,144,128]{2,1,0:T(8,128)(2,1)S(1)}, bf16[1,144,128]{2,1,0:T(8,128)(2,1)S(1)}, u32[]{:S(2)}, u32[]{:S(2)}) %collective-permute-start) | collective-permute-done | bytes 36896 | tf_op jit(solution)/shard_map/ppermute | solution.py:348
  7.4 2.5 %collective-permute-start.5 = (bf16[2,144,128]{2,1,0:T(8,128)(2,1)S(1)}, bf16[2,144,128]{2,1,0:T(8,128)(2,1)S(1)}, u32[]{:S(2)}, u32[]{:S(2)}) collective-permute-start(bf16[2,144,128]{2,1,0:T(8,128)(2,1)S(1)} %join.4.after.refs_0_), channel_id=1, source_target_pairs={{6,0},{4,2},{2,4},{0,6},{14,8},{12,10},{10,12},{8,14},{7,1},{5,3},... | collective-permute-start | bytes 221192 | tf_op jit(solution)/shard_map/ppermute | solution.py:348
  9.9 0.7 %collective-permute-start.1 = (bf16[2,144,128]{2,1,0:T(8,128)(2,1)S(1)}, bf16[2,144,128]{2,1,0:T(8,128)(2,1)S(1)}, u32[]{:S(2)}, u32[]{:S(2)}) collective-permute-start(bf16[2,144,128]{2,1,0:T(8,128)(2,1)S(1)} %join.4.after.refs_0_), channel_id=1, source_target_pairs={{4,0},{0,4},{12,8},{8,12},{5,1},{1,5},{13,9},{9,13},{6,2},{2,6},{1... | collective-permute-start | bytes 221192 | tf_op jit(solution)/shard_map/ppermute | solution.py:348
  10.6 0.3 %collective-permute-start.4 = (bf16[1,128,128]{2,1,0:T(8,128)(2,1)S(1)}, bf16[1,128,128]{2,1,0:T(8,128)(2,1)S(1)}, u32[]{:S(2)}, u32[]{:S(2)}) collective-permute-start(bf16[1,128,128]{2,1,0:T(8,128)(2,1)S(1)} %join.7), channel_id=1, source_target_pairs={{2,0},{0,2},{3,1},{1,3},{6,4},{4,6},{7,5},{5,7},{10,8},{8,10},{11,... | collective-permute-start | bytes 98312 | tf_op jit(solution)/shard_map/ppermute | solution.py:348
  10.9 1.6 %fetch.1 = (bf16[2,1024,512]{2,1,0:T(8,128)(2,1)S(1)}, s32[3]{0:T(128)S(4)}) custom-call(bf16[2,2,1024,512]{3,2,1,0:T(8,128)(2,1)} %constant.2.clone.table_hbm, s32[3]{0:T(128)} %plan_any.1, bf16[2,144,128]{2,1,0:T(8,128)(2,1)S(1)} %join.4.after.refs_0_), custom_call_target="tpu_custom_call" | custom-call | flops 8589934592 | tf_op jit(solution)/shard_map/fetch/pallas_call | solution.py:389
  12.5 1.7 %collective-permute-done.1.refs_1_ = bf16[2,144,128]{2,1,0:T(8,128)(2,1)S(1)} collective-permute-done((bf16[2,144,128]{2,1,0:T(8,128)(2,1)S(1)}, bf16[2,144,128]{2,1,0:T(8,128)(2,1)S(1)}, u32[]{:S(2)}, u32[]{:S(2)}) %collective-permute-start.1) | collective-permute-done | bytes 73760 | tf_op jit(solution)/shard_map/ppermute | solution.py:348
  14.2 1.1 %own_block.1 = (f32[64,512]{1,0:T(8,128)S(1)}, f32[64,512]{1,0:T(8,128)S(1)}, f32[4,8,2,8,128]{4,3,2,1,0:T(8,128)S(1)}, f32[4,128,128]{2,1,0:T(8,128)S(1)}) custom-call(bf16[2,1024,512]{2,1,0:T(8,128)(2,1)S(1)} %get-tuple-element.30.table, f32[2,8,128]{2,1,0:T(8,128)S(1)} %phase.1, bf16[4,144,128]{2,1,0:T(8,128)(2,1)S(1)} %join.5.mine_ref), custom_call_target="tpu_custom_call" | custom-call | flops 17179869184 | tf_op jit(solution)/shard_map/own_block/pallas_call | solution.py:389
  15.3 0.1 collective-permute-start.2
  15.4 0.2 weigh.1.weighted_ref
  15.6 0.0 collective-permute-done.3.first_ref
  15.6 0.0 collective-permute-done.4.second_ref
  15.6 0.1 partner.1
  15.7 0.0 collective-permute-done.5.across_ref
  15.7 0.7 %other_block.1 = (f32[64,512]{1,0:T(8,128)S(1)}, bf16[64,512]{1,0:T(8,128)(2,1)S(1)}) custom-call(bf16[2,1024,512]{2,1,0:T(8,128)(2,1)S(1)} %get-tuple-element.30.table, f32[8,8,4,2,8,128]{5,4,3,2,1,0:T(8,128)S(1)} %weigh.1.weighted_ref, f32[512,128]{1,0:T(8,128)S(1)} %get-tuple-element.42.real_ref, f32[512,128]{1,0:T(8,128)S(1)} %get-tuple-element.43.imag_ref, ...), custom_call_target="tpu_custom_call" | custom-call | tf_op jit(solution)/shard_map/other_block/pallas_call | solution.py:389
  16.4 0.6 %collective-permute-start.6 = (bf16[64,512]{1,0:T(8,128)(2,1)S(1)}, bf16[64,512]{1,0:T(8,128)(2,1)S(1)}, u32[]{:S(2)}, u32[]{:S(2)}) collective-permute-start(bf16[64,512]{1,0:T(8,128)(2,1)S(1)} %get-tuple-element.47), channel_id=1, source_target_pairs={{1,0},{0,1},{3,2},{2,3},{5,4},{4,5},{7,6},{6,7},{9,8},{8,9},{11,10... | collective-permute-start | bytes 196616 | tf_op jit(solution)/shard_map/ppermute | solution.py:348
  17.0 0.0 collective-permute-done.2.own_got_ref
  17.0 0.8 %settle.1 = (f32[3,64,512]{2,1,0:T(8,128)}, f32[64,512]{1,0:T(8,128)S(1)}) custom-call(f32[64,512]{1,0:T(8,128)S(1)} %get-tuple-element.33.own_kept_ref, f32[64,512]{1,0:T(8,128)S(1)} %collective-permute-done.2.own_got_ref, f32[64,512]{1,0:T(8,128)S(1)} %get-tuple-element.45.kept_ref), custom_call_target="tpu_custom_call" | custom-call | tf_op jit(solution)/shard_map/settle/pallas_call | solution.py:389
  17.8 0.1 collective-permute-done.6.got_ref
  17.9 0.7 %place.1 = f32[3,64,512]{2,1,0:T(8,128)} custom-call(s32[3]{0:T(128)S(4)} %get-tuple-element.28.is_own_ref, f32[64,512]{1,0:T(8,128)S(1)} %get-tuple-element.46.kept_ref, bf16[64,512]{1,0:T(8,128)(2,1)S(1)} %collective-permute-done.6.got_ref, f32[3,64,512]{2,1,0:T(8,128)} %get-tuple-element.48.steps_ref), custom_call_target="tpu_custom_call", output_to_operand_aliasing={{}: (3, {})} | custom-call | tf_op jit(solution)/shard_map/place/pallas_call | solution.py:389
  (5 shorter events, 0.1 us)
Async XLA Ops:
  0.9 6.4 %collective-permute-start = (bf16[1,144,128]{2,1,0:T(8,128)(2,1)S(1)}, bf16[1,144,128]{2,1,0:T(8,128)(2,1)S(1)}, u32[]{:S(2)}, u32[]{:S(2)}) collective-permute-start(bf16[1,144,128]{2,1,0:T(8,128)(2,1)S(1)} %prepare.1.after.refs_0_), channel_id=1, source_target_pairs={{8,0},{12,4},{0,8},{4,12},{9,1},{13,5},{1,9},{5,13},{10,2},{14,6},... | collective-permute-start | bytes 110600 | tf_op jit(solution)/shard_map/ppermute | solution.py:348
  5.0 10.6 %collective-permute-start.3 = (bf16[1,128,128]{2,1,0:T(8,128)(2,1)S(1)}, bf16[1,128,128]{2,1,0:T(8,128)(2,1)S(1)}, u32[]{:S(2)}, u32[]{:S(2)}) collective-permute-start(bf16[1,128,128]{2,1,0:T(8,128)(2,1)S(1)} %join.6), channel_id=1, source_target_pairs={{2,0},{0,2},{3,1},{1,3},{6,4},{4,6},{7,5},{5,7},{10,8},{8,10},{11,... | collective-permute-start | bytes 98312 | tf_op jit(solution)/shard_map/ppermute | solution.py:348
  7.4 8.4 %collective-permute-start.5 = (bf16[2,144,128]{2,1,0:T(8,128)(2,1)S(1)}, bf16[2,144,128]{2,1,0:T(8,128)(2,1)S(1)}, u32[]{:S(2)}, u32[]{:S(2)}) collective-permute-start(bf16[2,144,128]{2,1,0:T(8,128)(2,1)S(1)} %join.4.after.refs_0_), channel_id=1, source_target_pairs={{6,0},{4,2},{2,4},{0,6},{14,8},{12,10},{10,12},{8,14},{7,1},{5,3},... | collective-permute-start | bytes 221192 | tf_op jit(solution)/shard_map/ppermute | solution.py:348
  9.9 4.4 %collective-permute-start.1 = (bf16[2,144,128]{2,1,0:T(8,128)(2,1)S(1)}, bf16[2,144,128]{2,1,0:T(8,128)(2,1)S(1)}, u32[]{:S(2)}, u32[]{:S(2)}) collective-permute-start(bf16[2,144,128]{2,1,0:T(8,128)(2,1)S(1)} %join.4.after.refs_0_), channel_id=1, source_target_pairs={{4,0},{0,4},{12,8},{8,12},{5,1},{1,5},{13,9},{9,13},{6,2},{2,6},{1... | collective-permute-start | bytes 221192 | tf_op jit(solution)/shard_map/ppermute | solution.py:348
  10.6 5.0 %collective-permute-start.4 = (bf16[1,128,128]{2,1,0:T(8,128)(2,1)S(1)}, bf16[1,128,128]{2,1,0:T(8,128)(2,1)S(1)}, u32[]{:S(2)}, u32[]{:S(2)}) collective-permute-start(bf16[1,128,128]{2,1,0:T(8,128)(2,1)S(1)} %join.7), channel_id=1, source_target_pairs={{2,0},{0,2},{3,1},{1,3},{6,4},{4,6},{7,5},{5,7},{10,8},{8,10},{11,... | collective-permute-start | bytes 98312 | tf_op jit(solution)/shard_map/ppermute | solution.py:348
  15.3 1.7 %collective-permute-start.2 = (f32[64,512]{1,0:T(8,128)S(1)}, f32[64,512]{1,0:T(8,128)S(1)}, u32[]{:S(2)}, u32[]{:S(2)}) collective-permute-start(f32[64,512]{1,0:T(8,128)S(1)} %get-tuple-element.34), channel_id=1, source_target_pairs={{1,0},{0,1},{3,2},{2,3},{5,4},{4,5},{7,6},{6,7},{9,8},{8,9},{11,10... | collective-permute-start | bytes 393224 | tf_op jit(solution)/shard_map/ppermute | solution.py:348
  16.4 1.5 %collective-permute-start.6 = (bf16[64,512]{1,0:T(8,128)(2,1)S(1)}, bf16[64,512]{1,0:T(8,128)(2,1)S(1)}, u32[]{:S(2)}, u32[]{:S(2)}) collective-permute-start(bf16[64,512]{1,0:T(8,128)(2,1)S(1)} %get-tuple-element.47), channel_id=1, source_target_pairs={{1,0},{0,1},{3,2},{2,3},{5,4},{4,5},{7,6},{6,7},{9,8},{8,9},{11,10... | collective-permute-start | bytes 196616 | tf_op jit(solution)/shard_map/ppermute | solution.py:348

commit v25 on v24

--- a/solution.py
+++ b/solution.py
@@ -234,24 +234,26 @@
                 weighted_ref[a, j, g, 1] = local_ref[g, j, 1] * weight
 
 
-def partner_kernel(sizes, weighted_ref, first_ref, second_ref, real_x, imag_x):
+def across_kernel(sizes, weighted_ref, across_ref, real_x, imag_x):
     stations = sizes[0]
+    add_products(
+        stations, stations, 2,
+        lambda n, a: across_ref[n, pl.ds(a * 16, 16), :],
+        None,
+        lambda n, a, j: (weighted_ref[a, j, 2 + n, 0], weighted_ref[a, j, 2 + n, 1]),
+        real_x, imag_x,
+    )
+
+
+def other_block_kernel(
+    sizes, table, weighted_ref, real_ref, imag_ref, first_ref, second_ref, kept_ref, sent_ref, *scratch
+):
+    stations, bands, seg = sizes[:3]
     add_products(
         stations, stations, 2,
         lambda n, a: (first_ref, second_ref)[n][0, pl.ds(a * 16, 16), :],
         None,
         lambda n, a, j: (weighted_ref[a, j, n, 0], weighted_ref[a, j, n, 1]),
-        real_x, imag_x,
-    )
-
-
-def other_block_kernel(sizes, table, weighted_ref, real_ref, imag_ref, across_ref, kept_ref, sent_ref, *scratch):
-    stations, bands, seg = sizes[:3]
-    add_products(
-        stations, stations, 2,
-        lambda n, a: across_ref[n, pl.ds(a * 16, 16), :],
-        None,
-        lambda n, a, j: (weighted_ref[a, j, 2 + n, 0], weighted_ref[a, j, 2 + n, 1]),
         *scratch[:2],
         before=(real_ref, imag_ref),
     )
@@ -322,7 +324,7 @@
         at += count
 
 
-def join(*pieces, rows=None):
+def join(*pieces, rows=None, flops=0):
     pieces = [piece if isinstance(piece, tuple) else (piece, 0, piece.shape[0]) for piece in pieces]
     arrays = [piece[0] for piece in pieces]
     ranges = [piece[1:] for piece in pieces]
@@ -335,6 +337,7 @@
         in_specs=[vmem] * len(arrays),
         out_specs=vmem,
         compiler_params=pltpu.CompilerParams(vmem_limit_bytes=VMEM_BYTES),
+        cost_estimate=pl.CostEstimate(flops=flops, bytes_accessed=0, transcendentals=0),
         name="join",
     )(*arrays)
 
@@ -413,7 +416,7 @@
             ],
             table_const, plan_const, after,
             scratch=[pltpu.SMEM((STEPS,), jnp.int32), pltpu.SemaphoreType.DMA((2,))],
-            flops=4 * quarter, name="fetch",
+            name="fetch",
         )
 
     def products(count):
@@ -431,7 +434,9 @@
         distant, phase = lax.optimization_barrier((distant, phase))
         far = join(own, distant)
         near = exchange(far, "seg", 1)
-        across = fetch_from(far, ("seg", "sta"), lambda z, x: (z ^ 1, x ^ 1))
+        across = fetch_from(
+            join(far, rows=bare, flops=4 * quarter), ("seg", "sta"), lambda z, x: (z ^ 1, x ^ 1)
+        )
         partner_far = exchange(join(distant, rows=bare), "sta", 1)
         table, is_own = fetch(far)
         near, table = lax.optimization_barrier((near, table))
@@ -447,16 +452,16 @@
             flops=8 * quarter, name="weigh",
         )
         own_got = exchange(own_sent, "pol", 1)
-        weighted, partner_own, partner_far = lax.optimization_barrier((weighted, partner_own, partner_far))
+        weighted, across = lax.optimization_barrier((weighted, across))
         partial = call(
-            partner_kernel, [pltpu.VMEM((pairs * 8, LANES), f32)] * 2,
-            weighted, partner_own, partner_far,
-            name="partner",
-        )
-        partial, across = lax.optimization_barrier((partial, across))
+            across_kernel, [pltpu.VMEM((pairs * 8, LANES), f32)] * 2,
+            weighted, across,
+            name="across",
+        )
+        partial, partner_own, partner_far = lax.optimization_barrier((partial, partner_own, partner_far))
         kept, sent = call(
             other_block_kernel, [kept_shape, pltpu.VMEM((pairs, lags), jnp.bfloat16)],
-            table, weighted, *partial, across,
+            table, weighted, *partial, partner_own, partner_far,
             scratch=products(1), name="other_block",
         )
         got = exchange(sent, "pol", 1)

time: 18.9 us -> 18.6 us (0.984)
  starting transfers between devices: 9.85 us -> 9.29 us
  waiting for transfers between devices: 2.59 us -> 2.91 us
    ppermute x7, starting transfers between devices: 9.85 us -> 9.29 us  [fetch_from(): return lax.ppermute(value, axes, pairs)]
    ppermute x7, waiting for transfers between devices: 2.59 us -> 2.91 us  [fetch_from(): return lax.ppermute(value, axes, pairs)]
where the time goes in v25:
time: 18.6 us; the launch traced here: 18.4 us
  starting transfers between devices  9.29 us (50%)
  Pallas kernels  6.1 us (33%)
  waiting for transfers between devices  2.91 us (16%)
    ppermute x7, starting transfers between devices, fetch_from(): return lax.ppermute(value, axes, pairs)  9.29 us
    pallas_call x8, Pallas kernels, call(): pl.pallas_call(functools.partial(kernel, sizes), out_shape=out_shape, in_...  5.16 us
    ppermute x7, waiting for transfers between devices, fetch_from(): return lax.ppermute(value, axes, pairs)  2.91 us
    pallas_call x1, Pallas kernels, shards(): pl.pallas_call(functools.partial(prepare_kernel, (stations, bands, sta, b...  0.91 us
  transfers between devices with their start and end apart: 7, of which 3 were waited for; matrix products, arithmetic and copies ran while one was open for 0% of the time, Pallas kernels for 24%

profile of v25, /device:TPU:0, one launch (start us, length us, event | category | flops | bytes accessed | tf_op | source)
XLA Modules:
  0.0 18.4 jit_solution(6358877320359615736)
XLA Ops:
  0.0 0.9 %prepare.1.after.refs_0_ = bf16[1,144,128]{2,1,0:T(8,128)(2,1)S(1)} custom-call(bf16[128,128]{1,0:T(8,128)(2,1)} %bitcast.9, s32[8,16]{1,0:T(8,128)} %bitcast.10, s32[1,16]{1,0:T(1,128)} %refs_2_.1), custom_call_target="tpu_custom_call" | custom-call | tf_op jit(solution)/shard_map/prepare/pallas_call | solution.py:375
  0.9 4.1 %collective-permute-start = (bf16[1,144,128]{2,1,0:T(8,128)(2,1)S(1)}, bf16[1,144,128]{2,1,0:T(8,128)(2,1)S(1)}, u32[]{:S(2)}, u32[]{:S(2)}) collective-permute-start(bf16[1,144,128]{2,1,0:T(8,128)(2,1)S(1)} %prepare.1.after.refs_0_), channel_id=1, source_target_pairs={{8,0},{12,4},{0,8},{4,12},{9,1},{13,5},{1,9},{5,13},{10,2},{14,6},... | collective-permute-start | bytes 110600 | tf_op jit(solution)/shard_map/ppermute | solution.py:351
  5.0 1.5 %collective-permute-start.4 = (bf16[1,128,128]{2,1,0:T(8,128)(2,1)S(1)}, bf16[1,128,128]{2,1,0:T(8,128)(2,1)S(1)}, u32[]{:S(2)}, u32[]{:S(2)}) collective-permute-start(bf16[1,128,128]{2,1,0:T(8,128)(2,1)S(1)} %join.8), channel_id=1, source_target_pairs={{2,0},{0,2},{3,1},{1,3},{6,4},{4,6},{7,5},{5,7},{10,8},{8,10},{11,... | collective-permute-start | bytes 98312 | tf_op jit(solution)/shard_map/ppermute | solution.py:351
  6.6 0.8 %collective-permute-done.refs_1_.refs_0_ = bf16[1,144,128]{2,1,0:T(8,128)(2,1)S(1)} collective-permute-done((bf16[1,144,128]{2,1,0:T(8,128)(2,1)S(1)}, bf16[1,144,128]{2,1,0:T(8,128)(2,1)S(1)}, u32[]{:S(2)}, u32[]{:S(2)}) %collective-permute-start) | collective-permute-done | bytes 36896 | tf_op jit(solution)/shard_map/ppermute | solution.py:351
  7.4 1.5 %collective-permute-start.1 = (bf16[2,144,128]{2,1,0:T(8,128)(2,1)S(1)}, bf16[2,144,128]{2,1,0:T(8,128)(2,1)S(1)}, u32[]{:S(2)}, u32[]{:S(2)}) collective-permute-start(bf16[2,144,128]{2,1,0:T(8,128)(2,1)S(1)} %join.5.after.refs_0_), channel_id=1, source_target_pairs={{4,0},{0,4},{12,8},{8,12},{5,1},{1,5},{13,9},{9,13},{6,2},{2,6},{1... | collective-permute-start | bytes 221192 | tf_op jit(solution)/shard_map/ppermute | solution.py:351
  8.9 1.6 %collective-permute-start.5 = (bf16[1,128,128]{2,1,0:T(8,128)(2,1)S(1)}, bf16[1,128,128]{2,1,0:T(8,128)(2,1)S(1)}, u32[]{:S(2)}, u32[]{:S(2)}) collective-permute-start(bf16[1,128,128]{2,1,0:T(8,128)(2,1)S(1)} %join.9), channel_id=1, source_target_pairs={{2,0},{0,2},{3,1},{1,3},{6,4},{4,6},{7,5},{5,7},{10,8},{8,10},{11,... | collective-permute-start | bytes 98312 | tf_op jit(solution)/shard_map/ppermute | solution.py:351
  10.4 0.5 %collective-permute-start.3 = (bf16[2,128,128]{2,1,0:T(8,128)(2,1)S(1)}, bf16[2,128,128]{2,1,0:T(8,128)(2,1)S(1)}, u32[]{:S(2)}, u32[]{:S(2)}) collective-permute-start(bf16[2,128,128]{2,1,0:T(8,128)(2,1)S(1)} %join.7), channel_id=1, source_target_pairs={{6,0},{4,2},{2,4},{0,6},{14,8},{12,10},{10,12},{8,14},{7,1},{5,3},... | collective-permute-start | bytes 196616 | tf_op jit(solution)/shard_map/ppermute | solution.py:351
  10.9 1.6 %fetch.1 = (bf16[2,1024,512]{2,1,0:T(8,128)(2,1)S(1)}, s32[3]{0:T(128)S(4)}) custom-call(bf16[2,2,1024,512]{3,2,1,0:T(8,128)(2,1)} %constant.2.clone.table_hbm, s32[3]{0:T(128)} %plan_any.1, bf16[2,144,128]{2,1,0:T(8,128)(2,1)S(1)} %join.5.after.refs_0_), custom_call_target="tpu_custom_call" | custom-call | tf_op jit(solution)/shard_map/fetch/pallas_call | solution.py:392
  12.5 0.0 collective-permute-done.1.refs_1_
  12.6 1.1 %own_block.1 = (f32[64,512]{1,0:T(8,128)S(1)}, f32[64,512]{1,0:T(8,128)S(1)}, f32[4,8,2,8,128]{4,3,2,1,0:T(8,128)S(1)}, f32[4,128,128]{2,1,0:T(8,128)S(1)}) custom-call(bf16[2,1024,512]{2,1,0:T(8,128)(2,1)S(1)} %get-tuple-element.30.table, f32[2,8,128]{2,1,0:T(8,128)S(1)} %phase.1, bf16[4,144,128]{2,1,0:T(8,128)(2,1)S(1)} %join.6.mine_ref), custom_call_target="tpu_custom_call" | custom-call | flops 17179869184 | tf_op jit(solution)/shard_map/own_block/pallas_call | solution.py:392
  13.7 0.1 collective-permute-start.2
  13.8 0.2 weigh.1.weighted_ref
  13.9 1.7 %collective-permute-done.3.across_ref = bf16[2,128,128]{2,1,0:T(8,128)(2,1)S(1)} collective-permute-done((bf16[2,128,128]{2,1,0:T(8,128)(2,1)S(1)}, bf16[2,128,128]{2,1,0:T(8,128)(2,1)S(1)}, u32[]{:S(2)}, u32[]{:S(2)}) %collective-permute-start.3) | collective-permute-done | bytes 65568 | tf_op jit(solution)/shard_map/ppermute | solution.py:351
  15.6 0.1 across.1
  15.7 0.0 collective-permute-done.4.first_ref
  15.7 0.0 collective-permute-done.5.second_ref
  15.8 0.6 %other_block.1 = (f32[64,512]{1,0:T(8,128)S(1)}, bf16[64,512]{1,0:T(8,128)(2,1)S(1)}) custom-call(bf16[2,1024,512]{2,1,0:T(8,128)(2,1)S(1)} %get-tuple-element.30.table, f32[8,8,4,2,8,128]{5,4,3,2,1,0:T(8,128)S(1)} %weigh.1.weighted_ref, f32[512,128]{1,0:T(8,128)S(1)} %get-tuple-element.41.real_ref, f32[512,128]{1,0:T(8,128)S(1)} %get-tuple-element.42.imag_ref, ...), custom_call_target="tpu_custom_call" | custom-call | tf_op jit(solution)/shard_map/other_block/pallas_call | solution.py:392
  16.4 0.1 collective-permute-start.6
  16.5 0.0 collective-permute-done.2.own_got_ref
  16.5 0.8 %settle.1 = (f32[3,64,512]{2,1,0:T(8,128)}, f32[64,512]{1,0:T(8,128)S(1)}) custom-call(f32[64,512]{1,0:T(8,128)S(1)} %get-tuple-element.33.own_kept_ref, f32[64,512]{1,0:T(8,128)S(1)} %collective-permute-done.2.own_got_ref, f32[64,512]{1,0:T(8,128)S(1)} %get-tuple-element.45.kept_ref), custom_call_target="tpu_custom_call" | custom-call | tf_op jit(solution)/shard_map/settle/pallas_call | solution.py:392
  17.3 0.4 %collective-permute-done.6.got_ref = bf16[64,512]{1,0:T(8,128)(2,1)S(1)} collective-permute-done((bf16[64,512]{1,0:T(8,128)(2,1)S(1)}, bf16[64,512]{1,0:T(8,128)(2,1)S(1)}, u32[]{:S(2)}, u32[]{:S(2)}) %collective-permute-start.6) | collective-permute-done | bytes 65568 | tf_op jit(solution)/shard_map/ppermute | solution.py:351
  17.7 0.7 %place.1 = f32[3,64,512]{2,1,0:T(8,128)} custom-call(s32[3]{0:T(128)S(4)} %get-tuple-element.28.is_own_ref, f32[64,512]{1,0:T(8,128)S(1)} %get-tuple-element.46.kept_ref, bf16[64,512]{1,0:T(8,128)(2,1)S(1)} %collective-permute-done.6.got_ref, f32[3,64,512]{2,1,0:T(8,128)} %get-tuple-element.48.steps_ref), custom_call_target="tpu_custom_call", output_to_operand_aliasing={{}: (3, {})} | custom-call | tf_op jit(solution)/shard_map/place/pallas_call | solution.py:392
  (6 shorter events, 0.1 us)
Async XLA Ops:
  0.9 6.4 %collective-permute-start = (bf16[1,144,128]{2,1,0:T(8,128)(2,1)S(1)}, bf16[1,144,128]{2,1,0:T(8,128)(2,1)S(1)}, u32[]{:S(2)}, u32[]{:S(2)}) collective-permute-start(bf16[1,144,128]{2,1,0:T(8,128)(2,1)S(1)} %prepare.1.after.refs_0_), channel_id=1, source_target_pairs={{8,0},{12,4},{0,8},{4,12},{9,1},{13,5},{1,9},{5,13},{10,2},{14,6},... | collective-permute-start | bytes 110600 | tf_op jit(solution)/shard_map/ppermute | solution.py:351
  5.0 10.7 %collective-permute-start.4 = (bf16[1,128,128]{2,1,0:T(8,128)(2,1)S(1)}, bf16[1,128,128]{2,1,0:T(8,128)(2,1)S(1)}, u32[]{:S(2)}, u32[]{:S(2)}) collective-permute-start(bf16[1,128,128]{2,1,0:T(8,128)(2,1)S(1)} %join.8), channel_id=1, source_target_pairs={{2,0},{0,2},{3,1},{1,3},{6,4},{4,6},{7,5},{5,7},{10,8},{8,10},{11,... | collective-permute-start | bytes 98312 | tf_op jit(solution)/shard_map/ppermute | solution.py:351
  7.4 5.2 %collective-permute-start.1 = (bf16[2,144,128]{2,1,0:T(8,128)(2,1)S(1)}, bf16[2,144,128]{2,1,0:T(8,128)(2,1)S(1)}, u32[]{:S(2)}, u32[]{:S(2)}) collective-permute-start(bf16[2,144,128]{2,1,0:T(8,128)(2,1)S(1)} %join.5.after.refs_0_), channel_id=1, source_target_pairs={{4,0},{0,4},{12,8},{8,12},{5,1},{1,5},{13,9},{9,13},{6,2},{2,6},{1... | collective-permute-start | bytes 221192 | tf_op jit(solution)/shard_map/ppermute | solution.py:351
  8.9 6.9 %collective-permute-start.5 = (bf16[1,128,128]{2,1,0:T(8,128)(2,1)S(1)}, bf16[1,128,128]{2,1,0:T(8,128)(2,1)S(1)}, u32[]{:S(2)}, u32[]{:S(2)}) collective-permute-start(bf16[1,128,128]{2,1,0:T(8,128)(2,1)S(1)} %join.9), channel_id=1, source_target_pairs={{2,0},{0,2},{3,1},{1,3},{6,4},{4,6},{7,5},{5,7},{10,8},{8,10},{11,... | collective-permute-start | bytes 98312 | tf_op jit(solution)/shard_map/ppermute | solution.py:351
  10.4 5.2 %collective-permute-start.3 = (bf16[2,128,128]{2,1,0:T(8,128)(2,1)S(1)}, bf16[2,128,128]{2,1,0:T(8,128)(2,1)S(1)}, u32[]{:S(2)}, u32[]{:S(2)}) collective-permute-start(bf16[2,128,128]{2,1,0:T(8,128)(2,1)S(1)} %join.7), channel_id=1, source_target_pairs={{6,0},{4,2},{2,4},{0,6},{14,8},{12,10},{10,12},{8,14},{7,1},{5,3},... | collective-permute-start | bytes 196616 | tf_op jit(solution)/shard_map/ppermute | solution.py:351
  13.7 2.8 %collective-permute-start.2 = (f32[64,512]{1,0:T(8,128)S(1)}, f32[64,512]{1,0:T(8,128)S(1)}, u32[]{:S(2)}, u32[]{:S(2)}) collective-permute-start(f32[64,512]{1,0:T(8,128)S(1)} %get-tuple-element.34), channel_id=1, source_target_pairs={{1,0},{0,1},{3,2},{2,3},{5,4},{4,5},{7,6},{6,7},{9,8},{8,9},{11,10... | collective-permute-start | bytes 393224 | tf_op jit(solution)/shard_map/ppermute | solution.py:351
  16.4 1.3 %collective-permute-start.6 = (bf16[64,512]{1,0:T(8,128)(2,1)S(1)}, bf16[64,512]{1,0:T(8,128)(2,1)S(1)}, u32[]{:S(2)}, u32[]{:S(2)}) collective-permute-start(bf16[64,512]{1,0:T(8,128)(2,1)S(1)} %get-tuple-element.47), channel_id=1, source_target_pairs={{1,0},{0,1},{3,2},{2,3},{5,4},{4,5},{7,6},{6,7},{9,8},{8,9},{11,10... | collective-permute-start | bytes 196616 | tf_op jit(solution)/shard_map/ppermute | solution.py:351

commit v26 on v25

--- a/solution.py
+++ b/solution.py
@@ -434,10 +434,9 @@
         distant, phase = lax.optimization_barrier((distant, phase))
         far = join(own, distant)
         near = exchange(far, "seg", 1)
-        across = fetch_from(
-            join(far, rows=bare, flops=4 * quarter), ("seg", "sta"), lambda z, x: (z ^ 1, x ^ 1)
-        )
-        partner_far = exchange(join(distant, rows=bare), "sta", 1)
+        far_bare = join(far, rows=bare, flops=4 * quarter)
+        across = fetch_from(far_bare, ("seg", "sta"), lambda z, x: (z ^ 1, x ^ 1))
+        partner_far = exchange(join((far_bare, 1, 1)), "sta", 1)
         table, is_own = fetch(far)
         near, table = lax.optimization_barrier((near, table))
         mine = join(far, near)

time: 18.6 us -> 17.4 us (0.935)
  waiting for transfers between devices: 2.91 us -> 1.54 us
    ppermute x7, waiting for transfers between devices: 2.91 us -> 1.54 us  [fetch_from(): return lax.ppermute(value, axes, pairs)]
  transfers between devices with their start and end apart: 7 -> 7, of which waited for: 3 -> 4; matrix products, arithmetic and copies ran while one was open for 0% -> 0% of each run, Pallas kernels for 24% -> 26%
where the time goes in v26:
time: 17.4 us; the launch traced here: 17.2 us
  starting transfers between devices  9.45 us (54%)
  Pallas kernels  6.09 us (35%)
  waiting for transfers between devices  1.54 us (9%)
    ppermute x7, starting transfers between devices, fetch_from(): return lax.ppermute(value, axes, pairs)  9.45 us
    pallas_call x8, Pallas kernels, call(): pl.pallas_call(functools.partial(kernel, sizes), out_shape=out_shape, in_...  5.15 us
    ppermute x7, waiting for transfers between devices, fetch_from(): return lax.ppermute(value, axes, pairs)  1.54 us
    pallas_call x1, Pallas kernels, shards(): pl.pallas_call(functools.partial(prepare_kernel, (stations, bands, sta, b...  0.91 us
  transfers between devices with their start and end apart: 7, of which 4 were waited for; matrix products, arithmetic and copies ran while one was open for 0% of the time, Pallas kernels for 26%

profile of v26, /device:TPU:0, one launch (start us, length us, event | category | flops | bytes accessed | tf_op | source)
XLA Modules:
  0.0 17.2 jit_solution(11162605385583418571)
XLA Ops:
  0.0 0.9 %prepare.1.after.refs_0_ = bf16[1,144,128]{2,1,0:T(8,128)(2,1)S(1)} custom-call(bf16[128,128]{1,0:T(8,128)(2,1)} %bitcast.9, s32[8,16]{1,0:T(8,128)} %bitcast.10, s32[1,16]{1,0:T(1,128)} %refs_2_.1), custom_call_target="tpu_custom_call" | custom-call | tf_op jit(solution)/shard_map/prepare/pallas_call | solution.py:375
  0.9 4.1 %collective-permute-start = (bf16[1,144,128]{2,1,0:T(8,128)(2,1)S(1)}, bf16[1,144,128]{2,1,0:T(8,128)(2,1)S(1)}, u32[]{:S(2)}, u32[]{:S(2)}) collective-permute-start(bf16[1,144,128]{2,1,0:T(8,128)(2,1)S(1)} %prepare.1.after.refs_0_), channel_id=1, source_target_pairs={{8,0},{12,4},{0,8},{4,12},{9,1},{13,5},{1,9},{5,13},{10,2},{14,6},... | collective-permute-start | bytes 110600 | tf_op jit(solution)/shard_map/ppermute | solution.py:351
  5.0 1.5 %collective-permute-start.4 = (bf16[1,128,128]{2,1,0:T(8,128)(2,1)S(1)}, bf16[1,128,128]{2,1,0:T(8,128)(2,1)S(1)}, u32[]{:S(2)}, u32[]{:S(2)}) collective-permute-start(bf16[1,128,128]{2,1,0:T(8,128)(2,1)S(1)} %join.8), channel_id=1, source_target_pairs={{2,0},{0,2},{3,1},{1,3},{6,4},{4,6},{7,5},{5,7},{10,8},{8,10},{11,... | collective-permute-start | bytes 98312 | tf_op jit(solution)/shard_map/ppermute | solution.py:351
  6.6 0.8 %collective-permute-done.refs_1_ = bf16[1,144,128]{2,1,0:T(8,128)(2,1)S(1)} collective-permute-done((bf16[1,144,128]{2,1,0:T(8,128)(2,1)S(1)}, bf16[1,144,128]{2,1,0:T(8,128)(2,1)S(1)}, u32[]{:S(2)}, u32[]{:S(2)}) %collective-permute-start) | collective-permute-done | bytes 36896 | tf_op jit(solution)/shard_map/ppermute | solution.py:351
  7.4 1.5 %collective-permute-start.1 = (bf16[2,144,128]{2,1,0:T(8,128)(2,1)S(1)}, bf16[2,144,128]{2,1,0:T(8,128)(2,1)S(1)}, u32[]{:S(2)}, u32[]{:S(2)}) collective-permute-start(bf16[2,144,128]{2,1,0:T(8,128)(2,1)S(1)} %join.5.after.refs_0_), channel_id=1, source_target_pairs={{4,0},{0,4},{12,8},{8,12},{5,1},{1,5},{13,9},{9,13},{6,2},{2,6},{1... | collective-permute-start | bytes 221192 | tf_op jit(solution)/shard_map/ppermute | solution.py:351
  8.9 1.7 %collective-permute-start.3 = (bf16[2,128,128]{2,1,0:T(8,128)(2,1)S(1)}, bf16[2,128,128]{2,1,0:T(8,128)(2,1)S(1)}, u32[]{:S(2)}, u32[]{:S(2)}) collective-permute-start(bf16[2,128,128]{2,1,0:T(8,128)(2,1)S(1)} %join.7.refs_0_), channel_id=1, source_target_pairs={{6,0},{4,2},{2,4},{0,6},{14,8},{12,10},{10,12},{8,14},{7,1},{5,3},... | collective-permute-start | bytes 196616 | tf_op jit(solution)/shard_map/ppermute | solution.py:351
  10.6 0.3 %collective-permute-start.5 = (bf16[1,128,128]{2,1,0:T(8,128)(2,1)S(1)}, bf16[1,128,128]{2,1,0:T(8,128)(2,1)S(1)}, u32[]{:S(2)}, u32[]{:S(2)}) collective-permute-start(bf16[1,128,128]{2,1,0:T(8,128)(2,1)S(1)} %join.9), channel_id=1, source_target_pairs={{2,0},{0,2},{3,1},{1,3},{6,4},{4,6},{7,5},{5,7},{10,8},{8,10},{11,... | collective-permute-start | bytes 98312 | tf_op jit(solution)/shard_map/ppermute | solution.py:351
  10.9 1.6 %fetch.1 = (bf16[2,1024,512]{2,1,0:T(8,128)(2,1)S(1)}, s32[3]{0:T(128)S(4)}) custom-call(bf16[2,2,1024,512]{3,2,1,0:T(8,128)(2,1)} %constant.2.clone.table_hbm, s32[3]{0:T(128)} %plan_any.1, bf16[2,144,128]{2,1,0:T(8,128)(2,1)S(1)} %join.5.after.refs_0_), custom_call_target="tpu_custom_call" | custom-call | tf_op jit(solution)/shard_map/fetch/pallas_call | solution.py:392
  12.5 0.0 collective-permute-done.1.refs_1_
  12.6 1.1 %own_block.1 = (f32[64,512]{1,0:T(8,128)S(1)}, f32[64,512]{1,0:T(8,128)S(1)}, f32[4,8,2,8,128]{4,3,2,1,0:T(8,128)S(1)}, f32[4,128,128]{2,1,0:T(8,128)S(1)}) custom-call(bf16[2,1024,512]{2,1,0:T(8,128)(2,1)S(1)} %get-tuple-element.30.table, f32[2,8,128]{2,1,0:T(8,128)S(1)} %phase.1, bf16[4,144,128]{2,1,0:T(8,128)(2,1)S(1)} %join.6.mine_ref), custom_call_target="tpu_custom_call" | custom-call | flops 17179869184 | tf_op jit(solution)/shard_map/own_block/pallas_call | solution.py:392
  13.7 0.1 collective-permute-start.2
  13.8 0.2 weigh.1.weighted_ref
  13.9 0.2 %collective-permute-done.3.across_ref = bf16[2,128,128]{2,1,0:T(8,128)(2,1)S(1)} collective-permute-done((bf16[2,128,128]{2,1,0:T(8,128)(2,1)S(1)}, bf16[2,128,128]{2,1,0:T(8,128)(2,1)S(1)}, u32[]{:S(2)}, u32[]{:S(2)}) %collective-permute-start.3) | collective-permute-done | bytes 65568 | tf_op jit(solution)/shard_map/ppermute | solution.py:351
  14.1 0.1 across.1
  14.2 0.0 collective-permute-done.4.first_ref
  14.3 0.3 %collective-permute-done.5.second_ref = bf16[1,128,128]{2,1,0:T(8,128)(2,1)S(1)} collective-permute-done((bf16[1,128,128]{2,1,0:T(8,128)(2,1)S(1)}, bf16[1,128,128]{2,1,0:T(8,128)(2,1)S(1)}, u32[]{:S(2)}, u32[]{:S(2)}) %collective-permute-start.5) | collective-permute-done | bytes 32800 | tf_op jit(solution)/shard_map/ppermute | solution.py:351
  14.5 0.6 %other_block.1 = (f32[64,512]{1,0:T(8,128)S(1)}, bf16[64,512]{1,0:T(8,128)(2,1)S(1)}) custom-call(bf16[2,1024,512]{2,1,0:T(8,128)(2,1)S(1)} %get-tuple-element.30.table, f32[8,8,4,2,8,128]{5,4,3,2,1,0:T(8,128)S(1)} %weigh.1.weighted_ref, f32[512,128]{1,0:T(8,128)S(1)} %get-tuple-element.41.real_ref, f32[512,128]{1,0:T(8,128)S(1)} %get-tuple-element.42.imag_ref, ...), custom_call_target="tpu_custom_call" | custom-call | tf_op jit(solution)/shard_map/other_block/pallas_call | solution.py:392
  15.1 0.2 %collective-permute-start.6 = (bf16[64,512]{1,0:T(8,128)(2,1)S(1)}, bf16[64,512]{1,0:T(8,128)(2,1)S(1)}, u32[]{:S(2)}, u32[]{:S(2)}) collective-permute-start(bf16[64,512]{1,0:T(8,128)(2,1)S(1)} %get-tuple-element.47), channel_id=1, source_target_pairs={{1,0},{0,1},{3,2},{2,3},{5,4},{4,5},{7,6},{6,7},{9,8},{8,9},{11,10... | collective-permute-start | bytes 196616 | tf_op jit(solution)/shard_map/ppermute | solution.py:351
  15.4 0.0 collective-permute-done.2.own_got_ref
  15.4 0.8 %settle.1 = (f32[3,64,512]{2,1,0:T(8,128)}, f32[64,512]{1,0:T(8,128)S(1)}) custom-call(f32[64,512]{1,0:T(8,128)S(1)} %get-tuple-element.33.own_kept_ref, f32[64,512]{1,0:T(8,128)S(1)} %collective-permute-done.2.own_got_ref, f32[64,512]{1,0:T(8,128)S(1)} %get-tuple-element.45.kept_ref), custom_call_target="tpu_custom_call" | custom-call | tf_op jit(solution)/shard_map/settle/pallas_call | solution.py:392
  16.2 0.3 %collective-permute-done.6.got_ref = bf16[64,512]{1,0:T(8,128)(2,1)S(1)} collective-permute-done((bf16[64,512]{1,0:T(8,128)(2,1)S(1)}, bf16[64,512]{1,0:T(8,128)(2,1)S(1)}, u32[]{:S(2)}, u32[]{:S(2)}) %collective-permute-start.6) | collective-permute-done | bytes 65568 | tf_op jit(solution)/shard_map/ppermute | solution.py:351
  16.5 0.7 %place.1 = f32[3,64,512]{2,1,0:T(8,128)} custom-call(s32[3]{0:T(128)S(4)} %get-tuple-element.28.is_own_ref, f32[64,512]{1,0:T(8,128)S(1)} %get-tuple-element.46.kept_ref, bf16[64,512]{1,0:T(8,128)(2,1)S(1)} %collective-permute-done.6.got_ref, f32[3,64,512]{2,1,0:T(8,128)} %get-tuple-element.48.steps_ref), custom_call_target="tpu_custom_call", output_to_operand_aliasing={{}: (3, {})} | custom-call | tf_op jit(solution)/shard_map/place/pallas_call | solution.py:392
  (6 shorter events, 0.1 us)
Async XLA Ops:
  0.9 6.4 %collective-permute-start = (bf16[1,144,128]{2,1,0:T(8,128)(2,1)S(1)}, bf16[1,144,128]{2,1,0:T(8,128)(2,1)S(1)}, u32[]{:S(2)}, u32[]{:S(2)}) collective-permute-start(bf16[1,144,128]{2,1,0:T(8,128)(2,1)S(1)} %prepare.1.after.refs_0_), channel_id=1, source_target_pairs={{8,0},{12,4},{0,8},{4,12},{9,1},{13,5},{1,9},{5,13},{10,2},{14,6},... | collective-permute-start | bytes 110600 | tf_op jit(solution)/shard_map/ppermute | solution.py:351
  5.0 9.2 %collective-permute-start.4 = (bf16[1,128,128]{2,1,0:T(8,128)(2,1)S(1)}, bf16[1,128,128]{2,1,0:T(8,128)(2,1)S(1)}, u32[]{:S(2)}, u32[]{:S(2)}) collective-permute-start(bf16[1,128,128]{2,1,0:T(8,128)(2,1)S(1)} %join.8), channel_id=1, source_target_pairs={{2,0},{0,2},{3,1},{1,3},{6,4},{4,6},{7,5},{5,7},{10,8},{8,10},{11,... | collective-permute-start | bytes 98312 | tf_op jit(solution)/shard_map/ppermute | solution.py:351
  7.4 5.2 %collective-permute-start.1 = (bf16[2,144,128]{2,1,0:T(8,128)(2,1)S(1)}, bf16[2,144,128]{2,1,0:T(8,128)(2,1)S(1)}, u32[]{:S(2)}, u32[]{:S(2)}) collective-permute-start(bf16[2,144,128]{2,1,0:T(8,128)(2,1)S(1)} %join.5.after.refs_0_), channel_id=1, source_target_pairs={{4,0},{0,4},{12,8},{8,12},{5,1},{1,5},{13,9},{9,13},{6,2},{2,6},{1... | collective-permute-start | bytes 221192 | tf_op jit(solution)/shard_map/ppermute | solution.py:351
  8.9 5.2 %collective-permute-start.3 = (bf16[2,128,128]{2,1,0:T(8,128)(2,1)S(1)}, bf16[2,128,128]{2,1,0:T(8,128)(2,1)S(1)}, u32[]{:S(2)}, u32[]{:S(2)}) collective-permute-start(bf16[2,128,128]{2,1,0:T(8,128)(2,1)S(1)} %join.7.refs_0_), channel_id=1, source_target_pairs={{6,0},{4,2},{2,4},{0,6},{14,8},{12,10},{10,12},{8,14},{7,1},{5,3},... | collective-permute-start | bytes 196616 | tf_op jit(solution)/shard_map/ppermute | solution.py:351
  10.6 3.9 %collective-permute-start.5 = (bf16[1,128,128]{2,1,0:T(8,128)(2,1)S(1)}, bf16[1,128,128]{2,1,0:T(8,128)(2,1)S(1)}, u32[]{:S(2)}, u32[]{:S(2)}) collective-permute-start(bf16[1,128,128]{2,1,0:T(8,128)(2,1)S(1)} %join.9), channel_id=1, source_target_pairs={{2,0},{0,2},{3,1},{1,3},{6,4},{4,6},{7,5},{5,7},{10,8},{8,10},{11,... | collective-permute-start | bytes 98312 | tf_op jit(solution)/shard_map/ppermute | solution.py:351
  13.7 1.7 %collective-permute-start.2 = (f32[64,512]{1,0:T(8,128)S(1)}, f32[64,512]{1,0:T(8,128)S(1)}, u32[]{:S(2)}, u32[]{:S(2)}) collective-permute-start(f32[64,512]{1,0:T(8,128)S(1)} %get-tuple-element.34), channel_id=1, source_target_pairs={{1,0},{0,1},{3,2},{2,3},{5,4},{4,5},{7,6},{6,7},{9,8},{8,9},{11,10... | collective-permute-start | bytes 393224 | tf_op jit(solution)/shard_map/ppermute | solution.py:351
  15.1 1.3 %collective-permute-start.6 = (bf16[64,512]{1,0:T(8,128)(2,1)S(1)}, bf16[64,512]{1,0:T(8,128)(2,1)S(1)}, u32[]{:S(2)}, u32[]{:S(2)}) collective-permute-start(bf16[64,512]{1,0:T(8,128)(2,1)S(1)} %get-tuple-element.47), channel_id=1, source_target_pairs={{1,0},{0,1},{3,2},{2,3},{5,4},{4,5},{7,6},{6,7},{9,8},{8,9},{11,10... | collective-permute-start | bytes 196616 | tf_op jit(solution)/shard_map/ppermute | solution.py:351

commit v27 on v26

--- a/solution.py
+++ b/solution.py
@@ -234,26 +234,26 @@
                 weighted_ref[a, j, g, 1] = local_ref[g, j, 1] * weight
 
 
-def across_kernel(sizes, weighted_ref, across_ref, real_x, imag_x):
+def across_kernel(sizes, weighted_ref, first_ref, across_ref, real_x, imag_x):
     stations = sizes[0]
     add_products(
-        stations, stations, 2,
-        lambda n, a: across_ref[n, pl.ds(a * 16, 16), :],
+        stations, stations, 3,
+        lambda n, a: (across_ref[n - 1] if n else first_ref[0])[a * 16 : a * 16 + 16],
         None,
-        lambda n, a, j: (weighted_ref[a, j, 2 + n, 0], weighted_ref[a, j, 2 + n, 1]),
+        lambda n, a, j: (weighted_ref[a, j, n + (n > 0), 0], weighted_ref[a, j, n + (n > 0), 1]),
         real_x, imag_x,
     )
 
 
 def other_block_kernel(
-    sizes, table, weighted_ref, real_ref, imag_ref, first_ref, second_ref, kept_ref, sent_ref, *scratch
+    sizes, table, weighted_ref, real_ref, imag_ref, second_ref, kept_ref, sent_ref, *scratch
 ):
     stations, bands, seg = sizes[:3]
     add_products(
-        stations, stations, 2,
-        lambda n, a: (first_ref, second_ref)[n][0, pl.ds(a * 16, 16), :],
+        stations, stations, 1,
+        lambda n, a: second_ref[0, pl.ds(a * 16, 16), :],
         None,
-        lambda n, a, j: (weighted_ref[a, j, n, 0], weighted_ref[a, j, n, 1]),
+        lambda n, a, j: (weighted_ref[a, j, 1, 0], weighted_ref[a, j, 1, 1]),
         *scratch[:2],
         before=(real_ref, imag_ref),
     )
@@ -451,16 +451,16 @@
             flops=8 * quarter, name="weigh",
         )
         own_got = exchange(own_sent, "pol", 1)
-        weighted, across = lax.optimization_barrier((weighted, across))
+        weighted, across, partner_own = lax.optimization_barrier((weighted, across, partner_own))
         partial = call(
             across_kernel, [pltpu.VMEM((pairs * 8, LANES), f32)] * 2,
-            weighted, across,
+            weighted, partner_own, across,
             name="across",
         )
-        partial, partner_own, partner_far = lax.optimization_barrier((partial, partner_own, partner_far))
+        partial, partner_far = lax.optimization_barrier((partial, partner_far))
         kept, sent = call(
             other_block_kernel, [kept_shape, pltpu.VMEM((pairs, lags), jnp.bfloat16)],
-            table, weighted, *partial, partner_own, partner_far,
+            table, weighted, *partial, partner_far,
             scratch=products(1), name="other_block",
         )
         got = exchange(sent, "pol", 1)

time: 17.4 us -> 17.3 us (level)
  no operation moved by 1% of the time
where the time goes in v27:
time: 17.3 us; the launch traced here: 17.1 us
  starting transfers between devices  9.52 us (55%)
  Pallas kernels  6.12 us (35%)
  waiting for transfers between devices  1.39 us (8%)
    ppermute x7, starting transfers between devices, fetch_from(): return lax.ppermute(value, axes, pairs)  9.52 us
    pallas_call x8, Pallas kernels, call(): pl.pallas_call(functools.partial(kernel, sizes), out_shape=out_shape, in_...  5.18 us
    ppermute x7, waiting for transfers between devices, fetch_from(): return lax.ppermute(value, axes, pairs)  1.39 us
    pallas_call x1, Pallas kernels, shards(): pl.pallas_call(functools.partial(prepare_kernel, (stations, bands, sta, b...  0.91 us
  transfers between devices with their start and end apart: 7, of which 4 were waited for; matrix products, arithmetic and copies ran while one was open for 0% of the time, Pallas kernels for 26%

profile of v27, /device:TPU:0, one launch (start us, length us, event | category | flops | bytes accessed | tf_op | source)
XLA Modules:
  0.0 17.1 jit_solution(14270924065807079962)
XLA Ops:
  0.0 0.9 %prepare.1.after.refs_0_ = bf16[1,144,128]{2,1,0:T(8,128)(2,1)S(1)} custom-call(bf16[128,128]{1,0:T(8,128)(2,1)} %bitcast.9, s32[8,16]{1,0:T(8,128)} %bitcast.10, s32[1,16]{1,0:T(1,128)} %refs_2_.1), custom_call_target="tpu_custom_call" | custom-call | tf_op jit(solution)/shard_map/prepare/pallas_call | solution.py:375
  0.9 4.1 %collective-permute-start = (bf16[1,144,128]{2,1,0:T(8,128)(2,1)S(1)}, bf16[1,144,128]{2,1,0:T(8,128)(2,1)S(1)}, u32[]{:S(2)}, u32[]{:S(2)}) collective-permute-start(bf16[1,144,128]{2,1,0:T(8,128)(2,1)S(1)} %prepare.1.after.refs_0_), channel_id=1, source_target_pairs={{8,0},{12,4},{0,8},{4,12},{9,1},{13,5},{1,9},{5,13},{10,2},{14,6},... | collective-permute-start | bytes 110600 | tf_op jit(solution)/shard_map/ppermute | solution.py:351
  5.0 1.5 %collective-permute-start.4 = (bf16[1,128,128]{2,1,0:T(8,128)(2,1)S(1)}, bf16[1,128,128]{2,1,0:T(8,128)(2,1)S(1)}, u32[]{:S(2)}, u32[]{:S(2)}) collective-permute-start(bf16[1,128,128]{2,1,0:T(8,128)(2,1)S(1)} %join.8), channel_id=1, source_target_pairs={{2,0},{0,2},{3,1},{1,3},{6,4},{4,6},{7,5},{5,7},{10,8},{8,10},{11,... | collective-permute-start | bytes 98312 | tf_op jit(solution)/shard_map/ppermute | solution.py:351
  6.6 0.8 %collective-permute-done.refs_1_ = bf16[1,144,128]{2,1,0:T(8,128)(2,1)S(1)} collective-permute-done((bf16[1,144,128]{2,1,0:T(8,128)(2,1)S(1)}, bf16[1,144,128]{2,1,0:T(8,128)(2,1)S(1)}, u32[]{:S(2)}, u32[]{:S(2)}) %collective-permute-start) | collective-permute-done | bytes 36896 | tf_op jit(solution)/shard_map/ppermute | solution.py:351
  7.4 1.5 %collective-permute-start.1 = (bf16[2,144,128]{2,1,0:T(8,128)(2,1)S(1)}, bf16[2,144,128]{2,1,0:T(8,128)(2,1)S(1)}, u32[]{:S(2)}, u32[]{:S(2)}) collective-permute-start(bf16[2,144,128]{2,1,0:T(8,128)(2,1)S(1)} %join.5.after.refs_0_), channel_id=1, source_target_pairs={{4,0},{0,4},{12,8},{8,12},{5,1},{1,5},{13,9},{9,13},{6,2},{2,6},{1... | collective-permute-start | bytes 221192 | tf_op jit(solution)/shard_map/ppermute | solution.py:351
  8.9 1.7 %collective-permute-start.3 = (bf16[2,128,128]{2,1,0:T(8,128)(2,1)S(1)}, bf16[2,128,128]{2,1,0:T(8,128)(2,1)S(1)}, u32[]{:S(2)}, u32[]{:S(2)}) collective-permute-start(bf16[2,128,128]{2,1,0:T(8,128)(2,1)S(1)} %join.7.refs_0_), channel_id=1, source_target_pairs={{6,0},{4,2},{2,4},{0,6},{14,8},{12,10},{10,12},{8,14},{7,1},{5,3},... | collective-permute-start | bytes 196616 | tf_op jit(solution)/shard_map/ppermute | solution.py:351
  10.6 0.3 %collective-permute-start.5 = (bf16[1,128,128]{2,1,0:T(8,128)(2,1)S(1)}, bf16[1,128,128]{2,1,0:T(8,128)(2,1)S(1)}, u32[]{:S(2)}, u32[]{:S(2)}) collective-permute-start(bf16[1,128,128]{2,1,0:T(8,128)(2,1)S(1)} %join.9), channel_id=1, source_target_pairs={{2,0},{0,2},{3,1},{1,3},{6,4},{4,6},{7,5},{5,7},{10,8},{8,10},{11,... | collective-permute-start | bytes 98312 | tf_op jit(solution)/shard_map/ppermute | solution.py:351
  10.9 1.6 %fetch.1 = (bf16[2,1024,512]{2,1,0:T(8,128)(2,1)S(1)}, s32[3]{0:T(128)S(4)}) custom-call(bf16[2,2,1024,512]{3,2,1,0:T(8,128)(2,1)} %constant.2.clone.table_hbm, s32[3]{0:T(128)} %plan_any.1, bf16[2,144,128]{2,1,0:T(8,128)(2,1)S(1)} %join.5.after.refs_0_), custom_call_target="tpu_custom_call" | custom-call | tf_op jit(solution)/shard_map/fetch/pallas_call | solution.py:392
  12.5 0.0 collective-permute-done.1.refs_1_
  12.6 1.1 %own_block.1 = (f32[64,512]{1,0:T(8,128)S(1)}, f32[64,512]{1,0:T(8,128)S(1)}, f32[4,8,2,8,128]{4,3,2,1,0:T(8,128)S(1)}, f32[4,128,128]{2,1,0:T(8,128)S(1)}) custom-call(bf16[2,1024,512]{2,1,0:T(8,128)(2,1)S(1)} %get-tuple-element.30.table, f32[2,8,128]{2,1,0:T(8,128)S(1)} %phase.1, bf16[4,144,128]{2,1,0:T(8,128)(2,1)S(1)} %join.6.mine_ref), custom_call_target="tpu_custom_call" | custom-call | flops 17179869184 | tf_op jit(solution)/shard_map/own_block/pallas_call | solution.py:392
  13.7 0.1 collective-permute-start.2
  13.8 0.2 weigh.1.weighted_ref
  13.9 0.0 collective-permute-done.4.first_ref
  13.9 0.2 collective-permute-done.3.across_ref
  14.1 0.2 %across.1 = (f32[512,128]{1,0:T(8,128)S(1)}, f32[512,128]{1,0:T(8,128)S(1)}) custom-call(f32[8,8,4,2,8,128]{5,4,3,2,1,0:T(8,128)S(1)} %weigh.1.weighted_ref, bf16[1,128,128]{2,1,0:T(8,128)(2,1)S(1)} %collective-permute-done.4.first_ref, bf16[2,128,128]{2,1,0:T(8,128)(2,1)S(1)} %collective-permute-done.3.across_ref), custom_call_target="tpu_custom_call" | custom-call | tf_op jit(solution)/shard_map/across/pallas_call | solution.py:392
  14.3 0.2 %collective-permute-done.5.second_ref = bf16[1,128,128]{2,1,0:T(8,128)(2,1)S(1)} collective-permute-done((bf16[1,128,128]{2,1,0:T(8,128)(2,1)S(1)}, bf16[1,128,128]{2,1,0:T(8,128)(2,1)S(1)}, u32[]{:S(2)}, u32[]{:S(2)}) %collective-permute-start.5) | collective-permute-done | bytes 32800 | tf_op jit(solution)/shard_map/ppermute | solution.py:351
  14.5 0.5 %other_block.1 = (f32[64,512]{1,0:T(8,128)S(1)}, bf16[64,512]{1,0:T(8,128)(2,1)S(1)}) custom-call(bf16[2,1024,512]{2,1,0:T(8,128)(2,1)S(1)} %get-tuple-element.30.table, f32[8,8,4,2,8,128]{5,4,3,2,1,0:T(8,128)S(1)} %weigh.1.weighted_ref, f32[512,128]{1,0:T(8,128)S(1)} %get-tuple-element.42.real_ref, f32[512,128]{1,0:T(8,128)S(1)} %get-tuple-element.43.imag_ref, ...), custom_call_target="tpu_custom_call" | custom-call | tf_op jit(solution)/shard_map/other_block/pallas_call | solution.py:392
  15.1 0.3 %collective-permute-start.6 = (bf16[64,512]{1,0:T(8,128)(2,1)S(1)}, bf16[64,512]{1,0:T(8,128)(2,1)S(1)}, u32[]{:S(2)}, u32[]{:S(2)}) collective-permute-start(bf16[64,512]{1,0:T(8,128)(2,1)S(1)} %get-tuple-element.47), channel_id=1, source_target_pairs={{1,0},{0,1},{3,2},{2,3},{5,4},{4,5},{7,6},{6,7},{9,8},{8,9},{11,10... | collective-permute-start | bytes 196616 | tf_op jit(solution)/shard_map/ppermute | solution.py:351
  15.4 0.0 collective-permute-done.2.own_got_ref
  15.4 0.8 %settle.1 = (f32[3,64,512]{2,1,0:T(8,128)}, f32[64,512]{1,0:T(8,128)S(1)}) custom-call(f32[64,512]{1,0:T(8,128)S(1)} %get-tuple-element.33.own_kept_ref, f32[64,512]{1,0:T(8,128)S(1)} %collective-permute-done.2.own_got_ref, f32[64,512]{1,0:T(8,128)S(1)} %get-tuple-element.45.kept_ref), custom_call_target="tpu_custom_call" | custom-call | tf_op jit(solution)/shard_map/settle/pallas_call | solution.py:392
  16.2 0.2 %collective-permute-done.6.got_ref = bf16[64,512]{1,0:T(8,128)(2,1)S(1)} collective-permute-done((bf16[64,512]{1,0:T(8,128)(2,1)S(1)}, bf16[64,512]{1,0:T(8,128)(2,1)S(1)}, u32[]{:S(2)}, u32[]{:S(2)}) %collective-permute-start.6) | collective-permute-done | bytes 65568 | tf_op jit(solution)/shard_map/ppermute | solution.py:351
  16.4 0.7 %place.1 = f32[3,64,512]{2,1,0:T(8,128)} custom-call(s32[3]{0:T(128)S(4)} %get-tuple-element.28.is_own_ref, f32[64,512]{1,0:T(8,128)S(1)} %get-tuple-element.46.kept_ref, bf16[64,512]{1,0:T(8,128)(2,1)S(1)} %collective-permute-done.6.got_ref, f32[3,64,512]{2,1,0:T(8,128)} %get-tuple-element.48.steps_ref), custom_call_target="tpu_custom_call", output_to_operand_aliasing={{}: (3, {})} | custom-call | tf_op jit(solution)/shard_map/place/pallas_call | solution.py:392
  (6 shorter events, 0.1 us)
Async XLA Ops:
  0.9 6.4 %collective-permute-start = (bf16[1,144,128]{2,1,0:T(8,128)(2,1)S(1)}, bf16[1,144,128]{2,1,0:T(8,128)(2,1)S(1)}, u32[]{:S(2)}, u32[]{:S(2)}) collective-permute-start(bf16[1,144,128]{2,1,0:T(8,128)(2,1)S(1)} %prepare.1.after.refs_0_), channel_id=1, source_target_pairs={{8,0},{12,4},{0,8},{4,12},{9,1},{13,5},{1,9},{5,13},{10,2},{14,6},... | collective-permute-start | bytes 110600 | tf_op jit(solution)/shard_map/ppermute | solution.py:351
  5.0 8.9 %collective-permute-start.4 = (bf16[1,128,128]{2,1,0:T(8,128)(2,1)S(1)}, bf16[1,128,128]{2,1,0:T(8,128)(2,1)S(1)}, u32[]{:S(2)}, u32[]{:S(2)}) collective-permute-start(bf16[1,128,128]{2,1,0:T(8,128)(2,1)S(1)} %join.8), channel_id=1, source_target_pairs={{2,0},{0,2},{3,1},{1,3},{6,4},{4,6},{7,5},{5,7},{10,8},{8,10},{11,... | collective-permute-start | bytes 98312 | tf_op jit(solution)/shard_map/ppermute | solution.py:351
  7.4 5.2 %collective-permute-start.1 = (bf16[2,144,128]{2,1,0:T(8,128)(2,1)S(1)}, bf16[2,144,128]{2,1,0:T(8,128)(2,1)S(1)}, u32[]{:S(2)}, u32[]{:S(2)}) collective-permute-start(bf16[2,144,128]{2,1,0:T(8,128)(2,1)S(1)} %join.5.after.refs_0_), channel_id=1, source_target_pairs={{4,0},{0,4},{12,8},{8,12},{5,1},{1,5},{13,9},{9,13},{6,2},{2,6},{1... | collective-permute-start | bytes 221192 | tf_op jit(solution)/shard_map/ppermute | solution.py:351
  8.9 5.2 %collective-permute-start.3 = (bf16[2,128,128]{2,1,0:T(8,128)(2,1)S(1)}, bf16[2,128,128]{2,1,0:T(8,128)(2,1)S(1)}, u32[]{:S(2)}, u32[]{:S(2)}) collective-permute-start(bf16[2,128,128]{2,1,0:T(8,128)(2,1)S(1)} %join.7.refs_0_), channel_id=1, source_target_pairs={{6,0},{4,2},{2,4},{0,6},{14,8},{12,10},{10,12},{8,14},{7,1},{5,3},... | collective-permute-start | bytes 196616 | tf_op jit(solution)/shard_map/ppermute | solution.py:351
  10.6 3.9 %collective-permute-start.5 = (bf16[1,128,128]{2,1,0:T(8,128)(2,1)S(1)}, bf16[1,128,128]{2,1,0:T(8,128)(2,1)S(1)}, u32[]{:S(2)}, u32[]{:S(2)}) collective-permute-start(bf16[1,128,128]{2,1,0:T(8,128)(2,1)S(1)} %join.9), channel_id=1, source_target_pairs={{2,0},{0,2},{3,1},{1,3},{6,4},{4,6},{7,5},{5,7},{10,8},{8,10},{11,... | collective-permute-start | bytes 98312 | tf_op jit(solution)/shard_map/ppermute | solution.py:351
  13.7 1.7 %collective-permute-start.2 = (f32[64,512]{1,0:T(8,128)S(1)}, f32[64,512]{1,0:T(8,128)S(1)}, u32[]{:S(2)}, u32[]{:S(2)}) collective-permute-start(f32[64,512]{1,0:T(8,128)S(1)} %get-tuple-element.34), channel_id=1, source_target_pairs={{1,0},{0,1},{3,2},{2,3},{5,4},{4,5},{7,6},{6,7},{9,8},{8,9},{11,10... | collective-permute-start | bytes 393224 | tf_op jit(solution)/shard_map/ppermute | solution.py:351
  15.1 1.3 %collective-permute-start.6 = (bf16[64,512]{1,0:T(8,128)(2,1)S(1)}, bf16[64,512]{1,0:T(8,128)(2,1)S(1)}, u32[]{:S(2)}, u32[]{:S(2)}) collective-permute-start(bf16[64,512]{1,0:T(8,128)(2,1)S(1)} %get-tuple-element.47), channel_id=1, source_target_pairs={{1,0},{0,1},{3,2},{2,3},{5,4},{4,5},{7,6},{6,7},{9,8},{8,9},{11,10... | collective-permute-start | bytes 196616 | tf_op jit(solution)/shard_map/ppermute | solution.py:351
